TPU v7x, 512 devices: a whole 4x8x8 slice. The times are simulated.
512 devices in a mesh: tm: 8 (over y), tile: 64 (over x, z, core).
Axes of the slice: x: 4, y: 8, z: 8, core: 2. Of those that a mesh axis runs over, the one named last changes fastest.
Arguments:
- frames: bfloat16 [8, 64, 256, 128], P('tm', None, 'tile'), may hold values from -6 to 6
- back_shift: int32 [8, 2, 2, 256, 128], P('tm', None, None, 'tile'), may hold values from -2 to 1, as said below
- back_fraction: float32 [8, 2, 2, 256, 128], P('tm', None, None, 'tile'), may hold values from 0 to 1, as said below
- ahead_shift: int32 [8, 2, 2, 256, 128], P('tm', None, None, 'tile'), may hold values from -2 to 1, as said below
- ahead_fraction: float32 [8, 2, 2, 256, 128], P('tm', None, None, 'tile'), may hold values from 0 to 1, as said below
- back_mixer: bfloat16 [64, 192], replicated, may hold values from -0.75 to 0.75
- back_inner: bfloat16 [64, 576], replicated, may hold values from -0.25 to 0.25
- back_outer: bfloat16 [64, 576], replicated, may hold values from -0.25 to 0.25
- ahead_mixer: bfloat16 [64, 256], replicated, may hold values from -0.75 to 0.75
- ahead_inner: bfloat16 [64, 576], replicated, may hold values from -0.25 to 0.25
- ahead_outer: bfloat16 [64, 576], replicated, may hold values from -0.25 to 0.25
Outputs:
- back_features: bfloat16 [8, 64, 256, 128], P('tm', None, 'tile')
- ahead_features: bfloat16 [8, 64, 256, 128], P('tm', None, 'tile')
Inputs may be any that keep to these rules, and one draw needn't show every extreme that they name: `back_shift`: row and column shifts of each sampling position. `ahead_shift`: row and column shifts of each sampling position. `back_fraction`: fractional parts of each sampling position. `ahead_fraction`: fractional parts of each sampling position.
All inputs are finite; a program needn't handle non-finite values.
Results may differ from a plain program's by a relative error of at most 0.034.
Values may be sent and summed in bfloat16 or wider, within the bound.
No kernel may reach another device: no remote copies, remote signals or barrier semaphores. Data moves between devices by JAX's collectives and lax.ppermute only.
A program may use at most 128 MiB of HBM per device.

v0:
```python
import jax
import jax.numpy as jnp
from jax import lax
from jax.sharding import PartitionSpec as P

R = 2


def shifted(shard, axis, by):
    count = lax.axis_size(axis)
    pairs = [(i, i + by) for i in range(count) if 0 <= i + by < count]
    return lax.ppermute(shard, axis, pairs)


def extended(shard, sides, width):
    for axis, dim in sides:
        count, length = (lax.axis_size(axis), shard.shape[dim])
        up = [(i, (i + 1) % count) for i in range(count - 1)]
        down = [(j, i) for i, j in up]
        last = lax.slice_in_dim(shard, length - width, length, axis=dim)
        leading = lax.slice_in_dim(shard, 0, width, axis=dim)
        before = lax.ppermute(last, axis, up)
        after = lax.ppermute(leading, axis, down)
        shard = jnp.concatenate([before, shard, after], axis=dim)
    return shard


def leaky(values):
    return jnp.maximum(values, 0.1 * values)


def widen_cols(values, margin):
    spread = [(0, 0)] * (values.ndim - 1) + [(margin, margin)]
    return jnp.pad(values, spread)


def keep_cells(values, first_row, total_rows, first_col, total_cols):
    row_pos = first_row + lax.broadcasted_iota(jnp.int32, (1, values.shape[1], 1), 1)
    col_pos = first_col + lax.broadcasted_iota(jnp.int32, (1, 1, values.shape[2]), 2)
    inside = (row_pos >= 0) & (row_pos < total_rows) & (col_pos >= 0) & (col_pos < total_cols)
    return jnp.where(inside, values, jnp.zeros_like(values))


def sample_piece(source, shifts, fractions):
    rows = shifts.shape[1]
    cols = shifts.shape[2]
    level_count = 2 * R + 1
    low_weight = (1.0 - fractions[1]).astype(jnp.bfloat16)
    high_weight = fractions[1].astype(jnp.bfloat16)
    nothing = jnp.zeros((), jnp.bfloat16)
    level_ids = lax.broadcasted_iota(jnp.int32, (level_count, 1, 1), 0)
    size = min(128, cols)
    band = jnp.stack(
        [source[:, level : level + rows, 0 : size + 2 * R] for level in range(level_count)]
    )
    places = lax.broadcasted_iota(jnp.int32, (1, 1, size + 2 * R), 2)
    target_col = (lax.broadcasted_iota(jnp.int32, (1, size), 1) + shifts[1] + R)[:, :, None]
    low_part = low_weight[:, 0:size, None]
    high_part = high_weight[:, 0:size, None]
    horizontal = jnp.where(
        places == target_col, low_part, jnp.where(places == target_col + 1, high_part, nothing)
    )
    row_shift = shifts[0][None]
    outputs = []
    for rise in range(2):
        chosen = row_shift + R + rise == level_ids
        weights = jnp.where(chosen[..., None], horizontal[None], nothing)
        outputs.append(
            jnp.einsum("lcrv,lrjv->crj", band, weights, preferred_element_type=jnp.float32)
        )
    first_parts = outputs[0]
    second_parts = outputs[1]
    total = (1.0 - fractions[0])[None] * first_parts + fractions[0][None] * second_parts
    return total.astype(jnp.bfloat16)


def conv_piece(values, kernel):
    rows = values.shape[1] - 2
    cols = values.shape[2] - 2
    stacked = jnp.concatenate(
        [
            values[:, above : above + rows, across : across + cols]
            for above in range(3)
            for across in range(3)
        ],
        axis=0,
    )
    return jnp.einsum("ok,krw->orw", kernel, stacked, preferred_element_type=jnp.float32)


def join_piece(side_rows, priors, shifts, fractions, mixer):
    newest = sample_piece(priors[0], shifts[0], fractions[0])
    older = sample_piece(priors[1], shifts[1], fractions[1])
    inputs = jnp.concatenate([side_rows, newest, older], axis=0)
    return leaky(jnp.einsum("ok,krw->orw", mixer, inputs, preferred_element_type=jnp.float32))


def finish_link(joined, inner, outer, first_row, total_rows, first_col, total_cols):
    hidden = keep_cells(
        leaky(conv_piece(joined, inner)), first_row - 1, total_rows, first_col - 1, total_cols
    ).astype(jnp.bfloat16)
    return (joined[:, 2:-2, 2:-2].astype(jnp.float32) + conv_piece(hidden, outer)).astype(
        jnp.bfloat16
    )


def chain_wave(side_rows, shifts, fractions, mixer, inner, outer, direction):
    chain_len = lax.axis_size("tm")
    tile_rows = side_rows.shape[1]
    width = side_rows.shape[2]
    total_rows = tile_rows * lax.axis_size("tile")
    first_row = lax.axis_index("tile") * tile_rows
    channels = mixer.shape[0]
    carried = jnp.zeros((2, channels, tile_rows, width), jnp.bfloat16)
    for turn_index in range(chain_len):
        if direction < 0:
            priors = shifted(carried, "tm", -1)
        else:
            priors = shifted(carried, "tm", 1)
        widened = widen_cols(extended(priors, (("tile", 2),), R), R)
        own_joined = join_piece(side_rows, widened, shifts, fractions, mixer).astype(jnp.bfloat16)
        joined = widen_cols(extended(own_joined, (("tile", 1),), 2), 2)
        updated = finish_link(joined, inner, outer, first_row, total_rows, 0, width)
        carried = jnp.stack([updated, priors[0]])
    return carried[0]


def shards(
    frames,
    back_shift,
    back_fraction,
    ahead_shift,
    ahead_fraction,
    back_mixer,
    back_inner,
    back_outer,
    ahead_mixer,
    ahead_inner,
    ahead_outer,
):
    current = frames[0]
    backward = chain_wave(
        current, back_shift[0], back_fraction[0], back_mixer, back_inner, back_outer, -1
    )
    combined = jnp.concatenate([current, backward], axis=0)
    forward = chain_wave(
        combined, ahead_shift[0], ahead_fraction[0], ahead_mixer, ahead_inner, ahead_outer, 1
    )
    return (backward[None], forward[None])


def solution(mesh):
    in_specs = (
        P("tm", None, "tile", None),
        P("tm", None, None, "tile", None),
        P("tm", None, None, "tile", None),
        P("tm", None, None, "tile", None),
        P("tm", None, None, "tile", None),
        P(),
        P(),
        P(),
        P(),
        P(),
        P(),
    )
    out_specs = (P("tm", None, "tile", None), P("tm", None, "tile", None))
    return jax.shard_map(shards, mesh=mesh, in_specs=in_specs, out_specs=out_specs, check_vma=False)
```

profile of v0, /device:TPU:36, one launch (start us, length us, event | category | flops | bytes accessed | tf_op | source)
XLA Modules:
  0.0 710.7 jit_solution(6779292774927281785)
XLA Ops:
  3.0 3.5 collective-permute-start.40
  13.2 9.8 %collective-permute-start.2 = (bf16[2,64,2,128]{3,1,2,0:T(8,128)(2,1)S(1)}, bf16[2,64,2,128]{3,1,2,0:T(8,128)(2,1)S(1)}, u32[]{:S(2)}, u32[]{:S(2)}) collective-permute-start(bf16[2,64,2,128]{3,1,2,0:T(8,128)(2,1)S(1)} %get-tuple-element.67), channel_id=1, source_target_pairs={{1,0},{2,1},{3,2},{4,3},{5,4},{6,5},{7,6},{8,7},{9,8},{10,9},{11,1... | collective-permute-start | bytes 196616 | tf_op jit(solution)/shard_map/ppermute | solution.py:23
  25.0 5.7 collective-permute-done.1
  40.2 4.8 collective-permute-done.3
  47.6 3.6 collective-permute-start.5
  59.6 4.5 collective-permute-done.6
  73.6 4.9 collective-permute-done.8
  80.9 4.8 collective-permute-start.10
  92.6 5.3 collective-permute-done.11
  107.3 5.3 collective-permute-start.42
  117.0 5.6 collective-permute-start.15
  125.1 4.9 collective-permute-start.17
  132.2 5.5 collective-permute-done.16
  147.2 4.9 collective-permute-done.18
  154.6 5.3 collective-permute-start.20
  166.7 5.3 collective-permute-done.21
  181.5 4.9 collective-permute-done.23
  188.8 5.6 collective-permute-start.25
  201.3 5.3 collective-permute-done.26
  216.0 4.9 collective-permute-done.28
  223.4 5.6 collective-permute-start.30
  235.8 5.2 collective-permute-done.31
  252.0 3.4 collective-permute-done.33
  257.9 5.6 collective-permute-start.35
  271.6 4.0 collective-permute-done.36
  286.0 4.0 collective-permute-done.38
  297.0 4.9 collective-permute-done.43
  320.4 6.6 collective-permute-done.45
  331.4 5.3 collective-permute-done.46
  355.3 4.9 collective-permute-done.48
  378.7 6.1 collective-permute-done.50
  389.7 4.9 collective-permute-done.51
  413.2 4.9 collective-permute-done.53
  436.6 6.1 collective-permute-done.55
  447.1 5.3 collective-permute-done.56
  471.0 4.9 collective-permute-done.58
  494.5 6.1 collective-permute-done.60
  505.0 5.3 collective-permute-done.61
  528.9 4.9 collective-permute-done.63
  552.3 6.1 collective-permute-done.65
  563.0 5.1 collective-permute-done.66
  586.8 4.9 collective-permute-done.68
  610.2 6.1 collective-permute-done.70
  620.7 5.3 collective-permute-done.71
  644.6 4.9 collective-permute-done.73
  668.1 6.1 collective-permute-done.75
  678.6 5.3 collective-permute-done.76
  703.2 4.2 collective-permute-done.78
  (861 shorter events, 455.2 us)
Async XLA Ops:
  0.7 12.5 %collective-permute-start = (bf16[2,64,4,128]{3,1,2,0:T(8,128)(2,1)S(1)}, bf16[2,64,4,128]{3,1,2,0:T(8,128)(2,1)S(1)}, u32[]{:S(2)}, u32[]{:S(2)}) collective-permute-start(bf16[2,64,4,128]{3,1,2,0:T(8,128)(2,1)S(1)} %broadcast.519), channel_id=1, source_target_pairs={{64,0},{128,64},{192,128},{256,192},{320,256},{384,320},{448,384},... | collective-permute-start | bytes 393224 | tf_op jit(solution)/shard_map/ppermute | solution.py:12
  3.0 104.3 %collective-permute-start.40 = (bf16[2,64,4,128]{3,1,2,0:T(8,128)(2,1)S(1)}, bf16[2,64,4,128]{3,1,2,0:T(8,128)(2,1)S(1)}, u32[]{:S(2)}, u32[]{:S(2)}) collective-permute-start(bf16[2,64,4,128]{3,1,2,0:T(8,128)(2,1)S(1)} %broadcast.519), channel_id=1, source_target_pairs={{0,64},{64,128},{128,192},{192,256},{256,320},{320,384},{384,448},... | collective-permute-start | bytes 393224 | tf_op jit(solution)/shard_map/ppermute | solution.py:12
  13.2 11.8 %collective-permute-start.2 = (bf16[2,64,2,128]{3,1,2,0:T(8,128)(2,1)S(1)}, bf16[2,64,2,128]{3,1,2,0:T(8,128)(2,1)S(1)}, u32[]{:S(2)}, u32[]{:S(2)}) collective-permute-start(bf16[2,64,2,128]{3,1,2,0:T(8,128)(2,1)S(1)} %get-tuple-element.67), channel_id=1, source_target_pairs={{1,0},{2,1},{3,2},{4,3},{5,4},{6,5},{7,6},{8,7},{9,8},{10,9},{11,1... | collective-permute-start | bytes 196616 | tf_op jit(solution)/shard_map/ppermute | solution.py:23
  23.0 7.7 %collective-permute-start.1 = (bf16[2,64,2,128]{3,1,2,0:T(8,128)(2,1)S(1)}, bf16[2,64,2,128]{3,1,2,0:T(8,128)(2,1)S(1)}, u32[]{:S(2)}, u32[]{:S(2)}) collective-permute-start(bf16[2,64,2,128]{3,1,2,0:T(8,128)(2,1)S(1)} %get-tuple-element.66), channel_id=1, source_target_pairs={{0,1},{1,2},{2,3},{3,4},{4,5},{5,6},{6,7},{7,8},{8,9},{9,10},{10,1... | collective-permute-start | bytes 196616 | tf_op jit(solution)/shard_map/ppermute | solution.py:22
  37.7 7.3 %collective-permute-start.3 = (bf16[64,2,128]{2,0,1:T(8,128)(2,1)S(1)}, bf16[64,2,128]{2,0,1:T(8,128)(2,1)S(1)}, u32[]{:S(2)}, u32[]{:S(2)}) collective-permute-start(bf16[64,2,128]{2,0,1:T(8,128)(2,1)S(1)} %get-tuple-element.98), channel_id=1, source_target_pairs={{0,1},{1,2},{2,3},{3,4},{4,5},{5,6},{6,7},{7,8},{8,9},{9,10},{10,1... | collective-permute-start | bytes 98312 | tf_op jit(solution)/shard_map/ppermute | solution.py:22
  56.4 7.7 %collective-permute-start.6 = (bf16[2,64,2,128]{3,1,2,0:T(8,128)(2,1)S(1)}, bf16[2,64,2,128]{3,1,2,0:T(8,128)(2,1)S(1)}, u32[]{:S(2)}, u32[]{:S(2)}) collective-permute-start(bf16[2,64,2,128]{3,1,2,0:T(8,128)(2,1)S(1)} %get-tuple-element.64), channel_id=1, source_target_pairs={{0,1},{1,2},{2,3},{3,4},{4,5},{5,6},{6,7},{7,8},{8,9},{9,10},{10,1... | collective-permute-start | bytes 196616 | tf_op jit(solution)/shard_map/ppermute | solution.py:22
  71.1 7.3 %collective-permute-start.8 = (bf16[64,2,128]{2,0,1:T(8,128)(2,1)S(1)}, bf16[64,2,128]{2,0,1:T(8,128)(2,1)S(1)}, u32[]{:S(2)}, u32[]{:S(2)}) collective-permute-start(bf16[64,2,128]{2,0,1:T(8,128)(2,1)S(1)} %get-tuple-element.96), channel_id=1, source_target_pairs={{0,1},{1,2},{2,3},{3,4},{4,5},{5,6},{6,7},{7,8},{8,9},{9,10},{10,1... | collective-permute-start | bytes 98312 | tf_op jit(solution)/shard_map/ppermute | solution.py:22
  90.2 7.7 %collective-permute-start.11 = (bf16[2,64,2,128]{3,1,2,0:T(8,128)(2,1)S(1)}, bf16[2,64,2,128]{3,1,2,0:T(8,128)(2,1)S(1)}, u32[]{:S(2)}, u32[]{:S(2)}) collective-permute-start(bf16[2,64,2,128]{3,1,2,0:T(8,128)(2,1)S(1)} %get-tuple-element.62), channel_id=1, source_target_pairs={{0,1},{1,2},{2,3},{3,4},{4,5},{5,6},{6,7},{7,8},{8,9},{9,10},{10,1... | collective-permute-start | bytes 196616 | tf_op jit(solution)/shard_map/ppermute | solution.py:22
  103.0 11.6 %collective-permute-start.14 = (bf16[64,2,128]{2,0,1:T(8,128)(2,1)S(1)}, bf16[64,2,128]{2,0,1:T(8,128)(2,1)S(1)}, u32[]{:S(2)}, u32[]{:S(2)}) collective-permute-start(bf16[64,2,128]{2,0,1:T(8,128)(2,1)S(1)} %get-tuple-element.95), channel_id=1, source_target_pairs={{1,0},{2,1},{3,2},{4,3},{5,4},{6,5},{7,6},{8,7},{9,8},{10,9},{11,1... | collective-permute-start | bytes 98312 | tf_op jit(solution)/shard_map/ppermute | solution.py:23
  104.9 9.7 %collective-permute-start.13 = (bf16[64,2,128]{2,0,1:T(8,128)(2,1)S(1)}, bf16[64,2,128]{2,0,1:T(8,128)(2,1)S(1)}, u32[]{:S(2)}, u32[]{:S(2)}) collective-permute-start(bf16[64,2,128]{2,0,1:T(8,128)(2,1)S(1)} %get-tuple-element.94), channel_id=1, source_target_pairs={{0,1},{1,2},{2,3},{3,4},{4,5},{5,6},{6,7},{7,8},{8,9},{9,10},{10,1... | collective-permute-start | bytes 98312 | tf_op jit(solution)/shard_map/ppermute | solution.py:22
  107.3 15.3 %collective-permute-start.42 = (bf16[2,64,2,128]{3,1,2,0:T(8,128)(2,1)S(1)}, bf16[2,64,2,128]{3,1,2,0:T(8,128)(2,1)S(1)}, u32[]{:S(2)}, u32[]{:S(2)}) collective-permute-start(bf16[2,64,2,128]{3,1,2,0:T(8,128)(2,1)S(1)} %get-tuple-element.51), channel_id=1, source_target_pairs={{1,0},{2,1},{3,2},{4,3},{5,4},{6,5},{7,6},{8,7},{9,8},{10,9},{11,1... | collective-permute-start | bytes 196616 | tf_op jit(solution)/shard_map/ppermute | solution.py:23
  112.6 10.0 %collective-permute-start.41 = (bf16[2,64,2,128]{3,1,2,0:T(8,128)(2,1)S(1)}, bf16[2,64,2,128]{3,1,2,0:T(8,128)(2,1)S(1)}, u32[]{:S(2)}, u32[]{:S(2)}) collective-permute-start(bf16[2,64,2,128]{3,1,2,0:T(8,128)(2,1)S(1)} %get-tuple-element.50), channel_id=1, source_target_pairs={{0,1},{1,2},{2,3},{3,4},{4,5},{5,6},{6,7},{7,8},{8,9},{9,10},{10,1... | collective-permute-start | bytes 196616 | tf_op jit(solution)/shard_map/ppermute | solution.py:22
  117.0 8.1 %collective-permute-start.15 = (bf16[2,64,4,128]{3,1,2,0:T(8,128)(2,1)S(1)}, bf16[2,64,4,128]{3,1,2,0:T(8,128)(2,1)S(1)}, u32[]{:S(2)}, u32[]{:S(2)}) collective-permute-start(bf16[2,64,4,128]{3,1,2,0:T(8,128)(2,1)S(1)} %pad_maximum_fusion.11), channel_id=1, source_target_pairs={{64,0},{128,64},{192,128},{256,192},{320,256},{384,320},{448,384},... | collective-permute-start | bytes 393224 | tf_op jit(solution)/shard_map/ppermute | solution.py:12
  130.0 7.7 %collective-permute-start.16 = (bf16[2,64,2,128]{3,1,2,0:T(8,128)(2,1)S(1)}, bf16[2,64,2,128]{3,1,2,0:T(8,128)(2,1)S(1)}, u32[]{:S(2)}, u32[]{:S(2)}) collective-permute-start(bf16[2,64,2,128]{3,1,2,0:T(8,128)(2,1)S(1)} %get-tuple-element.60), channel_id=1, source_target_pairs={{0,1},{1,2},{2,3},{3,4},{4,5},{5,6},{6,7},{7,8},{8,9},{9,10},{10,1... | collective-permute-start | bytes 196616 | tf_op jit(solution)/shard_map/ppermute | solution.py:22
  144.8 7.3 %collective-permute-start.18 = (bf16[64,2,128]{2,0,1:T(8,128)(2,1)S(1)}, bf16[64,2,128]{2,0,1:T(8,128)(2,1)S(1)}, u32[]{:S(2)}, u32[]{:S(2)}) collective-permute-start(bf16[64,2,128]{2,0,1:T(8,128)(2,1)S(1)} %get-tuple-element.92), channel_id=1, source_target_pairs={{0,1},{1,2},{2,3},{3,4},{4,5},{5,6},{6,7},{7,8},{8,9},{9,10},{10,1... | collective-permute-start | bytes 98312 | tf_op jit(solution)/shard_map/ppermute | solution.py:22
  154.6 7.8 %collective-permute-start.20 = (bf16[2,64,4,128]{3,1,2,0:T(8,128)(2,1)S(1)}, bf16[2,64,4,128]{3,1,2,0:T(8,128)(2,1)S(1)}, u32[]{:S(2)}, u32[]{:S(2)}) collective-permute-start(bf16[2,64,4,128]{3,1,2,0:T(8,128)(2,1)S(1)} %pad_maximum_fusion.12), channel_id=1, source_target_pairs={{64,0},{128,64},{192,128},{256,192},{320,256},{384,320},{448,384},... | collective-permute-start | bytes 393224 | tf_op jit(solution)/shard_map/ppermute | solution.py:12
  164.3 7.7 %collective-permute-start.21 = (bf16[2,64,2,128]{3,1,2,0:T(8,128)(2,1)S(1)}, bf16[2,64,2,128]{3,1,2,0:T(8,128)(2,1)S(1)}, u32[]{:S(2)}, u32[]{:S(2)}) collective-permute-start(bf16[2,64,2,128]{3,1,2,0:T(8,128)(2,1)S(1)} %get-tuple-element.58), channel_id=1, source_target_pairs={{0,1},{1,2},{2,3},{3,4},{4,5},{5,6},{6,7},{7,8},{8,9},{9,10},{10,1... | collective-permute-start | bytes 196616 | tf_op jit(solution)/shard_map/ppermute | solution.py:22
  179.0 7.3 %collective-permute-start.23 = (bf16[64,2,128]{2,0,1:T(8,128)(2,1)S(1)}, bf16[64,2,128]{2,0,1:T(8,128)(2,1)S(1)}, u32[]{:S(2)}, u32[]{:S(2)}) collective-permute-start(bf16[64,2,128]{2,0,1:T(8,128)(2,1)S(1)} %get-tuple-element.90), channel_id=1, source_target_pairs={{0,1},{1,2},{2,3},{3,4},{4,5},{5,6},{6,7},{7,8},{8,9},{9,10},{10,1... | collective-permute-start | bytes 98312 | tf_op jit(solution)/shard_map/ppermute | solution.py:22
  188.8 8.1 %collective-permute-start.25 = (bf16[2,64,4,128]{3,1,2,0:T(8,128)(2,1)S(1)}, bf16[2,64,4,128]{3,1,2,0:T(8,128)(2,1)S(1)}, u32[]{:S(2)}, u32[]{:S(2)}) collective-permute-start(bf16[2,64,4,128]{3,1,2,0:T(8,128)(2,1)S(1)} %pad_maximum_fusion.13), channel_id=1, source_target_pairs={{64,0},{128,64},{192,128},{256,192},{320,256},{384,320},{448,384},... | collective-permute-start | bytes 393224 | tf_op jit(solution)/shard_map/ppermute | solution.py:12
  198.8 7.7 %collective-permute-start.26 = (bf16[2,64,2,128]{3,1,2,0:T(8,128)(2,1)S(1)}, bf16[2,64,2,128]{3,1,2,0:T(8,128)(2,1)S(1)}, u32[]{:S(2)}, u32[]{:S(2)}) collective-permute-start(bf16[2,64,2,128]{3,1,2,0:T(8,128)(2,1)S(1)} %get-tuple-element.56), channel_id=1, source_target_pairs={{0,1},{1,2},{2,3},{3,4},{4,5},{5,6},{6,7},{7,8},{8,9},{9,10},{10,1... | collective-permute-start | bytes 196616 | tf_op jit(solution)/shard_map/ppermute | solution.py:22
  213.5 7.3 %collective-permute-start.28 = (bf16[64,2,128]{2,0,1:T(8,128)(2,1)S(1)}, bf16[64,2,128]{2,0,1:T(8,128)(2,1)S(1)}, u32[]{:S(2)}, u32[]{:S(2)}) collective-permute-start(bf16[64,2,128]{2,0,1:T(8,128)(2,1)S(1)} %get-tuple-element.88), channel_id=1, source_target_pairs={{0,1},{1,2},{2,3},{3,4},{4,5},{5,6},{6,7},{7,8},{8,9},{9,10},{10,1... | collective-permute-start | bytes 98312 | tf_op jit(solution)/shard_map/ppermute | solution.py:22
  223.4 8.1 %collective-permute-start.30 = (bf16[2,64,4,128]{3,1,2,0:T(8,128)(2,1)S(1)}, bf16[2,64,4,128]{3,1,2,0:T(8,128)(2,1)S(1)}, u32[]{:S(2)}, u32[]{:S(2)}) collective-permute-start(bf16[2,64,4,128]{3,1,2,0:T(8,128)(2,1)S(1)} %pad_maximum_fusion.14), channel_id=1, source_target_pairs={{64,0},{128,64},{192,128},{256,192},{320,256},{384,320},{448,384},... | collective-permute-start | bytes 393224 | tf_op jit(solution)/shard_map/ppermute | solution.py:12
  233.4 7.7 %collective-permute-start.31 = (bf16[2,64,2,128]{3,1,2,0:T(8,128)(2,1)S(1)}, bf16[2,64,2,128]{3,1,2,0:T(8,128)(2,1)S(1)}, u32[]{:S(2)}, u32[]{:S(2)}) collective-permute-start(bf16[2,64,2,128]{3,1,2,0:T(8,128)(2,1)S(1)} %get-tuple-element.54), channel_id=1, source_target_pairs={{0,1},{1,2},{2,3},{3,4},{4,5},{5,6},{6,7},{7,8},{8,9},{9,10},{10,1... | collective-permute-start | bytes 196616 | tf_op jit(solution)/shard_map/ppermute | solution.py:22
  248.1 7.3 %collective-permute-start.33 = (bf16[64,2,128]{2,0,1:T(8,128)(2,1)S(1)}, bf16[64,2,128]{2,0,1:T(8,128)(2,1)S(1)}, u32[]{:S(2)}, u32[]{:S(2)}) collective-permute-start(bf16[64,2,128]{2,0,1:T(8,128)(2,1)S(1)} %get-tuple-element.86), channel_id=1, source_target_pairs={{0,1},{1,2},{2,3},{3,4},{4,5},{5,6},{6,7},{7,8},{8,9},{9,10},{10,1... | collective-permute-start | bytes 98312 | tf_op jit(solution)/shard_map/ppermute | solution.py:22
  257.9 8.1 %collective-permute-start.35 = (bf16[2,64,4,128]{3,1,2,0:T(8,128)(2,1)S(1)}, bf16[2,64,4,128]{3,1,2,0:T(8,128)(2,1)S(1)}, u32[]{:S(2)}, u32[]{:S(2)}) collective-permute-start(bf16[2,64,4,128]{3,1,2,0:T(8,128)(2,1)S(1)} %pad_maximum_fusion.15), channel_id=1, source_target_pairs={{64,0},{128,64},{192,128},{256,192},{320,256},{384,320},{448,384},... | collective-permute-start | bytes 393224 | tf_op jit(solution)/shard_map/ppermute | solution.py:12
  267.9 7.7 %collective-permute-start.36 = (bf16[2,64,2,128]{3,1,2,0:T(8,128)(2,1)S(1)}, bf16[2,64,2,128]{3,1,2,0:T(8,128)(2,1)S(1)}, u32[]{:S(2)}, u32[]{:S(2)}) collective-permute-start(bf16[2,64,2,128]{3,1,2,0:T(8,128)(2,1)S(1)} %get-tuple-element.52), channel_id=1, source_target_pairs={{0,1},{1,2},{2,3},{3,4},{4,5},{5,6},{6,7},{7,8},{8,9},{9,10},{10,1... | collective-permute-start | bytes 196616 | tf_op jit(solution)/shard_map/ppermute | solution.py:22
  282.6 7.3 %collective-permute-start.38 = (bf16[64,2,128]{2,0,1:T(8,128)(2,1)S(1)}, bf16[64,2,128]{2,0,1:T(8,128)(2,1)S(1)}, u32[]{:S(2)}, u32[]{:S(2)}) collective-permute-start(bf16[64,2,128]{2,0,1:T(8,128)(2,1)S(1)} %get-tuple-element.84), channel_id=1, source_target_pairs={{0,1},{1,2},{2,3},{3,4},{4,5},{5,6},{6,7},{7,8},{8,9},{9,10},{10,1... | collective-permute-start | bytes 98312 | tf_op jit(solution)/shard_map/ppermute | solution.py:22
  294.5 7.3 %collective-permute-start.43 = (bf16[64,2,128]{2,0,1:T(8,128)(2,1)S(1)}, bf16[64,2,128]{2,0,1:T(8,128)(2,1)S(1)}, u32[]{:S(2)}, u32[]{:S(2)}) collective-permute-start(bf16[64,2,128]{2,0,1:T(8,128)(2,1)S(1)} %get-tuple-element.82), channel_id=1, source_target_pairs={{0,1},{1,2},{2,3},{3,4},{4,5},{5,6},{6,7},{7,8},{8,9},{9,10},{10,1... | collective-permute-start | bytes 98312 | tf_op jit(solution)/shard_map/ppermute | solution.py:22
  318.5 8.5 %collective-permute-start.45 = (bf16[2,64,4,128]{3,1,2,0:T(8,128)(2,1)S(1)}, bf16[2,64,4,128]{3,1,2,0:T(8,128)(2,1)S(1)}, u32[]{:S(2)}, u32[]{:S(2)}) collective-permute-start(bf16[2,64,4,128]{3,1,2,0:T(8,128)(2,1)S(1)} %pad_maximum_fusion.16), channel_id=1, source_target_pairs={{0,64},{64,128},{128,192},{192,256},{256,320},{320,384},{384,448},... | collective-permute-start | bytes 393224 | tf_op jit(solution)/shard_map/ppermute | solution.py:12
  329.0 7.7 %collective-permute-start.46 = (bf16[2,64,2,128]{3,1,2,0:T(8,128)(2,1)S(1)}, bf16[2,64,2,128]{3,1,2,0:T(8,128)(2,1)S(1)}, u32[]{:S(2)}, u32[]{:S(2)}) collective-permute-start(bf16[2,64,2,128]{3,1,2,0:T(8,128)(2,1)S(1)} %get-tuple-element.48), channel_id=1, source_target_pairs={{0,1},{1,2},{2,3},{3,4},{4,5},{5,6},{6,7},{7,8},{8,9},{9,10},{10,1... | collective-permute-start | bytes 196616 | tf_op jit(solution)/shard_map/ppermute | solution.py:22
  352.9 7.3 %collective-permute-start.48 = (bf16[64,2,128]{2,0,1:T(8,128)(2,1)S(1)}, bf16[64,2,128]{2,0,1:T(8,128)(2,1)S(1)}, u32[]{:S(2)}, u32[]{:S(2)}) collective-permute-start(bf16[64,2,128]{2,0,1:T(8,128)(2,1)S(1)} %get-tuple-element.80), channel_id=1, source_target_pairs={{0,1},{1,2},{2,3},{3,4},{4,5},{5,6},{6,7},{7,8},{8,9},{9,10},{10,1... | collective-permute-start | bytes 98312 | tf_op jit(solution)/shard_map/ppermute | solution.py:22
  376.8 8.1 %collective-permute-start.50 = (bf16[2,64,4,128]{3,1,2,0:T(8,128)(2,1)S(1)}, bf16[2,64,4,128]{3,1,2,0:T(8,128)(2,1)S(1)}, u32[]{:S(2)}, u32[]{:S(2)}) collective-permute-start(bf16[2,64,4,128]{3,1,2,0:T(8,128)(2,1)S(1)} %pad_maximum_fusion.17), channel_id=1, source_target_pairs={{0,64},{64,128},{128,192},{192,256},{256,320},{320,384},{384,448},... | collective-permute-start | bytes 393224 | tf_op jit(solution)/shard_map/ppermute | solution.py:12
  386.8 7.7 %collective-permute-start.51 = (bf16[2,64,2,128]{3,1,2,0:T(8,128)(2,1)S(1)}, bf16[2,64,2,128]{3,1,2,0:T(8,128)(2,1)S(1)}, u32[]{:S(2)}, u32[]{:S(2)}) collective-permute-start(bf16[2,64,2,128]{3,1,2,0:T(8,128)(2,1)S(1)} %get-tuple-element.46), channel_id=1, source_target_pairs={{0,1},{1,2},{2,3},{3,4},{4,5},{5,6},{6,7},{7,8},{8,9},{9,10},{10,1... | collective-permute-start | bytes 196616 | tf_op jit(solution)/shard_map/ppermute | solution.py:22
  410.7 7.3 %collective-permute-start.53 = (bf16[64,2,128]{2,0,1:T(8,128)(2,1)S(1)}, bf16[64,2,128]{2,0,1:T(8,128)(2,1)S(1)}, u32[]{:S(2)}, u32[]{:S(2)}) collective-permute-start(bf16[64,2,128]{2,0,1:T(8,128)(2,1)S(1)} %get-tuple-element.78), channel_id=1, source_target_pairs={{0,1},{1,2},{2,3},{3,4},{4,5},{5,6},{6,7},{7,8},{8,9},{9,10},{10,1... | collective-permute-start | bytes 98312 | tf_op jit(solution)/shard_map/ppermute | solution.py:22
  434.7 8.1 %collective-permute-start.55 = (bf16[2,64,4,128]{3,1,2,0:T(8,128)(2,1)S(1)}, bf16[2,64,4,128]{3,1,2,0:T(8,128)(2,1)S(1)}, u32[]{:S(2)}, u32[]{:S(2)}) collective-permute-start(bf16[2,64,4,128]{3,1,2,0:T(8,128)(2,1)S(1)} %pad_maximum_fusion.18), channel_id=1, source_target_pairs={{0,64},{64,128},{128,192},{192,256},{256,320},{320,384},{384,448},... | collective-permute-start | bytes 393224 | tf_op jit(solution)/shard_map/ppermute | solution.py:12
  444.7 7.7 %collective-permute-start.56 = (bf16[2,64,2,128]{3,1,2,0:T(8,128)(2,1)S(1)}, bf16[2,64,2,128]{3,1,2,0:T(8,128)(2,1)S(1)}, u32[]{:S(2)}, u32[]{:S(2)}) collective-permute-start(bf16[2,64,2,128]{3,1,2,0:T(8,128)(2,1)S(1)} %get-tuple-element.44), channel_id=1, source_target_pairs={{0,1},{1,2},{2,3},{3,4},{4,5},{5,6},{6,7},{7,8},{8,9},{9,10},{10,1... | collective-permute-start | bytes 196616 | tf_op jit(solution)/shard_map/ppermute | solution.py:22
  468.6 7.3 %collective-permute-start.58 = (bf16[64,2,128]{2,0,1:T(8,128)(2,1)S(1)}, bf16[64,2,128]{2,0,1:T(8,128)(2,1)S(1)}, u32[]{:S(2)}, u32[]{:S(2)}) collective-permute-start(bf16[64,2,128]{2,0,1:T(8,128)(2,1)S(1)} %get-tuple-element.76), channel_id=1, source_target_pairs={{0,1},{1,2},{2,3},{3,4},{4,5},{5,6},{6,7},{7,8},{8,9},{9,10},{10,1... | collective-permute-start | bytes 98312 | tf_op jit(solution)/shard_map/ppermute | solution.py:22
  492.6 8.1 %collective-permute-start.60 = (bf16[2,64,4,128]{3,1,2,0:T(8,128)(2,1)S(1)}, bf16[2,64,4,128]{3,1,2,0:T(8,128)(2,1)S(1)}, u32[]{:S(2)}, u32[]{:S(2)}) collective-permute-start(bf16[2,64,4,128]{3,1,2,0:T(8,128)(2,1)S(1)} %pad_maximum_fusion.19), channel_id=1, source_target_pairs={{0,64},{64,128},{128,192},{192,256},{256,320},{320,384},{384,448},... | collective-permute-start | bytes 393224 | tf_op jit(solution)/shard_map/ppermute | solution.py:12
  502.6 7.7 %collective-permute-start.61 = (bf16[2,64,2,128]{3,1,2,0:T(8,128)(2,1)S(1)}, bf16[2,64,2,128]{3,1,2,0:T(8,128)(2,1)S(1)}, u32[]{:S(2)}, u32[]{:S(2)}) collective-permute-start(bf16[2,64,2,128]{3,1,2,0:T(8,128)(2,1)S(1)} %get-tuple-element.42), channel_id=1, source_target_pairs={{0,1},{1,2},{2,3},{3,4},{4,5},{5,6},{6,7},{7,8},{8,9},{9,10},{10,1... | collective-permute-start | bytes 196616 | tf_op jit(solution)/shard_map/ppermute | solution.py:22
  526.5 7.3 %collective-permute-start.63 = (bf16[64,2,128]{2,0,1:T(8,128)(2,1)S(1)}, bf16[64,2,128]{2,0,1:T(8,128)(2,1)S(1)}, u32[]{:S(2)}, u32[]{:S(2)}) collective-permute-start(bf16[64,2,128]{2,0,1:T(8,128)(2,1)S(1)} %get-tuple-element.74), channel_id=1, source_target_pairs={{0,1},{1,2},{2,3},{3,4},{4,5},{5,6},{6,7},{7,8},{8,9},{9,10},{10,1... | collective-permute-start | bytes 98312 | tf_op jit(solution)/shard_map/ppermute | solution.py:22
  550.4 8.1 %collective-permute-start.65 = (bf16[2,64,4,128]{3,1,2,0:T(8,128)(2,1)S(1)}, bf16[2,64,4,128]{3,1,2,0:T(8,128)(2,1)S(1)}, u32[]{:S(2)}, u32[]{:S(2)}) collective-permute-start(bf16[2,64,4,128]{3,1,2,0:T(8,128)(2,1)S(1)} %pad_maximum_fusion.20), channel_id=1, source_target_pairs={{0,64},{64,128},{128,192},{192,256},{256,320},{320,384},{384,448},... | collective-permute-start | bytes 393224 | tf_op jit(solution)/shard_map/ppermute | solution.py:12
  560.4 7.7 %collective-permute-start.66 = (bf16[2,64,2,128]{3,1,2,0:T(8,128)(2,1)S(1)}, bf16[2,64,2,128]{3,1,2,0:T(8,128)(2,1)S(1)}, u32[]{:S(2)}, u32[]{:S(2)}) collective-permute-start(bf16[2,64,2,128]{3,1,2,0:T(8,128)(2,1)S(1)} %get-tuple-element.40), channel_id=1, source_target_pairs={{0,1},{1,2},{2,3},{3,4},{4,5},{5,6},{6,7},{7,8},{8,9},{9,10},{10,1... | collective-permute-start | bytes 196616 | tf_op jit(solution)/shard_map/ppermute | solution.py:22
  608.3 8.1 %collective-permute-start.70 = (bf16[2,64,4,128]{3,1,2,0:T(8,128)(2,1)S(1)}, bf16[2,64,4,128]{3,1,2,0:T(8,128)(2,1)S(1)}, u32[]{:S(2)}, u32[]{:S(2)}) collective-permute-start(bf16[2,64,4,128]{3,1,2,0:T(8,128)(2,1)S(1)} %pad_maximum_fusion.21), channel_id=1, source_target_pairs={{0,64},{64,128},{128,192},{192,256},{256,320},{320,384},{384,448},... | collective-permute-start | bytes 393224 | tf_op jit(solution)/shard_map/ppermute | solution.py:12
  618.3 7.7 %collective-permute-start.71 = (bf16[2,64,2,128]{3,1,2,0:T(8,128)(2,1)S(1)}, bf16[2,64,2,128]{3,1,2,0:T(8,128)(2,1)S(1)}, u32[]{:S(2)}, u32[]{:S(2)}) collective-permute-start(bf16[2,64,2,128]{3,1,2,0:T(8,128)(2,1)S(1)} %get-tuple-element.38), channel_id=1, source_target_pairs={{0,1},{1,2},{2,3},{3,4},{4,5},{5,6},{6,7},{7,8},{8,9},{9,10},{10,1... | collective-permute-start | bytes 196616 | tf_op jit(solution)/shard_map/ppermute | solution.py:22
  642.2 7.3 %collective-permute-start.73 = (bf16[64,2,128]{2,0,1:T(8,128)(2,1)S(1)}, bf16[64,2,128]{2,0,1:T(8,128)(2,1)S(1)}, u32[]{:S(2)}, u32[]{:S(2)}) collective-permute-start(bf16[64,2,128]{2,0,1:T(8,128)(2,1)S(1)} %get-tuple-element.70), channel_id=1, source_target_pairs={{0,1},{1,2},{2,3},{3,4},{4,5},{5,6},{6,7},{7,8},{8,9},{9,10},{10,1... | collective-permute-start | bytes 98312 | tf_op jit(solution)/shard_map/ppermute | solution.py:22
  666.2 8.1 %collective-permute-start.75 = (bf16[2,64,4,128]{3,1,2,0:T(8,128)(2,1)S(1)}, bf16[2,64,4,128]{3,1,2,0:T(8,128)(2,1)S(1)}, u32[]{:S(2)}, u32[]{:S(2)}) collective-permute-start(bf16[2,64,4,128]{3,1,2,0:T(8,128)(2,1)S(1)} %pad_maximum_fusion.22), channel_id=1, source_target_pairs={{0,64},{64,128},{128,192},{192,256},{256,320},{320,384},{384,448},... | collective-permute-start | bytes 393224 | tf_op jit(solution)/shard_map/ppermute | solution.py:12
  676.2 7.7 %collective-permute-start.76 = (bf16[2,64,2,128]{3,1,2,0:T(8,128)(2,1)S(1)}, bf16[2,64,2,128]{3,1,2,0:T(8,128)(2,1)S(1)}, u32[]{:S(2)}, u32[]{:S(2)}) collective-permute-start(bf16[2,64,2,128]{3,1,2,0:T(8,128)(2,1)S(1)} %get-tuple-element.36), channel_id=1, source_target_pairs={{0,1},{1,2},{2,3},{3,4},{4,5},{5,6},{6,7},{7,8},{8,9},{9,10},{10,1... | collective-permute-start | bytes 196616 | tf_op jit(solution)/shard_map/ppermute | solution.py:22
  700.1 7.3 %collective-permute-start.78 = (bf16[64,2,128]{2,0,1:T(8,128)(2,1)S(1)}, bf16[64,2,128]{2,0,1:T(8,128)(2,1)S(1)}, u32[]{:S(2)}, u32[]{:S(2)}) collective-permute-start(bf16[64,2,128]{2,0,1:T(8,128)(2,1)S(1)} %get-tuple-element.68), channel_id=1, source_target_pairs={{0,1},{1,2},{2,3},{3,4},{4,5},{5,6},{6,7},{7,8},{8,9},{9,10},{10,1... | collective-permute-start | bytes 98312 | tf_op jit(solution)/shard_map/ppermute | solution.py:22
  (69 other events, 823.7 us)
where the time goes:
time: 723 us; the launch traced here: 711 us
  waiting for transfers between devices  208 us (29%)
  starting transfers between devices  207 us (29%)
  local copies, waits for them, and re-layouts  156 us (22%)
  matrix products  122 us (17%)
  other arithmetic  12.4 us (2%)
    ppermute x32, waiting for transfers between devices, extended(): before = lax.ppermute(last, axis, up)  147 us
    unnamed x433, local copies, waits for them, and re-layouts  132 us
    dot_general x64, matrix products, sample_piece(): jnp.einsum('lcrv,lrjv->crj', band, weights, preferred_element_type=jnp.fl...  90 us
    ppermute x32, starting transfers between devices, extended(): before = lax.ppermute(last, axis, up)  76.5 us
    ppermute x32, starting transfers between devices, extended(): after = lax.ppermute(leading, axis, down)  75.7 us
    ppermute x16, waiting for transfers between devices, shifted(): return lax.ppermute(shard, axis, pairs)  60.4 us
    ppermute x16, starting transfers between devices, shifted(): return lax.ppermute(shard, axis, pairs)  55.2 us
    dot_general x32, matrix products, conv_piece(): jnp.einsum('ok,krw->orw', kernel, stacked, preferred_element_type=jnp.flo...  29.2 us
  transfers between devices with their start and end apart: 80, of which 44 were waited for; matrix products, arithmetic and copies ran while one was open for 5% of the time, Pallas kernels for 0%

commit v1 on v0

v1 whole, which is shorter than its diff:
```python
import functools

import jax
import jax.numpy as jnp
from jax import lax
from jax.experimental import pallas as pl
from jax.experimental.pallas import tpu as pltpu
from jax.sharding import PartitionSpec as P

R = 2
C = 64
W = 128
ROWS = 4
H = 256
FRAMES = 8
EXT = ROWS + 2 * R
ACC = jnp.bfloat16


def leaky(values):
    return jnp.maximum(values, 0.1 * values)


def tap_weights(params, row0):
    sy, sx, qy, qx = (params[n] for n in range(4))
    rows = row0 + lax.broadcasted_iota(jnp.int32, (EXT, W), 0)
    cols = lax.broadcasted_iota(jnp.int32, (EXT, W), 1)
    out = {}
    across = []
    for dx in range(-R, R + 1):
        u = jnp.where(sx == dx, 1.0 - qx, jnp.where(sx == dx - 1, qx, 0.0))
        across.append(jnp.where((cols + dx >= 0) & (cols + dx < W), u, 0.0))
    for dy in range(-R, R + 1):
        v = jnp.where(sy == dy, 1.0 - qy, jnp.where(sy == dy - 1, qy, 0.0))
        v = jnp.where((rows + dy >= 0) & (rows + dy < H), v, 0.0)
        for dx in range(-R, R + 1):
            w = v * across[dx + R]
            out[dy, dx] = pltpu.roll(w, dx % W, 1) if dx else w
    return out


def step_kernel(priors, parts, first_row, *refs):
    refs = list(refs)
    sources = [[refs.pop(0) for _ in range(3)] for _ in range(priors)]
    sides = [[refs.pop(0) for _ in range(3)] for _ in range(parts)]
    params = refs.pop(0) if priors else None
    mixer, inner, outer, out, stack, joined, hidden, wts = refs
    row0 = first_row[0] - R

    def side_row(trio, r):
        up, own, down = trio
        up_rows, down_rows = up.shape[0] // C, down.shape[0] // C
        if r < R:
            return up[pl.ds((up_rows - R + r) * C, C), :]
        if r < R + ROWS:
            return own[pl.ds((r - R) * C, C), :]
        return down[pl.ds((r - R - ROWS) * C, C), :]

    def source_row(trio, o):
        return (trio[0], (o + ROWS) * C) if o < 0 else (trio[1], o * C) if o < ROWS else (trio[2], (o - ROWS) * C)

    for p in range(priors):
        for (dy, dx), w in tap_weights(params[p], row0).items():
            wts[p * 25 + (dy + R) * 5 + dx + R] = w

    depth = (parts + priors) * C
    for r in range(EXT):
        for p in range(priors):
            taps = {}
            for dy in range(-R, R + 1):
                for dx in range(-R, R + 1):
                    w = wts[p * 25 + (dy + R) * 5 + dx + R, pl.ds(r, 1), :]
                    taps[dy, dx] = jnp.broadcast_to(w, (16, W)).astype(ACC)
            for ch in range(0, C, 16):
                g = []
                for dy in range(-R, R + 1):
                    ref, at = source_row(sources[p], r - R + dy)
                    g.append(ref[pl.ds(at + ch, 16), :].astype(ACC))
                total = None
                for dx in range(-R, R + 1):
                    t = g[0] * taps[-R, dx]
                    for dy in range(-R + 1, R + 1):
                        t = t + g[dy + R] * taps[dy, dx]
                    t = t.astype(jnp.float32)
                    t = pltpu.roll(t, -dx % W, 1) if dx else t
                    total = t if total is None else total + t
                stack[pl.ds(p * C + ch, 16), pl.ds(r * W, W)] = total.astype(jnp.bfloat16)

    for r in range(0, EXT, 2):
        pieces = [
            jnp.concatenate([side_row(trio, r), side_row(trio, r + 1)], axis=1) for trio in sides
        ]
        if priors:
            pieces.append(stack[pl.ds(0, priors * C), pl.ds(r * W, 2 * W)])
        data = jnp.concatenate(pieces, axis=0)
        both = leaky(jnp.dot(mixer[:, pl.ds(0, depth)], data, preferred_element_type=jnp.float32))
        for n in range(2):
            value = both[:, n * W : (n + 1) * W]
            if not R <= r + n < R + ROWS:
                at = row0 + r + n
                keep = jnp.where((at >= 0) & (at < H), 1.0, 0.0)
                value = value * keep
            joined[pl.ds((r + n) * C, C), :] = value.astype(jnp.bfloat16)

    cols = lax.broadcasted_iota(jnp.int32, (C, W), 1)

    def conv_pair(source, kernel, r):
        data = jnp.concatenate(
            [source[pl.ds(r * C, 3 * C), :], source[pl.ds((r + 1) * C, 3 * C), :]], axis=1
        )
        res = jnp.dot(kernel[...], data, preferred_element_type=jnp.float32)
        outs = []
        for n in range(2):
            part = res[:, n * W : (n + 1) * W]
            left = jnp.where(cols >= 1, pltpu.roll(part[0:C], 1, 1), 0.0)
            right = jnp.where(cols < W - 1, pltpu.roll(part[2 * C : 3 * C], W - 1, 1), 0.0)
            outs.append(left + part[C : 2 * C] + right)
        return outs

    for r in range(0, ROWS + 2, 2):
        for n, value in enumerate(conv_pair(joined, inner, r)):
            value = leaky(value)
            if r + n in (0, ROWS + 1):
                at = row0 + 1 + r + n
                value = value * jnp.where((at >= 0) & (at < H), 1.0, 0.0)
            hidden[pl.ds((r + n) * C, C), :] = value.astype(jnp.bfloat16)

    for r in range(0, ROWS, 2):
        for n, value in enumerate(conv_pair(hidden, outer, r)):
            base = joined[pl.ds((r + n + R) * C, C), :].astype(jnp.float32)
            out[pl.ds((r + n) * C, C), :] = (base + value).astype(jnp.bfloat16)


def run_step(first_row, sources, sides, params, weights):
    priors, parts = len(sources), len(sides)
    operands = [first_row]
    for trio in list(sources) + list(sides):
        operands += list(trio)
    if priors:
        operands.append(params)
    operands += list(weights)
    vmem = pl.BlockSpec(memory_space=pltpu.VMEM)
    specs = [pl.BlockSpec(memory_space=pltpu.SMEM)] + [vmem] * (len(operands) - 1)
    return pl.pallas_call(
        functools.partial(step_kernel, priors, parts),
        out_shape=jax.ShapeDtypeStruct((ROWS * C, W), jnp.bfloat16),
        in_specs=specs,
        out_specs=vmem,
        scratch_shapes=[
            pltpu.VMEM((2 * C, EXT * W), jnp.bfloat16),
            pltpu.VMEM((EXT * C, W), jnp.bfloat16),
            pltpu.VMEM(((ROWS + 2) * C, W), jnp.bfloat16),
            pltpu.VMEM((50, EXT, W), jnp.float32),
        ],
        compiler_params=pltpu.CompilerParams(vmem_limit_bytes=16 * 2**20),
        name="step",
    )(*operands)


def neighbours(shard):
    count = lax.axis_size("tile")
    up = lax.ppermute(shard, "tile", [(i, i + 1) for i in range(count - 1)])
    down = lax.ppermute(shard, "tile", [(i + 1, i) for i in range(count - 1)])
    return up, down


def conv_matrix(kernel):
    return kernel.reshape(C, 3, 3, C).transpose(2, 0, 1, 3).reshape(3 * C, 3 * C)


def shards(
    frames,
    back_shift,
    back_fraction,
    ahead_shift,
    ahead_fraction,
    back_mixer,
    back_inner,
    back_outer,
    ahead_mixer,
    ahead_inner,
    ahead_outer,
):
    tile = lax.axis_index("tile")
    turn = lax.axis_index("tm")
    first_row = (tile * ROWS).astype(jnp.int32).reshape(1)

    own = frames[0].transpose(1, 0, 2).reshape(ROWS * C, W)

    def pack(shift, fraction):
        return jnp.concatenate([shift[0].astype(jnp.bfloat16), fraction[0].astype(jnp.bfloat16)], axis=1)

    own_params = jnp.stack([pack(back_shift, back_fraction), pack(ahead_shift, ahead_fraction)])
    own_params = own_params.transpose(3, 0, 1, 2, 4).reshape(ROWS * 16, W)
    mine = jnp.concatenate([own, own_params], axis=0)
    clip = lax.all_gather(mine, "tm", axis=0)

    count = lax.axis_size("tile")
    low = jnp.concatenate([clip[:, 2 * C : 4 * C], clip[:, 4 * C + 32 : 4 * C + 64]], axis=1)
    high = jnp.concatenate([clip[:, 0 : 2 * C], clip[:, 4 * C : 4 * C + 32]], axis=1)
    above = lax.ppermute(low, "tile", [(i, i + 1) for i in range(count - 1)])
    below = lax.ppermute(high, "tile", [(i + 1, i) for i in range(count - 1)])
    rows = jnp.concatenate([above[:, 2 * C :], clip[:, 4 * C :], below[:, 2 * C :]], axis=1)
    params = rows.reshape(FRAMES, EXT, 2, 2, 4, W).transpose(2, 0, 3, 4, 1, 5).astype(jnp.float32)
    frame_trios = [(above[t, : 2 * C], clip[t, : 4 * C], below[t, : 2 * C]) for t in range(FRAMES)]

    def chain(order, way, extra, weights):
        done = {}
        history = []
        for n, t in enumerate(order):
            sides = [frame_trios[t]] + ([extra[t]] if extra else [])
            new = run_step(first_row, history[:2], sides, params[way, t], weights)
            if n + 1 < FRAMES or not extra:
                up, down = neighbours(new)
                history.insert(0, (up, new, down))
                done[t] = (up, new, down)
            else:
                done[t] = (None, new, None)
        return done

    back = chain(
        range(FRAMES - 1, -1, -1), 0, None, (back_mixer, conv_matrix(back_inner), conv_matrix(back_outer))
    )
    ahead = chain(
        range(FRAMES), 1, back, (ahead_mixer, conv_matrix(ahead_inner), conv_matrix(ahead_outer))
    )

    def pick(done):
        value = done[0][1]
        for t in range(1, FRAMES):
            value = jnp.where(turn == t, done[t][1], value)
        return value.reshape(ROWS, C, W).transpose(1, 0, 2)[None]

    return pick(back), pick(ahead)


def solution(mesh):
    in_specs = (
        P("tm", None, "tile", None),
        P("tm", None, None, "tile", None),
        P("tm", None, None, "tile", None),
        P("tm", None, None, "tile", None),
        P("tm", None, None, "tile", None),
        P(),
        P(),
        P(),
        P(),
        P(),
        P(),
    )
    out_specs = (P("tm", None, "tile", None), P("tm", None, "tile", None))
    return jax.shard_map(shards, mesh=mesh, in_specs=in_specs, out_specs=out_specs, check_vma=False)
```

time: 723 us -> 222 us (0.31)
  the two profiles are of different devices: /device:TPU:36 before, /device:TPU:6 now
where the time goes in v1:
time: 222 us; the launch traced here: 220 us
  waiting for transfers between devices  78.2 us (35%)
  starting transfers between devices  76.6 us (35%)
  blocking collectives  27.3 us (12%)
  Pallas kernels  26.9 us (12%)
  local copies, waits for them, and re-layouts  8.22 us (4%)
    ppermute x15, waiting for transfers between devices, neighbours(): up = lax.ppermute(shard, 'tile', [(i, i + 1) for i in range(count - 1)])  75.9 us
    ppermute x15, starting transfers between devices, neighbours(): up = lax.ppermute(shard, 'tile', [(i, i + 1) for i in range(count - 1)])  35.6 us
    ppermute x15, starting transfers between devices, neighbours(): down = lax.ppermute(shard, 'tile', [(i + 1, i) for i in range(count - 1)])  33.3 us
    all_gather x1, blocking collectives, shards(): clip = lax.all_gather(mine, 'tm', axis=0)  27.3 us
    pallas_call x16, Pallas kernels, run_step(): pl.pallas_call(functools.partial(step_kernel, priors, parts), out_shape=j...  26.9 us
    ppermute x1, starting transfers between devices, shards(): below = lax.ppermute(high, 'tile', [(i + 1, i) for i in range(count - 1)])  5.74 us
  transfers between devices with their start and end apart: 32, of which 16 were waited for; matrix products, arithmetic and copies ran while one was open for 2% of the time, Pallas kernels for 0%

profile of v1, /device:TPU:6, one launch (start us, length us, event | category | flops | bytes accessed | tf_op | source)
XLA Modules:
  0.0 220.3 jit_solution(2676395336051755737)
XLA Ops:
  2.9 27.3 %all-gather = bf16[2560,128]{1,0:T(8,128)(2,1)S(1)} all-gather(bf16[320,128]{1,0:T(8,128)(2,1)S(1)} %pad_maximum_fusion.2), channel_id=2, replica_groups=mesh['tm'=8,'tile'=64] {'tm'}, dimensions={0}, use_global_device_ids=true | all-gather | bytes 737280 | tf_op jit(solution)/shard_map/all_gather | solution.py:196
  30.4 1.9 collective-permute-start
  33.0 5.7 %collective-permute-start.1 = (bf16[8,160,128]{2,1,0:T(8,128)(2,1)}, bf16[8,160,128]{2,1,0:T(8,128)(2,1)S(1)}, u32[]{:S(2)}, u32[]{:S(2)}) collective-permute-start(bf16[8,160,128]{2,1,0:T(8,128)(2,1)} %pad_maximum_fusion.1), channel_id=1, source_target_pairs={{1,0},{2,1},{3,2},{4,3},{5,4},{6,5},{7,6},{8,7},{9,8},{10,9},{11,1... | collective-permute-start | bytes 983048 | tf_op jit(solution)/shard_map/ppermute | solution.py:202
  41.5 2.2 collective-permute-done.1
  44.5 6.0 %collective-permute-start.3 = (bf16[256,128]{1,0:T(8,128)(2,1)S(1)}, bf16[256,128]{1,0:T(8,128)(2,1)S(1)}, u32[]{:S(2)}, u32[]{:S(2)}) collective-permute-start(bf16[256,128]{1,0:T(8,128)(2,1)S(1)} %step.16.refs_1_.refs_4_.refs_10_), channel_id=1, source_target_pairs={{1,0},{2,1},{3,2},{4,3},{5,4},{6,5},{7,6},{8,7},{9,8},{10,9},{11,1... | collective-permute-start | bytes 196616 | tf_op jit(solution)/shard_map/ppermute | solution.py:163
  50.5 1.9 collective-permute-start.2
  53.6 4.6 %collective-permute-done.2.refs_0_.refs_3_.refs_9_ = bf16[256,128]{1,0:T(8,128)(2,1)S(1)} collective-permute-done((bf16[256,128]{1,0:T(8,128)(2,1)S(1)}, bf16[256,128]{1,0:T(8,128)(2,1)S(1)}, u32[]{:S(2)}, u32[]{:S(2)}) %collective-permute-start.2) | collective-permute-done | bytes 65568 | tf_op jit(solution)/shard_map/ppermute | solution.py:162
  59.6 1.9 collective-permute-start.5
  61.5 2.4 %collective-permute-start.4 = (bf16[256,128]{1,0:T(8,128)(2,1)S(1)}, bf16[256,128]{1,0:T(8,128)(2,1)S(1)}, u32[]{:S(2)}, u32[]{:S(2)}) collective-permute-start(bf16[256,128]{1,0:T(8,128)(2,1)S(1)} %step.17.refs_1_.refs_4_.refs_10_), channel_id=1, source_target_pairs={{0,1},{1,2},{2,3},{3,4},{4,5},{5,6},{6,7},{7,8},{8,9},{9,10},{10,1... | collective-permute-start | bytes 196616 | tf_op jit(solution)/shard_map/ppermute | solution.py:162
  63.9 5.3 %collective-permute-done.4.refs_0_.refs_3_.refs_9_ = bf16[256,128]{1,0:T(8,128)(2,1)S(1)} collective-permute-done((bf16[256,128]{1,0:T(8,128)(2,1)S(1)}, bf16[256,128]{1,0:T(8,128)(2,1)S(1)}, u32[]{:S(2)}, u32[]{:S(2)}) %collective-permute-start.4) | collective-permute-done | bytes 65568 | tf_op jit(solution)/shard_map/ppermute | solution.py:162
  71.1 1.9 collective-permute-start.7
  73.0 2.4 %collective-permute-start.6 = (bf16[256,128]{1,0:T(8,128)(2,1)S(1)}, bf16[256,128]{1,0:T(8,128)(2,1)S(1)}, u32[]{:S(2)}, u32[]{:S(2)}) collective-permute-start(bf16[256,128]{1,0:T(8,128)(2,1)S(1)} %step.18.refs_1_.refs_4_.refs_10_), channel_id=1, source_target_pairs={{0,1},{1,2},{2,3},{3,4},{4,5},{5,6},{6,7},{7,8},{8,9},{9,10},{10,1... | collective-permute-start | bytes 196616 | tf_op jit(solution)/shard_map/ppermute | solution.py:162
  75.4 5.3 %collective-permute-done.6.refs_0_.refs_3_.refs_9_ = bf16[256,128]{1,0:T(8,128)(2,1)S(1)} collective-permute-done((bf16[256,128]{1,0:T(8,128)(2,1)S(1)}, bf16[256,128]{1,0:T(8,128)(2,1)S(1)}, u32[]{:S(2)}, u32[]{:S(2)}) %collective-permute-start.6) | collective-permute-done | bytes 65568 | tf_op jit(solution)/shard_map/ppermute | solution.py:162
  82.6 1.9 collective-permute-start.9
  84.5 2.4 %collective-permute-start.8 = (bf16[256,128]{1,0:T(8,128)(2,1)S(1)}, bf16[256,128]{1,0:T(8,128)(2,1)S(1)}, u32[]{:S(2)}, u32[]{:S(2)}) collective-permute-start(bf16[256,128]{1,0:T(8,128)(2,1)S(1)} %step.19.refs_1_.refs_4_.refs_10_), channel_id=1, source_target_pairs={{0,1},{1,2},{2,3},{3,4},{4,5},{5,6},{6,7},{7,8},{8,9},{9,10},{10,1... | collective-permute-start | bytes 196616 | tf_op jit(solution)/shard_map/ppermute | solution.py:162
  86.9 5.3 %collective-permute-done.8.refs_0_.refs_3_.refs_9_ = bf16[256,128]{1,0:T(8,128)(2,1)S(1)} collective-permute-done((bf16[256,128]{1,0:T(8,128)(2,1)S(1)}, bf16[256,128]{1,0:T(8,128)(2,1)S(1)}, u32[]{:S(2)}, u32[]{:S(2)}) %collective-permute-start.8) | collective-permute-done | bytes 65568 | tf_op jit(solution)/shard_map/ppermute | solution.py:162
  94.1 1.9 collective-permute-start.11
  96.0 2.4 %collective-permute-start.10 = (bf16[256,128]{1,0:T(8,128)(2,1)S(1)}, bf16[256,128]{1,0:T(8,128)(2,1)S(1)}, u32[]{:S(2)}, u32[]{:S(2)}) collective-permute-start(bf16[256,128]{1,0:T(8,128)(2,1)S(1)} %step.20.refs_1_.refs_4_.refs_10_), channel_id=1, source_target_pairs={{0,1},{1,2},{2,3},{3,4},{4,5},{5,6},{6,7},{7,8},{8,9},{9,10},{10,1... | collective-permute-start | bytes 196616 | tf_op jit(solution)/shard_map/ppermute | solution.py:162
  98.4 5.3 %collective-permute-done.10.refs_0_.refs_3_.refs_9_ = bf16[256,128]{1,0:T(8,128)(2,1)S(1)} collective-permute-done((bf16[256,128]{1,0:T(8,128)(2,1)S(1)}, bf16[256,128]{1,0:T(8,128)(2,1)S(1)}, u32[]{:S(2)}, u32[]{:S(2)}) %collective-permute-start.10) | collective-permute-done | bytes 65568 | tf_op jit(solution)/shard_map/ppermute | solution.py:162
  105.6 1.9 collective-permute-start.13
  107.5 2.6 %collective-permute-start.12 = (bf16[256,128]{1,0:T(8,128)(2,1)S(1)}, bf16[256,128]{1,0:T(8,128)(2,1)S(1)}, u32[]{:S(2)}, u32[]{:S(2)}) collective-permute-start(bf16[256,128]{1,0:T(8,128)(2,1)S(1)} %step.21.refs_1_.refs_4_.refs_10_), channel_id=1, source_target_pairs={{0,1},{1,2},{2,3},{3,4},{4,5},{5,6},{6,7},{7,8},{8,9},{9,10},{10,1... | collective-permute-start | bytes 196616 | tf_op jit(solution)/shard_map/ppermute | solution.py:162
  110.1 5.1 %collective-permute-done.12.refs_0_.refs_3_.refs_9_ = bf16[256,128]{1,0:T(8,128)(2,1)S(1)} collective-permute-done((bf16[256,128]{1,0:T(8,128)(2,1)S(1)}, bf16[256,128]{1,0:T(8,128)(2,1)S(1)}, u32[]{:S(2)}, u32[]{:S(2)}) %collective-permute-start.12) | collective-permute-done | bytes 65568 | tf_op jit(solution)/shard_map/ppermute | solution.py:162
  117.1 1.9 collective-permute-start.15
  119.0 2.4 %collective-permute-start.14 = (bf16[256,128]{1,0:T(8,128)(2,1)S(1)}, bf16[256,128]{1,0:T(8,128)(2,1)S(1)}, u32[]{:S(2)}, u32[]{:S(2)}) collective-permute-start(bf16[256,128]{1,0:T(8,128)(2,1)S(1)} %step.22.refs_1_.refs_7_), channel_id=1, source_target_pairs={{0,1},{1,2},{2,3},{3,4},{4,5},{5,6},{6,7},{7,8},{8,9},{9,10},{10,1... | collective-permute-start | bytes 196616 | tf_op jit(solution)/shard_map/ppermute | solution.py:162
  121.4 5.3 %collective-permute-done.14.refs_0_.refs_6_ = bf16[256,128]{1,0:T(8,128)(2,1)S(1)} collective-permute-done((bf16[256,128]{1,0:T(8,128)(2,1)S(1)}, bf16[256,128]{1,0:T(8,128)(2,1)S(1)}, u32[]{:S(2)}, u32[]{:S(2)}) %collective-permute-start.14) | collective-permute-done | bytes 65568 | tf_op jit(solution)/shard_map/ppermute | solution.py:162
  128.6 1.9 collective-permute-start.17
  130.5 2.4 %collective-permute-start.16 = (bf16[256,128]{1,0:T(8,128)(2,1)S(1)}, bf16[256,128]{1,0:T(8,128)(2,1)S(1)}, u32[]{:S(2)}, u32[]{:S(2)}) collective-permute-start(bf16[256,128]{1,0:T(8,128)(2,1)S(1)} %step.23.refs_4_), channel_id=1, source_target_pairs={{0,1},{1,2},{2,3},{3,4},{4,5},{5,6},{6,7},{7,8},{8,9},{9,10},{10,1... | collective-permute-start | bytes 196616 | tf_op jit(solution)/shard_map/ppermute | solution.py:162
  134.7 3.6 %collective-permute-done.16.refs_3_ = bf16[256,128]{1,0:T(8,128)(2,1)S(1)} collective-permute-done((bf16[256,128]{1,0:T(8,128)(2,1)S(1)}, bf16[256,128]{1,0:T(8,128)(2,1)S(1)}, u32[]{:S(2)}, u32[]{:S(2)}) %collective-permute-start.16) | collective-permute-done | bytes 65568 | tf_op jit(solution)/shard_map/ppermute | solution.py:162
  139.0 2.3 %collective-permute-start.19 = (bf16[256,128]{1,0:T(8,128)(2,1)S(1)}, bf16[256,128]{1,0:T(8,128)(2,1)S(1)}, u32[]{:S(2)}, u32[]{:S(2)}) collective-permute-start(bf16[256,128]{1,0:T(8,128)(2,1)S(1)} %step.24.refs_1_.refs_4_), channel_id=1, source_target_pairs={{1,0},{2,1},{3,2},{4,3},{5,4},{6,5},{7,6},{8,7},{9,8},{10,9},{11,1... | collective-permute-start | bytes 196616 | tf_op jit(solution)/shard_map/ppermute | solution.py:163
  141.3 2.0 collective-permute-start.18
  143.3 5.6 %collective-permute-done.18.refs_0_.refs_3_ = bf16[256,128]{1,0:T(8,128)(2,1)S(1)} collective-permute-done((bf16[256,128]{1,0:T(8,128)(2,1)S(1)}, bf16[256,128]{1,0:T(8,128)(2,1)S(1)}, u32[]{:S(2)}, u32[]{:S(2)}) %collective-permute-start.18) | collective-permute-done | bytes 65568 | tf_op jit(solution)/shard_map/ppermute | solution.py:162
  150.3 1.9 collective-permute-start.21
  152.2 2.4 %collective-permute-start.20 = (bf16[256,128]{1,0:T(8,128)(2,1)S(1)}, bf16[256,128]{1,0:T(8,128)(2,1)S(1)}, u32[]{:S(2)}, u32[]{:S(2)}) collective-permute-start(bf16[256,128]{1,0:T(8,128)(2,1)S(1)} %step.25.refs_1_.refs_4_), channel_id=1, source_target_pairs={{0,1},{1,2},{2,3},{3,4},{4,5},{5,6},{6,7},{7,8},{8,9},{9,10},{10,1... | collective-permute-start | bytes 196616 | tf_op jit(solution)/shard_map/ppermute | solution.py:162
  154.7 5.3 %collective-permute-done.20.refs_0_.refs_3_ = bf16[256,128]{1,0:T(8,128)(2,1)S(1)} collective-permute-done((bf16[256,128]{1,0:T(8,128)(2,1)S(1)}, bf16[256,128]{1,0:T(8,128)(2,1)S(1)}, u32[]{:S(2)}, u32[]{:S(2)}) %collective-permute-start.20) | collective-permute-done | bytes 65568 | tf_op jit(solution)/shard_map/ppermute | solution.py:162
  161.9 1.9 collective-permute-start.23
  163.8 2.4 %collective-permute-start.22 = (bf16[256,128]{1,0:T(8,128)(2,1)S(1)}, bf16[256,128]{1,0:T(8,128)(2,1)S(1)}, u32[]{:S(2)}, u32[]{:S(2)}) collective-permute-start(bf16[256,128]{1,0:T(8,128)(2,1)S(1)} %step.26.refs_1_.refs_4_), channel_id=1, source_target_pairs={{0,1},{1,2},{2,3},{3,4},{4,5},{5,6},{6,7},{7,8},{8,9},{9,10},{10,1... | collective-permute-start | bytes 196616 | tf_op jit(solution)/shard_map/ppermute | solution.py:162
  166.2 5.3 %collective-permute-done.22.refs_0_.refs_3_ = bf16[256,128]{1,0:T(8,128)(2,1)S(1)} collective-permute-done((bf16[256,128]{1,0:T(8,128)(2,1)S(1)}, bf16[256,128]{1,0:T(8,128)(2,1)S(1)}, u32[]{:S(2)}, u32[]{:S(2)}) %collective-permute-start.22) | collective-permute-done | bytes 65568 | tf_op jit(solution)/shard_map/ppermute | solution.py:162
  173.4 1.9 collective-permute-start.25
  175.3 2.4 %collective-permute-start.24 = (bf16[256,128]{1,0:T(8,128)(2,1)S(1)}, bf16[256,128]{1,0:T(8,128)(2,1)S(1)}, u32[]{:S(2)}, u32[]{:S(2)}) collective-permute-start(bf16[256,128]{1,0:T(8,128)(2,1)S(1)} %step.27.refs_1_.refs_4_), channel_id=1, source_target_pairs={{0,1},{1,2},{2,3},{3,4},{4,5},{5,6},{6,7},{7,8},{8,9},{9,10},{10,1... | collective-permute-start | bytes 196616 | tf_op jit(solution)/shard_map/ppermute | solution.py:162
  177.8 5.3 %collective-permute-done.24.refs_0_.refs_3_ = bf16[256,128]{1,0:T(8,128)(2,1)S(1)} collective-permute-done((bf16[256,128]{1,0:T(8,128)(2,1)S(1)}, bf16[256,128]{1,0:T(8,128)(2,1)S(1)}, u32[]{:S(2)}, u32[]{:S(2)}) %collective-permute-start.24) | collective-permute-done | bytes 65568 | tf_op jit(solution)/shard_map/ppermute | solution.py:162
  183.0 1.9 step.28.refs_1_.refs_4_
  185.0 1.9 collective-permute-start.27
  186.9 2.6 %collective-permute-start.26 = (bf16[256,128]{1,0:T(8,128)(2,1)S(1)}, bf16[256,128]{1,0:T(8,128)(2,1)S(1)}, u32[]{:S(2)}, u32[]{:S(2)}) collective-permute-start(bf16[256,128]{1,0:T(8,128)(2,1)S(1)} %step.28.refs_1_.refs_4_), channel_id=1, source_target_pairs={{0,1},{1,2},{2,3},{3,4},{4,5},{5,6},{6,7},{7,8},{8,9},{9,10},{10,1... | collective-permute-start | bytes 196616 | tf_op jit(solution)/shard_map/ppermute | solution.py:162
  189.5 5.0 %collective-permute-done.26.refs_0_.refs_3_ = bf16[256,128]{1,0:T(8,128)(2,1)S(1)} collective-permute-done((bf16[256,128]{1,0:T(8,128)(2,1)S(1)}, bf16[256,128]{1,0:T(8,128)(2,1)S(1)}, u32[]{:S(2)}, u32[]{:S(2)}) %collective-permute-start.26) | collective-permute-done | bytes 65568 | tf_op jit(solution)/shard_map/ppermute | solution.py:162
  198.4 2.4 %collective-permute-start.28 = (bf16[256,128]{1,0:T(8,128)(2,1)S(1)}, bf16[256,128]{1,0:T(8,128)(2,1)S(1)}, u32[]{:S(2)}, u32[]{:S(2)}) collective-permute-start(bf16[256,128]{1,0:T(8,128)(2,1)S(1)} %step.29.refs_1_.refs_4_), channel_id=1, source_target_pairs={{0,1},{1,2},{2,3},{3,4},{4,5},{5,6},{6,7},{7,8},{8,9},{9,10},{10,1... | collective-permute-start | bytes 196616 | tf_op jit(solution)/shard_map/ppermute | solution.py:162
  200.9 5.3 %collective-permute-done.28.refs_0_.refs_3_ = bf16[256,128]{1,0:T(8,128)(2,1)S(1)} collective-permute-done((bf16[256,128]{1,0:T(8,128)(2,1)S(1)}, bf16[256,128]{1,0:T(8,128)(2,1)S(1)}, u32[]{:S(2)}, u32[]{:S(2)}) %collective-permute-start.28) | collective-permute-done | bytes 65568 | tf_op jit(solution)/shard_map/ppermute | solution.py:162
  209.9 2.4 %collective-permute-start.30 = (bf16[256,128]{1,0:T(8,128)(2,1)S(1)}, bf16[256,128]{1,0:T(8,128)(2,1)S(1)}, u32[]{:S(2)}, u32[]{:S(2)}) collective-permute-start(bf16[256,128]{1,0:T(8,128)(2,1)S(1)} %step.30.refs_1_), channel_id=1, source_target_pairs={{0,1},{1,2},{2,3},{3,4},{4,5},{5,6},{6,7},{7,8},{8,9},{9,10},{10,1... | collective-permute-start | bytes 196616 | tf_op jit(solution)/shard_map/ppermute | solution.py:162
  213.1 4.6 %collective-permute-done.30.refs_0_ = bf16[256,128]{1,0:T(8,128)(2,1)S(1)} collective-permute-done((bf16[256,128]{1,0:T(8,128)(2,1)S(1)}, bf16[256,128]{1,0:T(8,128)(2,1)S(1)}, u32[]{:S(2)}, u32[]{:S(2)}) %collective-permute-start.30) | collective-permute-done | bytes 65568 | tf_op jit(solution)/shard_map/ppermute | solution.py:162
  (94 shorter events, 38.8 us)
Async XLA Ops:
  0.6 0.7 copy-start.8
  1.3 0.7 copy-start.9
  1.4 0.7 copy-start.10
  2.0 0.8 copy-start.7
  30.4 11.1 %collective-permute-start = (bf16[8,160,128]{2,1,0:T(8,128)(2,1)S(1)}, bf16[8,160,128]{2,1,0:T(8,128)(2,1)S(1)}, u32[]{:S(2)}, u32[]{:S(2)}) collective-permute-start(bf16[8,160,128]{2,1,0:T(8,128)(2,1)S(1)} %pad_maximum_fusion), channel_id=1, source_target_pairs={{0,1},{1,2},{2,3},{3,4},{4,5},{5,6},{6,7},{7,8},{8,9},{9,10},{10,1... | collective-permute-start | bytes 983048 | tf_op jit(solution)/shard_map/ppermute | solution.py:201
  33.0 10.6 %collective-permute-start.1 = (bf16[8,160,128]{2,1,0:T(8,128)(2,1)}, bf16[8,160,128]{2,1,0:T(8,128)(2,1)S(1)}, u32[]{:S(2)}, u32[]{:S(2)}) collective-permute-start(bf16[8,160,128]{2,1,0:T(8,128)(2,1)} %pad_maximum_fusion.1), channel_id=1, source_target_pairs={{1,0},{2,1},{3,2},{4,3},{5,4},{6,5},{7,6},{8,7},{9,8},{10,9},{11,1... | collective-permute-start | bytes 983048 | tf_op jit(solution)/shard_map/ppermute | solution.py:202
  38.8 0.9 copy-start.3
  40.0 0.9 copy-start.4
  41.4 11.0 %copy-start.2 = (bf16[8,160,128]{2,1,0:T(8,128)(2,1)}, bf16[8,160,128]{2,1,0:T(8,128)(2,1)S(1)}, u32[]{:S(2)}) copy-start(bf16[8,160,128]{2,1,0:T(8,128)(2,1)S(1)} %collective-permute-done) | copy-start | bytes 983044
  41.5 2.2 %copy-start = (bf16[64,192]{1,0:T(8,128)(2,1)S(1)}, bf16[64,192]{1,0:T(8,128)(2,1)}, u32[]{:S(2)}) copy-start(bf16[64,192]{1,0:T(8,128)(2,1)} %refs_10_.12) | copy-start | bytes 73732
  44.5 9.1 %collective-permute-start.3 = (bf16[256,128]{1,0:T(8,128)(2,1)S(1)}, bf16[256,128]{1,0:T(8,128)(2,1)S(1)}, u32[]{:S(2)}, u32[]{:S(2)}) collective-permute-start(bf16[256,128]{1,0:T(8,128)(2,1)S(1)} %step.16.refs_1_.refs_4_.refs_10_), channel_id=1, source_target_pairs={{1,0},{2,1},{3,2},{4,3},{5,4},{6,5},{7,6},{8,7},{9,8},{10,9},{11,1... | collective-permute-start | bytes 196616 | tf_op jit(solution)/shard_map/ppermute | solution.py:163
  50.5 7.7 %collective-permute-start.2 = (bf16[256,128]{1,0:T(8,128)(2,1)S(1)}, bf16[256,128]{1,0:T(8,128)(2,1)S(1)}, u32[]{:S(2)}, u32[]{:S(2)}) collective-permute-start(bf16[256,128]{1,0:T(8,128)(2,1)S(1)} %step.16.refs_1_.refs_4_.refs_10_), channel_id=1, source_target_pairs={{0,1},{1,2},{2,3},{3,4},{4,5},{5,6},{6,7},{7,8},{8,9},{9,10},{10,1... | collective-permute-start | bytes 196616 | tf_op jit(solution)/shard_map/ppermute | solution.py:162
  52.4 0.8 slice-start
  59.6 4.3 %collective-permute-start.5 = (bf16[256,128]{1,0:T(8,128)(2,1)S(1)}, bf16[256,128]{1,0:T(8,128)(2,1)S(1)}, u32[]{:S(2)}, u32[]{:S(2)}) collective-permute-start(bf16[256,128]{1,0:T(8,128)(2,1)S(1)} %step.17.refs_1_.refs_4_.refs_10_), channel_id=1, source_target_pairs={{1,0},{2,1},{3,2},{4,3},{5,4},{6,5},{7,6},{8,7},{9,8},{10,9},{11,1... | collective-permute-start | bytes 196616 | tf_op jit(solution)/shard_map/ppermute | solution.py:163
  61.5 7.7 %collective-permute-start.4 = (bf16[256,128]{1,0:T(8,128)(2,1)S(1)}, bf16[256,128]{1,0:T(8,128)(2,1)S(1)}, u32[]{:S(2)}, u32[]{:S(2)}) collective-permute-start(bf16[256,128]{1,0:T(8,128)(2,1)S(1)} %step.17.refs_1_.refs_4_.refs_10_), channel_id=1, source_target_pairs={{0,1},{1,2},{2,3},{3,4},{4,5},{5,6},{6,7},{7,8},{8,9},{9,10},{10,1... | collective-permute-start | bytes 196616 | tf_op jit(solution)/shard_map/ppermute | solution.py:162
  71.1 4.3 %collective-permute-start.7 = (bf16[256,128]{1,0:T(8,128)(2,1)S(1)}, bf16[256,128]{1,0:T(8,128)(2,1)S(1)}, u32[]{:S(2)}, u32[]{:S(2)}) collective-permute-start(bf16[256,128]{1,0:T(8,128)(2,1)S(1)} %step.18.refs_1_.refs_4_.refs_10_), channel_id=1, source_target_pairs={{1,0},{2,1},{3,2},{4,3},{5,4},{6,5},{7,6},{8,7},{9,8},{10,9},{11,1... | collective-permute-start | bytes 196616 | tf_op jit(solution)/shard_map/ppermute | solution.py:163
  73.0 7.7 %collective-permute-start.6 = (bf16[256,128]{1,0:T(8,128)(2,1)S(1)}, bf16[256,128]{1,0:T(8,128)(2,1)S(1)}, u32[]{:S(2)}, u32[]{:S(2)}) collective-permute-start(bf16[256,128]{1,0:T(8,128)(2,1)S(1)} %step.18.refs_1_.refs_4_.refs_10_), channel_id=1, source_target_pairs={{0,1},{1,2},{2,3},{3,4},{4,5},{5,6},{6,7},{7,8},{8,9},{9,10},{10,1... | collective-permute-start | bytes 196616 | tf_op jit(solution)/shard_map/ppermute | solution.py:162
  82.6 4.3 %collective-permute-start.9 = (bf16[256,128]{1,0:T(8,128)(2,1)S(1)}, bf16[256,128]{1,0:T(8,128)(2,1)S(1)}, u32[]{:S(2)}, u32[]{:S(2)}) collective-permute-start(bf16[256,128]{1,0:T(8,128)(2,1)S(1)} %step.19.refs_1_.refs_4_.refs_10_), channel_id=1, source_target_pairs={{1,0},{2,1},{3,2},{4,3},{5,4},{6,5},{7,6},{8,7},{9,8},{10,9},{11,1... | collective-permute-start | bytes 196616 | tf_op jit(solution)/shard_map/ppermute | solution.py:163
  84.5 7.7 %collective-permute-start.8 = (bf16[256,128]{1,0:T(8,128)(2,1)S(1)}, bf16[256,128]{1,0:T(8,128)(2,1)S(1)}, u32[]{:S(2)}, u32[]{:S(2)}) collective-permute-start(bf16[256,128]{1,0:T(8,128)(2,1)S(1)} %step.19.refs_1_.refs_4_.refs_10_), channel_id=1, source_target_pairs={{0,1},{1,2},{2,3},{3,4},{4,5},{5,6},{6,7},{7,8},{8,9},{9,10},{10,1... | collective-permute-start | bytes 196616 | tf_op jit(solution)/shard_map/ppermute | solution.py:162
  94.1 4.3 %collective-permute-start.11 = (bf16[256,128]{1,0:T(8,128)(2,1)S(1)}, bf16[256,128]{1,0:T(8,128)(2,1)S(1)}, u32[]{:S(2)}, u32[]{:S(2)}) collective-permute-start(bf16[256,128]{1,0:T(8,128)(2,1)S(1)} %step.20.refs_1_.refs_4_.refs_10_), channel_id=1, source_target_pairs={{1,0},{2,1},{3,2},{4,3},{5,4},{6,5},{7,6},{8,7},{9,8},{10,9},{11,1... | collective-permute-start | bytes 196616 | tf_op jit(solution)/shard_map/ppermute | solution.py:163
  96.0 7.7 %collective-permute-start.10 = (bf16[256,128]{1,0:T(8,128)(2,1)S(1)}, bf16[256,128]{1,0:T(8,128)(2,1)S(1)}, u32[]{:S(2)}, u32[]{:S(2)}) collective-permute-start(bf16[256,128]{1,0:T(8,128)(2,1)S(1)} %step.20.refs_1_.refs_4_.refs_10_), channel_id=1, source_target_pairs={{0,1},{1,2},{2,3},{3,4},{4,5},{5,6},{6,7},{7,8},{8,9},{9,10},{10,1... | collective-permute-start | bytes 196616 | tf_op jit(solution)/shard_map/ppermute | solution.py:162
  105.6 4.5 %collective-permute-start.13 = (bf16[256,128]{1,0:T(8,128)(2,1)S(1)}, bf16[256,128]{1,0:T(8,128)(2,1)S(1)}, u32[]{:S(2)}, u32[]{:S(2)}) collective-permute-start(bf16[256,128]{1,0:T(8,128)(2,1)S(1)} %step.21.refs_1_.refs_4_.refs_10_), channel_id=1, source_target_pairs={{1,0},{2,1},{3,2},{4,3},{5,4},{6,5},{7,6},{8,7},{9,8},{10,9},{11,1... | collective-permute-start | bytes 196616 | tf_op jit(solution)/shard_map/ppermute | solution.py:163
  107.5 7.7 %collective-permute-start.12 = (bf16[256,128]{1,0:T(8,128)(2,1)S(1)}, bf16[256,128]{1,0:T(8,128)(2,1)S(1)}, u32[]{:S(2)}, u32[]{:S(2)}) collective-permute-start(bf16[256,128]{1,0:T(8,128)(2,1)S(1)} %step.21.refs_1_.refs_4_.refs_10_), channel_id=1, source_target_pairs={{0,1},{1,2},{2,3},{3,4},{4,5},{5,6},{6,7},{7,8},{8,9},{9,10},{10,1... | collective-permute-start | bytes 196616 | tf_op jit(solution)/shard_map/ppermute | solution.py:162
  117.1 4.3 %collective-permute-start.15 = (bf16[256,128]{1,0:T(8,128)(2,1)S(1)}, bf16[256,128]{1,0:T(8,128)(2,1)S(1)}, u32[]{:S(2)}, u32[]{:S(2)}) collective-permute-start(bf16[256,128]{1,0:T(8,128)(2,1)S(1)} %step.22.refs_1_.refs_7_), channel_id=1, source_target_pairs={{1,0},{2,1},{3,2},{4,3},{5,4},{6,5},{7,6},{8,7},{9,8},{10,9},{11,1... | collective-permute-start | bytes 196616 | tf_op jit(solution)/shard_map/ppermute | solution.py:163
  119.0 7.7 %collective-permute-start.14 = (bf16[256,128]{1,0:T(8,128)(2,1)S(1)}, bf16[256,128]{1,0:T(8,128)(2,1)S(1)}, u32[]{:S(2)}, u32[]{:S(2)}) collective-permute-start(bf16[256,128]{1,0:T(8,128)(2,1)S(1)} %step.22.refs_1_.refs_7_), channel_id=1, source_target_pairs={{0,1},{1,2},{2,3},{3,4},{4,5},{5,6},{6,7},{7,8},{8,9},{9,10},{10,1... | collective-permute-start | bytes 196616 | tf_op jit(solution)/shard_map/ppermute | solution.py:162
  126.7 6.2 %copy-start.5 = (bf16[64,576]{1,0:T(8,128)(2,1)S(1)}, bf16[64,576]{1,0:T(8,128)(2,1)}, u32[]{:S(2)}) copy-start(bf16[64,576]{1,0:T(8,128)(2,1)} %param.20) | copy-start | bytes 221188
  128.6 6.1 %collective-permute-start.17 = (bf16[256,128]{1,0:T(8,128)(2,1)S(1)}, bf16[256,128]{1,0:T(8,128)(2,1)S(1)}, u32[]{:S(2)}, u32[]{:S(2)}) collective-permute-start(bf16[256,128]{1,0:T(8,128)(2,1)S(1)} %step.23.refs_4_), channel_id=1, source_target_pairs={{1,0},{2,1},{3,2},{4,3},{5,4},{6,5},{7,6},{8,7},{9,8},{10,9},{11,1... | collective-permute-start | bytes 196616 | tf_op jit(solution)/shard_map/ppermute | solution.py:163
  130.5 7.7 %collective-permute-start.16 = (bf16[256,128]{1,0:T(8,128)(2,1)S(1)}, bf16[256,128]{1,0:T(8,128)(2,1)S(1)}, u32[]{:S(2)}, u32[]{:S(2)}) collective-permute-start(bf16[256,128]{1,0:T(8,128)(2,1)S(1)} %step.23.refs_4_), channel_id=1, source_target_pairs={{0,1},{1,2},{2,3},{3,4},{4,5},{5,6},{6,7},{7,8},{8,9},{9,10},{10,1... | collective-permute-start | bytes 196616 | tf_op jit(solution)/shard_map/ppermute | solution.py:162
  133.3 0.9 copy-start.6
  134.5 3.7 %copy-start.1 = (bf16[64,256]{1,0:T(8,128)(2,1)S(1)}, bf16[64,256]{1,0:T(8,128)(2,1)}, u32[]{:S(2)}) copy-start(bf16[64,256]{1,0:T(8,128)(2,1)} %refs_13_.11) | copy-start | bytes 98308
  139.0 4.3 %collective-permute-start.19 = (bf16[256,128]{1,0:T(8,128)(2,1)S(1)}, bf16[256,128]{1,0:T(8,128)(2,1)S(1)}, u32[]{:S(2)}, u32[]{:S(2)}) collective-permute-start(bf16[256,128]{1,0:T(8,128)(2,1)S(1)} %step.24.refs_1_.refs_4_), channel_id=1, source_target_pairs={{1,0},{2,1},{3,2},{4,3},{5,4},{6,5},{7,6},{8,7},{9,8},{10,9},{11,1... | collective-permute-start | bytes 196616 | tf_op jit(solution)/shard_map/ppermute | solution.py:163
  141.3 7.7 %collective-permute-start.18 = (bf16[256,128]{1,0:T(8,128)(2,1)S(1)}, bf16[256,128]{1,0:T(8,128)(2,1)S(1)}, u32[]{:S(2)}, u32[]{:S(2)}) collective-permute-start(bf16[256,128]{1,0:T(8,128)(2,1)S(1)} %step.24.refs_1_.refs_4_), channel_id=1, source_target_pairs={{0,1},{1,2},{2,3},{3,4},{4,5},{5,6},{6,7},{7,8},{8,9},{9,10},{10,1... | collective-permute-start | bytes 196616 | tf_op jit(solution)/shard_map/ppermute | solution.py:162
  150.3 4.3 %collective-permute-start.21 = (bf16[256,128]{1,0:T(8,128)(2,1)S(1)}, bf16[256,128]{1,0:T(8,128)(2,1)S(1)}, u32[]{:S(2)}, u32[]{:S(2)}) collective-permute-start(bf16[256,128]{1,0:T(8,128)(2,1)S(1)} %step.25.refs_1_.refs_4_), channel_id=1, source_target_pairs={{1,0},{2,1},{3,2},{4,3},{5,4},{6,5},{7,6},{8,7},{9,8},{10,9},{11,1... | collective-permute-start | bytes 196616 | tf_op jit(solution)/shard_map/ppermute | solution.py:163
  152.2 7.7 %collective-permute-start.20 = (bf16[256,128]{1,0:T(8,128)(2,1)S(1)}, bf16[256,128]{1,0:T(8,128)(2,1)S(1)}, u32[]{:S(2)}, u32[]{:S(2)}) collective-permute-start(bf16[256,128]{1,0:T(8,128)(2,1)S(1)} %step.25.refs_1_.refs_4_), channel_id=1, source_target_pairs={{0,1},{1,2},{2,3},{3,4},{4,5},{5,6},{6,7},{7,8},{8,9},{9,10},{10,1... | collective-permute-start | bytes 196616 | tf_op jit(solution)/shard_map/ppermute | solution.py:162
  161.9 4.3 %collective-permute-start.23 = (bf16[256,128]{1,0:T(8,128)(2,1)S(1)}, bf16[256,128]{1,0:T(8,128)(2,1)S(1)}, u32[]{:S(2)}, u32[]{:S(2)}) collective-permute-start(bf16[256,128]{1,0:T(8,128)(2,1)S(1)} %step.26.refs_1_.refs_4_), channel_id=1, source_target_pairs={{1,0},{2,1},{3,2},{4,3},{5,4},{6,5},{7,6},{8,7},{9,8},{10,9},{11,1... | collective-permute-start | bytes 196616 | tf_op jit(solution)/shard_map/ppermute | solution.py:163
  163.8 7.7 %collective-permute-start.22 = (bf16[256,128]{1,0:T(8,128)(2,1)S(1)}, bf16[256,128]{1,0:T(8,128)(2,1)S(1)}, u32[]{:S(2)}, u32[]{:S(2)}) collective-permute-start(bf16[256,128]{1,0:T(8,128)(2,1)S(1)} %step.26.refs_1_.refs_4_), channel_id=1, source_target_pairs={{0,1},{1,2},{2,3},{3,4},{4,5},{5,6},{6,7},{7,8},{8,9},{9,10},{10,1... | collective-permute-start | bytes 196616 | tf_op jit(solution)/shard_map/ppermute | solution.py:162
  173.4 4.3 %collective-permute-start.25 = (bf16[256,128]{1,0:T(8,128)(2,1)S(1)}, bf16[256,128]{1,0:T(8,128)(2,1)S(1)}, u32[]{:S(2)}, u32[]{:S(2)}) collective-permute-start(bf16[256,128]{1,0:T(8,128)(2,1)S(1)} %step.27.refs_1_.refs_4_), channel_id=1, source_target_pairs={{1,0},{2,1},{3,2},{4,3},{5,4},{6,5},{7,6},{8,7},{9,8},{10,9},{11,1... | collective-permute-start | bytes 196616 | tf_op jit(solution)/shard_map/ppermute | solution.py:163
  175.3 7.7 %collective-permute-start.24 = (bf16[256,128]{1,0:T(8,128)(2,1)S(1)}, bf16[256,128]{1,0:T(8,128)(2,1)S(1)}, u32[]{:S(2)}, u32[]{:S(2)}) collective-permute-start(bf16[256,128]{1,0:T(8,128)(2,1)S(1)} %step.27.refs_1_.refs_4_), channel_id=1, source_target_pairs={{0,1},{1,2},{2,3},{3,4},{4,5},{5,6},{6,7},{7,8},{8,9},{9,10},{10,1... | collective-permute-start | bytes 196616 | tf_op jit(solution)/shard_map/ppermute | solution.py:162
  185.0 4.6 %collective-permute-start.27 = (bf16[256,128]{1,0:T(8,128)(2,1)S(1)}, bf16[256,128]{1,0:T(8,128)(2,1)S(1)}, u32[]{:S(2)}, u32[]{:S(2)}) collective-permute-start(bf16[256,128]{1,0:T(8,128)(2,1)S(1)} %step.28.refs_1_.refs_4_), channel_id=1, source_target_pairs={{1,0},{2,1},{3,2},{4,3},{5,4},{6,5},{7,6},{8,7},{9,8},{10,9},{11,1... | collective-permute-start | bytes 196616 | tf_op jit(solution)/shard_map/ppermute | solution.py:163
  186.9 7.7 %collective-permute-start.26 = (bf16[256,128]{1,0:T(8,128)(2,1)S(1)}, bf16[256,128]{1,0:T(8,128)(2,1)S(1)}, u32[]{:S(2)}, u32[]{:S(2)}) collective-permute-start(bf16[256,128]{1,0:T(8,128)(2,1)S(1)} %step.28.refs_1_.refs_4_), channel_id=1, source_target_pairs={{0,1},{1,2},{2,3},{3,4},{4,5},{5,6},{6,7},{7,8},{8,9},{9,10},{10,1... | collective-permute-start | bytes 196616 | tf_op jit(solution)/shard_map/ppermute | solution.py:162
  196.5 4.4 %collective-permute-start.29 = (bf16[256,128]{1,0:T(8,128)(2,1)S(1)}, bf16[256,128]{1,0:T(8,128)(2,1)S(1)}, u32[]{:S(2)}, u32[]{:S(2)}) collective-permute-start(bf16[256,128]{1,0:T(8,128)(2,1)S(1)} %step.29.refs_1_.refs_4_), channel_id=1, source_target_pairs={{1,0},{2,1},{3,2},{4,3},{5,4},{6,5},{7,6},{8,7},{9,8},{10,9},{11,1... | collective-permute-start | bytes 196616 | tf_op jit(solution)/shard_map/ppermute | solution.py:163
  198.4 7.7 %collective-permute-start.28 = (bf16[256,128]{1,0:T(8,128)(2,1)S(1)}, bf16[256,128]{1,0:T(8,128)(2,1)S(1)}, u32[]{:S(2)}, u32[]{:S(2)}) collective-permute-start(bf16[256,128]{1,0:T(8,128)(2,1)S(1)} %step.29.refs_1_.refs_4_), channel_id=1, source_target_pairs={{0,1},{1,2},{2,3},{3,4},{4,5},{5,6},{6,7},{7,8},{8,9},{9,10},{10,1... | collective-permute-start | bytes 196616 | tf_op jit(solution)/shard_map/ppermute | solution.py:162
  208.0 5.1 %collective-permute-start.31 = (bf16[256,128]{1,0:T(8,128)(2,1)S(1)}, bf16[256,128]{1,0:T(8,128)(2,1)S(1)}, u32[]{:S(2)}, u32[]{:S(2)}) collective-permute-start(bf16[256,128]{1,0:T(8,128)(2,1)S(1)} %step.30.refs_1_), channel_id=1, source_target_pairs={{1,0},{2,1},{3,2},{4,3},{5,4},{6,5},{7,6},{8,7},{9,8},{10,9},{11,1... | collective-permute-start | bytes 196616 | tf_op jit(solution)/shard_map/ppermute | solution.py:163
  209.9 7.7 %collective-permute-start.30 = (bf16[256,128]{1,0:T(8,128)(2,1)S(1)}, bf16[256,128]{1,0:T(8,128)(2,1)S(1)}, u32[]{:S(2)}, u32[]{:S(2)}) collective-permute-start(bf16[256,128]{1,0:T(8,128)(2,1)S(1)} %step.30.refs_1_), channel_id=1, source_target_pairs={{0,1},{1,2},{2,3},{3,4},{4,5},{5,6},{6,7},{7,8},{8,9},{9,10},{10,1... | collective-permute-start | bytes 196616 | tf_op jit(solution)/shard_map/ppermute | solution.py:162

commit v2 on v1

v2 whole, which is shorter than its diff:
```python
import functools

import jax
import jax.numpy as jnp
from jax import lax
from jax.experimental import pallas as pl
from jax.experimental.pallas import tpu as pltpu
from jax.sharding import PartitionSpec as P

R = 2
C = 64
W = 128
ROWS = 4
H = 256
FRAMES = 8
EXT = ROWS + 2 * R


def leaky(values):
    return jnp.maximum(values, 0.1 * values)


def tap_weights(params, grid):
    sy, sx, qy, qx = (params[n] for n in range(4))
    rows = grid[0] + grid[1] * (lax.broadcasted_iota(jnp.int32, (EXT, W), 0) - R)
    cols = lax.broadcasted_iota(jnp.int32, (EXT, W), 1)
    out = []
    across = []
    for dx in range(-R, R + 1):
        u = jnp.where(sx == dx, 1.0 - qx, jnp.where(sx == dx - 1, qx, 0.0))
        across.append(jnp.where((cols + dx >= 0) & (cols + dx < W), u, 0.0))
    for dy in range(-R, R + 1):
        v = jnp.where(sy == dy, 1.0 - qy, jnp.where(sy == dy - 1, qy, 0.0))
        at = rows + grid[1] * dy
        v = jnp.where((at >= 0) & (at < H), v, 0.0)
        for dx in range(-R, R + 1):
            w = v * across[dx + R]
            out.append(pltpu.roll(w, dx % W, 1) if dx else w)
    return out


def far_row(trio, o):
    across, own, beside = trio
    if o < 0:
        return across, (-1 - o) * C
    if o < ROWS:
        return own, o * C
    return beside, (2 * ROWS - 1 - o) * C - (ROWS * C - beside.shape[0])


def sample_row(trio, r, taps, store):
    weights = [taps(n) for n in range(25)]
    for ch in range(0, C, 16):
        g = []
        for dy in range(-R, R + 1):
            ref, at = far_row(trio, r - R + dy)
            g.append(ref[pl.ds(at + ch, 16), :])
        total = None
        for dx in range(5):
            t = g[0] * weights[dx]
            for dy in range(1, 5):
                t = t + g[dy] * weights[dy * 5 + dx]
            t = t.astype(jnp.float32)
            t = pltpu.roll(t, (R - dx) % W, 1) if dx != R else t
            total = t if total is None else total + t
        store(ch, total.astype(jnp.bfloat16))


def prepare_kernel(priors, grid, *refs):
    refs = list(refs)
    older = [refs.pop(0) for _ in range(3)] if priors == 2 else None
    params, taps = refs.pop(0), refs.pop(0)
    for n, w in enumerate(tap_weights(params[0], grid)):
        for r in range(EXT):
            taps[r, n] = jnp.broadcast_to(w[r : r + 1], (16, W)).astype(jnp.bfloat16)
    if priors < 2:
        return
    stack, wts = refs
    for n, w in enumerate(tap_weights(params[1], grid)):
        wts[n] = w
    for r in range(EXT):

        def weight(n):
            return jnp.broadcast_to(wts[n, pl.ds(r, 1), :], (16, W)).astype(jnp.bfloat16)

        def store(ch, value):
            stack[pl.ds(ch, 16), pl.ds(r * W, W)] = value

        sample_row(older, r, weight, store)


def step_kernel(priors, parts, grid, *refs):
    refs = list(refs)
    sides = [[refs.pop(0) for _ in range(3)] for _ in range(parts)]
    newest = [refs.pop(0) for _ in range(3)] if priors else None
    taps = refs.pop(0) if priors else None
    older = refs.pop(0) if priors == 2 else None
    mixer, inner, outer, out, stack, joined, hidden = refs

    def keep(row):
        at = grid[0] + grid[1] * row
        return jnp.where((at >= 0) & (at < H), 1.0, 0.0)

    def side_row(trio, r):
        ref, at = far_row(trio, r - R)
        return ref[pl.ds(at, C), :]

    depth = (parts + priors) * C
    for r in (4, 6, 2, 0):
        for n in range(2 if priors else 0):

            def store(ch, value):
                stack[pl.ds(ch, 16), pl.ds((r + n) * W, W)] = value

            sample_row(newest, r + n, lambda k: taps[r + n, k], store)
        pieces = [
            jnp.concatenate([side_row(trio, r), side_row(trio, r + 1)], axis=1) for trio in sides
        ]
        if priors:
            pieces.append(stack[:, pl.ds(r * W, 2 * W)])
        if priors == 2:
            pieces.append(older[:, pl.ds(r * W, 2 * W)])
        data = jnp.concatenate(pieces, axis=0)
        both = leaky(jnp.dot(mixer[:, pl.ds(0, depth)], data, preferred_element_type=jnp.float32))
        for n in range(2):
            value = both[:, n * W : (n + 1) * W]
            if not R <= r + n < R + ROWS:
                value = value * keep(r + n - R)
            joined[pl.ds((r + n) * C, C), :] = value.astype(jnp.bfloat16)

    cols = lax.broadcasted_iota(jnp.int32, (C, W), 1)

    def conv_pair(source, kernel, r):
        data = jnp.concatenate(
            [source[pl.ds(r * C, 3 * C), :], source[pl.ds((r + 1) * C, 3 * C), :]], axis=1
        )
        res = jnp.dot(kernel[...], data, preferred_element_type=jnp.float32)
        outs = []
        for n in range(2):
            part = res[:, n * W : (n + 1) * W]
            left = jnp.where(cols >= 1, pltpu.roll(part[0:C], 1, 1), 0.0)
            right = jnp.where(cols < W - 1, pltpu.roll(part[2 * C : 3 * C], W - 1, 1), 0.0)
            outs.append(left + part[C : 2 * C] + right)
        return outs

    for r in (4, 2, 0):
        for n, value in enumerate(conv_pair(joined, inner, r)):
            value = leaky(value)
            if r + n in (0, ROWS + 1):
                value = value * keep(r + n - 1)
            hidden[pl.ds((r + n) * C, C), :] = value.astype(jnp.bfloat16)

    for r in (2, 0):
        for n, value in enumerate(conv_pair(hidden, outer, r)):
            base = joined[pl.ds((r + n + R) * C, C), :].astype(jnp.float32)
            out[pl.ds((r + n) * C, C), :] = (base + value).astype(jnp.bfloat16)


VMEM = pl.BlockSpec(memory_space=pltpu.VMEM)
SMEM = pl.BlockSpec(memory_space=pltpu.SMEM)
BF16 = jnp.bfloat16


def run_prepare(grid, older, params):
    operands = [grid] + (list(older) if older else []) + [params]
    outs = [jax.ShapeDtypeStruct((EXT, 25, 16, W), BF16)]
    if older:
        outs.append(jax.ShapeDtypeStruct((C, EXT * W), BF16))
    return pl.pallas_call(
        functools.partial(prepare_kernel, 2 if older else 1),
        out_shape=outs,
        in_specs=[SMEM] + [VMEM] * (len(operands) - 1),
        out_specs=[VMEM] * len(outs),
        scratch_shapes=[pltpu.VMEM((25, EXT, W), jnp.float32)] if older else [],
        compiler_params=pltpu.CompilerParams(vmem_limit_bytes=16 * 2**20),
        cost_estimate=pl.CostEstimate(flops=2 * 10**7, bytes_accessed=2**20, transcendentals=0),
        name="prepare",
    )(*operands)


def run_step(grid, sides, newest, prepared, weights):
    operands = [grid]
    for trio in sides:
        operands += list(trio)
    operands += (list(newest) if newest else []) + list(prepared) + list(weights)
    return pl.pallas_call(
        functools.partial(step_kernel, len(prepared), len(sides)),
        out_shape=jax.ShapeDtypeStruct((ROWS * C, W), BF16),
        in_specs=[SMEM] + [VMEM] * (len(operands) - 1),
        out_specs=VMEM,
        scratch_shapes=[
            pltpu.VMEM((C, EXT * W), BF16),
            pltpu.VMEM((EXT * C, W), BF16),
            pltpu.VMEM(((ROWS + 2) * C, W), BF16),
        ],
        compiler_params=pltpu.CompilerParams(vmem_limit_bytes=16 * 2**20),
        cost_estimate=pl.CostEstimate(flops=10**8, bytes_accessed=2**20, transcendentals=0),
        name="step",
    )(*operands)


def swap(for_across, for_beside):
    count = lax.axis_size("tile")
    pairs = [(i, i + 1) for i in range(1, count - 1, 2)]
    across = lax.ppermute(for_across, "tile", pairs + [(j, i) for i, j in pairs])
    beside = lax.ppermute(for_beside, "tile", [(i, i ^ 1) for i in range(count)])
    return across, beside


def conv_matrix(kernel, odd):
    taps = kernel.reshape(C, 3, 3, C)
    taps = jnp.where(odd, taps[:, ::-1], taps)
    return taps.transpose(2, 0, 1, 3).reshape(3 * C, 3 * C)


def shards(
    frames,
    back_shift,
    back_fraction,
    ahead_shift,
    ahead_fraction,
    back_mixer,
    back_inner,
    back_outer,
    ahead_mixer,
    ahead_inner,
    ahead_outer,
):
    tile = lax.axis_index("tile").astype(jnp.int32)
    turn = lax.axis_index("tm")
    odd = tile % 2 == 1
    grid = jnp.stack([tile * ROWS + jnp.where(odd, ROWS - 1, 0), jnp.where(odd, -1, 1)])

    def oriented(values, axis):
        return jnp.where(odd, jnp.flip(values, axis), values)

    own = oriented(frames[0].transpose(1, 0, 2), 0).reshape(ROWS * C, W)

    def pack(shift, fraction):
        sy, sx, qy, qx = shift[0, :, 0], shift[0, :, 1], fraction[0, :, 0], fraction[0, :, 1]
        sy = jnp.where(odd, -1 - sy, sy)
        qy = jnp.where(odd, 1.0 - qy, qy)
        values = jnp.stack([v.astype(BF16) for v in (sy, sx, qy, qx)], axis=1)
        return oriented(values.transpose(2, 0, 1, 3), 0)

    own_params = jnp.stack(
        [pack(back_shift, back_fraction), pack(ahead_shift, ahead_fraction)], axis=1
    ).reshape(ROWS * 16, W)
    mine = jnp.concatenate([own, own_params], axis=0)
    clip = lax.all_to_all(
        jnp.broadcast_to(mine[None], (FRAMES,) + mine.shape), "tm", split_axis=0, concat_axis=0
    )

    top = jnp.concatenate([clip[:, : 2 * C], clip[:, 4 * C : 4 * C + 32]], axis=1)
    low = jnp.concatenate([clip[:, 2 * C : 4 * C], clip[:, 4 * C + 32 :]], axis=1)
    across, beside = swap(top, low)

    def turned(halo):
        rows = halo[:, 2 * C :].reshape(FRAMES, 2, 2, 2, 4, W)[:, ::-1].astype(jnp.float32)
        return jnp.stack([-1.0 - rows[..., 0, :], rows[..., 1, :], 1.0 - rows[..., 2, :], rows[..., 3, :]], axis=4)

    mid = clip[:, 4 * C :].reshape(FRAMES, ROWS, 2, 2, 4, W).astype(jnp.float32)
    params = jnp.concatenate([turned(across), mid, turned(beside)], axis=1).transpose(2, 0, 3, 4, 1, 5)
    frame_trios = [(across[t, : 2 * C], clip[t, : 4 * C], beside[t, : 2 * C]) for t in range(FRAMES)]

    def chain(order, way, extra, weights):
        done = {}
        history = []
        for n, t in enumerate(order):
            sides = [frame_trios[t]] + ([extra[t]] if extra else [])
            prepared = run_prepare(grid, history[1] if n > 1 else None, params[way, t]) if n else []
            new = run_step(grid, sides, history[0] if n else None, prepared, weights)
            if n + 1 < FRAMES or not extra:
                far, near = swap(new, new)
                done[t] = (far, new, near)
                history.insert(0, done[t])
            else:
                done[t] = (None, new, None)
        return done

    back_weights = (back_mixer, conv_matrix(back_inner, odd), conv_matrix(back_outer, odd))
    ahead_weights = (ahead_mixer, conv_matrix(ahead_inner, odd), conv_matrix(ahead_outer, odd))
    back = chain(range(FRAMES - 1, -1, -1), 0, None, back_weights)
    ahead = chain(range(FRAMES), 1, back, ahead_weights)

    def pick(done):
        value = done[0][1]
        for t in range(1, FRAMES):
            value = jnp.where(turn == t, done[t][1], value)
        return oriented(value.reshape(ROWS, C, W), 0).transpose(1, 0, 2)[None]

    return pick(back), pick(ahead)


def solution(mesh):
    in_specs = (
        P("tm", None, "tile", None),
        P("tm", None, None, "tile", None),
        P("tm", None, None, "tile", None),
        P("tm", None, None, "tile", None),
        P("tm", None, None, "tile", None),
        P(),
        P(),
        P(),
        P(),
        P(),
        P(),
    )
    out_specs = (P("tm", None, "tile", None), P("tm", None, "tile", None))
    return jax.shard_map(shards, mesh=mesh, in_specs=in_specs, out_specs=out_specs, check_vma=False)
```

time: 222 us -> 199 us (0.90)
  the two profiles are of different devices: /device:TPU:6 before, /device:TPU:7 now
where the time goes in v2:
time: 199 us; the launch traced here: 198 us
  starting transfers between devices  119 us (60%)
  Pallas kernels  44.8 us (23%)
  waiting for transfers between devices  20.2 us (10%)
  local copies, waits for them, and re-layouts  10.1 us (5%)
    ppermute x16, starting transfers between devices, swap(): lax.ppermute(for_beside, 'tile', [(i, i ^ 1) for i in range(count)])  78.8 us
    ppermute x16, starting transfers between devices, swap(): lax.ppermute(for_across, 'tile', pairs + [(j, i) for i, j in pairs])  33.5 us
    pallas_call x16, Pallas kernels, run_step(): pl.pallas_call(functools.partial(step_kernel, len(prepared), len(sides)),...  29.1 us
    all_to_all x1, waiting for transfers between devices, shards(): lax.all_to_all(jnp.broadcast_to(mine[None], (FRAMES,) + mine.shape), 'tm'...  18.9 us
    pallas_call x14, Pallas kernels, run_prepare(): pl.pallas_call(functools.partial(prepare_kernel, 2 if older else 1), out_...  15.7 us
    all_to_all x1, starting transfers between devices, shards(): lax.all_to_all(jnp.broadcast_to(mine[None], (FRAMES,) + mine.shape), 'tm'...  6.95 us
    unnamed x31, local copies, waits for them, and re-layouts  6.76 us
  transfers between devices with their start and end apart: 33, of which 3 were waited for; matrix products, arithmetic and copies ran while one was open for 2% of the time, Pallas kernels for 8%

profile of v2, /device:TPU:7, one launch (start us, length us, event | category | flops | bytes accessed | tf_op | source)
XLA Modules:
  0.0 197.6 jit_solution(6761218573373927821)
XLA Ops:
  4.7 7.0 %all-to-all-start = ((bf16[8,320,128]{2,1,0:T(8,128)(2,1)}), bf16[8,320,128]{2,1,0:T(8,128)(2,1)S(1)}, u32[]{:S(2)}, u32[]{:S(2)}) async-start(bf16[8,320,128]{2,1,0:T(8,128)(2,1)} %broadcast_in_dim.12), calls=%async_computation | async-start | bytes 1310720 | tf_op jit(solution)/shard_map/all_to_all | solution.py:250
  13.5 18.9 %all-to-all-done = bf16[8,320,128]{2,1,0:T(8,128)(2,1)S(1)} async-done(((bf16[8,320,128]{2,1,0:T(8,128)(2,1)}), bf16[8,320,128]{2,1,0:T(8,128)(2,1)S(1)}, u32[]{:S(2)}, u32[]{:S(2)}) %all-to-all-start) | async-done | bytes 655392 | tf_op jit(solution)/shard_map/all_to_all | solution.py:250
  32.5 4.4 %collective-permute-start = (bf16[8,160,128]{2,1,0:T(8,128)(2,1)S(1)}, bf16[8,160,128]{2,1,0:T(8,128)(2,1)S(1)}, u32[]{:S(2)}, u32[]{:S(2)}) collective-permute-start(bf16[8,160,128]{2,1,0:T(8,128)(2,1)S(1)} %pad_maximum_fusion), channel_id=1, source_target_pairs={{1,2},{3,4},{5,6},{7,8},{9,10},{11,12},{13,14},{15,16},{17,18},{19... | collective-permute-start | bytes 983048 | tf_op jit(solution)/shard_map/ppermute | solution.py:205
  36.9 8.9 %collective-permute-start.1 = (bf16[8,160,128]{2,1,0:T(8,128)(2,1)S(1)}, bf16[8,160,128]{2,1,0:T(8,128)(2,1)S(1)}, u32[]{:S(2)}, u32[]{:S(2)}) collective-permute-start(bf16[8,160,128]{2,1,0:T(8,128)(2,1)S(1)} %pad_maximum_fusion.1), channel_id=1, source_target_pairs={{0,1},{1,0},{2,3},{3,2},{4,5},{5,4},{6,7},{7,6},{8,9},{9,8},{10,11... | collective-permute-start | bytes 983048 | tf_op jit(solution)/shard_map/ppermute | solution.py:206
  48.4 1.9 collective-permute-start.2
  50.3 8.0 %collective-permute-start.3 = (bf16[256,128]{1,0:T(8,128)(2,1)S(1)}, bf16[256,128]{1,0:T(8,128)(2,1)S(1)}, u32[]{:S(2)}, u32[]{:S(2)}) collective-permute-start(bf16[256,128]{1,0:T(8,128)(2,1)S(1)} %step.16.refs_4_.refs_1_), channel_id=1, source_target_pairs={{0,1},{1,0},{2,3},{3,2},{4,5},{5,4},{6,7},{7,6},{8,9},{9,8},{10,11... | collective-permute-start | bytes 196616 | tf_op jit(solution)/shard_map/ppermute | solution.py:206
  60.3 1.9 step.17.refs_4_.refs_1_
  62.1 1.9 collective-permute-start.4
  64.0 3.9 %collective-permute-start.5 = (bf16[256,128]{1,0:T(8,128)(2,1)S(1)}, bf16[256,128]{1,0:T(8,128)(2,1)S(1)}, u32[]{:S(2)}, u32[]{:S(2)}) collective-permute-start(bf16[256,128]{1,0:T(8,128)(2,1)S(1)} %step.17.refs_4_.refs_1_), channel_id=1, source_target_pairs={{0,1},{1,0},{2,3},{3,2},{4,5},{5,4},{6,7},{7,6},{8,9},{9,8},{10,11... | collective-permute-start | bytes 196616 | tf_op jit(solution)/shard_map/ppermute | solution.py:206
  69.1 1.9 step.18.refs_4_.refs_1_
  71.0 1.9 collective-permute-start.6
  73.0 4.5 %collective-permute-start.7 = (bf16[256,128]{1,0:T(8,128)(2,1)S(1)}, bf16[256,128]{1,0:T(8,128)(2,1)S(1)}, u32[]{:S(2)}, u32[]{:S(2)}) collective-permute-start(bf16[256,128]{1,0:T(8,128)(2,1)S(1)} %step.18.refs_4_.refs_1_), channel_id=1, source_target_pairs={{0,1},{1,0},{2,3},{3,2},{4,5},{5,4},{6,7},{7,6},{8,9},{9,8},{10,11... | collective-permute-start | bytes 196616 | tf_op jit(solution)/shard_map/ppermute | solution.py:206
  78.7 1.9 step.19.refs_4_.refs_1_
  80.7 1.9 collective-permute-start.8
  82.6 4.5 %collective-permute-start.9 = (bf16[256,128]{1,0:T(8,128)(2,1)S(1)}, bf16[256,128]{1,0:T(8,128)(2,1)S(1)}, u32[]{:S(2)}, u32[]{:S(2)}) collective-permute-start(bf16[256,128]{1,0:T(8,128)(2,1)S(1)} %step.19.refs_4_.refs_1_), channel_id=1, source_target_pairs={{0,1},{1,0},{2,3},{3,2},{4,5},{5,4},{6,7},{7,6},{8,9},{9,8},{10,11... | collective-permute-start | bytes 196616 | tf_op jit(solution)/shard_map/ppermute | solution.py:206
  88.3 1.9 step.20.refs_4_.refs_1_
  90.3 1.9 collective-permute-start.10
  92.2 4.7 %collective-permute-start.11 = (bf16[256,128]{1,0:T(8,128)(2,1)S(1)}, bf16[256,128]{1,0:T(8,128)(2,1)S(1)}, u32[]{:S(2)}, u32[]{:S(2)}) collective-permute-start(bf16[256,128]{1,0:T(8,128)(2,1)S(1)} %step.20.refs_4_.refs_1_), channel_id=1, source_target_pairs={{0,1},{1,0},{2,3},{3,2},{4,5},{5,4},{6,7},{7,6},{8,9},{9,8},{10,11... | collective-permute-start | bytes 196616 | tf_op jit(solution)/shard_map/ppermute | solution.py:206
  98.1 1.9 step.21.refs_4_.refs_1_
  100.0 1.9 collective-permute-start.12
  102.0 4.4 %collective-permute-start.13 = (bf16[256,128]{1,0:T(8,128)(2,1)S(1)}, bf16[256,128]{1,0:T(8,128)(2,1)S(1)}, u32[]{:S(2)}, u32[]{:S(2)}) collective-permute-start(bf16[256,128]{1,0:T(8,128)(2,1)S(1)} %step.21.refs_4_.refs_1_), channel_id=1, source_target_pairs={{0,1},{1,0},{2,3},{3,2},{4,5},{5,4},{6,7},{7,6},{8,9},{9,8},{10,11... | collective-permute-start | bytes 196616 | tf_op jit(solution)/shard_map/ppermute | solution.py:206
  107.6 1.9 step.22.refs_4_
  109.5 2.1 %collective-permute-start.14 = (bf16[256,128]{1,0:T(8,128)(2,1)S(1)}, bf16[256,128]{1,0:T(8,128)(2,1)S(1)}, u32[]{:S(2)}, u32[]{:S(2)}) collective-permute-start(bf16[256,128]{1,0:T(8,128)(2,1)S(1)} %step.22.refs_4_), channel_id=1, source_target_pairs={{1,2},{3,4},{5,6},{7,8},{9,10},{11,12},{13,14},{15,16},{17,18},{19... | collective-permute-start | bytes 196616 | tf_op jit(solution)/shard_map/ppermute | solution.py:205
  111.6 4.5 %collective-permute-start.15 = (bf16[256,128]{1,0:T(8,128)(2,1)S(1)}, bf16[256,128]{1,0:T(8,128)(2,1)S(1)}, u32[]{:S(2)}, u32[]{:S(2)}) collective-permute-start(bf16[256,128]{1,0:T(8,128)(2,1)S(1)} %step.22.refs_4_), channel_id=1, source_target_pairs={{0,1},{1,0},{2,3},{3,2},{4,5},{5,4},{6,7},{7,6},{8,9},{9,8},{10,11... | collective-permute-start | bytes 196616 | tf_op jit(solution)/shard_map/ppermute | solution.py:206
  117.6 1.9 step.23.refs_4_
  119.6 1.9 collective-permute-start.16
  121.5 4.2 %collective-permute-start.17 = (bf16[256,128]{1,0:T(8,128)(2,1)S(1)}, bf16[256,128]{1,0:T(8,128)(2,1)S(1)}, u32[]{:S(2)}, u32[]{:S(2)}) collective-permute-start(bf16[256,128]{1,0:T(8,128)(2,1)S(1)} %step.23.refs_4_), channel_id=1, source_target_pairs={{0,1},{1,0},{2,3},{3,2},{4,5},{5,4},{6,7},{7,6},{8,9},{9,8},{10,11... | collective-permute-start | bytes 196616 | tf_op jit(solution)/shard_map/ppermute | solution.py:206
  129.8 1.9 collective-permute-start.18
  131.7 3.8 %collective-permute-start.19 = (bf16[256,128]{1,0:T(8,128)(2,1)S(1)}, bf16[256,128]{1,0:T(8,128)(2,1)S(1)}, u32[]{:S(2)}, u32[]{:S(2)}) collective-permute-start(bf16[256,128]{1,0:T(8,128)(2,1)S(1)} %step.24.refs_7_.refs_1_), channel_id=1, source_target_pairs={{0,1},{1,0},{2,3},{3,2},{4,5},{5,4},{6,7},{7,6},{8,9},{9,8},{10,11... | collective-permute-start | bytes 196616 | tf_op jit(solution)/shard_map/ppermute | solution.py:206
  136.4 1.9 step.25.refs_7_.refs_1_
  138.3 2.1 %collective-permute-start.20 = (bf16[256,128]{1,0:T(8,128)(2,1)S(1)}, bf16[256,128]{1,0:T(8,128)(2,1)S(1)}, u32[]{:S(2)}, u32[]{:S(2)}) collective-permute-start(bf16[256,128]{1,0:T(8,128)(2,1)S(1)} %step.25.refs_7_.refs_1_), channel_id=1, source_target_pairs={{1,2},{3,4},{5,6},{7,8},{9,10},{11,12},{13,14},{15,16},{17,18},{19... | collective-permute-start | bytes 196616 | tf_op jit(solution)/shard_map/ppermute | solution.py:205
  140.4 4.7 %collective-permute-start.21 = (bf16[256,128]{1,0:T(8,128)(2,1)S(1)}, bf16[256,128]{1,0:T(8,128)(2,1)S(1)}, u32[]{:S(2)}, u32[]{:S(2)}) collective-permute-start(bf16[256,128]{1,0:T(8,128)(2,1)S(1)} %step.25.refs_7_.refs_1_), channel_id=1, source_target_pairs={{0,1},{1,0},{2,3},{3,2},{4,5},{5,4},{6,7},{7,6},{8,9},{9,8},{10,11... | collective-permute-start | bytes 196616 | tf_op jit(solution)/shard_map/ppermute | solution.py:206
  146.4 1.9 step.26.refs_7_.refs_1_
  148.2 1.9 collective-permute-start.22
  150.2 4.5 %collective-permute-start.23 = (bf16[256,128]{1,0:T(8,128)(2,1)S(1)}, bf16[256,128]{1,0:T(8,128)(2,1)S(1)}, u32[]{:S(2)}, u32[]{:S(2)}) collective-permute-start(bf16[256,128]{1,0:T(8,128)(2,1)S(1)} %step.26.refs_7_.refs_1_), channel_id=1, source_target_pairs={{0,1},{1,0},{2,3},{3,2},{4,5},{5,4},{6,7},{7,6},{8,9},{9,8},{10,11... | collective-permute-start | bytes 196616 | tf_op jit(solution)/shard_map/ppermute | solution.py:206
  155.9 1.9 step.27.refs_7_.refs_1_
  157.8 1.9 collective-permute-start.24
  159.8 4.8 %collective-permute-start.25 = (bf16[256,128]{1,0:T(8,128)(2,1)S(1)}, bf16[256,128]{1,0:T(8,128)(2,1)S(1)}, u32[]{:S(2)}, u32[]{:S(2)}) collective-permute-start(bf16[256,128]{1,0:T(8,128)(2,1)S(1)} %step.27.refs_7_.refs_1_), channel_id=1, source_target_pairs={{0,1},{1,0},{2,3},{3,2},{4,5},{5,4},{6,7},{7,6},{8,9},{9,8},{10,11... | collective-permute-start | bytes 196616 | tf_op jit(solution)/shard_map/ppermute | solution.py:206
  165.7 1.9 step.28.refs_7_.refs_1_
  167.6 1.9 collective-permute-start.26
  169.6 4.3 %collective-permute-start.27 = (bf16[256,128]{1,0:T(8,128)(2,1)S(1)}, bf16[256,128]{1,0:T(8,128)(2,1)S(1)}, u32[]{:S(2)}, u32[]{:S(2)}) collective-permute-start(bf16[256,128]{1,0:T(8,128)(2,1)S(1)} %step.28.refs_7_.refs_1_), channel_id=1, source_target_pairs={{0,1},{1,0},{2,3},{3,2},{4,5},{5,4},{6,7},{7,6},{8,9},{9,8},{10,11... | collective-permute-start | bytes 196616 | tf_op jit(solution)/shard_map/ppermute | solution.py:206
  175.1 1.9 step.29.refs_7_.refs_1_
  177.0 1.9 collective-permute-start.28
  178.9 4.5 %collective-permute-start.29 = (bf16[256,128]{1,0:T(8,128)(2,1)S(1)}, bf16[256,128]{1,0:T(8,128)(2,1)S(1)}, u32[]{:S(2)}, u32[]{:S(2)}) collective-permute-start(bf16[256,128]{1,0:T(8,128)(2,1)S(1)} %step.29.refs_7_.refs_1_), channel_id=1, source_target_pairs={{0,1},{1,0},{2,3},{3,2},{4,5},{5,4},{6,7},{7,6},{8,9},{9,8},{10,11... | collective-permute-start | bytes 196616 | tf_op jit(solution)/shard_map/ppermute | solution.py:206
  184.7 1.9 step.30.refs_7_
  186.6 1.9 collective-permute-start.30
  188.5 4.5 %collective-permute-start.31 = (bf16[256,128]{1,0:T(8,128)(2,1)S(1)}, bf16[256,128]{1,0:T(8,128)(2,1)S(1)}, u32[]{:S(2)}, u32[]{:S(2)}) collective-permute-start(bf16[256,128]{1,0:T(8,128)(2,1)S(1)} %step.30.refs_7_), channel_id=1, source_target_pairs={{0,1},{1,0},{2,3},{3,2},{4,5},{5,4},{6,7},{7,6},{8,9},{9,8},{10,11... | collective-permute-start | bytes 196616 | tf_op jit(solution)/shard_map/ppermute | solution.py:206
  195.0 1.9 step.31
  (137 shorter events, 31.3 us)
Async XLA Ops:
  0.6 0.7 copy-start.10
  0.6 0.7 copy-start.11
  1.3 0.7 copy-start.8
  2.1 0.7 copy-start.9
  2.8 0.8 copy-start.7
  4.7 7.0 %copy-start.3 = (bf16[64,576]{1,0:T(8,128)(2,1)S(1)}, bf16[64,576]{1,0:T(8,128)(2,1)}, u32[]{:S(2)}) copy-start(bf16[64,576]{1,0:T(8,128)(2,1)} %param.17) | copy-start | bytes 221188
  4.7 27.7 %all-to-all-start = ((bf16[8,320,128]{2,1,0:T(8,128)(2,1)}), bf16[8,320,128]{2,1,0:T(8,128)(2,1)S(1)}, u32[]{:S(2)}, u32[]{:S(2)}) async-start(bf16[8,320,128]{2,1,0:T(8,128)(2,1)} %broadcast_in_dim.12), calls=%async_computation | async-start | bytes 1310720 | tf_op jit(solution)/shard_map/all_to_all | solution.py:250
  11.6 0.9 copy-start.4
  32.5 13.5 %collective-permute-start = (bf16[8,160,128]{2,1,0:T(8,128)(2,1)S(1)}, bf16[8,160,128]{2,1,0:T(8,128)(2,1)S(1)}, u32[]{:S(2)}, u32[]{:S(2)}) collective-permute-start(bf16[8,160,128]{2,1,0:T(8,128)(2,1)S(1)} %pad_maximum_fusion), channel_id=1, source_target_pairs={{1,2},{3,4},{5,6},{7,8},{9,10},{11,12},{13,14},{15,16},{17,18},{19... | collective-permute-start | bytes 983048 | tf_op jit(solution)/shard_map/ppermute | solution.py:205
  36.9 10.1 %collective-permute-start.1 = (bf16[8,160,128]{2,1,0:T(8,128)(2,1)S(1)}, bf16[8,160,128]{2,1,0:T(8,128)(2,1)S(1)}, u32[]{:S(2)}, u32[]{:S(2)}) collective-permute-start(bf16[8,160,128]{2,1,0:T(8,128)(2,1)S(1)} %pad_maximum_fusion.1), channel_id=1, source_target_pairs={{0,1},{1,0},{2,3},{3,2},{4,5},{5,4},{6,7},{7,6},{8,9},{9,8},{10,11... | collective-permute-start | bytes 983048 | tf_op jit(solution)/shard_map/ppermute | solution.py:206
  46.0 1.0 copy-start
  48.4 11.9 %collective-permute-start.2 = (bf16[256,128]{1,0:T(8,128)(2,1)S(1)}, bf16[256,128]{1,0:T(8,128)(2,1)S(1)}, u32[]{:S(2)}, u32[]{:S(2)}) collective-permute-start(bf16[256,128]{1,0:T(8,128)(2,1)S(1)} %step.16.refs_4_.refs_1_), channel_id=1, source_target_pairs={{1,2},{3,4},{5,6},{7,8},{9,10},{11,12},{13,14},{15,16},{17,18},{19... | collective-permute-start | bytes 196616 | tf_op jit(solution)/shard_map/ppermute | solution.py:205
  50.3 10.0 %collective-permute-start.3 = (bf16[256,128]{1,0:T(8,128)(2,1)S(1)}, bf16[256,128]{1,0:T(8,128)(2,1)S(1)}, u32[]{:S(2)}, u32[]{:S(2)}) collective-permute-start(bf16[256,128]{1,0:T(8,128)(2,1)S(1)} %step.16.refs_4_.refs_1_), channel_id=1, source_target_pairs={{0,1},{1,0},{2,3},{3,2},{4,5},{5,4},{6,7},{7,6},{8,9},{9,8},{10,11... | collective-permute-start | bytes 196616 | tf_op jit(solution)/shard_map/ppermute | solution.py:206
  62.1 7.0 %collective-permute-start.4 = (bf16[256,128]{1,0:T(8,128)(2,1)S(1)}, bf16[256,128]{1,0:T(8,128)(2,1)S(1)}, u32[]{:S(2)}, u32[]{:S(2)}) collective-permute-start(bf16[256,128]{1,0:T(8,128)(2,1)S(1)} %step.17.refs_4_.refs_1_), channel_id=1, source_target_pairs={{1,2},{3,4},{5,6},{7,8},{9,10},{11,12},{13,14},{15,16},{17,18},{19... | collective-permute-start | bytes 196616 | tf_op jit(solution)/shard_map/ppermute | solution.py:205
  64.0 5.1 %collective-permute-start.5 = (bf16[256,128]{1,0:T(8,128)(2,1)S(1)}, bf16[256,128]{1,0:T(8,128)(2,1)S(1)}, u32[]{:S(2)}, u32[]{:S(2)}) collective-permute-start(bf16[256,128]{1,0:T(8,128)(2,1)S(1)} %step.17.refs_4_.refs_1_), channel_id=1, source_target_pairs={{0,1},{1,0},{2,3},{3,2},{4,5},{5,4},{6,7},{7,6},{8,9},{9,8},{10,11... | collective-permute-start | bytes 196616 | tf_op jit(solution)/shard_map/ppermute | solution.py:206
  71.0 7.7 %collective-permute-start.6 = (bf16[256,128]{1,0:T(8,128)(2,1)S(1)}, bf16[256,128]{1,0:T(8,128)(2,1)S(1)}, u32[]{:S(2)}, u32[]{:S(2)}) collective-permute-start(bf16[256,128]{1,0:T(8,128)(2,1)S(1)} %step.18.refs_4_.refs_1_), channel_id=1, source_target_pairs={{1,2},{3,4},{5,6},{7,8},{9,10},{11,12},{13,14},{15,16},{17,18},{19... | collective-permute-start | bytes 196616 | tf_op jit(solution)/shard_map/ppermute | solution.py:205
  73.0 5.8 %collective-permute-start.7 = (bf16[256,128]{1,0:T(8,128)(2,1)S(1)}, bf16[256,128]{1,0:T(8,128)(2,1)S(1)}, u32[]{:S(2)}, u32[]{:S(2)}) collective-permute-start(bf16[256,128]{1,0:T(8,128)(2,1)S(1)} %step.18.refs_4_.refs_1_), channel_id=1, source_target_pairs={{0,1},{1,0},{2,3},{3,2},{4,5},{5,4},{6,7},{7,6},{8,9},{9,8},{10,11... | collective-permute-start | bytes 196616 | tf_op jit(solution)/shard_map/ppermute | solution.py:206
  80.7 7.7 %collective-permute-start.8 = (bf16[256,128]{1,0:T(8,128)(2,1)S(1)}, bf16[256,128]{1,0:T(8,128)(2,1)S(1)}, u32[]{:S(2)}, u32[]{:S(2)}) collective-permute-start(bf16[256,128]{1,0:T(8,128)(2,1)S(1)} %step.19.refs_4_.refs_1_), channel_id=1, source_target_pairs={{1,2},{3,4},{5,6},{7,8},{9,10},{11,12},{13,14},{15,16},{17,18},{19... | collective-permute-start | bytes 196616 | tf_op jit(solution)/shard_map/ppermute | solution.py:205
  82.6 5.8 %collective-permute-start.9 = (bf16[256,128]{1,0:T(8,128)(2,1)S(1)}, bf16[256,128]{1,0:T(8,128)(2,1)S(1)}, u32[]{:S(2)}, u32[]{:S(2)}) collective-permute-start(bf16[256,128]{1,0:T(8,128)(2,1)S(1)} %step.19.refs_4_.refs_1_), channel_id=1, source_target_pairs={{0,1},{1,0},{2,3},{3,2},{4,5},{5,4},{6,7},{7,6},{8,9},{9,8},{10,11... | collective-permute-start | bytes 196616 | tf_op jit(solution)/shard_map/ppermute | solution.py:206
  90.3 7.9 %collective-permute-start.10 = (bf16[256,128]{1,0:T(8,128)(2,1)S(1)}, bf16[256,128]{1,0:T(8,128)(2,1)S(1)}, u32[]{:S(2)}, u32[]{:S(2)}) collective-permute-start(bf16[256,128]{1,0:T(8,128)(2,1)S(1)} %step.20.refs_4_.refs_1_), channel_id=1, source_target_pairs={{1,2},{3,4},{5,6},{7,8},{9,10},{11,12},{13,14},{15,16},{17,18},{19... | collective-permute-start | bytes 196616 | tf_op jit(solution)/shard_map/ppermute | solution.py:205
  92.2 5.9 %collective-permute-start.11 = (bf16[256,128]{1,0:T(8,128)(2,1)S(1)}, bf16[256,128]{1,0:T(8,128)(2,1)S(1)}, u32[]{:S(2)}, u32[]{:S(2)}) collective-permute-start(bf16[256,128]{1,0:T(8,128)(2,1)S(1)} %step.20.refs_4_.refs_1_), channel_id=1, source_target_pairs={{0,1},{1,0},{2,3},{3,2},{4,5},{5,4},{6,7},{7,6},{8,9},{9,8},{10,11... | collective-permute-start | bytes 196616 | tf_op jit(solution)/shard_map/ppermute | solution.py:206
  100.0 7.5 %collective-permute-start.12 = (bf16[256,128]{1,0:T(8,128)(2,1)S(1)}, bf16[256,128]{1,0:T(8,128)(2,1)S(1)}, u32[]{:S(2)}, u32[]{:S(2)}) collective-permute-start(bf16[256,128]{1,0:T(8,128)(2,1)S(1)} %step.21.refs_4_.refs_1_), channel_id=1, source_target_pairs={{1,2},{3,4},{5,6},{7,8},{9,10},{11,12},{13,14},{15,16},{17,18},{19... | collective-permute-start | bytes 196616 | tf_op jit(solution)/shard_map/ppermute | solution.py:205
  102.0 5.6 %collective-permute-start.13 = (bf16[256,128]{1,0:T(8,128)(2,1)S(1)}, bf16[256,128]{1,0:T(8,128)(2,1)S(1)}, u32[]{:S(2)}, u32[]{:S(2)}) collective-permute-start(bf16[256,128]{1,0:T(8,128)(2,1)S(1)} %step.21.refs_4_.refs_1_), channel_id=1, source_target_pairs={{0,1},{1,0},{2,3},{3,2},{4,5},{5,4},{6,7},{7,6},{8,9},{9,8},{10,11... | collective-permute-start | bytes 196616 | tf_op jit(solution)/shard_map/ppermute | solution.py:206
  107.6 8.5 %copy-start.5 = (bf16[64,576]{1,0:T(8,128)(2,1)S(1)}, bf16[64,576]{1,0:T(8,128)(2,1)}, u32[]{:S(2)}) copy-start(bf16[64,576]{1,0:T(8,128)(2,1)} %param.20) | copy-start | bytes 221188
  109.5 6.8 %copy-start.6 = (bf16[64,576]{1,0:T(8,128)(2,1)S(1)}, bf16[64,576]{1,0:T(8,128)(2,1)}, u32[]{:S(2)}) copy-start(bf16[64,576]{1,0:T(8,128)(2,1)} %param.21) | copy-start | bytes 221188
  109.5 8.1 %collective-permute-start.14 = (bf16[256,128]{1,0:T(8,128)(2,1)S(1)}, bf16[256,128]{1,0:T(8,128)(2,1)S(1)}, u32[]{:S(2)}, u32[]{:S(2)}) collective-permute-start(bf16[256,128]{1,0:T(8,128)(2,1)S(1)} %step.22.refs_4_), channel_id=1, source_target_pairs={{1,2},{3,4},{5,6},{7,8},{9,10},{11,12},{13,14},{15,16},{17,18},{19... | collective-permute-start | bytes 196616 | tf_op jit(solution)/shard_map/ppermute | solution.py:205
  111.6 6.1 %collective-permute-start.15 = (bf16[256,128]{1,0:T(8,128)(2,1)S(1)}, bf16[256,128]{1,0:T(8,128)(2,1)S(1)}, u32[]{:S(2)}, u32[]{:S(2)}) collective-permute-start(bf16[256,128]{1,0:T(8,128)(2,1)S(1)} %step.22.refs_4_), channel_id=1, source_target_pairs={{0,1},{1,0},{2,3},{3,2},{4,5},{5,4},{6,7},{7,6},{8,9},{9,8},{10,11... | collective-permute-start | bytes 196616 | tf_op jit(solution)/shard_map/ppermute | solution.py:206
  119.6 8.3 %collective-permute-start.16 = (bf16[256,128]{1,0:T(8,128)(2,1)S(1)}, bf16[256,128]{1,0:T(8,128)(2,1)S(1)}, u32[]{:S(2)}, u32[]{:S(2)}) collective-permute-start(bf16[256,128]{1,0:T(8,128)(2,1)S(1)} %step.23.refs_4_), channel_id=1, source_target_pairs={{1,2},{3,4},{5,6},{7,8},{9,10},{11,12},{13,14},{15,16},{17,18},{19... | collective-permute-start | bytes 196616 | tf_op jit(solution)/shard_map/ppermute | solution.py:205
  121.5 6.4 %collective-permute-start.17 = (bf16[256,128]{1,0:T(8,128)(2,1)S(1)}, bf16[256,128]{1,0:T(8,128)(2,1)S(1)}, u32[]{:S(2)}, u32[]{:S(2)}) collective-permute-start(bf16[256,128]{1,0:T(8,128)(2,1)S(1)} %step.23.refs_4_), channel_id=1, source_target_pairs={{0,1},{1,0},{2,3},{3,2},{4,5},{5,4},{6,7},{7,6},{8,9},{9,8},{10,11... | collective-permute-start | bytes 196616 | tf_op jit(solution)/shard_map/ppermute | solution.py:206
  126.6 0.9 copy-start.2
  127.7 0.8 copy-start.1
  129.8 6.4 %collective-permute-start.18 = (bf16[256,128]{1,0:T(8,128)(2,1)S(1)}, bf16[256,128]{1,0:T(8,128)(2,1)S(1)}, u32[]{:S(2)}, u32[]{:S(2)}) collective-permute-start(bf16[256,128]{1,0:T(8,128)(2,1)S(1)} %step.24.refs_7_.refs_1_), channel_id=1, source_target_pairs={{1,2},{3,4},{5,6},{7,8},{9,10},{11,12},{13,14},{15,16},{17,18},{19... | collective-permute-start | bytes 196616 | tf_op jit(solution)/shard_map/ppermute | solution.py:205
  131.7 4.7 %collective-permute-start.19 = (bf16[256,128]{1,0:T(8,128)(2,1)S(1)}, bf16[256,128]{1,0:T(8,128)(2,1)S(1)}, u32[]{:S(2)}, u32[]{:S(2)}) collective-permute-start(bf16[256,128]{1,0:T(8,128)(2,1)S(1)} %step.24.refs_7_.refs_1_), channel_id=1, source_target_pairs={{0,1},{1,0},{2,3},{3,2},{4,5},{5,4},{6,7},{7,6},{8,9},{9,8},{10,11... | collective-permute-start | bytes 196616 | tf_op jit(solution)/shard_map/ppermute | solution.py:206
  138.3 8.0 %collective-permute-start.20 = (bf16[256,128]{1,0:T(8,128)(2,1)S(1)}, bf16[256,128]{1,0:T(8,128)(2,1)S(1)}, u32[]{:S(2)}, u32[]{:S(2)}) collective-permute-start(bf16[256,128]{1,0:T(8,128)(2,1)S(1)} %step.25.refs_7_.refs_1_), channel_id=1, source_target_pairs={{1,2},{3,4},{5,6},{7,8},{9,10},{11,12},{13,14},{15,16},{17,18},{19... | collective-permute-start | bytes 196616 | tf_op jit(solution)/shard_map/ppermute | solution.py:205
  140.4 5.9 %collective-permute-start.21 = (bf16[256,128]{1,0:T(8,128)(2,1)S(1)}, bf16[256,128]{1,0:T(8,128)(2,1)S(1)}, u32[]{:S(2)}, u32[]{:S(2)}) collective-permute-start(bf16[256,128]{1,0:T(8,128)(2,1)S(1)} %step.25.refs_7_.refs_1_), channel_id=1, source_target_pairs={{0,1},{1,0},{2,3},{3,2},{4,5},{5,4},{6,7},{7,6},{8,9},{9,8},{10,11... | collective-permute-start | bytes 196616 | tf_op jit(solution)/shard_map/ppermute | solution.py:206
  148.2 7.7 %collective-permute-start.22 = (bf16[256,128]{1,0:T(8,128)(2,1)S(1)}, bf16[256,128]{1,0:T(8,128)(2,1)S(1)}, u32[]{:S(2)}, u32[]{:S(2)}) collective-permute-start(bf16[256,128]{1,0:T(8,128)(2,1)S(1)} %step.26.refs_7_.refs_1_), channel_id=1, source_target_pairs={{1,2},{3,4},{5,6},{7,8},{9,10},{11,12},{13,14},{15,16},{17,18},{19... | collective-permute-start | bytes 196616 | tf_op jit(solution)/shard_map/ppermute | solution.py:205
  150.2 5.8 %collective-permute-start.23 = (bf16[256,128]{1,0:T(8,128)(2,1)S(1)}, bf16[256,128]{1,0:T(8,128)(2,1)S(1)}, u32[]{:S(2)}, u32[]{:S(2)}) collective-permute-start(bf16[256,128]{1,0:T(8,128)(2,1)S(1)} %step.26.refs_7_.refs_1_), channel_id=1, source_target_pairs={{0,1},{1,0},{2,3},{3,2},{4,5},{5,4},{6,7},{7,6},{8,9},{9,8},{10,11... | collective-permute-start | bytes 196616 | tf_op jit(solution)/shard_map/ppermute | solution.py:206
  157.8 7.9 %collective-permute-start.24 = (bf16[256,128]{1,0:T(8,128)(2,1)S(1)}, bf16[256,128]{1,0:T(8,128)(2,1)S(1)}, u32[]{:S(2)}, u32[]{:S(2)}) collective-permute-start(bf16[256,128]{1,0:T(8,128)(2,1)S(1)} %step.27.refs_7_.refs_1_), channel_id=1, source_target_pairs={{1,2},{3,4},{5,6},{7,8},{9,10},{11,12},{13,14},{15,16},{17,18},{19... | collective-permute-start | bytes 196616 | tf_op jit(solution)/shard_map/ppermute | solution.py:205
  159.8 6.0 %collective-permute-start.25 = (bf16[256,128]{1,0:T(8,128)(2,1)S(1)}, bf16[256,128]{1,0:T(8,128)(2,1)S(1)}, u32[]{:S(2)}, u32[]{:S(2)}) collective-permute-start(bf16[256,128]{1,0:T(8,128)(2,1)S(1)} %step.27.refs_7_.refs_1_), channel_id=1, source_target_pairs={{0,1},{1,0},{2,3},{3,2},{4,5},{5,4},{6,7},{7,6},{8,9},{9,8},{10,11... | collective-permute-start | bytes 196616 | tf_op jit(solution)/shard_map/ppermute | solution.py:206
  167.6 7.5 %collective-permute-start.26 = (bf16[256,128]{1,0:T(8,128)(2,1)S(1)}, bf16[256,128]{1,0:T(8,128)(2,1)S(1)}, u32[]{:S(2)}, u32[]{:S(2)}) collective-permute-start(bf16[256,128]{1,0:T(8,128)(2,1)S(1)} %step.28.refs_7_.refs_1_), channel_id=1, source_target_pairs={{1,2},{3,4},{5,6},{7,8},{9,10},{11,12},{13,14},{15,16},{17,18},{19... | collective-permute-start | bytes 196616 | tf_op jit(solution)/shard_map/ppermute | solution.py:205
  169.6 5.6 %collective-permute-start.27 = (bf16[256,128]{1,0:T(8,128)(2,1)S(1)}, bf16[256,128]{1,0:T(8,128)(2,1)S(1)}, u32[]{:S(2)}, u32[]{:S(2)}) collective-permute-start(bf16[256,128]{1,0:T(8,128)(2,1)S(1)} %step.28.refs_7_.refs_1_), channel_id=1, source_target_pairs={{0,1},{1,0},{2,3},{3,2},{4,5},{5,4},{6,7},{7,6},{8,9},{9,8},{10,11... | collective-permute-start | bytes 196616 | tf_op jit(solution)/shard_map/ppermute | solution.py:206
  177.0 7.7 %collective-permute-start.28 = (bf16[256,128]{1,0:T(8,128)(2,1)S(1)}, bf16[256,128]{1,0:T(8,128)(2,1)S(1)}, u32[]{:S(2)}, u32[]{:S(2)}) collective-permute-start(bf16[256,128]{1,0:T(8,128)(2,1)S(1)} %step.29.refs_7_.refs_1_), channel_id=1, source_target_pairs={{1,2},{3,4},{5,6},{7,8},{9,10},{11,12},{13,14},{15,16},{17,18},{19... | collective-permute-start | bytes 196616 | tf_op jit(solution)/shard_map/ppermute | solution.py:205
  178.9 5.8 %collective-permute-start.29 = (bf16[256,128]{1,0:T(8,128)(2,1)S(1)}, bf16[256,128]{1,0:T(8,128)(2,1)S(1)}, u32[]{:S(2)}, u32[]{:S(2)}) collective-permute-start(bf16[256,128]{1,0:T(8,128)(2,1)S(1)} %step.29.refs_7_.refs_1_), channel_id=1, source_target_pairs={{0,1},{1,0},{2,3},{3,2},{4,5},{5,4},{6,7},{7,6},{8,9},{9,8},{10,11... | collective-permute-start | bytes 196616 | tf_op jit(solution)/shard_map/ppermute | solution.py:206
  186.6 8.4 %collective-permute-start.30 = (bf16[256,128]{1,0:T(8,128)(2,1)S(1)}, bf16[256,128]{1,0:T(8,128)(2,1)S(1)}, u32[]{:S(2)}, u32[]{:S(2)}) collective-permute-start(bf16[256,128]{1,0:T(8,128)(2,1)S(1)} %step.30.refs_7_), channel_id=1, source_target_pairs={{1,2},{3,4},{5,6},{7,8},{9,10},{11,12},{13,14},{15,16},{17,18},{19... | collective-permute-start | bytes 196616 | tf_op jit(solution)/shard_map/ppermute | solution.py:205
  188.5 6.4 %collective-permute-start.31 = (bf16[256,128]{1,0:T(8,128)(2,1)S(1)}, bf16[256,128]{1,0:T(8,128)(2,1)S(1)}, u32[]{:S(2)}, u32[]{:S(2)}) collective-permute-start(bf16[256,128]{1,0:T(8,128)(2,1)S(1)} %step.30.refs_7_), channel_id=1, source_target_pairs={{0,1},{1,0},{2,3},{3,2},{4,5},{5,4},{6,7},{7,6},{8,9},{9,8},{10,11... | collective-permute-start | bytes 196616 | tf_op jit(solution)/shard_map/ppermute | solution.py:206

commit v3 on v2

--- a/solution.py
+++ b/solution.py
@@ -66,8 +66,9 @@
         store(ch, total.astype(jnp.bfloat16))
 
 
-def prepare_kernel(priors, grid, *refs):
+def prepare_kernel(priors, first, sense, *refs):
     refs = list(refs)
+    grid = (first[0], sense[0])
     older = [refs.pop(0) for _ in range(3)] if priors == 2 else None
     params, taps = refs.pop(0), refs.pop(0)
     for n, w in enumerate(tap_weights(params[0], grid)):
@@ -89,8 +90,9 @@
         sample_row(older, r, weight, store)
 
 
-def step_kernel(priors, parts, grid, *refs):
+def step_kernel(priors, parts, first, sense, *refs):
     refs = list(refs)
+    grid = (first[0], sense[0])
     sides = [[refs.pop(0) for _ in range(3)] for _ in range(parts)]
     newest = [refs.pop(0) for _ in range(3)] if priors else None
     taps = refs.pop(0) if priors else None
@@ -162,14 +164,14 @@
 
 
 def run_prepare(grid, older, params):
-    operands = [grid] + (list(older) if older else []) + [params]
+    operands = list(grid) + (list(older) if older else []) + [params]
     outs = [jax.ShapeDtypeStruct((EXT, 25, 16, W), BF16)]
     if older:
         outs.append(jax.ShapeDtypeStruct((C, EXT * W), BF16))
     return pl.pallas_call(
         functools.partial(prepare_kernel, 2 if older else 1),
         out_shape=outs,
-        in_specs=[SMEM] + [VMEM] * (len(operands) - 1),
+        in_specs=[SMEM, SMEM] + [VMEM] * (len(operands) - 2),
         out_specs=[VMEM] * len(outs),
         scratch_shapes=[pltpu.VMEM((25, EXT, W), jnp.float32)] if older else [],
         compiler_params=pltpu.CompilerParams(vmem_limit_bytes=16 * 2**20),
@@ -179,14 +181,14 @@
 
 
 def run_step(grid, sides, newest, prepared, weights):
-    operands = [grid]
+    operands = list(grid)
     for trio in sides:
         operands += list(trio)
     operands += (list(newest) if newest else []) + list(prepared) + list(weights)
     return pl.pallas_call(
         functools.partial(step_kernel, len(prepared), len(sides)),
         out_shape=jax.ShapeDtypeStruct((ROWS * C, W), BF16),
-        in_specs=[SMEM] + [VMEM] * (len(operands) - 1),
+        in_specs=[SMEM, SMEM] + [VMEM] * (len(operands) - 2),
         out_specs=VMEM,
         scratch_shapes=[
             pltpu.VMEM((C, EXT * W), BF16),
@@ -199,12 +201,31 @@
     )(*operands)
 
 
+def place(replica, low, p, count):
+    x, z, core = p // 16, p // 2 % 8, p % 2
+    half = z // 4
+    level = 7 - z if half else z
+    level = level if low else 7 - level
+    return (2 * replica + half) * count + x * 16 + level * 2 + core
+
+
+def mirror(q):
+    return q // 16 * 16 + (7 - q // 2 % 8) * 2 + q % 2
+
+
 def swap(for_across, for_beside):
     count = lax.axis_size("tile")
-    pairs = [(i, i + 1) for i in range(1, count - 1, 2)]
-    across = lax.ppermute(for_across, "tile", pairs + [(j, i) for i, j in pairs])
-    beside = lax.ppermute(for_beside, "tile", [(i, i ^ 1) for i in range(count)])
-    return across, beside
+    across, beside = [], []
+    for replica in range(4):
+        for low in (True, False):
+            at = [place(replica, low, p, count) for p in range(count)]
+            for p in range(count):
+                beside.append((at[p], at[p ^ 1]))
+                other = p + 1 if p % 2 else p - 1
+                if 0 <= other < count:
+                    across.append((at[p], at[other]))
+    axes = ("tm", "tile")
+    return lax.ppermute(for_across, axes, across), lax.ppermute(for_beside, axes, beside)
 
 
 def conv_matrix(kernel, odd):
@@ -226,10 +247,16 @@
     ahead_inner,
     ahead_outer,
 ):
-    tile = lax.axis_index("tile").astype(jnp.int32)
-    turn = lax.axis_index("tm")
-    odd = tile % 2 == 1
-    grid = jnp.stack([tile * ROWS + jnp.where(odd, ROWS - 1, 0), jnp.where(odd, -1, 1)])
+    where = lax.axis_index("tile").astype(jnp.int32)
+    turn = lax.axis_index("tm").astype(jnp.int32)
+    odd = where % 2 == 1
+    upper = where // 2 % 8 >= 4
+    home = upper == (turn % 2 == 1)
+    tile = jnp.where(home, where, mirror(where))
+    grid = (
+        (tile * ROWS + jnp.where(odd, ROWS - 1, 0)).reshape(1),
+        jnp.where(odd, -1, 1).astype(jnp.int32).reshape(1),
+    )
 
     def oriented(values, axis):
         return jnp.where(odd, jnp.flip(values, axis), values)
@@ -247,8 +274,11 @@
         [pack(back_shift, back_fraction), pack(ahead_shift, ahead_fraction)], axis=1
     ).reshape(ROWS * 16, W)
     mine = jnp.concatenate([own, own_params], axis=0)
+    other = lax.ppermute(mine, "tile", [(q, mirror(q)) for q in range(lax.axis_size("tile"))])
+    for_even = jnp.where(upper, other, mine)
+    for_odd = jnp.where(upper, mine, other)
     clip = lax.all_to_all(
-        jnp.broadcast_to(mine[None], (FRAMES,) + mine.shape), "tm", split_axis=0, concat_axis=0
+        jnp.stack([for_even, for_odd] * (FRAMES // 2)), "tm", split_axis=0, concat_axis=0
     )
 
     top = jnp.concatenate([clip[:, : 2 * C], clip[:, 4 * C : 4 * C + 32]], axis=1)
@@ -283,13 +313,26 @@
     back = chain(range(FRAMES - 1, -1, -1), 0, None, back_weights)
     ahead = chain(range(FRAMES), 1, back, ahead_weights)
 
-    def pick(done):
+    def pick(done, frame):
         value = done[0][1]
         for t in range(1, FRAMES):
-            value = jnp.where(turn == t, done[t][1], value)
-        return oriented(value.reshape(ROWS, C, W), 0).transpose(1, 0, 2)[None]
-
-    return pick(back), pick(ahead)
+            value = jnp.where(frame == t, done[t][1], value)
+        return value
+
+    def results(frame):
+        return jnp.stack([pick(back, frame), pick(ahead, frame)])
+
+    count = lax.axis_size("tile")
+    gives = [
+        (t * count + q, (t ^ 1) * count + q)
+        for t in range(FRAMES)
+        for q in range(count)
+        if (q // 2 % 8 >= 4) == (t % 2 == 1)
+    ]
+    given = lax.ppermute(results(turn ^ 1), ("tm", "tile"), gives)
+    final = jnp.where(home, results(turn), given).reshape(2, ROWS, C, W)
+    final = oriented(final, 1).transpose(0, 2, 1, 3)
+    return final[0][None], final[1][None]
 
 
 def solution(mesh):

time: 199 us -> 192 us (0.965)
  the two profiles are of different devices: /device:TPU:7 before, /device:TPU:8 now
where the time goes in v3:
time: 192 us; the launch traced here: 190 us
  starting transfers between devices  111 us (58%)
  waiting for transfers between devices  32.2 us (17%)
  Pallas kernels  28.6 us (15%)
  local copies, waits for them, and re-layouts  13.5 us (7%)
  other arithmetic  2.97 us (2%)
    ppermute x16, starting transfers between devices, swap(): lax.ppermute(for_beside, axes, beside)  55.9 us
    ppermute x16, starting transfers between devices, swap(): lax.ppermute(for_across, axes, across)  35.4 us
    pallas_call x16, Pallas kernels, run_step(): pl.pallas_call(functools.partial(step_kernel, len(prepared), len(sides)),...  20.5 us
    all_to_all x1, waiting for transfers between devices, shards(): lax.all_to_all(jnp.stack([for_even, for_odd] * (FRAMES // 2)), 'tm', spli...  17.3 us
    ppermute x1, starting transfers between devices, shards(): lax.ppermute(mine, 'tile', [(q, mirror(q)) for q in range(lax.axis_size('...  10.9 us
    unnamed x33, local copies, waits for them, and re-layouts  9.26 us
    pallas_call x14, Pallas kernels, run_prepare(): pl.pallas_call(functools.partial(prepare_kernel, 2 if older else 1), out_...  8.14 us
    all_to_all x1, starting transfers between devices, shards(): lax.all_to_all(jnp.stack([for_even, for_odd] * (FRAMES // 2)), 'tm', spli...  7.68 us
  transfers between devices with their start and end apart: 35, of which 15 were waited for; matrix products, arithmetic and copies ran while one was open for 2% of the time, Pallas kernels for 4%

profile of v3, /device:TPU:8, one launch (start us, length us, event | category | flops | bytes accessed | tf_op | source)
XLA Modules:
  0.0 190.3 jit_solution(10240970317302297112)
XLA Ops:
  3.9 10.9 %collective-permute-start = (bf16[320,128]{1,0:T(8,128)(2,1)S(1)}, bf16[320,128]{1,0:T(8,128)(2,1)S(1)}, u32[]{:S(2)}, u32[]{:S(2)}) collective-permute-start(bf16[320,128]{1,0:T(8,128)(2,1)S(1)} %pad_maximum_fusion.3), channel_id=1, source_target_pairs={{0,14},{1,15},{2,12},{3,13},{4,10},{5,11},{6,8},{7,9},{8,6},{9,7},... | collective-permute-start | bytes 245768 | tf_op jit(solution)/shard_map/ppermute | solution.py:277
  14.8 4.1 %collective-permute-done = bf16[320,128]{1,0:T(8,128)(2,1)S(1)} collective-permute-done((bf16[320,128]{1,0:T(8,128)(2,1)S(1)}, bf16[320,128]{1,0:T(8,128)(2,1)S(1)}, u32[]{:S(2)}, u32[]{:S(2)}) %collective-permute-start) | collective-permute-done | bytes 81952 | tf_op jit(solution)/shard_map/ppermute | solution.py:277
  24.1 7.7 %all-to-all-start = ((bf16[8,320,128]{2,1,0:T(8,128)(2,1)}), bf16[8,320,128]{2,1,0:T(8,128)(2,1)S(1)}, u32[]{:S(2)}, u32[]{:S(2)}) async-start(bf16[8,320,128]{2,1,0:T(8,128)(2,1)} %bitcast_dynamic-update-slice_fusion.3), calls=%async_computation | async-start | bytes 1310720 | tf_op jit(solution)/shard_map/all_to_all | solution.py:280
  33.6 17.3 %all-to-all-done = bf16[8,320,128]{2,1,0:T(8,128)(2,1)S(1)} async-done(((bf16[8,320,128]{2,1,0:T(8,128)(2,1)}), bf16[8,320,128]{2,1,0:T(8,128)(2,1)S(1)}, u32[]{:S(2)}, u32[]{:S(2)}) %all-to-all-start) | async-done | bytes 655392 | tf_op jit(solution)/shard_map/all_to_all | solution.py:280
  50.9 1.9 %collective-permute-start.1 = (bf16[8,160,128]{2,1,0:T(8,128)(2,1)S(1)}, bf16[8,160,128]{2,1,0:T(8,128)(2,1)S(1)}, u32[]{:S(2)}, u32[]{:S(2)}) collective-permute-start(bf16[8,160,128]{2,1,0:T(8,128)(2,1)S(1)} %pad_maximum_fusion), channel_id=1, source_target_pairs={{1,2},{2,1},{3,4},{4,3},{5,6},{6,5},{7,70},{70,7},{71,68},{68,71},... | collective-permute-start | bytes 983048 | tf_op jit(solution)/shard_map/ppermute | solution.py:228
  52.9 4.4 %collective-permute-start.2 = (bf16[8,160,128]{2,1,0:T(8,128)(2,1)S(1)}, bf16[8,160,128]{2,1,0:T(8,128)(2,1)S(1)}, u32[]{:S(2)}, u32[]{:S(2)}) collective-permute-start(bf16[8,160,128]{2,1,0:T(8,128)(2,1)S(1)} %pad_maximum_fusion.1), channel_id=1, source_target_pairs={{0,1},{1,0},{2,3},{3,2},{4,5},{5,4},{6,7},{7,6},{70,71},{71,70},{6... | collective-permute-start | bytes 983048 | tf_op jit(solution)/shard_map/ppermute | solution.py:228
  57.5 1.8 collective-permute-done.1
  60.9 1.9 %collective-permute-start.3 = (bf16[256,128]{1,0:T(8,128)(2,1)S(1)}, bf16[256,128]{1,0:T(8,128)(2,1)S(1)}, u32[]{:S(2)}, u32[]{:S(2)}) collective-permute-start(bf16[256,128]{1,0:T(8,128)(2,1)S(1)} %step.16.refs_4_.refs_1_), channel_id=1, source_target_pairs={{1,2},{2,1},{3,4},{4,3},{5,6},{6,5},{7,70},{70,7},{71,68},{68,71},... | collective-permute-start | bytes 196616 | tf_op jit(solution)/shard_map/ppermute | solution.py:228
  62.8 5.3 %collective-permute-start.4 = (bf16[256,128]{1,0:T(8,128)(2,1)S(1)}, bf16[256,128]{1,0:T(8,128)(2,1)S(1)}, u32[]{:S(2)}, u32[]{:S(2)}) collective-permute-start(bf16[256,128]{1,0:T(8,128)(2,1)S(1)} %step.16.refs_4_.refs_1_), channel_id=1, source_target_pairs={{0,1},{1,0},{2,3},{3,2},{4,5},{5,4},{6,7},{7,6},{70,71},{71,70},{6... | collective-permute-start | bytes 196616 | tf_op jit(solution)/shard_map/ppermute | solution.py:228
  70.8 1.9 %collective-permute-start.5 = (bf16[256,128]{1,0:T(8,128)(2,1)S(1)}, bf16[256,128]{1,0:T(8,128)(2,1)S(1)}, u32[]{:S(2)}, u32[]{:S(2)}) collective-permute-start(bf16[256,128]{1,0:T(8,128)(2,1)S(1)} %step.17.refs_4_.refs_1_), channel_id=1, source_target_pairs={{1,2},{2,1},{3,4},{4,3},{5,6},{6,5},{7,70},{70,7},{71,68},{68,71},... | collective-permute-start | bytes 196616 | tf_op jit(solution)/shard_map/ppermute | solution.py:228
  72.7 3.2 %collective-permute-start.6 = (bf16[256,128]{1,0:T(8,128)(2,1)S(1)}, bf16[256,128]{1,0:T(8,128)(2,1)S(1)}, u32[]{:S(2)}, u32[]{:S(2)}) collective-permute-start(bf16[256,128]{1,0:T(8,128)(2,1)S(1)} %step.17.refs_4_.refs_1_), channel_id=1, source_target_pairs={{0,1},{1,0},{2,3},{3,2},{4,5},{5,4},{6,7},{7,6},{70,71},{71,70},{6... | collective-permute-start | bytes 196616 | tf_op jit(solution)/shard_map/ppermute | solution.py:228
  76.8 1.4 step.18.refs_4_.refs_1_
  78.2 2.7 %collective-permute-start.7 = (bf16[256,128]{1,0:T(8,128)(2,1)S(1)}, bf16[256,128]{1,0:T(8,128)(2,1)S(1)}, u32[]{:S(2)}, u32[]{:S(2)}) collective-permute-start(bf16[256,128]{1,0:T(8,128)(2,1)S(1)} %step.18.refs_4_.refs_1_), channel_id=1, source_target_pairs={{1,2},{2,1},{3,4},{4,3},{5,6},{6,5},{7,70},{70,7},{71,68},{68,71},... | collective-permute-start | bytes 196616 | tf_op jit(solution)/shard_map/ppermute | solution.py:228
  80.9 2.9 %collective-permute-start.8 = (bf16[256,128]{1,0:T(8,128)(2,1)S(1)}, bf16[256,128]{1,0:T(8,128)(2,1)S(1)}, u32[]{:S(2)}, u32[]{:S(2)}) collective-permute-start(bf16[256,128]{1,0:T(8,128)(2,1)S(1)} %step.18.refs_4_.refs_1_), channel_id=1, source_target_pairs={{0,1},{1,0},{2,3},{3,2},{4,5},{5,4},{6,7},{7,6},{70,71},{71,70},{6... | collective-permute-start | bytes 196616 | tf_op jit(solution)/shard_map/ppermute | solution.py:228
  84.7 1.4 step.19.refs_4_.refs_1_
  86.1 2.2 %collective-permute-start.9 = (bf16[256,128]{1,0:T(8,128)(2,1)S(1)}, bf16[256,128]{1,0:T(8,128)(2,1)S(1)}, u32[]{:S(2)}, u32[]{:S(2)}) collective-permute-start(bf16[256,128]{1,0:T(8,128)(2,1)S(1)} %step.19.refs_4_.refs_1_), channel_id=1, source_target_pairs={{1,2},{2,1},{3,4},{4,3},{5,6},{6,5},{7,70},{70,7},{71,68},{68,71},... | collective-permute-start | bytes 196616 | tf_op jit(solution)/shard_map/ppermute | solution.py:228
  88.3 3.4 %collective-permute-start.10 = (bf16[256,128]{1,0:T(8,128)(2,1)S(1)}, bf16[256,128]{1,0:T(8,128)(2,1)S(1)}, u32[]{:S(2)}, u32[]{:S(2)}) collective-permute-start(bf16[256,128]{1,0:T(8,128)(2,1)S(1)} %step.19.refs_4_.refs_1_), channel_id=1, source_target_pairs={{0,1},{1,0},{2,3},{3,2},{4,5},{5,4},{6,7},{7,6},{70,71},{71,70},{6... | collective-permute-start | bytes 196616 | tf_op jit(solution)/shard_map/ppermute | solution.py:228
  92.5 1.4 step.20.refs_4_.refs_1_
  93.9 2.2 %collective-permute-start.11 = (bf16[256,128]{1,0:T(8,128)(2,1)S(1)}, bf16[256,128]{1,0:T(8,128)(2,1)S(1)}, u32[]{:S(2)}, u32[]{:S(2)}) collective-permute-start(bf16[256,128]{1,0:T(8,128)(2,1)S(1)} %step.20.refs_4_.refs_1_), channel_id=1, source_target_pairs={{1,2},{2,1},{3,4},{4,3},{5,6},{6,5},{7,70},{70,7},{71,68},{68,71},... | collective-permute-start | bytes 196616 | tf_op jit(solution)/shard_map/ppermute | solution.py:228
  96.2 3.5 %collective-permute-start.12 = (bf16[256,128]{1,0:T(8,128)(2,1)S(1)}, bf16[256,128]{1,0:T(8,128)(2,1)S(1)}, u32[]{:S(2)}, u32[]{:S(2)}) collective-permute-start(bf16[256,128]{1,0:T(8,128)(2,1)S(1)} %step.20.refs_4_.refs_1_), channel_id=1, source_target_pairs={{0,1},{1,0},{2,3},{3,2},{4,5},{5,4},{6,7},{7,6},{70,71},{71,70},{6... | collective-permute-start | bytes 196616 | tf_op jit(solution)/shard_map/ppermute | solution.py:228
  100.4 1.4 step.21.refs_4_.refs_1_
  101.8 2.2 %collective-permute-start.13 = (bf16[256,128]{1,0:T(8,128)(2,1)S(1)}, bf16[256,128]{1,0:T(8,128)(2,1)S(1)}, u32[]{:S(2)}, u32[]{:S(2)}) collective-permute-start(bf16[256,128]{1,0:T(8,128)(2,1)S(1)} %step.21.refs_4_.refs_1_), channel_id=1, source_target_pairs={{1,2},{2,1},{3,4},{4,3},{5,6},{6,5},{7,70},{70,7},{71,68},{68,71},... | collective-permute-start | bytes 196616 | tf_op jit(solution)/shard_map/ppermute | solution.py:228
  104.0 3.4 %collective-permute-start.14 = (bf16[256,128]{1,0:T(8,128)(2,1)S(1)}, bf16[256,128]{1,0:T(8,128)(2,1)S(1)}, u32[]{:S(2)}, u32[]{:S(2)}) collective-permute-start(bf16[256,128]{1,0:T(8,128)(2,1)S(1)} %step.21.refs_4_.refs_1_), channel_id=1, source_target_pairs={{0,1},{1,0},{2,3},{3,2},{4,5},{5,4},{6,7},{7,6},{70,71},{71,70},{6... | collective-permute-start | bytes 196616 | tf_op jit(solution)/shard_map/ppermute | solution.py:228
  108.3 1.4 step.22.refs_4_
  109.7 2.4 %collective-permute-start.15 = (bf16[256,128]{1,0:T(8,128)(2,1)S(1)}, bf16[256,128]{1,0:T(8,128)(2,1)S(1)}, u32[]{:S(2)}, u32[]{:S(2)}) collective-permute-start(bf16[256,128]{1,0:T(8,128)(2,1)S(1)} %step.22.refs_4_), channel_id=1, source_target_pairs={{1,2},{2,1},{3,4},{4,3},{5,6},{6,5},{7,70},{70,7},{71,68},{68,71},... | collective-permute-start | bytes 196616 | tf_op jit(solution)/shard_map/ppermute | solution.py:228
  112.0 3.4 %collective-permute-start.16 = (bf16[256,128]{1,0:T(8,128)(2,1)S(1)}, bf16[256,128]{1,0:T(8,128)(2,1)S(1)}, u32[]{:S(2)}, u32[]{:S(2)}) collective-permute-start(bf16[256,128]{1,0:T(8,128)(2,1)S(1)} %step.22.refs_4_), channel_id=1, source_target_pairs={{0,1},{1,0},{2,3},{3,2},{4,5},{5,4},{6,7},{7,6},{70,71},{71,70},{6... | collective-permute-start | bytes 196616 | tf_op jit(solution)/shard_map/ppermute | solution.py:228
  116.4 1.4 step.23.refs_4_
  117.8 2.1 %collective-permute-start.17 = (bf16[256,128]{1,0:T(8,128)(2,1)S(1)}, bf16[256,128]{1,0:T(8,128)(2,1)S(1)}, u32[]{:S(2)}, u32[]{:S(2)}) collective-permute-start(bf16[256,128]{1,0:T(8,128)(2,1)S(1)} %step.23.refs_4_), channel_id=1, source_target_pairs={{1,2},{2,1},{3,4},{4,3},{5,6},{6,5},{7,70},{70,7},{71,68},{68,71},... | collective-permute-start | bytes 196616 | tf_op jit(solution)/shard_map/ppermute | solution.py:228
  119.9 3.4 %collective-permute-start.18 = (bf16[256,128]{1,0:T(8,128)(2,1)S(1)}, bf16[256,128]{1,0:T(8,128)(2,1)S(1)}, u32[]{:S(2)}, u32[]{:S(2)}) collective-permute-start(bf16[256,128]{1,0:T(8,128)(2,1)S(1)} %step.23.refs_4_), channel_id=1, source_target_pairs={{0,1},{1,0},{2,3},{3,2},{4,5},{5,4},{6,7},{7,6},{70,71},{71,70},{6... | collective-permute-start | bytes 196616 | tf_op jit(solution)/shard_map/ppermute | solution.py:228
  126.8 2.0 %collective-permute-start.19 = (bf16[256,128]{1,0:T(8,128)(2,1)S(1)}, bf16[256,128]{1,0:T(8,128)(2,1)S(1)}, u32[]{:S(2)}, u32[]{:S(2)}) collective-permute-start(bf16[256,128]{1,0:T(8,128)(2,1)S(1)} %step.24.refs_7_.refs_1_), channel_id=1, source_target_pairs={{1,2},{2,1},{3,4},{4,3},{5,6},{6,5},{7,70},{70,7},{71,68},{68,71},... | collective-permute-start | bytes 196616 | tf_op jit(solution)/shard_map/ppermute | solution.py:228
  128.8 3.2 %collective-permute-start.20 = (bf16[256,128]{1,0:T(8,128)(2,1)S(1)}, bf16[256,128]{1,0:T(8,128)(2,1)S(1)}, u32[]{:S(2)}, u32[]{:S(2)}) collective-permute-start(bf16[256,128]{1,0:T(8,128)(2,1)S(1)} %step.24.refs_7_.refs_1_), channel_id=1, source_target_pairs={{0,1},{1,0},{2,3},{3,2},{4,5},{5,4},{6,7},{7,6},{70,71},{71,70},{6... | collective-permute-start | bytes 196616 | tf_op jit(solution)/shard_map/ppermute | solution.py:228
  132.9 1.4 step.25.refs_7_.refs_1_
  134.3 2.6 %collective-permute-start.21 = (bf16[256,128]{1,0:T(8,128)(2,1)S(1)}, bf16[256,128]{1,0:T(8,128)(2,1)S(1)}, u32[]{:S(2)}, u32[]{:S(2)}) collective-permute-start(bf16[256,128]{1,0:T(8,128)(2,1)S(1)} %step.25.refs_7_.refs_1_), channel_id=1, source_target_pairs={{1,2},{2,1},{3,4},{4,3},{5,6},{6,5},{7,70},{70,7},{71,68},{68,71},... | collective-permute-start | bytes 196616 | tf_op jit(solution)/shard_map/ppermute | solution.py:228
  136.9 3.0 %collective-permute-start.22 = (bf16[256,128]{1,0:T(8,128)(2,1)S(1)}, bf16[256,128]{1,0:T(8,128)(2,1)S(1)}, u32[]{:S(2)}, u32[]{:S(2)}) collective-permute-start(bf16[256,128]{1,0:T(8,128)(2,1)S(1)} %step.25.refs_7_.refs_1_), channel_id=1, source_target_pairs={{0,1},{1,0},{2,3},{3,2},{4,5},{5,4},{6,7},{7,6},{70,71},{71,70},{6... | collective-permute-start | bytes 196616 | tf_op jit(solution)/shard_map/ppermute | solution.py:228
  142.1 2.2 %collective-permute-start.23 = (bf16[256,128]{1,0:T(8,128)(2,1)S(1)}, bf16[256,128]{1,0:T(8,128)(2,1)S(1)}, u32[]{:S(2)}, u32[]{:S(2)}) collective-permute-start(bf16[256,128]{1,0:T(8,128)(2,1)S(1)} %step.26.refs_7_.refs_1_), channel_id=1, source_target_pairs={{1,2},{2,1},{3,4},{4,3},{5,6},{6,5},{7,70},{70,7},{71,68},{68,71},... | collective-permute-start | bytes 196616 | tf_op jit(solution)/shard_map/ppermute | solution.py:228
  144.3 3.4 %collective-permute-start.24 = (bf16[256,128]{1,0:T(8,128)(2,1)S(1)}, bf16[256,128]{1,0:T(8,128)(2,1)S(1)}, u32[]{:S(2)}, u32[]{:S(2)}) collective-permute-start(bf16[256,128]{1,0:T(8,128)(2,1)S(1)} %step.26.refs_7_.refs_1_), channel_id=1, source_target_pairs={{0,1},{1,0},{2,3},{3,2},{4,5},{5,4},{6,7},{7,6},{70,71},{71,70},{6... | collective-permute-start | bytes 196616 | tf_op jit(solution)/shard_map/ppermute | solution.py:228
  148.6 1.3 step.27.refs_7_.refs_1_
  149.9 2.2 %collective-permute-start.25 = (bf16[256,128]{1,0:T(8,128)(2,1)S(1)}, bf16[256,128]{1,0:T(8,128)(2,1)S(1)}, u32[]{:S(2)}, u32[]{:S(2)}) collective-permute-start(bf16[256,128]{1,0:T(8,128)(2,1)S(1)} %step.27.refs_7_.refs_1_), channel_id=1, source_target_pairs={{1,2},{2,1},{3,4},{4,3},{5,6},{6,5},{7,70},{70,7},{71,68},{68,71},... | collective-permute-start | bytes 196616 | tf_op jit(solution)/shard_map/ppermute | solution.py:228
  152.2 3.6 %collective-permute-start.26 = (bf16[256,128]{1,0:T(8,128)(2,1)S(1)}, bf16[256,128]{1,0:T(8,128)(2,1)S(1)}, u32[]{:S(2)}, u32[]{:S(2)}) collective-permute-start(bf16[256,128]{1,0:T(8,128)(2,1)S(1)} %step.27.refs_7_.refs_1_), channel_id=1, source_target_pairs={{0,1},{1,0},{2,3},{3,2},{4,5},{5,4},{6,7},{7,6},{70,71},{71,70},{6... | collective-permute-start | bytes 196616 | tf_op jit(solution)/shard_map/ppermute | solution.py:228
  156.4 1.3 step.28.refs_7_.refs_1_
  157.8 2.2 %collective-permute-start.27 = (bf16[256,128]{1,0:T(8,128)(2,1)S(1)}, bf16[256,128]{1,0:T(8,128)(2,1)S(1)}, u32[]{:S(2)}, u32[]{:S(2)}) collective-permute-start(bf16[256,128]{1,0:T(8,128)(2,1)S(1)} %step.28.refs_7_.refs_1_), channel_id=1, source_target_pairs={{1,2},{2,1},{3,4},{4,3},{5,6},{6,5},{7,70},{70,7},{71,68},{68,71},... | collective-permute-start | bytes 196616 | tf_op jit(solution)/shard_map/ppermute | solution.py:228
  160.0 3.4 %collective-permute-start.28 = (bf16[256,128]{1,0:T(8,128)(2,1)S(1)}, bf16[256,128]{1,0:T(8,128)(2,1)S(1)}, u32[]{:S(2)}, u32[]{:S(2)}) collective-permute-start(bf16[256,128]{1,0:T(8,128)(2,1)S(1)} %step.28.refs_7_.refs_1_), channel_id=1, source_target_pairs={{0,1},{1,0},{2,3},{3,2},{4,5},{5,4},{6,7},{7,6},{70,71},{71,70},{6... | collective-permute-start | bytes 196616 | tf_op jit(solution)/shard_map/ppermute | solution.py:228
  165.6 2.3 %collective-permute-start.29 = (bf16[256,128]{1,0:T(8,128)(2,1)S(1)}, bf16[256,128]{1,0:T(8,128)(2,1)S(1)}, u32[]{:S(2)}, u32[]{:S(2)}) collective-permute-start(bf16[256,128]{1,0:T(8,128)(2,1)S(1)} %step.29.refs_7_.refs_1_), channel_id=1, source_target_pairs={{1,2},{2,1},{3,4},{4,3},{5,6},{6,5},{7,70},{70,7},{71,68},{68,71},... | collective-permute-start | bytes 196616 | tf_op jit(solution)/shard_map/ppermute | solution.py:228
  167.9 3.3 %collective-permute-start.30 = (bf16[256,128]{1,0:T(8,128)(2,1)S(1)}, bf16[256,128]{1,0:T(8,128)(2,1)S(1)}, u32[]{:S(2)}, u32[]{:S(2)}) collective-permute-start(bf16[256,128]{1,0:T(8,128)(2,1)S(1)} %step.29.refs_7_.refs_1_), channel_id=1, source_target_pairs={{0,1},{1,0},{2,3},{3,2},{4,5},{5,4},{6,7},{7,6},{70,71},{71,70},{6... | collective-permute-start | bytes 196616 | tf_op jit(solution)/shard_map/ppermute | solution.py:228
  173.4 2.2 %collective-permute-start.31 = (bf16[256,128]{1,0:T(8,128)(2,1)S(1)}, bf16[256,128]{1,0:T(8,128)(2,1)S(1)}, u32[]{:S(2)}, u32[]{:S(2)}) collective-permute-start(bf16[256,128]{1,0:T(8,128)(2,1)S(1)} %step.30.refs_7_), channel_id=1, source_target_pairs={{1,2},{2,1},{3,4},{4,3},{5,6},{6,5},{7,70},{70,7},{71,68},{68,71},... | collective-permute-start | bytes 196616 | tf_op jit(solution)/shard_map/ppermute | solution.py:228
  175.7 3.4 %collective-permute-start.32 = (bf16[256,128]{1,0:T(8,128)(2,1)S(1)}, bf16[256,128]{1,0:T(8,128)(2,1)S(1)}, u32[]{:S(2)}, u32[]{:S(2)}) collective-permute-start(bf16[256,128]{1,0:T(8,128)(2,1)S(1)} %step.30.refs_7_), channel_id=1, source_target_pairs={{0,1},{1,0},{2,3},{3,2},{4,5},{5,4},{6,7},{7,6},{70,71},{71,70},{6... | collective-permute-start | bytes 196616 | tf_op jit(solution)/shard_map/ppermute | solution.py:228
  179.9 1.3 step.31
  182.7 6.4 %collective-permute-done.33 = bf16[2,256,128]{2,1,0:T(8,128)(2,1)S(1)} collective-permute-done((bf16[2,256,128]{2,1,0:T(8,128)(2,1)S(1)}, bf16[2,256,128]{2,1,0:T(8,128)(2,1)S(1)}, u32[]{:S(2)}, u32[]{:S(2)}) %collective-permute-start.33) | collective-permute-done | bytes 131104 | tf_op jit(solution)/shard_map/ppermute | solution.py:332
  (152 shorter events, 35.3 us)
Async XLA Ops:
  0.6 0.7 copy-start.10
  0.6 0.7 copy-start.11
  1.3 0.7 copy-start.8
  2.1 0.7 copy-start.9
  2.8 0.8 copy-start.3
  3.9 15.1 %collective-permute-start = (bf16[320,128]{1,0:T(8,128)(2,1)S(1)}, bf16[320,128]{1,0:T(8,128)(2,1)S(1)}, u32[]{:S(2)}, u32[]{:S(2)}) collective-permute-start(bf16[320,128]{1,0:T(8,128)(2,1)S(1)} %pad_maximum_fusion.3), channel_id=1, source_target_pairs={{0,14},{1,15},{2,12},{3,13},{4,10},{5,11},{6,8},{7,9},{8,6},{9,7},... | collective-permute-start | bytes 245768 | tf_op jit(solution)/shard_map/ppermute | solution.py:277
  24.1 7.7 %copy-start.4 = (bf16[64,576]{1,0:T(8,128)(2,1)S(1)}, bf16[64,576]{1,0:T(8,128)(2,1)}, u32[]{:S(2)}) copy-start(bf16[64,576]{1,0:T(8,128)(2,1)} %param.17) | copy-start | bytes 221188
  24.1 26.7 %all-to-all-start = ((bf16[8,320,128]{2,1,0:T(8,128)(2,1)}), bf16[8,320,128]{2,1,0:T(8,128)(2,1)S(1)}, u32[]{:S(2)}, u32[]{:S(2)}) async-start(bf16[8,320,128]{2,1,0:T(8,128)(2,1)} %bitcast_dynamic-update-slice_fusion.3), calls=%async_computation | async-start | bytes 1310720 | tf_op jit(solution)/shard_map/all_to_all | solution.py:280
  31.8 0.9 copy-start.5
  50.9 8.4 %collective-permute-start.1 = (bf16[8,160,128]{2,1,0:T(8,128)(2,1)S(1)}, bf16[8,160,128]{2,1,0:T(8,128)(2,1)S(1)}, u32[]{:S(2)}, u32[]{:S(2)}) collective-permute-start(bf16[8,160,128]{2,1,0:T(8,128)(2,1)S(1)} %pad_maximum_fusion), channel_id=1, source_target_pairs={{1,2},{2,1},{3,4},{4,3},{5,6},{6,5},{7,70},{70,7},{71,68},{68,71},... | collective-permute-start | bytes 983048 | tf_op jit(solution)/shard_map/ppermute | solution.py:228
  52.9 6.5 %collective-permute-start.2 = (bf16[8,160,128]{2,1,0:T(8,128)(2,1)S(1)}, bf16[8,160,128]{2,1,0:T(8,128)(2,1)S(1)}, u32[]{:S(2)}, u32[]{:S(2)}) collective-permute-start(bf16[8,160,128]{2,1,0:T(8,128)(2,1)S(1)} %pad_maximum_fusion.1), channel_id=1, source_target_pairs={{0,1},{1,0},{2,3},{3,2},{4,5},{5,4},{6,7},{7,6},{70,71},{71,70},{6... | collective-permute-start | bytes 983048 | tf_op jit(solution)/shard_map/ppermute | solution.py:228
  59.3 0.8 copy-start.1
  60.9 8.6 %collective-permute-start.3 = (bf16[256,128]{1,0:T(8,128)(2,1)S(1)}, bf16[256,128]{1,0:T(8,128)(2,1)S(1)}, u32[]{:S(2)}, u32[]{:S(2)}) collective-permute-start(bf16[256,128]{1,0:T(8,128)(2,1)S(1)} %step.16.refs_4_.refs_1_), channel_id=1, source_target_pairs={{1,2},{2,1},{3,4},{4,3},{5,6},{6,5},{7,70},{70,7},{71,68},{68,71},... | collective-permute-start | bytes 196616 | tf_op jit(solution)/shard_map/ppermute | solution.py:228
  62.8 6.7 %collective-permute-start.4 = (bf16[256,128]{1,0:T(8,128)(2,1)S(1)}, bf16[256,128]{1,0:T(8,128)(2,1)S(1)}, u32[]{:S(2)}, u32[]{:S(2)}) collective-permute-start(bf16[256,128]{1,0:T(8,128)(2,1)S(1)} %step.16.refs_4_.refs_1_), channel_id=1, source_target_pairs={{0,1},{1,0},{2,3},{3,2},{4,5},{5,4},{6,7},{7,6},{70,71},{71,70},{6... | collective-permute-start | bytes 196616 | tf_op jit(solution)/shard_map/ppermute | solution.py:228
  70.8 5.8 %collective-permute-start.5 = (bf16[256,128]{1,0:T(8,128)(2,1)S(1)}, bf16[256,128]{1,0:T(8,128)(2,1)S(1)}, u32[]{:S(2)}, u32[]{:S(2)}) collective-permute-start(bf16[256,128]{1,0:T(8,128)(2,1)S(1)} %step.17.refs_4_.refs_1_), channel_id=1, source_target_pairs={{1,2},{2,1},{3,4},{4,3},{5,6},{6,5},{7,70},{70,7},{71,68},{68,71},... | collective-permute-start | bytes 196616 | tf_op jit(solution)/shard_map/ppermute | solution.py:228
  72.7 4.1 %collective-permute-start.6 = (bf16[256,128]{1,0:T(8,128)(2,1)S(1)}, bf16[256,128]{1,0:T(8,128)(2,1)S(1)}, u32[]{:S(2)}, u32[]{:S(2)}) collective-permute-start(bf16[256,128]{1,0:T(8,128)(2,1)S(1)} %step.17.refs_4_.refs_1_), channel_id=1, source_target_pairs={{0,1},{1,0},{2,3},{3,2},{4,5},{5,4},{6,7},{7,6},{70,71},{71,70},{6... | collective-permute-start | bytes 196616 | tf_op jit(solution)/shard_map/ppermute | solution.py:228
  78.2 6.3 %collective-permute-start.7 = (bf16[256,128]{1,0:T(8,128)(2,1)S(1)}, bf16[256,128]{1,0:T(8,128)(2,1)S(1)}, u32[]{:S(2)}, u32[]{:S(2)}) collective-permute-start(bf16[256,128]{1,0:T(8,128)(2,1)S(1)} %step.18.refs_4_.refs_1_), channel_id=1, source_target_pairs={{1,2},{2,1},{3,4},{4,3},{5,6},{6,5},{7,70},{70,7},{71,68},{68,71},... | collective-permute-start | bytes 196616 | tf_op jit(solution)/shard_map/ppermute | solution.py:228
  80.9 3.8 %collective-permute-start.8 = (bf16[256,128]{1,0:T(8,128)(2,1)S(1)}, bf16[256,128]{1,0:T(8,128)(2,1)S(1)}, u32[]{:S(2)}, u32[]{:S(2)}) collective-permute-start(bf16[256,128]{1,0:T(8,128)(2,1)S(1)} %step.18.refs_4_.refs_1_), channel_id=1, source_target_pairs={{0,1},{1,0},{2,3},{3,2},{4,5},{5,4},{6,7},{7,6},{70,71},{71,70},{6... | collective-permute-start | bytes 196616 | tf_op jit(solution)/shard_map/ppermute | solution.py:228
  86.1 6.3 %collective-permute-start.9 = (bf16[256,128]{1,0:T(8,128)(2,1)S(1)}, bf16[256,128]{1,0:T(8,128)(2,1)S(1)}, u32[]{:S(2)}, u32[]{:S(2)}) collective-permute-start(bf16[256,128]{1,0:T(8,128)(2,1)S(1)} %step.19.refs_4_.refs_1_), channel_id=1, source_target_pairs={{1,2},{2,1},{3,4},{4,3},{5,6},{6,5},{7,70},{70,7},{71,68},{68,71},... | collective-permute-start | bytes 196616 | tf_op jit(solution)/shard_map/ppermute | solution.py:228
  88.3 4.3 %collective-permute-start.10 = (bf16[256,128]{1,0:T(8,128)(2,1)S(1)}, bf16[256,128]{1,0:T(8,128)(2,1)S(1)}, u32[]{:S(2)}, u32[]{:S(2)}) collective-permute-start(bf16[256,128]{1,0:T(8,128)(2,1)S(1)} %step.19.refs_4_.refs_1_), channel_id=1, source_target_pairs={{0,1},{1,0},{2,3},{3,2},{4,5},{5,4},{6,7},{7,6},{70,71},{71,70},{6... | collective-permute-start | bytes 196616 | tf_op jit(solution)/shard_map/ppermute | solution.py:228
  93.9 6.5 %collective-permute-start.11 = (bf16[256,128]{1,0:T(8,128)(2,1)S(1)}, bf16[256,128]{1,0:T(8,128)(2,1)S(1)}, u32[]{:S(2)}, u32[]{:S(2)}) collective-permute-start(bf16[256,128]{1,0:T(8,128)(2,1)S(1)} %step.20.refs_4_.refs_1_), channel_id=1, source_target_pairs={{1,2},{2,1},{3,4},{4,3},{5,6},{6,5},{7,70},{70,7},{71,68},{68,71},... | collective-permute-start | bytes 196616 | tf_op jit(solution)/shard_map/ppermute | solution.py:228
  96.2 4.2 %collective-permute-start.12 = (bf16[256,128]{1,0:T(8,128)(2,1)S(1)}, bf16[256,128]{1,0:T(8,128)(2,1)S(1)}, u32[]{:S(2)}, u32[]{:S(2)}) collective-permute-start(bf16[256,128]{1,0:T(8,128)(2,1)S(1)} %step.20.refs_4_.refs_1_), channel_id=1, source_target_pairs={{0,1},{1,0},{2,3},{3,2},{4,5},{5,4},{6,7},{7,6},{70,71},{71,70},{6... | collective-permute-start | bytes 196616 | tf_op jit(solution)/shard_map/ppermute | solution.py:228
  101.8 6.3 %collective-permute-start.13 = (bf16[256,128]{1,0:T(8,128)(2,1)S(1)}, bf16[256,128]{1,0:T(8,128)(2,1)S(1)}, u32[]{:S(2)}, u32[]{:S(2)}) collective-permute-start(bf16[256,128]{1,0:T(8,128)(2,1)S(1)} %step.21.refs_4_.refs_1_), channel_id=1, source_target_pairs={{1,2},{2,1},{3,4},{4,3},{5,6},{6,5},{7,70},{70,7},{71,68},{68,71},... | collective-permute-start | bytes 196616 | tf_op jit(solution)/shard_map/ppermute | solution.py:228
  104.0 4.2 %collective-permute-start.14 = (bf16[256,128]{1,0:T(8,128)(2,1)S(1)}, bf16[256,128]{1,0:T(8,128)(2,1)S(1)}, u32[]{:S(2)}, u32[]{:S(2)}) collective-permute-start(bf16[256,128]{1,0:T(8,128)(2,1)S(1)} %step.21.refs_4_.refs_1_), channel_id=1, source_target_pairs={{0,1},{1,0},{2,3},{3,2},{4,5},{5,4},{6,7},{7,6},{70,71},{71,70},{6... | collective-permute-start | bytes 196616 | tf_op jit(solution)/shard_map/ppermute | solution.py:228
  108.3 7.1 %copy-start.6 = (bf16[64,576]{1,0:T(8,128)(2,1)S(1)}, bf16[64,576]{1,0:T(8,128)(2,1)}, u32[]{:S(2)}) copy-start(bf16[64,576]{1,0:T(8,128)(2,1)} %param.20) | copy-start | bytes 221188
  109.7 5.9 %copy-start.7 = (bf16[64,576]{1,0:T(8,128)(2,1)S(1)}, bf16[64,576]{1,0:T(8,128)(2,1)}, u32[]{:S(2)}) copy-start(bf16[64,576]{1,0:T(8,128)(2,1)} %param.21) | copy-start | bytes 221188
  109.7 6.7 %collective-permute-start.15 = (bf16[256,128]{1,0:T(8,128)(2,1)S(1)}, bf16[256,128]{1,0:T(8,128)(2,1)S(1)}, u32[]{:S(2)}, u32[]{:S(2)}) collective-permute-start(bf16[256,128]{1,0:T(8,128)(2,1)S(1)} %step.22.refs_4_), channel_id=1, source_target_pairs={{1,2},{2,1},{3,4},{4,3},{5,6},{6,5},{7,70},{70,7},{71,68},{68,71},... | collective-permute-start | bytes 196616 | tf_op jit(solution)/shard_map/ppermute | solution.py:228
  112.0 4.4 %collective-permute-start.16 = (bf16[256,128]{1,0:T(8,128)(2,1)S(1)}, bf16[256,128]{1,0:T(8,128)(2,1)S(1)}, u32[]{:S(2)}, u32[]{:S(2)}) collective-permute-start(bf16[256,128]{1,0:T(8,128)(2,1)S(1)} %step.22.refs_4_), channel_id=1, source_target_pairs={{0,1},{1,0},{2,3},{3,2},{4,5},{5,4},{6,7},{7,6},{70,71},{71,70},{6... | collective-permute-start | bytes 196616 | tf_op jit(solution)/shard_map/ppermute | solution.py:228
  117.8 7.7 %collective-permute-start.17 = (bf16[256,128]{1,0:T(8,128)(2,1)S(1)}, bf16[256,128]{1,0:T(8,128)(2,1)S(1)}, u32[]{:S(2)}, u32[]{:S(2)}) collective-permute-start(bf16[256,128]{1,0:T(8,128)(2,1)S(1)} %step.23.refs_4_), channel_id=1, source_target_pairs={{1,2},{2,1},{3,4},{4,3},{5,6},{6,5},{7,70},{70,7},{71,68},{68,71},... | collective-permute-start | bytes 196616 | tf_op jit(solution)/shard_map/ppermute | solution.py:228
  119.9 5.5 %collective-permute-start.18 = (bf16[256,128]{1,0:T(8,128)(2,1)S(1)}, bf16[256,128]{1,0:T(8,128)(2,1)S(1)}, u32[]{:S(2)}, u32[]{:S(2)}) collective-permute-start(bf16[256,128]{1,0:T(8,128)(2,1)S(1)} %step.23.refs_4_), channel_id=1, source_target_pairs={{0,1},{1,0},{2,3},{3,2},{4,5},{5,4},{6,7},{7,6},{70,71},{71,70},{6... | collective-permute-start | bytes 196616 | tf_op jit(solution)/shard_map/ppermute | solution.py:228
  124.2 0.9 copy-start.2
  125.2 0.8 copy-start
  126.8 5.6 %collective-permute-start.19 = (bf16[256,128]{1,0:T(8,128)(2,1)S(1)}, bf16[256,128]{1,0:T(8,128)(2,1)S(1)}, u32[]{:S(2)}, u32[]{:S(2)}) collective-permute-start(bf16[256,128]{1,0:T(8,128)(2,1)S(1)} %step.24.refs_7_.refs_1_), channel_id=1, source_target_pairs={{1,2},{2,1},{3,4},{4,3},{5,6},{6,5},{7,70},{70,7},{71,68},{68,71},... | collective-permute-start | bytes 196616 | tf_op jit(solution)/shard_map/ppermute | solution.py:228
  128.8 4.1 %collective-permute-start.20 = (bf16[256,128]{1,0:T(8,128)(2,1)S(1)}, bf16[256,128]{1,0:T(8,128)(2,1)S(1)}, u32[]{:S(2)}, u32[]{:S(2)}) collective-permute-start(bf16[256,128]{1,0:T(8,128)(2,1)S(1)} %step.24.refs_7_.refs_1_), channel_id=1, source_target_pairs={{0,1},{1,0},{2,3},{3,2},{4,5},{5,4},{6,7},{7,6},{70,71},{71,70},{6... | collective-permute-start | bytes 196616 | tf_op jit(solution)/shard_map/ppermute | solution.py:228
  134.3 6.3 %collective-permute-start.21 = (bf16[256,128]{1,0:T(8,128)(2,1)S(1)}, bf16[256,128]{1,0:T(8,128)(2,1)S(1)}, u32[]{:S(2)}, u32[]{:S(2)}) collective-permute-start(bf16[256,128]{1,0:T(8,128)(2,1)S(1)} %step.25.refs_7_.refs_1_), channel_id=1, source_target_pairs={{1,2},{2,1},{3,4},{4,3},{5,6},{6,5},{7,70},{70,7},{71,68},{68,71},... | collective-permute-start | bytes 196616 | tf_op jit(solution)/shard_map/ppermute | solution.py:228
  136.9 3.8 %collective-permute-start.22 = (bf16[256,128]{1,0:T(8,128)(2,1)S(1)}, bf16[256,128]{1,0:T(8,128)(2,1)S(1)}, u32[]{:S(2)}, u32[]{:S(2)}) collective-permute-start(bf16[256,128]{1,0:T(8,128)(2,1)S(1)} %step.25.refs_7_.refs_1_), channel_id=1, source_target_pairs={{0,1},{1,0},{2,3},{3,2},{4,5},{5,4},{6,7},{7,6},{70,71},{71,70},{6... | collective-permute-start | bytes 196616 | tf_op jit(solution)/shard_map/ppermute | solution.py:228
  142.1 6.3 %collective-permute-start.23 = (bf16[256,128]{1,0:T(8,128)(2,1)S(1)}, bf16[256,128]{1,0:T(8,128)(2,1)S(1)}, u32[]{:S(2)}, u32[]{:S(2)}) collective-permute-start(bf16[256,128]{1,0:T(8,128)(2,1)S(1)} %step.26.refs_7_.refs_1_), channel_id=1, source_target_pairs={{1,2},{2,1},{3,4},{4,3},{5,6},{6,5},{7,70},{70,7},{71,68},{68,71},... | collective-permute-start | bytes 196616 | tf_op jit(solution)/shard_map/ppermute | solution.py:228
  144.3 4.2 %collective-permute-start.24 = (bf16[256,128]{1,0:T(8,128)(2,1)S(1)}, bf16[256,128]{1,0:T(8,128)(2,1)S(1)}, u32[]{:S(2)}, u32[]{:S(2)}) collective-permute-start(bf16[256,128]{1,0:T(8,128)(2,1)S(1)} %step.26.refs_7_.refs_1_), channel_id=1, source_target_pairs={{0,1},{1,0},{2,3},{3,2},{4,5},{5,4},{6,7},{7,6},{70,71},{71,70},{6... | collective-permute-start | bytes 196616 | tf_op jit(solution)/shard_map/ppermute | solution.py:228
  149.9 6.5 %collective-permute-start.25 = (bf16[256,128]{1,0:T(8,128)(2,1)S(1)}, bf16[256,128]{1,0:T(8,128)(2,1)S(1)}, u32[]{:S(2)}, u32[]{:S(2)}) collective-permute-start(bf16[256,128]{1,0:T(8,128)(2,1)S(1)} %step.27.refs_7_.refs_1_), channel_id=1, source_target_pairs={{1,2},{2,1},{3,4},{4,3},{5,6},{6,5},{7,70},{70,7},{71,68},{68,71},... | collective-permute-start | bytes 196616 | tf_op jit(solution)/shard_map/ppermute | solution.py:228
  152.2 4.3 %collective-permute-start.26 = (bf16[256,128]{1,0:T(8,128)(2,1)S(1)}, bf16[256,128]{1,0:T(8,128)(2,1)S(1)}, u32[]{:S(2)}, u32[]{:S(2)}) collective-permute-start(bf16[256,128]{1,0:T(8,128)(2,1)S(1)} %step.27.refs_7_.refs_1_), channel_id=1, source_target_pairs={{0,1},{1,0},{2,3},{3,2},{4,5},{5,4},{6,7},{7,6},{70,71},{71,70},{6... | collective-permute-start | bytes 196616 | tf_op jit(solution)/shard_map/ppermute | solution.py:228
  157.8 6.3 %collective-permute-start.27 = (bf16[256,128]{1,0:T(8,128)(2,1)S(1)}, bf16[256,128]{1,0:T(8,128)(2,1)S(1)}, u32[]{:S(2)}, u32[]{:S(2)}) collective-permute-start(bf16[256,128]{1,0:T(8,128)(2,1)S(1)} %step.28.refs_7_.refs_1_), channel_id=1, source_target_pairs={{1,2},{2,1},{3,4},{4,3},{5,6},{6,5},{7,70},{70,7},{71,68},{68,71},... | collective-permute-start | bytes 196616 | tf_op jit(solution)/shard_map/ppermute | solution.py:228
  160.0 4.2 %collective-permute-start.28 = (bf16[256,128]{1,0:T(8,128)(2,1)S(1)}, bf16[256,128]{1,0:T(8,128)(2,1)S(1)}, u32[]{:S(2)}, u32[]{:S(2)}) collective-permute-start(bf16[256,128]{1,0:T(8,128)(2,1)S(1)} %step.28.refs_7_.refs_1_), channel_id=1, source_target_pairs={{0,1},{1,0},{2,3},{3,2},{4,5},{5,4},{6,7},{7,6},{70,71},{71,70},{6... | collective-permute-start | bytes 196616 | tf_op jit(solution)/shard_map/ppermute | solution.py:228
  165.6 6.3 %collective-permute-start.29 = (bf16[256,128]{1,0:T(8,128)(2,1)S(1)}, bf16[256,128]{1,0:T(8,128)(2,1)S(1)}, u32[]{:S(2)}, u32[]{:S(2)}) collective-permute-start(bf16[256,128]{1,0:T(8,128)(2,1)S(1)} %step.29.refs_7_.refs_1_), channel_id=1, source_target_pairs={{1,2},{2,1},{3,4},{4,3},{5,6},{6,5},{7,70},{70,7},{71,68},{68,71},... | collective-permute-start | bytes 196616 | tf_op jit(solution)/shard_map/ppermute | solution.py:228
  167.9 4.2 %collective-permute-start.30 = (bf16[256,128]{1,0:T(8,128)(2,1)S(1)}, bf16[256,128]{1,0:T(8,128)(2,1)S(1)}, u32[]{:S(2)}, u32[]{:S(2)}) collective-permute-start(bf16[256,128]{1,0:T(8,128)(2,1)S(1)} %step.29.refs_7_.refs_1_), channel_id=1, source_target_pairs={{0,1},{1,0},{2,3},{3,2},{4,5},{5,4},{6,7},{7,6},{70,71},{71,70},{6... | collective-permute-start | bytes 196616 | tf_op jit(solution)/shard_map/ppermute | solution.py:228
  173.4 6.3 %collective-permute-start.31 = (bf16[256,128]{1,0:T(8,128)(2,1)S(1)}, bf16[256,128]{1,0:T(8,128)(2,1)S(1)}, u32[]{:S(2)}, u32[]{:S(2)}) collective-permute-start(bf16[256,128]{1,0:T(8,128)(2,1)S(1)} %step.30.refs_7_), channel_id=1, source_target_pairs={{1,2},{2,1},{3,4},{4,3},{5,6},{6,5},{7,70},{70,7},{71,68},{68,71},... | collective-permute-start | bytes 196616 | tf_op jit(solution)/shard_map/ppermute | solution.py:228
  175.7 4.3 %collective-permute-start.32 = (bf16[256,128]{1,0:T(8,128)(2,1)S(1)}, bf16[256,128]{1,0:T(8,128)(2,1)S(1)}, u32[]{:S(2)}, u32[]{:S(2)}) collective-permute-start(bf16[256,128]{1,0:T(8,128)(2,1)S(1)} %step.30.refs_7_), channel_id=1, source_target_pairs={{0,1},{1,0},{2,3},{3,2},{4,5},{5,4},{6,7},{7,6},{70,71},{71,70},{6... | collective-permute-start | bytes 196616 | tf_op jit(solution)/shard_map/ppermute | solution.py:228
  181.3 7.7 %collective-permute-start.33 = (bf16[2,256,128]{2,1,0:T(8,128)(2,1)S(1)}, bf16[2,256,128]{2,1,0:T(8,128)(2,1)S(1)}, u32[]{:S(2)}, u32[]{:S(2)}) collective-permute-start(bf16[2,256,128]{2,1,0:T(8,128)(2,1)S(1)} %pad_maximum_fusion.2), channel_id=1, source_target_pairs={{0,64},{1,65},{2,66},{3,67},{4,68},{5,69},{6,70},{7,71},{16,80},{1... | collective-permute-start | bytes 393224 | tf_op jit(solution)/shard_map/ppermute | solution.py:332

commit v4 on v2

--- a/solution.py
+++ b/solution.py
@@ -14,6 +14,7 @@
 H = 256
 FRAMES = 8
 EXT = ROWS + 2 * R
+EARLY = EXT // 2
 
 
 def leaky(values):
@@ -66,34 +67,46 @@
         store(ch, total.astype(jnp.bfloat16))
 
 
-def prepare_kernel(priors, grid, *refs):
+def prepare_kernel(priors, first, sense, *refs):
     refs = list(refs)
+    grid = (first[0], sense[0])
+    newest = [refs.pop(0) for _ in range(2)] + [None]
     older = [refs.pop(0) for _ in range(3)] if priors == 2 else None
-    params, taps = refs.pop(0), refs.pop(0)
-    for n, w in enumerate(tap_weights(params[0], grid)):
-        for r in range(EXT):
-            taps[r, n] = jnp.broadcast_to(w[r : r + 1], (16, W)).astype(jnp.bfloat16)
-    if priors < 2:
-        return
-    stack, wts = refs
-    for n, w in enumerate(tap_weights(params[1], grid)):
-        wts[n] = w
-    for r in range(EXT):
-
-        def weight(n):
-            return jnp.broadcast_to(wts[n, pl.ds(r, 1), :], (16, W)).astype(jnp.bfloat16)
+    params, taps, early = refs.pop(0), refs.pop(0), refs.pop(0)
+    stack = refs.pop(0) if priors == 2 else None
+    wts = refs.pop(0)
+
+    for p in range(priors):
+        for n, w in enumerate(tap_weights(params[p], grid)):
+            wts[p * 25 + n] = w
+
+    def weight(p, r, n):
+        return jnp.broadcast_to(wts[p * 25 + n, pl.ds(r, 1), :], (16, W)).astype(jnp.bfloat16)
+
+    for r in range(EARLY):
+
+        def store_early(ch, value):
+            early[pl.ds(ch, 16), pl.ds(r * W, W)] = value
+
+        sample_row(newest, r, lambda n: weight(0, r, n), store_early)
+    for r in range(EARLY, EXT):
+        for n in range(25):
+            taps[r - EARLY, n] = weight(0, r, n)
+    for r in range(EXT if older else 0):
 
         def store(ch, value):
             stack[pl.ds(ch, 16), pl.ds(r * W, W)] = value
 
-        sample_row(older, r, weight, store)
-
-
-def step_kernel(priors, parts, grid, *refs):
+        sample_row(older, r, lambda n: weight(1, r, n), store)
+
+
+def step_kernel(priors, parts, first, sense, *refs):
     refs = list(refs)
+    grid = (first[0], sense[0])
     sides = [[refs.pop(0) for _ in range(3)] for _ in range(parts)]
     newest = [refs.pop(0) for _ in range(3)] if priors else None
     taps = refs.pop(0) if priors else None
+    early = refs.pop(0) if priors else None
     older = refs.pop(0) if priors == 2 else None
     mixer, inner, outer, out, stack, joined, hidden = refs
 
@@ -106,18 +119,19 @@
         return ref[pl.ds(at, C), :]
 
     depth = (parts + priors) * C
-    for r in (4, 6, 2, 0):
-        for n in range(2 if priors else 0):
+    for r in range(0, EXT, 2):
+        for n in range(2 if priors and r >= EARLY else 0):
 
             def store(ch, value):
-                stack[pl.ds(ch, 16), pl.ds((r + n) * W, W)] = value
-
-            sample_row(newest, r + n, lambda k: taps[r + n, k], store)
+                stack[pl.ds(ch, 16), pl.ds((r + n - EARLY) * W, W)] = value
+
+            sample_row(newest, r + n, lambda k: taps[r + n - EARLY, k], store)
         pieces = [
             jnp.concatenate([side_row(trio, r), side_row(trio, r + 1)], axis=1) for trio in sides
         ]
         if priors:
-            pieces.append(stack[:, pl.ds(r * W, 2 * W)])
+            near = early[:, pl.ds(r * W, 2 * W)] if r < EARLY else stack[:, pl.ds((r - EARLY) * W, 2 * W)]
+            pieces.append(near)
         if priors == 2:
             pieces.append(older[:, pl.ds(r * W, 2 * W)])
         data = jnp.concatenate(pieces, axis=0)
@@ -143,14 +157,14 @@
             outs.append(left + part[C : 2 * C] + right)
         return outs
 
-    for r in (4, 2, 0):
+    for r in (0, 2, 4):
         for n, value in enumerate(conv_pair(joined, inner, r)):
             value = leaky(value)
             if r + n in (0, ROWS + 1):
                 value = value * keep(r + n - 1)
             hidden[pl.ds((r + n) * C, C), :] = value.astype(jnp.bfloat16)
 
-    for r in (2, 0):
+    for r in (0, 2):
         for n, value in enumerate(conv_pair(hidden, outer, r)):
             base = joined[pl.ds((r + n + R) * C, C), :].astype(jnp.float32)
             out[pl.ds((r + n) * C, C), :] = (base + value).astype(jnp.bfloat16)
@@ -161,17 +175,20 @@
 BF16 = jnp.bfloat16
 
 
-def run_prepare(grid, older, params):
-    operands = [grid] + (list(older) if older else []) + [params]
-    outs = [jax.ShapeDtypeStruct((EXT, 25, 16, W), BF16)]
+def run_prepare(grid, newest, older, params):
+    operands = list(grid) + list(newest[:2]) + (list(older) if older else []) + [params]
+    outs = [
+        jax.ShapeDtypeStruct((EXT - EARLY, 25, 16, W), BF16),
+        jax.ShapeDtypeStruct((C, EARLY * W), BF16),
+    ]
     if older:
         outs.append(jax.ShapeDtypeStruct((C, EXT * W), BF16))
     return pl.pallas_call(
         functools.partial(prepare_kernel, 2 if older else 1),
         out_shape=outs,
-        in_specs=[SMEM] + [VMEM] * (len(operands) - 1),
+        in_specs=[SMEM, SMEM] + [VMEM] * (len(operands) - 2),
         out_specs=[VMEM] * len(outs),
-        scratch_shapes=[pltpu.VMEM((25, EXT, W), jnp.float32)] if older else [],
+        scratch_shapes=[pltpu.VMEM((50, EXT, W), jnp.float32)],
         compiler_params=pltpu.CompilerParams(vmem_limit_bytes=16 * 2**20),
         cost_estimate=pl.CostEstimate(flops=2 * 10**7, bytes_accessed=2**20, transcendentals=0),
         name="prepare",
@@ -179,17 +196,17 @@
 
 
 def run_step(grid, sides, newest, prepared, weights):
-    operands = [grid]
+    operands = list(grid)
     for trio in sides:
         operands += list(trio)
     operands += (list(newest) if newest else []) + list(prepared) + list(weights)
     return pl.pallas_call(
-        functools.partial(step_kernel, len(prepared), len(sides)),
+        functools.partial(step_kernel, max(0, len(prepared) - 1), len(sides)),
         out_shape=jax.ShapeDtypeStruct((ROWS * C, W), BF16),
-        in_specs=[SMEM] + [VMEM] * (len(operands) - 1),
+        in_specs=[SMEM, SMEM] + [VMEM] * (len(operands) - 2),
         out_specs=VMEM,
         scratch_shapes=[
-            pltpu.VMEM((C, EXT * W), BF16),
+            pltpu.VMEM((C, (EXT - EARLY) * W), BF16),
             pltpu.VMEM((EXT * C, W), BF16),
             pltpu.VMEM(((ROWS + 2) * C, W), BF16),
         ],
@@ -229,7 +246,10 @@
     tile = lax.axis_index("tile").astype(jnp.int32)
     turn = lax.axis_index("tm")
     odd = tile % 2 == 1
-    grid = jnp.stack([tile * ROWS + jnp.where(odd, ROWS - 1, 0), jnp.where(odd, -1, 1)])
+    grid = (
+        (tile * ROWS + jnp.where(odd, ROWS - 1, 0)).reshape(1),
+        jnp.where(odd, -1, 1).astype(jnp.int32).reshape(1),
+    )
 
     def oriented(values, axis):
         return jnp.where(odd, jnp.flip(values, axis), values)
@@ -268,7 +288,9 @@
         history = []
         for n, t in enumerate(order):
             sides = [frame_trios[t]] + ([extra[t]] if extra else [])
-            prepared = run_prepare(grid, history[1] if n > 1 else None, params[way, t]) if n else []
+            prepared = []
+            if n:
+                prepared = run_prepare(grid, history[0], history[1] if n > 1 else None, params[way, t])
             new = run_step(grid, sides, history[0] if n else None, prepared, weights)
             if n + 1 < FRAMES or not extra:
                 far, near = swap(new, new)

time: 199 us -> 199 us (level)
  the two profiles are of different devices: /device:TPU:7 before, /device:TPU:6 now
where the time goes in v4:
time: 199 us; the launch traced here: 198 us
  starting transfers between devices  111 us (56%)
  waiting for transfers between devices  45.8 us (23%)
  Pallas kernels  26.9 us (14%)
  local copies, waits for them, and re-layouts  10.8 us (5%)
    ppermute x16, starting transfers between devices, swap(): lax.ppermute(for_across, 'tile', pairs + [(j, i) for i, j in pairs])  72.9 us
    ppermute x16, starting transfers between devices, swap(): lax.ppermute(for_beside, 'tile', [(i, i ^ 1) for i in range(count)])  31.1 us
    ppermute x16, waiting for transfers between devices, swap(): lax.ppermute(for_across, 'tile', pairs + [(j, i) for i, j in pairs])  26.7 us
    all_to_all x1, waiting for transfers between devices, shards(): lax.all_to_all(jnp.broadcast_to(mine[None], (FRAMES,) + mine.shape), 'tm'...  18.5 us
    pallas_call x16, Pallas kernels, run_step(): pl.pallas_call(functools.partial(step_kernel, max(0, len(prepared) - 1),...  15.5 us
    pallas_call x14, Pallas kernels, run_prepare(): pl.pallas_call(functools.partial(prepare_kernel, 2 if older else 1), out_...  11.5 us
    unnamed x31, local copies, waits for them, and re-layouts  7.46 us
    all_to_all x1, starting transfers between devices, shards(): lax.all_to_all(jnp.broadcast_to(mine[None], (FRAMES,) + mine.shape), 'tm'...  7.23 us
  transfers between devices with their start and end apart: 33, of which 16 were waited for; matrix products, arithmetic and copies ran while one was open for 2% of the time, Pallas kernels for 6%

profile of v4, /device:TPU:6, one launch (start us, length us, event | category | flops | bytes accessed | tf_op | source)
XLA Modules:
  0.0 197.9 jit_solution(8964425741794929771)
XLA Ops:
  4.7 7.2 %all-to-all-start = ((bf16[8,320,128]{2,1,0:T(8,128)(2,1)}), bf16[8,320,128]{2,1,0:T(8,128)(2,1)S(1)}, u32[]{:S(2)}, u32[]{:S(2)}) async-start(bf16[8,320,128]{2,1,0:T(8,128)(2,1)} %broadcast_in_dim.12), calls=%async_computation | async-start | bytes 1310720 | tf_op jit(solution)/shard_map/all_to_all | solution.py:270
  13.7 18.5 %all-to-all-done = bf16[8,320,128]{2,1,0:T(8,128)(2,1)S(1)} async-done(((bf16[8,320,128]{2,1,0:T(8,128)(2,1)}), bf16[8,320,128]{2,1,0:T(8,128)(2,1)S(1)}, u32[]{:S(2)}, u32[]{:S(2)}) %all-to-all-start) | async-done | bytes 655392 | tf_op jit(solution)/shard_map/all_to_all | solution.py:270
  32.3 1.9 collective-permute-start.1
  34.3 11.3 %collective-permute-start = (bf16[8,160,128]{2,1,0:T(8,128)(2,1)S(1)}, bf16[8,160,128]{2,1,0:T(8,128)(2,1)S(1)}, u32[]{:S(2)}, u32[]{:S(2)}) collective-permute-start(bf16[8,160,128]{2,1,0:T(8,128)(2,1)S(1)} %pad_maximum_fusion), channel_id=1, source_target_pairs={{1,2},{3,4},{5,6},{7,8},{9,10},{11,12},{13,14},{15,16},{17,18},{19... | collective-permute-start | bytes 983048 | tf_op jit(solution)/shard_map/ppermute | solution.py:222
  46.2 4.1 %collective-permute-done = bf16[8,160,128]{2,1,0:T(8,128)(2,1)S(1)} collective-permute-done((bf16[8,160,128]{2,1,0:T(8,128)(2,1)S(1)}, bf16[8,160,128]{2,1,0:T(8,128)(2,1)S(1)}, u32[]{:S(2)}, u32[]{:S(2)}) %collective-permute-start) | collective-permute-done | bytes 327712 | tf_op jit(solution)/shard_map/ppermute | solution.py:222
  52.3 5.7 %collective-permute-start.2 = (bf16[256,128]{1,0:T(8,128)(2,1)S(1)}, bf16[256,128]{1,0:T(8,128)(2,1)S(1)}, u32[]{:S(2)}, u32[]{:S(2)}) collective-permute-start(bf16[256,128]{1,0:T(8,128)(2,1)S(1)} %step.16.refs_1_.refs_4_.refs_3_), channel_id=1, source_target_pairs={{1,2},{3,4},{5,6},{7,8},{9,10},{11,12},{13,14},{15,16},{17,18},{19... | collective-permute-start | bytes 196616 | tf_op jit(solution)/shard_map/ppermute | solution.py:222
  58.1 1.9 collective-permute-start.3
  62.2 4.9 %collective-permute-start.4 = (bf16[256,128]{1,0:T(8,128)(2,1)S(1)}, bf16[256,128]{1,0:T(8,128)(2,1)S(1)}, u32[]{:S(2)}, u32[]{:S(2)}) collective-permute-start(bf16[256,128]{1,0:T(8,128)(2,1)S(1)} %step.17.refs_1_.refs_4_.refs_3_), channel_id=1, source_target_pairs={{1,2},{3,4},{5,6},{7,8},{9,10},{11,12},{13,14},{15,16},{17,18},{19... | collective-permute-start | bytes 196616 | tf_op jit(solution)/shard_map/ppermute | solution.py:222
  67.1 1.9 collective-permute-start.5
  70.8 1.0 step.18.refs_1_.refs_4_.refs_3_
  71.8 4.9 %collective-permute-start.6 = (bf16[256,128]{1,0:T(8,128)(2,1)S(1)}, bf16[256,128]{1,0:T(8,128)(2,1)S(1)}, u32[]{:S(2)}, u32[]{:S(2)}) collective-permute-start(bf16[256,128]{1,0:T(8,128)(2,1)S(1)} %step.18.refs_1_.refs_4_.refs_3_), channel_id=1, source_target_pairs={{1,2},{3,4},{5,6},{7,8},{9,10},{11,12},{13,14},{15,16},{17,18},{19... | collective-permute-start | bytes 196616 | tf_op jit(solution)/shard_map/ppermute | solution.py:222
  76.8 1.9 collective-permute-start.7
  80.4 1.0 step.19.refs_1_.refs_4_.refs_3_
  81.4 4.9 %collective-permute-start.8 = (bf16[256,128]{1,0:T(8,128)(2,1)S(1)}, bf16[256,128]{1,0:T(8,128)(2,1)S(1)}, u32[]{:S(2)}, u32[]{:S(2)}) collective-permute-start(bf16[256,128]{1,0:T(8,128)(2,1)S(1)} %step.19.refs_1_.refs_4_.refs_3_), channel_id=1, source_target_pairs={{1,2},{3,4},{5,6},{7,8},{9,10},{11,12},{13,14},{15,16},{17,18},{19... | collective-permute-start | bytes 196616 | tf_op jit(solution)/shard_map/ppermute | solution.py:222
  86.4 1.9 collective-permute-start.9
  90.0 1.0 step.20.refs_1_.refs_4_.refs_3_
  91.0 4.9 %collective-permute-start.10 = (bf16[256,128]{1,0:T(8,128)(2,1)S(1)}, bf16[256,128]{1,0:T(8,128)(2,1)S(1)}, u32[]{:S(2)}, u32[]{:S(2)}) collective-permute-start(bf16[256,128]{1,0:T(8,128)(2,1)S(1)} %step.20.refs_1_.refs_4_.refs_3_), channel_id=1, source_target_pairs={{1,2},{3,4},{5,6},{7,8},{9,10},{11,12},{13,14},{15,16},{17,18},{19... | collective-permute-start | bytes 196616 | tf_op jit(solution)/shard_map/ppermute | solution.py:222
  96.0 1.9 collective-permute-start.11
  99.6 1.0 step.21.refs_1_.refs_4_.refs_3_
  100.6 4.9 %collective-permute-start.12 = (bf16[256,128]{1,0:T(8,128)(2,1)S(1)}, bf16[256,128]{1,0:T(8,128)(2,1)S(1)}, u32[]{:S(2)}, u32[]{:S(2)}) collective-permute-start(bf16[256,128]{1,0:T(8,128)(2,1)S(1)} %step.21.refs_1_.refs_4_.refs_3_), channel_id=1, source_target_pairs={{1,2},{3,4},{5,6},{7,8},{9,10},{11,12},{13,14},{15,16},{17,18},{19... | collective-permute-start | bytes 196616 | tf_op jit(solution)/shard_map/ppermute | solution.py:222
  105.6 2.1 %collective-permute-start.13 = (bf16[256,128]{1,0:T(8,128)(2,1)S(1)}, bf16[256,128]{1,0:T(8,128)(2,1)S(1)}, u32[]{:S(2)}, u32[]{:S(2)}) collective-permute-start(bf16[256,128]{1,0:T(8,128)(2,1)S(1)} %step.21.refs_1_.refs_4_.refs_3_), channel_id=1, source_target_pairs={{0,1},{1,0},{2,3},{3,2},{4,5},{5,4},{6,7},{7,6},{8,9},{9,8},{10,11... | collective-permute-start | bytes 196616 | tf_op jit(solution)/shard_map/ppermute | solution.py:223
  109.3 1.0 step.22.refs_1_.refs_4_
  110.3 5.1 %collective-permute-start.14 = (bf16[256,128]{1,0:T(8,128)(2,1)S(1)}, bf16[256,128]{1,0:T(8,128)(2,1)S(1)}, u32[]{:S(2)}, u32[]{:S(2)}) collective-permute-start(bf16[256,128]{1,0:T(8,128)(2,1)S(1)} %step.22.refs_1_.refs_4_), channel_id=1, source_target_pairs={{1,2},{3,4},{5,6},{7,8},{9,10},{11,12},{13,14},{15,16},{17,18},{19... | collective-permute-start | bytes 196616 | tf_op jit(solution)/shard_map/ppermute | solution.py:222
  115.4 1.9 collective-permute-start.15
  119.0 1.0 step.23.refs_4_
  120.0 4.9 %collective-permute-start.16 = (bf16[256,128]{1,0:T(8,128)(2,1)S(1)}, bf16[256,128]{1,0:T(8,128)(2,1)S(1)}, u32[]{:S(2)}, u32[]{:S(2)}) collective-permute-start(bf16[256,128]{1,0:T(8,128)(2,1)S(1)} %step.23.refs_4_), channel_id=1, source_target_pairs={{1,2},{3,4},{5,6},{7,8},{9,10},{11,12},{13,14},{15,16},{17,18},{19... | collective-permute-start | bytes 196616 | tf_op jit(solution)/shard_map/ppermute | solution.py:222
  125.0 1.9 collective-permute-start.17
  130.4 3.0 %collective-permute-start.18 = (bf16[256,128]{1,0:T(8,128)(2,1)S(1)}, bf16[256,128]{1,0:T(8,128)(2,1)S(1)}, u32[]{:S(2)}, u32[]{:S(2)}) collective-permute-start(bf16[256,128]{1,0:T(8,128)(2,1)S(1)} %step.24.refs_1_.refs_7_.refs_3_), channel_id=1, source_target_pairs={{1,2},{3,4},{5,6},{7,8},{9,10},{11,12},{13,14},{15,16},{17,18},{19... | collective-permute-start | bytes 196616 | tf_op jit(solution)/shard_map/ppermute | solution.py:222
  133.4 1.9 collective-permute-start.19
  135.4 2.7 %collective-permute-done.18.refs_0_.refs_6_.refs_2_ = bf16[256,128]{1,0:T(8,128)(2,1)S(1)} collective-permute-done((bf16[256,128]{1,0:T(8,128)(2,1)S(1)}, bf16[256,128]{1,0:T(8,128)(2,1)S(1)}, u32[]{:S(2)}, u32[]{:S(2)}) %collective-permute-start.18) | collective-permute-done | bytes 65568 | tf_op jit(solution)/shard_map/ppermute | solution.py:222
  139.5 3.0 %collective-permute-start.20 = (bf16[256,128]{1,0:T(8,128)(2,1)S(1)}, bf16[256,128]{1,0:T(8,128)(2,1)S(1)}, u32[]{:S(2)}, u32[]{:S(2)}) collective-permute-start(bf16[256,128]{1,0:T(8,128)(2,1)S(1)} %step.25.refs_1_.refs_7_.refs_3_), channel_id=1, source_target_pairs={{1,2},{3,4},{5,6},{7,8},{9,10},{11,12},{13,14},{15,16},{17,18},{19... | collective-permute-start | bytes 196616 | tf_op jit(solution)/shard_map/ppermute | solution.py:222
  142.5 1.9 collective-permute-start.21
  144.4 2.7 %collective-permute-done.20.refs_0_.refs_6_.refs_2_ = bf16[256,128]{1,0:T(8,128)(2,1)S(1)} collective-permute-done((bf16[256,128]{1,0:T(8,128)(2,1)S(1)}, bf16[256,128]{1,0:T(8,128)(2,1)S(1)}, u32[]{:S(2)}, u32[]{:S(2)}) %collective-permute-start.20) | collective-permute-done | bytes 65568 | tf_op jit(solution)/shard_map/ppermute | solution.py:222
  149.1 3.0 %collective-permute-start.22 = (bf16[256,128]{1,0:T(8,128)(2,1)S(1)}, bf16[256,128]{1,0:T(8,128)(2,1)S(1)}, u32[]{:S(2)}, u32[]{:S(2)}) collective-permute-start(bf16[256,128]{1,0:T(8,128)(2,1)S(1)} %step.26.refs_1_.refs_7_.refs_3_), channel_id=1, source_target_pairs={{1,2},{3,4},{5,6},{7,8},{9,10},{11,12},{13,14},{15,16},{17,18},{19... | collective-permute-start | bytes 196616 | tf_op jit(solution)/shard_map/ppermute | solution.py:222
  152.1 1.9 collective-permute-start.23
  154.1 2.7 %collective-permute-done.22.refs_0_.refs_6_.refs_2_ = bf16[256,128]{1,0:T(8,128)(2,1)S(1)} collective-permute-done((bf16[256,128]{1,0:T(8,128)(2,1)S(1)}, bf16[256,128]{1,0:T(8,128)(2,1)S(1)}, u32[]{:S(2)}, u32[]{:S(2)}) %collective-permute-start.22) | collective-permute-done | bytes 65568 | tf_op jit(solution)/shard_map/ppermute | solution.py:222
  158.7 3.0 %collective-permute-start.24 = (bf16[256,128]{1,0:T(8,128)(2,1)S(1)}, bf16[256,128]{1,0:T(8,128)(2,1)S(1)}, u32[]{:S(2)}, u32[]{:S(2)}) collective-permute-start(bf16[256,128]{1,0:T(8,128)(2,1)S(1)} %step.27.refs_1_.refs_7_.refs_3_), channel_id=1, source_target_pairs={{1,2},{3,4},{5,6},{7,8},{9,10},{11,12},{13,14},{15,16},{17,18},{19... | collective-permute-start | bytes 196616 | tf_op jit(solution)/shard_map/ppermute | solution.py:222
  161.7 1.9 collective-permute-start.25
  163.7 2.7 %collective-permute-done.24.refs_0_.refs_6_.refs_2_ = bf16[256,128]{1,0:T(8,128)(2,1)S(1)} collective-permute-done((bf16[256,128]{1,0:T(8,128)(2,1)S(1)}, bf16[256,128]{1,0:T(8,128)(2,1)S(1)}, u32[]{:S(2)}, u32[]{:S(2)}) %collective-permute-start.24) | collective-permute-done | bytes 65568 | tf_op jit(solution)/shard_map/ppermute | solution.py:222
  168.3 3.0 %collective-permute-start.26 = (bf16[256,128]{1,0:T(8,128)(2,1)S(1)}, bf16[256,128]{1,0:T(8,128)(2,1)S(1)}, u32[]{:S(2)}, u32[]{:S(2)}) collective-permute-start(bf16[256,128]{1,0:T(8,128)(2,1)S(1)} %step.28.refs_1_.refs_7_.refs_3_), channel_id=1, source_target_pairs={{1,2},{3,4},{5,6},{7,8},{9,10},{11,12},{13,14},{15,16},{17,18},{19... | collective-permute-start | bytes 196616 | tf_op jit(solution)/shard_map/ppermute | solution.py:222
  171.3 2.1 %collective-permute-start.27 = (bf16[256,128]{1,0:T(8,128)(2,1)S(1)}, bf16[256,128]{1,0:T(8,128)(2,1)S(1)}, u32[]{:S(2)}, u32[]{:S(2)}) collective-permute-start(bf16[256,128]{1,0:T(8,128)(2,1)S(1)} %step.28.refs_1_.refs_7_.refs_3_), channel_id=1, source_target_pairs={{0,1},{1,0},{2,3},{3,2},{4,5},{5,4},{6,7},{7,6},{8,9},{9,8},{10,11... | collective-permute-start | bytes 196616 | tf_op jit(solution)/shard_map/ppermute | solution.py:223
  173.5 2.5 %collective-permute-done.26.refs_0_.refs_6_.refs_2_ = bf16[256,128]{1,0:T(8,128)(2,1)S(1)} collective-permute-done((bf16[256,128]{1,0:T(8,128)(2,1)S(1)}, bf16[256,128]{1,0:T(8,128)(2,1)S(1)}, u32[]{:S(2)}, u32[]{:S(2)}) %collective-permute-start.26) | collective-permute-done | bytes 65568 | tf_op jit(solution)/shard_map/ppermute | solution.py:222
  177.9 3.0 %collective-permute-start.28 = (bf16[256,128]{1,0:T(8,128)(2,1)S(1)}, bf16[256,128]{1,0:T(8,128)(2,1)S(1)}, u32[]{:S(2)}, u32[]{:S(2)}) collective-permute-start(bf16[256,128]{1,0:T(8,128)(2,1)S(1)} %step.29.refs_1_.refs_7_.refs_3_), channel_id=1, source_target_pairs={{1,2},{3,4},{5,6},{7,8},{9,10},{11,12},{13,14},{15,16},{17,18},{19... | collective-permute-start | bytes 196616 | tf_op jit(solution)/shard_map/ppermute | solution.py:222
  180.9 1.9 collective-permute-start.29
  182.9 2.7 %collective-permute-done.28.refs_0_.refs_6_.refs_2_ = bf16[256,128]{1,0:T(8,128)(2,1)S(1)} collective-permute-done((bf16[256,128]{1,0:T(8,128)(2,1)S(1)}, bf16[256,128]{1,0:T(8,128)(2,1)S(1)}, u32[]{:S(2)}, u32[]{:S(2)}) %collective-permute-start.28) | collective-permute-done | bytes 65568 | tf_op jit(solution)/shard_map/ppermute | solution.py:222
  187.5 3.0 %collective-permute-start.30 = (bf16[256,128]{1,0:T(8,128)(2,1)S(1)}, bf16[256,128]{1,0:T(8,128)(2,1)S(1)}, u32[]{:S(2)}, u32[]{:S(2)}) collective-permute-start(bf16[256,128]{1,0:T(8,128)(2,1)S(1)} %step.30.refs_1_.refs_7_), channel_id=1, source_target_pairs={{1,2},{3,4},{5,6},{7,8},{9,10},{11,12},{13,14},{15,16},{17,18},{19... | collective-permute-start | bytes 196616 | tf_op jit(solution)/shard_map/ppermute | solution.py:222
  190.6 1.9 collective-permute-start.31
  193.2 2.0 %collective-permute-done.30.refs_0_.refs_6_ = bf16[256,128]{1,0:T(8,128)(2,1)S(1)} collective-permute-done((bf16[256,128]{1,0:T(8,128)(2,1)S(1)}, bf16[256,128]{1,0:T(8,128)(2,1)S(1)}, u32[]{:S(2)}, u32[]{:S(2)}) %collective-permute-start.30) | collective-permute-done | bytes 65568 | tf_op jit(solution)/shard_map/ppermute | solution.py:222
  (136 shorter events, 38.3 us)
Async XLA Ops:
  0.6 0.7 copy-start.10
  0.6 0.7 copy-start.11
  1.3 0.7 copy-start.8
  2.1 0.7 copy-start.9
  2.8 0.8 copy-start.7
  4.7 7.2 %copy-start.3 = (bf16[64,576]{1,0:T(8,128)(2,1)S(1)}, bf16[64,576]{1,0:T(8,128)(2,1)}, u32[]{:S(2)}) copy-start(bf16[64,576]{1,0:T(8,128)(2,1)} %param.17) | copy-start | bytes 221188
  4.7 27.5 %all-to-all-start = ((bf16[8,320,128]{2,1,0:T(8,128)(2,1)}), bf16[8,320,128]{2,1,0:T(8,128)(2,1)S(1)}, u32[]{:S(2)}, u32[]{:S(2)}) async-start(bf16[8,320,128]{2,1,0:T(8,128)(2,1)} %broadcast_in_dim.12), calls=%async_computation | async-start | bytes 1310720 | tf_op jit(solution)/shard_map/all_to_all | solution.py:270
  11.9 0.9 copy-start.4
  32.3 13.5 %collective-permute-start.1 = (bf16[8,160,128]{2,1,0:T(8,128)(2,1)S(1)}, bf16[8,160,128]{2,1,0:T(8,128)(2,1)S(1)}, u32[]{:S(2)}, u32[]{:S(2)}) collective-permute-start(bf16[8,160,128]{2,1,0:T(8,128)(2,1)S(1)} %pad_maximum_fusion.1), channel_id=1, source_target_pairs={{0,1},{1,0},{2,3},{3,2},{4,5},{5,4},{6,7},{7,6},{8,9},{9,8},{10,11... | collective-permute-start | bytes 983048 | tf_op jit(solution)/shard_map/ppermute | solution.py:223
  34.3 16.1 %collective-permute-start = (bf16[8,160,128]{2,1,0:T(8,128)(2,1)S(1)}, bf16[8,160,128]{2,1,0:T(8,128)(2,1)S(1)}, u32[]{:S(2)}, u32[]{:S(2)}) collective-permute-start(bf16[8,160,128]{2,1,0:T(8,128)(2,1)S(1)} %pad_maximum_fusion), channel_id=1, source_target_pairs={{1,2},{3,4},{5,6},{7,8},{9,10},{11,12},{13,14},{15,16},{17,18},{19... | collective-permute-start | bytes 983048 | tf_op jit(solution)/shard_map/ppermute | solution.py:222
  50.8 0.8 copy-start.1
  52.3 8.0 %collective-permute-start.2 = (bf16[256,128]{1,0:T(8,128)(2,1)S(1)}, bf16[256,128]{1,0:T(8,128)(2,1)S(1)}, u32[]{:S(2)}, u32[]{:S(2)}) collective-permute-start(bf16[256,128]{1,0:T(8,128)(2,1)S(1)} %step.16.refs_1_.refs_4_.refs_3_), channel_id=1, source_target_pairs={{1,2},{3,4},{5,6},{7,8},{9,10},{11,12},{13,14},{15,16},{17,18},{19... | collective-permute-start | bytes 196616 | tf_op jit(solution)/shard_map/ppermute | solution.py:222
  58.1 3.1 %collective-permute-start.3 = (bf16[256,128]{1,0:T(8,128)(2,1)S(1)}, bf16[256,128]{1,0:T(8,128)(2,1)S(1)}, u32[]{:S(2)}, u32[]{:S(2)}) collective-permute-start(bf16[256,128]{1,0:T(8,128)(2,1)S(1)} %step.16.refs_1_.refs_4_.refs_3_), channel_id=1, source_target_pairs={{0,1},{1,0},{2,3},{3,2},{4,5},{5,4},{6,7},{7,6},{8,9},{9,8},{10,11... | collective-permute-start | bytes 196616 | tf_op jit(solution)/shard_map/ppermute | solution.py:223
  62.2 7.7 %collective-permute-start.4 = (bf16[256,128]{1,0:T(8,128)(2,1)S(1)}, bf16[256,128]{1,0:T(8,128)(2,1)S(1)}, u32[]{:S(2)}, u32[]{:S(2)}) collective-permute-start(bf16[256,128]{1,0:T(8,128)(2,1)S(1)} %step.17.refs_1_.refs_4_.refs_3_), channel_id=1, source_target_pairs={{1,2},{3,4},{5,6},{7,8},{9,10},{11,12},{13,14},{15,16},{17,18},{19... | collective-permute-start | bytes 196616 | tf_op jit(solution)/shard_map/ppermute | solution.py:222
  67.1 3.7 %collective-permute-start.5 = (bf16[256,128]{1,0:T(8,128)(2,1)S(1)}, bf16[256,128]{1,0:T(8,128)(2,1)S(1)}, u32[]{:S(2)}, u32[]{:S(2)}) collective-permute-start(bf16[256,128]{1,0:T(8,128)(2,1)S(1)} %step.17.refs_1_.refs_4_.refs_3_), channel_id=1, source_target_pairs={{0,1},{1,0},{2,3},{3,2},{4,5},{5,4},{6,7},{7,6},{8,9},{9,8},{10,11... | collective-permute-start | bytes 196616 | tf_op jit(solution)/shard_map/ppermute | solution.py:223
  71.8 7.7 %collective-permute-start.6 = (bf16[256,128]{1,0:T(8,128)(2,1)S(1)}, bf16[256,128]{1,0:T(8,128)(2,1)S(1)}, u32[]{:S(2)}, u32[]{:S(2)}) collective-permute-start(bf16[256,128]{1,0:T(8,128)(2,1)S(1)} %step.18.refs_1_.refs_4_.refs_3_), channel_id=1, source_target_pairs={{1,2},{3,4},{5,6},{7,8},{9,10},{11,12},{13,14},{15,16},{17,18},{19... | collective-permute-start | bytes 196616 | tf_op jit(solution)/shard_map/ppermute | solution.py:222
  76.8 3.7 %collective-permute-start.7 = (bf16[256,128]{1,0:T(8,128)(2,1)S(1)}, bf16[256,128]{1,0:T(8,128)(2,1)S(1)}, u32[]{:S(2)}, u32[]{:S(2)}) collective-permute-start(bf16[256,128]{1,0:T(8,128)(2,1)S(1)} %step.18.refs_1_.refs_4_.refs_3_), channel_id=1, source_target_pairs={{0,1},{1,0},{2,3},{3,2},{4,5},{5,4},{6,7},{7,6},{8,9},{9,8},{10,11... | collective-permute-start | bytes 196616 | tf_op jit(solution)/shard_map/ppermute | solution.py:223
  81.4 7.7 %collective-permute-start.8 = (bf16[256,128]{1,0:T(8,128)(2,1)S(1)}, bf16[256,128]{1,0:T(8,128)(2,1)S(1)}, u32[]{:S(2)}, u32[]{:S(2)}) collective-permute-start(bf16[256,128]{1,0:T(8,128)(2,1)S(1)} %step.19.refs_1_.refs_4_.refs_3_), channel_id=1, source_target_pairs={{1,2},{3,4},{5,6},{7,8},{9,10},{11,12},{13,14},{15,16},{17,18},{19... | collective-permute-start | bytes 196616 | tf_op jit(solution)/shard_map/ppermute | solution.py:222
  86.4 3.7 %collective-permute-start.9 = (bf16[256,128]{1,0:T(8,128)(2,1)S(1)}, bf16[256,128]{1,0:T(8,128)(2,1)S(1)}, u32[]{:S(2)}, u32[]{:S(2)}) collective-permute-start(bf16[256,128]{1,0:T(8,128)(2,1)S(1)} %step.19.refs_1_.refs_4_.refs_3_), channel_id=1, source_target_pairs={{0,1},{1,0},{2,3},{3,2},{4,5},{5,4},{6,7},{7,6},{8,9},{9,8},{10,11... | collective-permute-start | bytes 196616 | tf_op jit(solution)/shard_map/ppermute | solution.py:223
  91.0 7.7 %collective-permute-start.10 = (bf16[256,128]{1,0:T(8,128)(2,1)S(1)}, bf16[256,128]{1,0:T(8,128)(2,1)S(1)}, u32[]{:S(2)}, u32[]{:S(2)}) collective-permute-start(bf16[256,128]{1,0:T(8,128)(2,1)S(1)} %step.20.refs_1_.refs_4_.refs_3_), channel_id=1, source_target_pairs={{1,2},{3,4},{5,6},{7,8},{9,10},{11,12},{13,14},{15,16},{17,18},{19... | collective-permute-start | bytes 196616 | tf_op jit(solution)/shard_map/ppermute | solution.py:222
  96.0 3.7 %collective-permute-start.11 = (bf16[256,128]{1,0:T(8,128)(2,1)S(1)}, bf16[256,128]{1,0:T(8,128)(2,1)S(1)}, u32[]{:S(2)}, u32[]{:S(2)}) collective-permute-start(bf16[256,128]{1,0:T(8,128)(2,1)S(1)} %step.20.refs_1_.refs_4_.refs_3_), channel_id=1, source_target_pairs={{0,1},{1,0},{2,3},{3,2},{4,5},{5,4},{6,7},{7,6},{8,9},{9,8},{10,11... | collective-permute-start | bytes 196616 | tf_op jit(solution)/shard_map/ppermute | solution.py:223
  100.6 7.7 %collective-permute-start.12 = (bf16[256,128]{1,0:T(8,128)(2,1)S(1)}, bf16[256,128]{1,0:T(8,128)(2,1)S(1)}, u32[]{:S(2)}, u32[]{:S(2)}) collective-permute-start(bf16[256,128]{1,0:T(8,128)(2,1)S(1)} %step.21.refs_1_.refs_4_.refs_3_), channel_id=1, source_target_pairs={{1,2},{3,4},{5,6},{7,8},{9,10},{11,12},{13,14},{15,16},{17,18},{19... | collective-permute-start | bytes 196616 | tf_op jit(solution)/shard_map/ppermute | solution.py:222
  105.6 3.7 %collective-permute-start.13 = (bf16[256,128]{1,0:T(8,128)(2,1)S(1)}, bf16[256,128]{1,0:T(8,128)(2,1)S(1)}, u32[]{:S(2)}, u32[]{:S(2)}) collective-permute-start(bf16[256,128]{1,0:T(8,128)(2,1)S(1)} %step.21.refs_1_.refs_4_.refs_3_), channel_id=1, source_target_pairs={{0,1},{1,0},{2,3},{3,2},{4,5},{5,4},{6,7},{7,6},{8,9},{9,8},{10,11... | collective-permute-start | bytes 196616 | tf_op jit(solution)/shard_map/ppermute | solution.py:223
  109.3 8.0 %copy-start.5 = (bf16[64,576]{1,0:T(8,128)(2,1)S(1)}, bf16[64,576]{1,0:T(8,128)(2,1)}, u32[]{:S(2)}) copy-start(bf16[64,576]{1,0:T(8,128)(2,1)} %param.20) | copy-start | bytes 221188
  110.3 7.2 %copy-start.6 = (bf16[64,576]{1,0:T(8,128)(2,1)S(1)}, bf16[64,576]{1,0:T(8,128)(2,1)}, u32[]{:S(2)}) copy-start(bf16[64,576]{1,0:T(8,128)(2,1)} %param.21) | copy-start | bytes 221188
  110.3 7.8 %collective-permute-start.14 = (bf16[256,128]{1,0:T(8,128)(2,1)S(1)}, bf16[256,128]{1,0:T(8,128)(2,1)S(1)}, u32[]{:S(2)}, u32[]{:S(2)}) collective-permute-start(bf16[256,128]{1,0:T(8,128)(2,1)S(1)} %step.22.refs_1_.refs_4_), channel_id=1, source_target_pairs={{1,2},{3,4},{5,6},{7,8},{9,10},{11,12},{13,14},{15,16},{17,18},{19... | collective-permute-start | bytes 196616 | tf_op jit(solution)/shard_map/ppermute | solution.py:222
  115.4 3.7 %collective-permute-start.15 = (bf16[256,128]{1,0:T(8,128)(2,1)S(1)}, bf16[256,128]{1,0:T(8,128)(2,1)S(1)}, u32[]{:S(2)}, u32[]{:S(2)}) collective-permute-start(bf16[256,128]{1,0:T(8,128)(2,1)S(1)} %step.22.refs_1_.refs_4_), channel_id=1, source_target_pairs={{0,1},{1,0},{2,3},{3,2},{4,5},{5,4},{6,7},{7,6},{8,9},{9,8},{10,11... | collective-permute-start | bytes 196616 | tf_op jit(solution)/shard_map/ppermute | solution.py:223
  120.0 9.0 %collective-permute-start.16 = (bf16[256,128]{1,0:T(8,128)(2,1)S(1)}, bf16[256,128]{1,0:T(8,128)(2,1)S(1)}, u32[]{:S(2)}, u32[]{:S(2)}) collective-permute-start(bf16[256,128]{1,0:T(8,128)(2,1)S(1)} %step.23.refs_4_), channel_id=1, source_target_pairs={{1,2},{3,4},{5,6},{7,8},{9,10},{11,12},{13,14},{15,16},{17,18},{19... | collective-permute-start | bytes 196616 | tf_op jit(solution)/shard_map/ppermute | solution.py:222
  125.0 4.1 %collective-permute-start.17 = (bf16[256,128]{1,0:T(8,128)(2,1)S(1)}, bf16[256,128]{1,0:T(8,128)(2,1)S(1)}, u32[]{:S(2)}, u32[]{:S(2)}) collective-permute-start(bf16[256,128]{1,0:T(8,128)(2,1)S(1)} %step.23.refs_4_), channel_id=1, source_target_pairs={{0,1},{1,0},{2,3},{3,2},{4,5},{5,4},{6,7},{7,6},{8,9},{9,8},{10,11... | collective-permute-start | bytes 196616 | tf_op jit(solution)/shard_map/ppermute | solution.py:223
  127.8 0.9 copy-start.2
  128.9 0.8 copy-start
  130.4 7.7 %collective-permute-start.18 = (bf16[256,128]{1,0:T(8,128)(2,1)S(1)}, bf16[256,128]{1,0:T(8,128)(2,1)S(1)}, u32[]{:S(2)}, u32[]{:S(2)}) collective-permute-start(bf16[256,128]{1,0:T(8,128)(2,1)S(1)} %step.24.refs_1_.refs_7_.refs_3_), channel_id=1, source_target_pairs={{1,2},{3,4},{5,6},{7,8},{9,10},{11,12},{13,14},{15,16},{17,18},{19... | collective-permute-start | bytes 196616 | tf_op jit(solution)/shard_map/ppermute | solution.py:222
  133.4 5.0 %collective-permute-start.19 = (bf16[256,128]{1,0:T(8,128)(2,1)S(1)}, bf16[256,128]{1,0:T(8,128)(2,1)S(1)}, u32[]{:S(2)}, u32[]{:S(2)}) collective-permute-start(bf16[256,128]{1,0:T(8,128)(2,1)S(1)} %step.24.refs_1_.refs_7_.refs_3_), channel_id=1, source_target_pairs={{0,1},{1,0},{2,3},{3,2},{4,5},{5,4},{6,7},{7,6},{8,9},{9,8},{10,11... | collective-permute-start | bytes 196616 | tf_op jit(solution)/shard_map/ppermute | solution.py:223
  139.5 7.7 %collective-permute-start.20 = (bf16[256,128]{1,0:T(8,128)(2,1)S(1)}, bf16[256,128]{1,0:T(8,128)(2,1)S(1)}, u32[]{:S(2)}, u32[]{:S(2)}) collective-permute-start(bf16[256,128]{1,0:T(8,128)(2,1)S(1)} %step.25.refs_1_.refs_7_.refs_3_), channel_id=1, source_target_pairs={{1,2},{3,4},{5,6},{7,8},{9,10},{11,12},{13,14},{15,16},{17,18},{19... | collective-permute-start | bytes 196616 | tf_op jit(solution)/shard_map/ppermute | solution.py:222
  142.5 5.6 %collective-permute-start.21 = (bf16[256,128]{1,0:T(8,128)(2,1)S(1)}, bf16[256,128]{1,0:T(8,128)(2,1)S(1)}, u32[]{:S(2)}, u32[]{:S(2)}) collective-permute-start(bf16[256,128]{1,0:T(8,128)(2,1)S(1)} %step.25.refs_1_.refs_7_.refs_3_), channel_id=1, source_target_pairs={{0,1},{1,0},{2,3},{3,2},{4,5},{5,4},{6,7},{7,6},{8,9},{9,8},{10,11... | collective-permute-start | bytes 196616 | tf_op jit(solution)/shard_map/ppermute | solution.py:223
  149.1 7.7 %collective-permute-start.22 = (bf16[256,128]{1,0:T(8,128)(2,1)S(1)}, bf16[256,128]{1,0:T(8,128)(2,1)S(1)}, u32[]{:S(2)}, u32[]{:S(2)}) collective-permute-start(bf16[256,128]{1,0:T(8,128)(2,1)S(1)} %step.26.refs_1_.refs_7_.refs_3_), channel_id=1, source_target_pairs={{1,2},{3,4},{5,6},{7,8},{9,10},{11,12},{13,14},{15,16},{17,18},{19... | collective-permute-start | bytes 196616 | tf_op jit(solution)/shard_map/ppermute | solution.py:222
  152.1 5.6 %collective-permute-start.23 = (bf16[256,128]{1,0:T(8,128)(2,1)S(1)}, bf16[256,128]{1,0:T(8,128)(2,1)S(1)}, u32[]{:S(2)}, u32[]{:S(2)}) collective-permute-start(bf16[256,128]{1,0:T(8,128)(2,1)S(1)} %step.26.refs_1_.refs_7_.refs_3_), channel_id=1, source_target_pairs={{0,1},{1,0},{2,3},{3,2},{4,5},{5,4},{6,7},{7,6},{8,9},{9,8},{10,11... | collective-permute-start | bytes 196616 | tf_op jit(solution)/shard_map/ppermute | solution.py:223
  158.7 7.7 %collective-permute-start.24 = (bf16[256,128]{1,0:T(8,128)(2,1)S(1)}, bf16[256,128]{1,0:T(8,128)(2,1)S(1)}, u32[]{:S(2)}, u32[]{:S(2)}) collective-permute-start(bf16[256,128]{1,0:T(8,128)(2,1)S(1)} %step.27.refs_1_.refs_7_.refs_3_), channel_id=1, source_target_pairs={{1,2},{3,4},{5,6},{7,8},{9,10},{11,12},{13,14},{15,16},{17,18},{19... | collective-permute-start | bytes 196616 | tf_op jit(solution)/shard_map/ppermute | solution.py:222
  161.7 5.6 %collective-permute-start.25 = (bf16[256,128]{1,0:T(8,128)(2,1)S(1)}, bf16[256,128]{1,0:T(8,128)(2,1)S(1)}, u32[]{:S(2)}, u32[]{:S(2)}) collective-permute-start(bf16[256,128]{1,0:T(8,128)(2,1)S(1)} %step.27.refs_1_.refs_7_.refs_3_), channel_id=1, source_target_pairs={{0,1},{1,0},{2,3},{3,2},{4,5},{5,4},{6,7},{7,6},{8,9},{9,8},{10,11... | collective-permute-start | bytes 196616 | tf_op jit(solution)/shard_map/ppermute | solution.py:223
  168.3 7.7 %collective-permute-start.26 = (bf16[256,128]{1,0:T(8,128)(2,1)S(1)}, bf16[256,128]{1,0:T(8,128)(2,1)S(1)}, u32[]{:S(2)}, u32[]{:S(2)}) collective-permute-start(bf16[256,128]{1,0:T(8,128)(2,1)S(1)} %step.28.refs_1_.refs_7_.refs_3_), channel_id=1, source_target_pairs={{1,2},{3,4},{5,6},{7,8},{9,10},{11,12},{13,14},{15,16},{17,18},{19... | collective-permute-start | bytes 196616 | tf_op jit(solution)/shard_map/ppermute | solution.py:222
  171.3 5.6 %collective-permute-start.27 = (bf16[256,128]{1,0:T(8,128)(2,1)S(1)}, bf16[256,128]{1,0:T(8,128)(2,1)S(1)}, u32[]{:S(2)}, u32[]{:S(2)}) collective-permute-start(bf16[256,128]{1,0:T(8,128)(2,1)S(1)} %step.28.refs_1_.refs_7_.refs_3_), channel_id=1, source_target_pairs={{0,1},{1,0},{2,3},{3,2},{4,5},{5,4},{6,7},{7,6},{8,9},{9,8},{10,11... | collective-permute-start | bytes 196616 | tf_op jit(solution)/shard_map/ppermute | solution.py:223
  177.9 7.7 %collective-permute-start.28 = (bf16[256,128]{1,0:T(8,128)(2,1)S(1)}, bf16[256,128]{1,0:T(8,128)(2,1)S(1)}, u32[]{:S(2)}, u32[]{:S(2)}) collective-permute-start(bf16[256,128]{1,0:T(8,128)(2,1)S(1)} %step.29.refs_1_.refs_7_.refs_3_), channel_id=1, source_target_pairs={{1,2},{3,4},{5,6},{7,8},{9,10},{11,12},{13,14},{15,16},{17,18},{19... | collective-permute-start | bytes 196616 | tf_op jit(solution)/shard_map/ppermute | solution.py:222
  180.9 5.6 %collective-permute-start.29 = (bf16[256,128]{1,0:T(8,128)(2,1)S(1)}, bf16[256,128]{1,0:T(8,128)(2,1)S(1)}, u32[]{:S(2)}, u32[]{:S(2)}) collective-permute-start(bf16[256,128]{1,0:T(8,128)(2,1)S(1)} %step.29.refs_1_.refs_7_.refs_3_), channel_id=1, source_target_pairs={{0,1},{1,0},{2,3},{3,2},{4,5},{5,4},{6,7},{7,6},{8,9},{9,8},{10,11... | collective-permute-start | bytes 196616 | tf_op jit(solution)/shard_map/ppermute | solution.py:223
  187.5 7.7 %collective-permute-start.30 = (bf16[256,128]{1,0:T(8,128)(2,1)S(1)}, bf16[256,128]{1,0:T(8,128)(2,1)S(1)}, u32[]{:S(2)}, u32[]{:S(2)}) collective-permute-start(bf16[256,128]{1,0:T(8,128)(2,1)S(1)} %step.30.refs_1_.refs_7_), channel_id=1, source_target_pairs={{1,2},{3,4},{5,6},{7,8},{9,10},{11,12},{13,14},{15,16},{17,18},{19... | collective-permute-start | bytes 196616 | tf_op jit(solution)/shard_map/ppermute | solution.py:222
  190.6 5.6 %collective-permute-start.31 = (bf16[256,128]{1,0:T(8,128)(2,1)S(1)}, bf16[256,128]{1,0:T(8,128)(2,1)S(1)}, u32[]{:S(2)}, u32[]{:S(2)}) collective-permute-start(bf16[256,128]{1,0:T(8,128)(2,1)S(1)} %step.30.refs_1_.refs_7_), channel_id=1, source_target_pairs={{0,1},{1,0},{2,3},{3,2},{4,5},{5,4},{6,7},{7,6},{8,9},{9,8},{10,11... | collective-permute-start | bytes 196616 | tf_op jit(solution)/shard_map/ppermute | solution.py:223

commit v5 on v3

--- a/solution.py
+++ b/solution.py
@@ -14,6 +14,7 @@
 H = 256
 FRAMES = 8
 EXT = ROWS + 2 * R
+EARLY = EXT // 2
 
 
 def leaky(values):
@@ -60,10 +61,9 @@
             t = g[0] * weights[dx]
             for dy in range(1, 5):
                 t = t + g[dy] * weights[dy * 5 + dx]
-            t = t.astype(jnp.float32)
             t = pltpu.roll(t, (R - dx) % W, 1) if dx != R else t
             total = t if total is None else total + t
-        store(ch, total.astype(jnp.bfloat16))
+        store(ch, total)
 
 
 def prepare_kernel(priors, first, sense, *refs):
@@ -90,12 +90,22 @@
         sample_row(older, r, weight, store)
 
 
+def middle_kernel(own, beside, taps, stack):
+    for r in range(EARLY, EXT):
+
+        def store(ch, value):
+            stack[pl.ds(ch, 16), pl.ds((r - EARLY) * W, W)] = value
+
+        sample_row((None, own, beside), r, lambda n: taps[r, n], store)
+
+
 def step_kernel(priors, parts, first, sense, *refs):
     refs = list(refs)
     grid = (first[0], sense[0])
     sides = [[refs.pop(0) for _ in range(3)] for _ in range(parts)]
-    newest = [refs.pop(0) for _ in range(3)] if priors else None
+    newest = [refs.pop(0) for _ in range(2)] + [None] if priors else None
     taps = refs.pop(0) if priors else None
+    middle = refs.pop(0) if priors else None
     older = refs.pop(0) if priors == 2 else None
     mixer, inner, outer, out, stack, joined, hidden = refs
 
@@ -108,8 +118,8 @@
         return ref[pl.ds(at, C), :]
 
     depth = (parts + priors) * C
-    for r in (4, 6, 2, 0):
-        for n in range(2 if priors else 0):
+    for r in (0, 2, 4, 6):
+        for n in range(2 if priors and r < EARLY else 0):
 
             def store(ch, value):
                 stack[pl.ds(ch, 16), pl.ds((r + n) * W, W)] = value
@@ -119,7 +129,8 @@
             jnp.concatenate([side_row(trio, r), side_row(trio, r + 1)], axis=1) for trio in sides
         ]
         if priors:
-            pieces.append(stack[:, pl.ds(r * W, 2 * W)])
+            near = stack[:, pl.ds(r * W, 2 * W)] if r < EARLY else middle[:, pl.ds((r - EARLY) * W, 2 * W)]
+            pieces.append(near)
         if priors == 2:
             pieces.append(older[:, pl.ds(r * W, 2 * W)])
         data = jnp.concatenate(pieces, axis=0)
@@ -145,14 +156,14 @@
             outs.append(left + part[C : 2 * C] + right)
         return outs
 
-    for r in (4, 2, 0):
+    for r in (0, 2, 4):
         for n, value in enumerate(conv_pair(joined, inner, r)):
             value = leaky(value)
             if r + n in (0, ROWS + 1):
                 value = value * keep(r + n - 1)
             hidden[pl.ds((r + n) * C, C), :] = value.astype(jnp.bfloat16)
 
-    for r in (2, 0):
+    for r in (0, 2):
         for n, value in enumerate(conv_pair(hidden, outer, r)):
             base = joined[pl.ds((r + n + R) * C, C), :].astype(jnp.float32)
             out[pl.ds((r + n) * C, C), :] = (base + value).astype(jnp.bfloat16)
@@ -175,23 +186,35 @@
         out_specs=[VMEM] * len(outs),
         scratch_shapes=[pltpu.VMEM((25, EXT, W), jnp.float32)] if older else [],
         compiler_params=pltpu.CompilerParams(vmem_limit_bytes=16 * 2**20),
-        cost_estimate=pl.CostEstimate(flops=2 * 10**7, bytes_accessed=2**20, transcendentals=0),
+        cost_estimate=pl.CostEstimate(flops=10**10, bytes_accessed=2**20, transcendentals=0),
         name="prepare",
     )(*operands)
+
+
+def run_middle(newest, taps):
+    return pl.pallas_call(
+        middle_kernel,
+        out_shape=jax.ShapeDtypeStruct((C, (EXT - EARLY) * W), BF16),
+        in_specs=[VMEM] * 3,
+        out_specs=VMEM,
+        compiler_params=pltpu.CompilerParams(vmem_limit_bytes=16 * 2**20),
+        cost_estimate=pl.CostEstimate(flops=10**6, bytes_accessed=2**10, transcendentals=0),
+        name="middle",
+    )(newest[1], newest[2], taps)
 
 
 def run_step(grid, sides, newest, prepared, weights):
     operands = list(grid)
     for trio in sides:
         operands += list(trio)
-    operands += (list(newest) if newest else []) + list(prepared) + list(weights)
+    operands += (list(newest[:2]) if newest else []) + list(prepared) + list(weights)
     return pl.pallas_call(
-        functools.partial(step_kernel, len(prepared), len(sides)),
+        functools.partial(step_kernel, max(0, len(prepared) - 1), len(sides)),
         out_shape=jax.ShapeDtypeStruct((ROWS * C, W), BF16),
         in_specs=[SMEM, SMEM] + [VMEM] * (len(operands) - 2),
         out_specs=VMEM,
         scratch_shapes=[
-            pltpu.VMEM((C, EXT * W), BF16),
+            pltpu.VMEM((C, EARLY * W), BF16),
             pltpu.VMEM((EXT * C, W), BF16),
             pltpu.VMEM(((ROWS + 2) * C, W), BF16),
         ],
@@ -263,22 +286,27 @@
 
     own = oriented(frames[0].transpose(1, 0, 2), 0).reshape(ROWS * C, W)
 
-    def pack(shift, fraction):
-        sy, sx, qy, qx = shift[0, :, 0], shift[0, :, 1], fraction[0, :, 0], fraction[0, :, 1]
-        sy = jnp.where(odd, -1 - sy, sy)
-        qy = jnp.where(odd, 1.0 - qy, qy)
-        values = jnp.stack([v.astype(BF16) for v in (sy, sx, qy, qx)], axis=1)
-        return oriented(values.transpose(2, 0, 1, 3), 0)
-
-    own_params = jnp.stack(
-        [pack(back_shift, back_fraction), pack(ahead_shift, ahead_fraction)], axis=1
-    ).reshape(ROWS * 16, W)
+    raw = jnp.concatenate(
+        [
+            jnp.concatenate([back_shift.astype(jnp.float32), back_fraction], axis=2),
+            jnp.concatenate([ahead_shift.astype(jnp.float32), ahead_fraction], axis=2),
+        ]
+    )
+    first = jnp.where(odd, -1.0 - raw[:, :, 0:1], raw[:, :, 0:1])
+    third = jnp.where(odd, 1.0 - raw[:, :, 2:3], raw[:, :, 2:3])
+    raw = jnp.concatenate([first, raw[:, :, 1:2], third, raw[:, :, 3:4]], axis=2).astype(BF16)
+    own_params = oriented(raw.transpose(3, 0, 1, 2, 4), 0).reshape(ROWS * 16, W)
     mine = jnp.concatenate([own, own_params], axis=0)
     other = lax.ppermute(mine, "tile", [(q, mirror(q)) for q in range(lax.axis_size("tile"))])
     for_even = jnp.where(upper, other, mine)
     for_odd = jnp.where(upper, mine, other)
     clip = lax.all_to_all(
-        jnp.stack([for_even, for_odd] * (FRAMES // 2)), "tm", split_axis=0, concat_axis=0
+        jnp.broadcast_to(jnp.stack([for_even, for_odd])[None], (FRAMES // 2, 2) + mine.shape).reshape(
+            (FRAMES,) + mine.shape
+        ),
+        "tm",
+        split_axis=0,
+        concat_axis=0,
     )
 
     top = jnp.concatenate([clip[:, : 2 * C], clip[:, 4 * C : 4 * C + 32]], axis=1)
@@ -298,7 +326,10 @@
         history = []
         for n, t in enumerate(order):
             sides = [frame_trios[t]] + ([extra[t]] if extra else [])
-            prepared = run_prepare(grid, history[1] if n > 1 else None, params[way, t]) if n else []
+            prepared = []
+            if n:
+                taps, *older = run_prepare(grid, history[1] if n > 1 else None, params[way, t])
+                prepared = [taps, run_middle(history[0], taps)] + older
             new = run_step(grid, sides, history[0] if n else None, prepared, weights)
             if n + 1 < FRAMES or not extra:
                 far, near = swap(new, new)

time: 192 us -> 184 us (0.958)
  other arithmetic: 2.97 us -> 1.01 us
    all_to_all x1, waiting for transfers between devices: 17.3 us -> 13.9 us  [shards(): lax.all_to_all(jnp.broadcast_to(jnp.stack([for_even, for_odd])[None], (FR...]
    unnamed x33 -> x39, local copies, waits for them, and re-layouts: 9.26 us -> 7.79 us
    pallas_call x16 -> x30, Pallas kernels: 20.5 us -> 19.5 us  [the longest x16 15.9 us: run_step(): pl.pallas_call(functools.partial(step_kernel, max(0, len(prepared) - 1),...]
  transfers between devices with their start and end apart: 35 -> 35, of which waited for: 15 -> 18; matrix products, arithmetic and copies ran while one was open for 2% -> 2% of each run, Pallas kernels for 4% -> 6%
where the time goes in v5:
time: 184 us; the launch traced here: 183 us
  starting transfers between devices  110 us (60%)
  waiting for transfers between devices  30.4 us (17%)
  Pallas kernels  27.3 us (15%)
  local copies, waits for them, and re-layouts  12.2 us (7%)
    ppermute x16, starting transfers between devices, swap(): lax.ppermute(for_beside, axes, beside)  54.2 us
    ppermute x16, starting transfers between devices, swap(): lax.ppermute(for_across, axes, across)  36.3 us
    pallas_call x16, Pallas kernels, run_step(): pl.pallas_call(functools.partial(step_kernel, max(0, len(prepared) - 1),...  15.9 us
    all_to_all x1, waiting for transfers between devices, shards(): lax.all_to_all(jnp.broadcast_to(jnp.stack([for_even, for_odd])[None], (FR...  13.9 us
    ppermute x1, starting transfers between devices, shards(): lax.ppermute(mine, 'tile', [(q, mirror(q)) for q in range(lax.axis_size('...  10.9 us
    pallas_call x14, Pallas kernels, run_prepare(): pl.pallas_call(functools.partial(prepare_kernel, 2 if older else 1), out_...  7.8 us
    unnamed x39, local copies, waits for them, and re-layouts  7.79 us
    all_to_all x1, starting transfers between devices, shards(): lax.all_to_all(jnp.broadcast_to(jnp.stack([for_even, for_odd])[None], (FR...  7.55 us
  transfers between devices with their start and end apart: 35, of which 18 were waited for; matrix products, arithmetic and copies ran while one was open for 2% of the time, Pallas kernels for 6%

profile of v5, /device:TPU:8, one launch (start us, length us, event | category | flops | bytes accessed | tf_op | source)
XLA Modules:
  0.0 182.8 jit_solution(14711417596253349834)
XLA Ops:
  3.7 10.9 %collective-permute-start = (bf16[320,128]{1,0:T(8,128)(2,1)S(1)}, bf16[320,128]{1,0:T(8,128)(2,1)S(1)}, u32[]{:S(2)}, u32[]{:S(2)}) collective-permute-start(bf16[320,128]{1,0:T(8,128)(2,1)S(1)} %pad_maximum_fusion.4), channel_id=1, source_target_pairs={{0,14},{1,15},{2,12},{3,13},{4,10},{5,11},{6,8},{7,9},{8,6},{9,7},... | collective-permute-start | bytes 245768 | tf_op jit(solution)/shard_map/ppermute | solution.py:300
  14.7 4.1 %collective-permute-done = bf16[320,128]{1,0:T(8,128)(2,1)S(1)} collective-permute-done((bf16[320,128]{1,0:T(8,128)(2,1)S(1)}, bf16[320,128]{1,0:T(8,128)(2,1)S(1)}, u32[]{:S(2)}, u32[]{:S(2)}) %collective-permute-start) | collective-permute-done | bytes 81952 | tf_op jit(solution)/shard_map/ppermute | solution.py:300
  19.9 7.5 %all-to-all-start = ((bf16[8,320,128]{2,1,0:T(8,128)(2,1)}), bf16[8,320,128]{2,1,0:T(8,128)(2,1)S(1)}, u32[]{:S(2)}, u32[]{:S(2)}) async-start(bf16[8,320,128]{2,1,0:T(8,128)(2,1)} %bitcast.9), calls=%async_computation | async-start | bytes 1310720 | tf_op jit(solution)/shard_map/all_to_all | solution.py:303
  32.6 13.9 %all-to-all-done = bf16[8,320,128]{2,1,0:T(8,128)(2,1)S(1)} async-done(((bf16[8,320,128]{2,1,0:T(8,128)(2,1)}), bf16[8,320,128]{2,1,0:T(8,128)(2,1)S(1)}, u32[]{:S(2)}, u32[]{:S(2)}) %all-to-all-start) | async-done | bytes 655392 | tf_op jit(solution)/shard_map/all_to_all | solution.py:303
  46.5 1.9 %collective-permute-start.1 = (bf16[8,160,128]{2,1,0:T(8,128)(2,1)S(1)}, bf16[8,160,128]{2,1,0:T(8,128)(2,1)S(1)}, u32[]{:S(2)}, u32[]{:S(2)}) collective-permute-start(bf16[8,160,128]{2,1,0:T(8,128)(2,1)S(1)} %pad_maximum_fusion), channel_id=1, source_target_pairs={{1,2},{2,1},{3,4},{4,3},{5,6},{6,5},{7,70},{70,7},{71,68},{68,71},... | collective-permute-start | bytes 983048 | tf_op jit(solution)/shard_map/ppermute | solution.py:251
  48.5 4.4 %collective-permute-start.2 = (bf16[8,160,128]{2,1,0:T(8,128)(2,1)S(1)}, bf16[8,160,128]{2,1,0:T(8,128)(2,1)S(1)}, u32[]{:S(2)}, u32[]{:S(2)}) collective-permute-start(bf16[8,160,128]{2,1,0:T(8,128)(2,1)S(1)} %pad_maximum_fusion.1), channel_id=1, source_target_pairs={{0,1},{1,0},{2,3},{3,2},{4,5},{5,4},{6,7},{7,6},{70,71},{71,70},{6... | collective-permute-start | bytes 983048 | tf_op jit(solution)/shard_map/ppermute | solution.py:251
  53.1 1.8 %collective-permute-done.1 = bf16[8,160,128]{2,1,0:T(8,128)(2,1)S(1)} collective-permute-done((bf16[8,160,128]{2,1,0:T(8,128)(2,1)S(1)}, bf16[8,160,128]{2,1,0:T(8,128)(2,1)S(1)}, u32[]{:S(2)}, u32[]{:S(2)}) %collective-permute-start.1) | collective-permute-done | bytes 327712 | tf_op jit(solution)/shard_map/ppermute | solution.py:251
  56.5 1.9 %collective-permute-start.3 = (bf16[256,128]{1,0:T(8,128)(2,1)S(1)}, bf16[256,128]{1,0:T(8,128)(2,1)S(1)}, u32[]{:S(2)}, u32[]{:S(2)}) collective-permute-start(bf16[256,128]{1,0:T(8,128)(2,1)S(1)} %step.16.own.refs_4_.refs_1_), channel_id=1, source_target_pairs={{1,2},{2,1},{3,4},{4,3},{5,6},{6,5},{7,70},{70,7},{71,68},{68,71},... | collective-permute-start | bytes 196616 | tf_op jit(solution)/shard_map/ppermute | solution.py:251
  58.4 5.3 %collective-permute-start.4 = (bf16[256,128]{1,0:T(8,128)(2,1)S(1)}, bf16[256,128]{1,0:T(8,128)(2,1)S(1)}, u32[]{:S(2)}, u32[]{:S(2)}) collective-permute-start(bf16[256,128]{1,0:T(8,128)(2,1)S(1)} %step.16.own.refs_4_.refs_1_), channel_id=1, source_target_pairs={{0,1},{1,0},{2,3},{3,2},{4,5},{5,4},{6,7},{7,6},{70,71},{71,70},{6... | collective-permute-start | bytes 196616 | tf_op jit(solution)/shard_map/ppermute | solution.py:251
  66.5 1.9 %collective-permute-start.5 = (bf16[256,128]{1,0:T(8,128)(2,1)S(1)}, bf16[256,128]{1,0:T(8,128)(2,1)S(1)}, u32[]{:S(2)}, u32[]{:S(2)}) collective-permute-start(bf16[256,128]{1,0:T(8,128)(2,1)S(1)} %step.17.own.refs_4_.refs_1_), channel_id=1, source_target_pairs={{1,2},{2,1},{3,4},{4,3},{5,6},{6,5},{7,70},{70,7},{71,68},{68,71},... | collective-permute-start | bytes 196616 | tf_op jit(solution)/shard_map/ppermute | solution.py:251
  68.4 2.8 %collective-permute-start.6 = (bf16[256,128]{1,0:T(8,128)(2,1)S(1)}, bf16[256,128]{1,0:T(8,128)(2,1)S(1)}, u32[]{:S(2)}, u32[]{:S(2)}) collective-permute-start(bf16[256,128]{1,0:T(8,128)(2,1)S(1)} %step.17.own.refs_4_.refs_1_), channel_id=1, source_target_pairs={{0,1},{1,0},{2,3},{3,2},{4,5},{5,4},{6,7},{7,6},{70,71},{71,70},{6... | collective-permute-start | bytes 196616 | tf_op jit(solution)/shard_map/ppermute | solution.py:251
  72.4 1.0 step.18.own.refs_4_.refs_1_
  73.4 3.1 %collective-permute-start.7 = (bf16[256,128]{1,0:T(8,128)(2,1)S(1)}, bf16[256,128]{1,0:T(8,128)(2,1)S(1)}, u32[]{:S(2)}, u32[]{:S(2)}) collective-permute-start(bf16[256,128]{1,0:T(8,128)(2,1)S(1)} %step.18.own.refs_4_.refs_1_), channel_id=1, source_target_pairs={{1,2},{2,1},{3,4},{4,3},{5,6},{6,5},{7,70},{70,7},{71,68},{68,71},... | collective-permute-start | bytes 196616 | tf_op jit(solution)/shard_map/ppermute | solution.py:251
  76.5 2.8 %collective-permute-start.8 = (bf16[256,128]{1,0:T(8,128)(2,1)S(1)}, bf16[256,128]{1,0:T(8,128)(2,1)S(1)}, u32[]{:S(2)}, u32[]{:S(2)}) collective-permute-start(bf16[256,128]{1,0:T(8,128)(2,1)S(1)} %step.18.own.refs_4_.refs_1_), channel_id=1, source_target_pairs={{0,1},{1,0},{2,3},{3,2},{4,5},{5,4},{6,7},{7,6},{70,71},{71,70},{6... | collective-permute-start | bytes 196616 | tf_op jit(solution)/shard_map/ppermute | solution.py:251
  80.5 1.0 step.19.own.refs_4_.refs_1_
  81.5 1.9 %collective-permute-start.9 = (bf16[256,128]{1,0:T(8,128)(2,1)S(1)}, bf16[256,128]{1,0:T(8,128)(2,1)S(1)}, u32[]{:S(2)}, u32[]{:S(2)}) collective-permute-start(bf16[256,128]{1,0:T(8,128)(2,1)S(1)} %step.19.own.refs_4_.refs_1_), channel_id=1, source_target_pairs={{1,2},{2,1},{3,4},{4,3},{5,6},{6,5},{7,70},{70,7},{71,68},{68,71},... | collective-permute-start | bytes 196616 | tf_op jit(solution)/shard_map/ppermute | solution.py:251
  83.5 3.4 %collective-permute-start.10 = (bf16[256,128]{1,0:T(8,128)(2,1)S(1)}, bf16[256,128]{1,0:T(8,128)(2,1)S(1)}, u32[]{:S(2)}, u32[]{:S(2)}) collective-permute-start(bf16[256,128]{1,0:T(8,128)(2,1)S(1)} %step.19.own.refs_4_.refs_1_), channel_id=1, source_target_pairs={{0,1},{1,0},{2,3},{3,2},{4,5},{5,4},{6,7},{7,6},{70,71},{71,70},{6... | collective-permute-start | bytes 196616 | tf_op jit(solution)/shard_map/ppermute | solution.py:251
  88.0 1.0 step.20.own.refs_4_.refs_1_
  89.1 2.5 %collective-permute-start.11 = (bf16[256,128]{1,0:T(8,128)(2,1)S(1)}, bf16[256,128]{1,0:T(8,128)(2,1)S(1)}, u32[]{:S(2)}, u32[]{:S(2)}) collective-permute-start(bf16[256,128]{1,0:T(8,128)(2,1)S(1)} %step.20.own.refs_4_.refs_1_), channel_id=1, source_target_pairs={{1,2},{2,1},{3,4},{4,3},{5,6},{6,5},{7,70},{70,7},{71,68},{68,71},... | collective-permute-start | bytes 196616 | tf_op jit(solution)/shard_map/ppermute | solution.py:251
  91.6 3.3 %collective-permute-start.12 = (bf16[256,128]{1,0:T(8,128)(2,1)S(1)}, bf16[256,128]{1,0:T(8,128)(2,1)S(1)}, u32[]{:S(2)}, u32[]{:S(2)}) collective-permute-start(bf16[256,128]{1,0:T(8,128)(2,1)S(1)} %step.20.own.refs_4_.refs_1_), channel_id=1, source_target_pairs={{0,1},{1,0},{2,3},{3,2},{4,5},{5,4},{6,7},{7,6},{70,71},{71,70},{6... | collective-permute-start | bytes 196616 | tf_op jit(solution)/shard_map/ppermute | solution.py:251
  95.9 1.0 step.21.own.refs_4_.refs_1_
  96.9 2.2 %collective-permute-start.13 = (bf16[256,128]{1,0:T(8,128)(2,1)S(1)}, bf16[256,128]{1,0:T(8,128)(2,1)S(1)}, u32[]{:S(2)}, u32[]{:S(2)}) collective-permute-start(bf16[256,128]{1,0:T(8,128)(2,1)S(1)} %step.21.own.refs_4_.refs_1_), channel_id=1, source_target_pairs={{1,2},{2,1},{3,4},{4,3},{5,6},{6,5},{7,70},{70,7},{71,68},{68,71},... | collective-permute-start | bytes 196616 | tf_op jit(solution)/shard_map/ppermute | solution.py:251
  99.1 3.2 %collective-permute-start.14 = (bf16[256,128]{1,0:T(8,128)(2,1)S(1)}, bf16[256,128]{1,0:T(8,128)(2,1)S(1)}, u32[]{:S(2)}, u32[]{:S(2)}) collective-permute-start(bf16[256,128]{1,0:T(8,128)(2,1)S(1)} %step.21.own.refs_4_.refs_1_), channel_id=1, source_target_pairs={{0,1},{1,0},{2,3},{3,2},{4,5},{5,4},{6,7},{7,6},{70,71},{71,70},{6... | collective-permute-start | bytes 196616 | tf_op jit(solution)/shard_map/ppermute | solution.py:251
  103.4 1.0 step.22.own.refs_4_
  104.4 2.5 %collective-permute-start.15 = (bf16[256,128]{1,0:T(8,128)(2,1)S(1)}, bf16[256,128]{1,0:T(8,128)(2,1)S(1)}, u32[]{:S(2)}, u32[]{:S(2)}) collective-permute-start(bf16[256,128]{1,0:T(8,128)(2,1)S(1)} %step.22.own.refs_4_), channel_id=1, source_target_pairs={{1,2},{2,1},{3,4},{4,3},{5,6},{6,5},{7,70},{70,7},{71,68},{68,71},... | collective-permute-start | bytes 196616 | tf_op jit(solution)/shard_map/ppermute | solution.py:251
  107.0 3.2 %collective-permute-start.16 = (bf16[256,128]{1,0:T(8,128)(2,1)S(1)}, bf16[256,128]{1,0:T(8,128)(2,1)S(1)}, u32[]{:S(2)}, u32[]{:S(2)}) collective-permute-start(bf16[256,128]{1,0:T(8,128)(2,1)S(1)} %step.22.own.refs_4_), channel_id=1, source_target_pairs={{0,1},{1,0},{2,3},{3,2},{4,5},{5,4},{6,7},{7,6},{70,71},{71,70},{6... | collective-permute-start | bytes 196616 | tf_op jit(solution)/shard_map/ppermute | solution.py:251
  111.3 1.0 step.23.refs_4_
  112.3 2.2 %collective-permute-start.17 = (bf16[256,128]{1,0:T(8,128)(2,1)S(1)}, bf16[256,128]{1,0:T(8,128)(2,1)S(1)}, u32[]{:S(2)}, u32[]{:S(2)}) collective-permute-start(bf16[256,128]{1,0:T(8,128)(2,1)S(1)} %step.23.refs_4_), channel_id=1, source_target_pairs={{1,2},{2,1},{3,4},{4,3},{5,6},{6,5},{7,70},{70,7},{71,68},{68,71},... | collective-permute-start | bytes 196616 | tf_op jit(solution)/shard_map/ppermute | solution.py:251
  114.5 3.2 %collective-permute-start.18 = (bf16[256,128]{1,0:T(8,128)(2,1)S(1)}, bf16[256,128]{1,0:T(8,128)(2,1)S(1)}, u32[]{:S(2)}, u32[]{:S(2)}) collective-permute-start(bf16[256,128]{1,0:T(8,128)(2,1)S(1)} %step.23.refs_4_), channel_id=1, source_target_pairs={{0,1},{1,0},{2,3},{3,2},{4,5},{5,4},{6,7},{7,6},{70,71},{71,70},{6... | collective-permute-start | bytes 196616 | tf_op jit(solution)/shard_map/ppermute | solution.py:251
  119.3 2.5 %collective-permute-start.19 = (bf16[256,128]{1,0:T(8,128)(2,1)S(1)}, bf16[256,128]{1,0:T(8,128)(2,1)S(1)}, u32[]{:S(2)}, u32[]{:S(2)}) collective-permute-start(bf16[256,128]{1,0:T(8,128)(2,1)S(1)} %step.24.own.refs_7_.refs_1_), channel_id=1, source_target_pairs={{1,2},{2,1},{3,4},{4,3},{5,6},{6,5},{7,70},{70,7},{71,68},{68,71},... | collective-permute-start | bytes 196616 | tf_op jit(solution)/shard_map/ppermute | solution.py:251
  121.8 3.2 %collective-permute-start.20 = (bf16[256,128]{1,0:T(8,128)(2,1)S(1)}, bf16[256,128]{1,0:T(8,128)(2,1)S(1)}, u32[]{:S(2)}, u32[]{:S(2)}) collective-permute-start(bf16[256,128]{1,0:T(8,128)(2,1)S(1)} %step.24.own.refs_7_.refs_1_), channel_id=1, source_target_pairs={{0,1},{1,0},{2,3},{3,2},{4,5},{5,4},{6,7},{7,6},{70,71},{71,70},{6... | collective-permute-start | bytes 196616 | tf_op jit(solution)/shard_map/ppermute | solution.py:251
  126.2 1.0 step.25.own.refs_7_.refs_1_
  127.2 2.2 %collective-permute-start.21 = (bf16[256,128]{1,0:T(8,128)(2,1)S(1)}, bf16[256,128]{1,0:T(8,128)(2,1)S(1)}, u32[]{:S(2)}, u32[]{:S(2)}) collective-permute-start(bf16[256,128]{1,0:T(8,128)(2,1)S(1)} %step.25.own.refs_7_.refs_1_), channel_id=1, source_target_pairs={{1,2},{2,1},{3,4},{4,3},{5,6},{6,5},{7,70},{70,7},{71,68},{68,71},... | collective-permute-start | bytes 196616 | tf_op jit(solution)/shard_map/ppermute | solution.py:251
  129.4 3.4 %collective-permute-start.22 = (bf16[256,128]{1,0:T(8,128)(2,1)S(1)}, bf16[256,128]{1,0:T(8,128)(2,1)S(1)}, u32[]{:S(2)}, u32[]{:S(2)}) collective-permute-start(bf16[256,128]{1,0:T(8,128)(2,1)S(1)} %step.25.own.refs_7_.refs_1_), channel_id=1, source_target_pairs={{0,1},{1,0},{2,3},{3,2},{4,5},{5,4},{6,7},{7,6},{70,71},{71,70},{6... | collective-permute-start | bytes 196616 | tf_op jit(solution)/shard_map/ppermute | solution.py:251
  135.0 2.2 %collective-permute-start.23 = (bf16[256,128]{1,0:T(8,128)(2,1)S(1)}, bf16[256,128]{1,0:T(8,128)(2,1)S(1)}, u32[]{:S(2)}, u32[]{:S(2)}) collective-permute-start(bf16[256,128]{1,0:T(8,128)(2,1)S(1)} %step.26.own.refs_7_.refs_1_), channel_id=1, source_target_pairs={{1,2},{2,1},{3,4},{4,3},{5,6},{6,5},{7,70},{70,7},{71,68},{68,71},... | collective-permute-start | bytes 196616 | tf_op jit(solution)/shard_map/ppermute | solution.py:251
  137.2 3.2 %collective-permute-start.24 = (bf16[256,128]{1,0:T(8,128)(2,1)S(1)}, bf16[256,128]{1,0:T(8,128)(2,1)S(1)}, u32[]{:S(2)}, u32[]{:S(2)}) collective-permute-start(bf16[256,128]{1,0:T(8,128)(2,1)S(1)} %step.26.own.refs_7_.refs_1_), channel_id=1, source_target_pairs={{0,1},{1,0},{2,3},{3,2},{4,5},{5,4},{6,7},{7,6},{70,71},{71,70},{6... | collective-permute-start | bytes 196616 | tf_op jit(solution)/shard_map/ppermute | solution.py:251
  142.6 2.4 %collective-permute-start.25 = (bf16[256,128]{1,0:T(8,128)(2,1)S(1)}, bf16[256,128]{1,0:T(8,128)(2,1)S(1)}, u32[]{:S(2)}, u32[]{:S(2)}) collective-permute-start(bf16[256,128]{1,0:T(8,128)(2,1)S(1)} %step.27.own.refs_7_.refs_1_), channel_id=1, source_target_pairs={{1,2},{2,1},{3,4},{4,3},{5,6},{6,5},{7,70},{70,7},{71,68},{68,71},... | collective-permute-start | bytes 196616 | tf_op jit(solution)/shard_map/ppermute | solution.py:251
  145.0 3.2 %collective-permute-start.26 = (bf16[256,128]{1,0:T(8,128)(2,1)S(1)}, bf16[256,128]{1,0:T(8,128)(2,1)S(1)}, u32[]{:S(2)}, u32[]{:S(2)}) collective-permute-start(bf16[256,128]{1,0:T(8,128)(2,1)S(1)} %step.27.own.refs_7_.refs_1_), channel_id=1, source_target_pairs={{0,1},{1,0},{2,3},{3,2},{4,5},{5,4},{6,7},{7,6},{70,71},{71,70},{6... | collective-permute-start | bytes 196616 | tf_op jit(solution)/shard_map/ppermute | solution.py:251
  149.3 1.0 step.28.own.refs_7_.refs_1_
  150.4 2.2 %collective-permute-start.27 = (bf16[256,128]{1,0:T(8,128)(2,1)S(1)}, bf16[256,128]{1,0:T(8,128)(2,1)S(1)}, u32[]{:S(2)}, u32[]{:S(2)}) collective-permute-start(bf16[256,128]{1,0:T(8,128)(2,1)S(1)} %step.28.own.refs_7_.refs_1_), channel_id=1, source_target_pairs={{1,2},{2,1},{3,4},{4,3},{5,6},{6,5},{7,70},{70,7},{71,68},{68,71},... | collective-permute-start | bytes 196616 | tf_op jit(solution)/shard_map/ppermute | solution.py:251
  152.6 3.4 %collective-permute-start.28 = (bf16[256,128]{1,0:T(8,128)(2,1)S(1)}, bf16[256,128]{1,0:T(8,128)(2,1)S(1)}, u32[]{:S(2)}, u32[]{:S(2)}) collective-permute-start(bf16[256,128]{1,0:T(8,128)(2,1)S(1)} %step.28.own.refs_7_.refs_1_), channel_id=1, source_target_pairs={{0,1},{1,0},{2,3},{3,2},{4,5},{5,4},{6,7},{7,6},{70,71},{71,70},{6... | collective-permute-start | bytes 196616 | tf_op jit(solution)/shard_map/ppermute | solution.py:251
  157.9 2.4 %collective-permute-start.29 = (bf16[256,128]{1,0:T(8,128)(2,1)S(1)}, bf16[256,128]{1,0:T(8,128)(2,1)S(1)}, u32[]{:S(2)}, u32[]{:S(2)}) collective-permute-start(bf16[256,128]{1,0:T(8,128)(2,1)S(1)} %step.29.own.refs_7_.refs_1_), channel_id=1, source_target_pairs={{1,2},{2,1},{3,4},{4,3},{5,6},{6,5},{7,70},{70,7},{71,68},{68,71},... | collective-permute-start | bytes 196616 | tf_op jit(solution)/shard_map/ppermute | solution.py:251
  160.4 3.2 %collective-permute-start.30 = (bf16[256,128]{1,0:T(8,128)(2,1)S(1)}, bf16[256,128]{1,0:T(8,128)(2,1)S(1)}, u32[]{:S(2)}, u32[]{:S(2)}) collective-permute-start(bf16[256,128]{1,0:T(8,128)(2,1)S(1)} %step.29.own.refs_7_.refs_1_), channel_id=1, source_target_pairs={{0,1},{1,0},{2,3},{3,2},{4,5},{5,4},{6,7},{7,6},{70,71},{71,70},{6... | collective-permute-start | bytes 196616 | tf_op jit(solution)/shard_map/ppermute | solution.py:251
  164.7 1.0 step.30.own.refs_7_
  165.7 2.2 %collective-permute-start.31 = (bf16[256,128]{1,0:T(8,128)(2,1)S(1)}, bf16[256,128]{1,0:T(8,128)(2,1)S(1)}, u32[]{:S(2)}, u32[]{:S(2)}) collective-permute-start(bf16[256,128]{1,0:T(8,128)(2,1)S(1)} %step.30.own.refs_7_), channel_id=1, source_target_pairs={{1,2},{2,1},{3,4},{4,3},{5,6},{6,5},{7,70},{70,7},{71,68},{68,71},... | collective-permute-start | bytes 196616 | tf_op jit(solution)/shard_map/ppermute | solution.py:251
  168.0 3.2 %collective-permute-start.32 = (bf16[256,128]{1,0:T(8,128)(2,1)S(1)}, bf16[256,128]{1,0:T(8,128)(2,1)S(1)}, u32[]{:S(2)}, u32[]{:S(2)}) collective-permute-start(bf16[256,128]{1,0:T(8,128)(2,1)S(1)} %step.30.own.refs_7_), channel_id=1, source_target_pairs={{0,1},{1,0},{2,3},{3,2},{4,5},{5,4},{6,7},{7,6},{70,71},{71,70},{6... | collective-permute-start | bytes 196616 | tf_op jit(solution)/shard_map/ppermute | solution.py:251
  173.9 1.3 collective-permute-start.33
  175.3 6.3 %collective-permute-done.33 = bf16[2,256,128]{2,1,0:T(8,128)(2,1)S(1)} collective-permute-done((bf16[2,256,128]{2,1,0:T(8,128)(2,1)S(1)}, bf16[2,256,128]{2,1,0:T(8,128)(2,1)S(1)}, u32[]{:S(2)}, u32[]{:S(2)}) %collective-permute-start.33) | collective-permute-done | bytes 131104 | tf_op jit(solution)/shard_map/ppermute | solution.py:363
  (160 shorter events, 35.5 us)
Async XLA Ops:
  2.0 0.7 copy-start.14
  2.8 0.8 copy-start.12
  3.7 15.1 %collective-permute-start = (bf16[320,128]{1,0:T(8,128)(2,1)S(1)}, bf16[320,128]{1,0:T(8,128)(2,1)S(1)}, u32[]{:S(2)}, u32[]{:S(2)}) collective-permute-start(bf16[320,128]{1,0:T(8,128)(2,1)S(1)} %pad_maximum_fusion.4), channel_id=1, source_target_pairs={{0,14},{1,15},{2,12},{3,13},{4,10},{5,11},{6,8},{7,9},{8,6},{9,7},... | collective-permute-start | bytes 245768 | tf_op jit(solution)/shard_map/ppermute | solution.py:300
  19.9 26.6 %all-to-all-start = ((bf16[8,320,128]{2,1,0:T(8,128)(2,1)}), bf16[8,320,128]{2,1,0:T(8,128)(2,1)S(1)}, u32[]{:S(2)}, u32[]{:S(2)}) async-start(bf16[8,320,128]{2,1,0:T(8,128)(2,1)} %bitcast.9), calls=%async_computation | async-start | bytes 1310720 | tf_op jit(solution)/shard_map/all_to_all | solution.py:303
  27.4 0.9 copy-start.8
  28.3 0.9 copy-start.9
  29.9 0.9 copy-start.10
  30.8 0.9 copy-start.11
  46.5 8.4 %collective-permute-start.1 = (bf16[8,160,128]{2,1,0:T(8,128)(2,1)S(1)}, bf16[8,160,128]{2,1,0:T(8,128)(2,1)S(1)}, u32[]{:S(2)}, u32[]{:S(2)}) collective-permute-start(bf16[8,160,128]{2,1,0:T(8,128)(2,1)S(1)} %pad_maximum_fusion), channel_id=1, source_target_pairs={{1,2},{2,1},{3,4},{4,3},{5,6},{6,5},{7,70},{70,7},{71,68},{68,71},... | collective-permute-start | bytes 983048 | tf_op jit(solution)/shard_map/ppermute | solution.py:251
  48.5 6.5 %collective-permute-start.2 = (bf16[8,160,128]{2,1,0:T(8,128)(2,1)S(1)}, bf16[8,160,128]{2,1,0:T(8,128)(2,1)S(1)}, u32[]{:S(2)}, u32[]{:S(2)}) collective-permute-start(bf16[8,160,128]{2,1,0:T(8,128)(2,1)S(1)} %pad_maximum_fusion.1), channel_id=1, source_target_pairs={{0,1},{1,0},{2,3},{3,2},{4,5},{5,4},{6,7},{7,6},{70,71},{71,70},{6... | collective-permute-start | bytes 983048 | tf_op jit(solution)/shard_map/ppermute | solution.py:251
  53.0 2.1 %copy-start.2 = (bf16[256,128]{1,0:T(8,128)(2,1)}, bf16[256,128]{1,0:T(8,128)(2,1)S(1)}, u32[]{:S(2)}) copy-start(bf16[256,128]{1,0:T(8,128)(2,1)S(1)} %get-tuple-element.59.refs_1_) | copy-start | bytes 196612
  55.0 0.8 copy-start.1
  55.0 1.5 copy-start.6
  56.5 9.0 %collective-permute-start.3 = (bf16[256,128]{1,0:T(8,128)(2,1)S(1)}, bf16[256,128]{1,0:T(8,128)(2,1)S(1)}, u32[]{:S(2)}, u32[]{:S(2)}) collective-permute-start(bf16[256,128]{1,0:T(8,128)(2,1)S(1)} %step.16.own.refs_4_.refs_1_), channel_id=1, source_target_pairs={{1,2},{2,1},{3,4},{4,3},{5,6},{6,5},{7,70},{70,7},{71,68},{68,71},... | collective-permute-start | bytes 196616 | tf_op jit(solution)/shard_map/ppermute | solution.py:251
  58.4 6.8 %collective-permute-start.4 = (bf16[256,128]{1,0:T(8,128)(2,1)S(1)}, bf16[256,128]{1,0:T(8,128)(2,1)S(1)}, u32[]{:S(2)}, u32[]{:S(2)}) collective-permute-start(bf16[256,128]{1,0:T(8,128)(2,1)S(1)} %step.16.own.refs_4_.refs_1_), channel_id=1, source_target_pairs={{0,1},{1,0},{2,3},{3,2},{4,5},{5,4},{6,7},{7,6},{70,71},{71,70},{6... | collective-permute-start | bytes 196616 | tf_op jit(solution)/shard_map/ppermute | solution.py:251
  66.5 5.9 %collective-permute-start.5 = (bf16[256,128]{1,0:T(8,128)(2,1)S(1)}, bf16[256,128]{1,0:T(8,128)(2,1)S(1)}, u32[]{:S(2)}, u32[]{:S(2)}) collective-permute-start(bf16[256,128]{1,0:T(8,128)(2,1)S(1)} %step.17.own.refs_4_.refs_1_), channel_id=1, source_target_pairs={{1,2},{2,1},{3,4},{4,3},{5,6},{6,5},{7,70},{70,7},{71,68},{68,71},... | collective-permute-start | bytes 196616 | tf_op jit(solution)/shard_map/ppermute | solution.py:251
  68.4 3.7 %collective-permute-start.6 = (bf16[256,128]{1,0:T(8,128)(2,1)S(1)}, bf16[256,128]{1,0:T(8,128)(2,1)S(1)}, u32[]{:S(2)}, u32[]{:S(2)}) collective-permute-start(bf16[256,128]{1,0:T(8,128)(2,1)S(1)} %step.17.own.refs_4_.refs_1_), channel_id=1, source_target_pairs={{0,1},{1,0},{2,3},{3,2},{4,5},{5,4},{6,7},{7,6},{70,71},{71,70},{6... | collective-permute-start | bytes 196616 | tf_op jit(solution)/shard_map/ppermute | solution.py:251
  73.4 7.1 %collective-permute-start.7 = (bf16[256,128]{1,0:T(8,128)(2,1)S(1)}, bf16[256,128]{1,0:T(8,128)(2,1)S(1)}, u32[]{:S(2)}, u32[]{:S(2)}) collective-permute-start(bf16[256,128]{1,0:T(8,128)(2,1)S(1)} %step.18.own.refs_4_.refs_1_), channel_id=1, source_target_pairs={{1,2},{2,1},{3,4},{4,3},{5,6},{6,5},{7,70},{70,7},{71,68},{68,71},... | collective-permute-start | bytes 196616 | tf_op jit(solution)/shard_map/ppermute | solution.py:251
  76.5 3.7 %collective-permute-start.8 = (bf16[256,128]{1,0:T(8,128)(2,1)S(1)}, bf16[256,128]{1,0:T(8,128)(2,1)S(1)}, u32[]{:S(2)}, u32[]{:S(2)}) collective-permute-start(bf16[256,128]{1,0:T(8,128)(2,1)S(1)} %step.18.own.refs_4_.refs_1_), channel_id=1, source_target_pairs={{0,1},{1,0},{2,3},{3,2},{4,5},{5,4},{6,7},{7,6},{70,71},{71,70},{6... | collective-permute-start | bytes 196616 | tf_op jit(solution)/shard_map/ppermute | solution.py:251
  81.5 6.5 %collective-permute-start.9 = (bf16[256,128]{1,0:T(8,128)(2,1)S(1)}, bf16[256,128]{1,0:T(8,128)(2,1)S(1)}, u32[]{:S(2)}, u32[]{:S(2)}) collective-permute-start(bf16[256,128]{1,0:T(8,128)(2,1)S(1)} %step.19.own.refs_4_.refs_1_), channel_id=1, source_target_pairs={{1,2},{2,1},{3,4},{4,3},{5,6},{6,5},{7,70},{70,7},{71,68},{68,71},... | collective-permute-start | bytes 196616 | tf_op jit(solution)/shard_map/ppermute | solution.py:251
  83.5 4.3 %collective-permute-start.10 = (bf16[256,128]{1,0:T(8,128)(2,1)S(1)}, bf16[256,128]{1,0:T(8,128)(2,1)S(1)}, u32[]{:S(2)}, u32[]{:S(2)}) collective-permute-start(bf16[256,128]{1,0:T(8,128)(2,1)S(1)} %step.19.own.refs_4_.refs_1_), channel_id=1, source_target_pairs={{0,1},{1,0},{2,3},{3,2},{4,5},{5,4},{6,7},{7,6},{70,71},{71,70},{6... | collective-permute-start | bytes 196616 | tf_op jit(solution)/shard_map/ppermute | solution.py:251
  89.1 6.8 %collective-permute-start.11 = (bf16[256,128]{1,0:T(8,128)(2,1)S(1)}, bf16[256,128]{1,0:T(8,128)(2,1)S(1)}, u32[]{:S(2)}, u32[]{:S(2)}) collective-permute-start(bf16[256,128]{1,0:T(8,128)(2,1)S(1)} %step.20.own.refs_4_.refs_1_), channel_id=1, source_target_pairs={{1,2},{2,1},{3,4},{4,3},{5,6},{6,5},{7,70},{70,7},{71,68},{68,71},... | collective-permute-start | bytes 196616 | tf_op jit(solution)/shard_map/ppermute | solution.py:251
  91.6 4.0 %collective-permute-start.12 = (bf16[256,128]{1,0:T(8,128)(2,1)S(1)}, bf16[256,128]{1,0:T(8,128)(2,1)S(1)}, u32[]{:S(2)}, u32[]{:S(2)}) collective-permute-start(bf16[256,128]{1,0:T(8,128)(2,1)S(1)} %step.20.own.refs_4_.refs_1_), channel_id=1, source_target_pairs={{0,1},{1,0},{2,3},{3,2},{4,5},{5,4},{6,7},{7,6},{70,71},{71,70},{6... | collective-permute-start | bytes 196616 | tf_op jit(solution)/shard_map/ppermute | solution.py:251
  96.9 6.5 %collective-permute-start.13 = (bf16[256,128]{1,0:T(8,128)(2,1)S(1)}, bf16[256,128]{1,0:T(8,128)(2,1)S(1)}, u32[]{:S(2)}, u32[]{:S(2)}) collective-permute-start(bf16[256,128]{1,0:T(8,128)(2,1)S(1)} %step.21.own.refs_4_.refs_1_), channel_id=1, source_target_pairs={{1,2},{2,1},{3,4},{4,3},{5,6},{6,5},{7,70},{70,7},{71,68},{68,71},... | collective-permute-start | bytes 196616 | tf_op jit(solution)/shard_map/ppermute | solution.py:251
  99.1 4.0 %collective-permute-start.14 = (bf16[256,128]{1,0:T(8,128)(2,1)S(1)}, bf16[256,128]{1,0:T(8,128)(2,1)S(1)}, u32[]{:S(2)}, u32[]{:S(2)}) collective-permute-start(bf16[256,128]{1,0:T(8,128)(2,1)S(1)} %step.21.own.refs_4_.refs_1_), channel_id=1, source_target_pairs={{0,1},{1,0},{2,3},{3,2},{4,5},{5,4},{6,7},{7,6},{70,71},{71,70},{6... | collective-permute-start | bytes 196616 | tf_op jit(solution)/shard_map/ppermute | solution.py:251
  104.4 6.8 %collective-permute-start.15 = (bf16[256,128]{1,0:T(8,128)(2,1)S(1)}, bf16[256,128]{1,0:T(8,128)(2,1)S(1)}, u32[]{:S(2)}, u32[]{:S(2)}) collective-permute-start(bf16[256,128]{1,0:T(8,128)(2,1)S(1)} %step.22.own.refs_4_), channel_id=1, source_target_pairs={{1,2},{2,1},{3,4},{4,3},{5,6},{6,5},{7,70},{70,7},{71,68},{68,71},... | collective-permute-start | bytes 196616 | tf_op jit(solution)/shard_map/ppermute | solution.py:251
  107.0 4.0 %collective-permute-start.16 = (bf16[256,128]{1,0:T(8,128)(2,1)S(1)}, bf16[256,128]{1,0:T(8,128)(2,1)S(1)}, u32[]{:S(2)}, u32[]{:S(2)}) collective-permute-start(bf16[256,128]{1,0:T(8,128)(2,1)S(1)} %step.22.own.refs_4_), channel_id=1, source_target_pairs={{0,1},{1,0},{2,3},{3,2},{4,5},{5,4},{6,7},{7,6},{70,71},{71,70},{6... | collective-permute-start | bytes 196616 | tf_op jit(solution)/shard_map/ppermute | solution.py:251
  112.3 6.2 %copy-start = (bf16[64,256]{1,0:T(8,128)(2,1)S(1)}, bf16[64,256]{1,0:T(8,128)(2,1)}, u32[]{:S(2)}) copy-start(bf16[64,256]{1,0:T(8,128)(2,1)} %refs_11_.11) | copy-start | bytes 98308
  112.3 5.6 %collective-permute-start.17 = (bf16[256,128]{1,0:T(8,128)(2,1)S(1)}, bf16[256,128]{1,0:T(8,128)(2,1)S(1)}, u32[]{:S(2)}, u32[]{:S(2)}) collective-permute-start(bf16[256,128]{1,0:T(8,128)(2,1)S(1)} %step.23.refs_4_), channel_id=1, source_target_pairs={{1,2},{2,1},{3,4},{4,3},{5,6},{6,5},{7,70},{70,7},{71,68},{68,71},... | collective-permute-start | bytes 196616 | tf_op jit(solution)/shard_map/ppermute | solution.py:251
  114.5 4.0 %collective-permute-start.18 = (bf16[256,128]{1,0:T(8,128)(2,1)S(1)}, bf16[256,128]{1,0:T(8,128)(2,1)S(1)}, u32[]{:S(2)}, u32[]{:S(2)}) collective-permute-start(bf16[256,128]{1,0:T(8,128)(2,1)S(1)} %step.23.refs_4_), channel_id=1, source_target_pairs={{0,1},{1,0},{2,3},{3,2},{4,5},{5,4},{6,7},{7,6},{70,71},{71,70},{6... | collective-permute-start | bytes 196616 | tf_op jit(solution)/shard_map/ppermute | solution.py:251
  119.3 6.8 %collective-permute-start.19 = (bf16[256,128]{1,0:T(8,128)(2,1)S(1)}, bf16[256,128]{1,0:T(8,128)(2,1)S(1)}, u32[]{:S(2)}, u32[]{:S(2)}) collective-permute-start(bf16[256,128]{1,0:T(8,128)(2,1)S(1)} %step.24.own.refs_7_.refs_1_), channel_id=1, source_target_pairs={{1,2},{2,1},{3,4},{4,3},{5,6},{6,5},{7,70},{70,7},{71,68},{68,71},... | collective-permute-start | bytes 196616 | tf_op jit(solution)/shard_map/ppermute | solution.py:251
  121.8 4.1 %collective-permute-start.20 = (bf16[256,128]{1,0:T(8,128)(2,1)S(1)}, bf16[256,128]{1,0:T(8,128)(2,1)S(1)}, u32[]{:S(2)}, u32[]{:S(2)}) collective-permute-start(bf16[256,128]{1,0:T(8,128)(2,1)S(1)} %step.24.own.refs_7_.refs_1_), channel_id=1, source_target_pairs={{0,1},{1,0},{2,3},{3,2},{4,5},{5,4},{6,7},{7,6},{70,71},{71,70},{6... | collective-permute-start | bytes 196616 | tf_op jit(solution)/shard_map/ppermute | solution.py:251
  127.2 6.8 %collective-permute-start.21 = (bf16[256,128]{1,0:T(8,128)(2,1)S(1)}, bf16[256,128]{1,0:T(8,128)(2,1)S(1)}, u32[]{:S(2)}, u32[]{:S(2)}) collective-permute-start(bf16[256,128]{1,0:T(8,128)(2,1)S(1)} %step.25.own.refs_7_.refs_1_), channel_id=1, source_target_pairs={{1,2},{2,1},{3,4},{4,3},{5,6},{6,5},{7,70},{70,7},{71,68},{68,71},... | collective-permute-start | bytes 196616 | tf_op jit(solution)/shard_map/ppermute | solution.py:251
  129.4 4.3 %collective-permute-start.22 = (bf16[256,128]{1,0:T(8,128)(2,1)S(1)}, bf16[256,128]{1,0:T(8,128)(2,1)S(1)}, u32[]{:S(2)}, u32[]{:S(2)}) collective-permute-start(bf16[256,128]{1,0:T(8,128)(2,1)S(1)} %step.25.own.refs_7_.refs_1_), channel_id=1, source_target_pairs={{0,1},{1,0},{2,3},{3,2},{4,5},{5,4},{6,7},{7,6},{70,71},{71,70},{6... | collective-permute-start | bytes 196616 | tf_op jit(solution)/shard_map/ppermute | solution.py:251
  135.0 6.5 %collective-permute-start.23 = (bf16[256,128]{1,0:T(8,128)(2,1)S(1)}, bf16[256,128]{1,0:T(8,128)(2,1)S(1)}, u32[]{:S(2)}, u32[]{:S(2)}) collective-permute-start(bf16[256,128]{1,0:T(8,128)(2,1)S(1)} %step.26.own.refs_7_.refs_1_), channel_id=1, source_target_pairs={{1,2},{2,1},{3,4},{4,3},{5,6},{6,5},{7,70},{70,7},{71,68},{68,71},... | collective-permute-start | bytes 196616 | tf_op jit(solution)/shard_map/ppermute | solution.py:251
  137.2 4.0 %collective-permute-start.24 = (bf16[256,128]{1,0:T(8,128)(2,1)S(1)}, bf16[256,128]{1,0:T(8,128)(2,1)S(1)}, u32[]{:S(2)}, u32[]{:S(2)}) collective-permute-start(bf16[256,128]{1,0:T(8,128)(2,1)S(1)} %step.26.own.refs_7_.refs_1_), channel_id=1, source_target_pairs={{0,1},{1,0},{2,3},{3,2},{4,5},{5,4},{6,7},{7,6},{70,71},{71,70},{6... | collective-permute-start | bytes 196616 | tf_op jit(solution)/shard_map/ppermute | solution.py:251
  142.6 6.8 %collective-permute-start.25 = (bf16[256,128]{1,0:T(8,128)(2,1)S(1)}, bf16[256,128]{1,0:T(8,128)(2,1)S(1)}, u32[]{:S(2)}, u32[]{:S(2)}) collective-permute-start(bf16[256,128]{1,0:T(8,128)(2,1)S(1)} %step.27.own.refs_7_.refs_1_), channel_id=1, source_target_pairs={{1,2},{2,1},{3,4},{4,3},{5,6},{6,5},{7,70},{70,7},{71,68},{68,71},... | collective-permute-start | bytes 196616 | tf_op jit(solution)/shard_map/ppermute | solution.py:251
  145.0 4.1 %collective-permute-start.26 = (bf16[256,128]{1,0:T(8,128)(2,1)S(1)}, bf16[256,128]{1,0:T(8,128)(2,1)S(1)}, u32[]{:S(2)}, u32[]{:S(2)}) collective-permute-start(bf16[256,128]{1,0:T(8,128)(2,1)S(1)} %step.27.own.refs_7_.refs_1_), channel_id=1, source_target_pairs={{0,1},{1,0},{2,3},{3,2},{4,5},{5,4},{6,7},{7,6},{70,71},{71,70},{6... | collective-permute-start | bytes 196616 | tf_op jit(solution)/shard_map/ppermute | solution.py:251
  150.4 6.5 %collective-permute-start.27 = (bf16[256,128]{1,0:T(8,128)(2,1)S(1)}, bf16[256,128]{1,0:T(8,128)(2,1)S(1)}, u32[]{:S(2)}, u32[]{:S(2)}) collective-permute-start(bf16[256,128]{1,0:T(8,128)(2,1)S(1)} %step.28.own.refs_7_.refs_1_), channel_id=1, source_target_pairs={{1,2},{2,1},{3,4},{4,3},{5,6},{6,5},{7,70},{70,7},{71,68},{68,71},... | collective-permute-start | bytes 196616 | tf_op jit(solution)/shard_map/ppermute | solution.py:251
  152.6 4.1 %collective-permute-start.28 = (bf16[256,128]{1,0:T(8,128)(2,1)S(1)}, bf16[256,128]{1,0:T(8,128)(2,1)S(1)}, u32[]{:S(2)}, u32[]{:S(2)}) collective-permute-start(bf16[256,128]{1,0:T(8,128)(2,1)S(1)} %step.28.own.refs_7_.refs_1_), channel_id=1, source_target_pairs={{0,1},{1,0},{2,3},{3,2},{4,5},{5,4},{6,7},{7,6},{70,71},{71,70},{6... | collective-permute-start | bytes 196616 | tf_op jit(solution)/shard_map/ppermute | solution.py:251
  157.9 6.8 %collective-permute-start.29 = (bf16[256,128]{1,0:T(8,128)(2,1)S(1)}, bf16[256,128]{1,0:T(8,128)(2,1)S(1)}, u32[]{:S(2)}, u32[]{:S(2)}) collective-permute-start(bf16[256,128]{1,0:T(8,128)(2,1)S(1)} %step.29.own.refs_7_.refs_1_), channel_id=1, source_target_pairs={{1,2},{2,1},{3,4},{4,3},{5,6},{6,5},{7,70},{70,7},{71,68},{68,71},... | collective-permute-start | bytes 196616 | tf_op jit(solution)/shard_map/ppermute | solution.py:251
  160.4 4.0 %collective-permute-start.30 = (bf16[256,128]{1,0:T(8,128)(2,1)S(1)}, bf16[256,128]{1,0:T(8,128)(2,1)S(1)}, u32[]{:S(2)}, u32[]{:S(2)}) collective-permute-start(bf16[256,128]{1,0:T(8,128)(2,1)S(1)} %step.29.own.refs_7_.refs_1_), channel_id=1, source_target_pairs={{0,1},{1,0},{2,3},{3,2},{4,5},{5,4},{6,7},{7,6},{70,71},{71,70},{6... | collective-permute-start | bytes 196616 | tf_op jit(solution)/shard_map/ppermute | solution.py:251
  165.7 6.5 %collective-permute-start.31 = (bf16[256,128]{1,0:T(8,128)(2,1)S(1)}, bf16[256,128]{1,0:T(8,128)(2,1)S(1)}, u32[]{:S(2)}, u32[]{:S(2)}) collective-permute-start(bf16[256,128]{1,0:T(8,128)(2,1)S(1)} %step.30.own.refs_7_), channel_id=1, source_target_pairs={{1,2},{2,1},{3,4},{4,3},{5,6},{6,5},{7,70},{70,7},{71,68},{68,71},... | collective-permute-start | bytes 196616 | tf_op jit(solution)/shard_map/ppermute | solution.py:251
  168.0 4.1 %collective-permute-start.32 = (bf16[256,128]{1,0:T(8,128)(2,1)S(1)}, bf16[256,128]{1,0:T(8,128)(2,1)S(1)}, u32[]{:S(2)}, u32[]{:S(2)}) collective-permute-start(bf16[256,128]{1,0:T(8,128)(2,1)S(1)} %step.30.own.refs_7_), channel_id=1, source_target_pairs={{0,1},{1,0},{2,3},{3,2},{4,5},{5,4},{6,7},{7,6},{70,71},{71,70},{6... | collective-permute-start | bytes 196616 | tf_op jit(solution)/shard_map/ppermute | solution.py:251
  172.0 0.8 copy-start.3
  172.0 0.8 copy-start.5
  172.0 0.8 copy-start.7
  173.9 7.6 %collective-permute-start.33 = (bf16[2,256,128]{2,1,0:T(8,128)(2,1)S(1)}, bf16[2,256,128]{2,1,0:T(8,128)(2,1)S(1)}, u32[]{:S(2)}, u32[]{:S(2)}) collective-permute-start(bf16[2,256,128]{2,1,0:T(8,128)(2,1)S(1)} %pad_maximum_fusion.3), channel_id=1, source_target_pairs={{0,64},{1,65},{2,66},{3,67},{4,68},{5,69},{6,70},{7,71},{16,80},{1... | collective-permute-start | bytes 393224 | tf_op jit(solution)/shard_map/ppermute | solution.py:363
  (4 other events, 2.7 us)

commit v6 on v5

--- a/solution.py
+++ b/solution.py
@@ -15,6 +15,11 @@
 FRAMES = 8
 EXT = ROWS + 2 * R
 EARLY = EXT // 2
+
+
+VMEM = pl.BlockSpec(memory_space=pltpu.VMEM)
+SMEM = pl.BlockSpec(memory_space=pltpu.SMEM)
+BF16 = jnp.bfloat16
 
 
 def leaky(values):
@@ -99,7 +104,7 @@
         sample_row((None, own, beside), r, lambda n: taps[r, n], store)
 
 
-def step_kernel(priors, parts, first, sense, *refs):
+def step_kernel(priors, parts, wide, first, sense, *refs):
     refs = list(refs)
     grid = (first[0], sense[0])
     sides = [[refs.pop(0) for _ in range(3)] for _ in range(parts)]
@@ -118,13 +123,33 @@
         return ref[pl.ds(at, C), :]
 
     depth = (parts + priors) * C
-    for r in (0, 2, 4, 6):
-        for n in range(2 if priors and r < EARLY else 0):
-
-            def store(ch, value):
-                stack[pl.ds(ch, 16), pl.ds((r + n) * W, W)] = value
-
-            sample_row(newest, r + n, lambda k: taps[r + n, k], store)
+    cols = lax.broadcasted_iota(jnp.int32, (C, W), 1)
+    span = 3 * C if wide else C
+    own = C if wide else 0
+
+    def put(ref, row, value):
+        value = value.astype(BF16)
+        ref[pl.ds(row * span + own, C), :] = value
+        if wide:
+            ref[pl.ds(row * span, C), :] = pltpu.roll(value, 1, 1) * (cols >= 1).astype(BF16)
+            ref[pl.ds(row * span + 2 * C, C), :] = pltpu.roll(value, W - 1, 1) * (cols < W - 1).astype(BF16)
+
+    def conv_pair(source, kernel, r):
+        data = jnp.concatenate(
+            [source[pl.ds(n * span, 3 * span), :] for n in (r, r + 1)], axis=1
+        )
+        res = jnp.dot(kernel[...], data, preferred_element_type=jnp.float32)
+        outs = []
+        for n in range(2):
+            part = res[:, n * W : (n + 1) * W]
+            if not wide:
+                left = jnp.where(cols >= 1, pltpu.roll(part[0:C], 1, 1), 0.0)
+                right = jnp.where(cols < W - 1, pltpu.roll(part[2 * C : 3 * C], W - 1, 1), 0.0)
+                part = left + part[C : 2 * C] + right
+            outs.append(part)
+        return outs
+
+    def join(r):
         pieces = [
             jnp.concatenate([side_row(trio, r), side_row(trio, r + 1)], axis=1) for trio in sides
         ]
@@ -139,39 +164,47 @@
             value = both[:, n * W : (n + 1) * W]
             if not R <= r + n < R + ROWS:
                 value = value * keep(r + n - R)
-            joined[pl.ds((r + n) * C, C), :] = value.astype(jnp.bfloat16)
-
-    cols = lax.broadcasted_iota(jnp.int32, (C, W), 1)
-
-    def conv_pair(source, kernel, r):
-        data = jnp.concatenate(
-            [source[pl.ds(r * C, 3 * C), :], source[pl.ds((r + 1) * C, 3 * C), :]], axis=1
-        )
-        res = jnp.dot(kernel[...], data, preferred_element_type=jnp.float32)
-        outs = []
-        for n in range(2):
-            part = res[:, n * W : (n + 1) * W]
-            left = jnp.where(cols >= 1, pltpu.roll(part[0:C], 1, 1), 0.0)
-            right = jnp.where(cols < W - 1, pltpu.roll(part[2 * C : 3 * C], W - 1, 1), 0.0)
-            outs.append(left + part[C : 2 * C] + right)
-        return outs
-
-    for r in (0, 2, 4):
+            put(joined, r + n, value)
+
+    def inside(r):
         for n, value in enumerate(conv_pair(joined, inner, r)):
             value = leaky(value)
             if r + n in (0, ROWS + 1):
                 value = value * keep(r + n - 1)
-            hidden[pl.ds((r + n) * C, C), :] = value.astype(jnp.bfloat16)
-
-    for r in (0, 2):
+            put(hidden, r + n, value)
+
+    join(4)
+    join(6)
+    inside(4)
+    for r in (2, 0):
+        for n in (1, 0) if priors else ():
+
+            def store(ch, value):
+                stack[pl.ds(ch, 16), pl.ds((r + n) * W, W)] = value
+
+            sample_row(newest, r + n, lambda k: taps[r + n, k], store)
+        join(r)
+        inside(r)
+    for r in (2, 0):
         for n, value in enumerate(conv_pair(hidden, outer, r)):
-            base = joined[pl.ds((r + n + R) * C, C), :].astype(jnp.float32)
-            out[pl.ds((r + n) * C, C), :] = (base + value).astype(jnp.bfloat16)
-
-
-VMEM = pl.BlockSpec(memory_space=pltpu.VMEM)
-SMEM = pl.BlockSpec(memory_space=pltpu.SMEM)
-BF16 = jnp.bfloat16
+            base = joined[pl.ds((r + n + R) * span + own, C), :].astype(jnp.float32)
+            out[pl.ds((r + n) * C, C), :] = (base + value).astype(BF16)
+
+
+def pack_kernel(sense, back_shift, back_fraction, ahead_shift, ahead_fraction, out):
+    turned = sense[0] < 0
+    sign = jnp.where(turned, -1.0, 1.0)
+    one = jnp.where(turned, 1.0, 0.0)
+    for r in range(ROWS):
+        row = pl.ds(jnp.where(turned, ROWS - 1 - r, r), 1)
+        rows = []
+        for shift, fraction in ((back_shift, back_fraction), (ahead_shift, ahead_fraction)):
+            for n in range(2):
+                rows.append(shift[0, n, 0, row, :].astype(jnp.float32) * sign - one)
+                rows.append(shift[0, n, 1, row, :].astype(jnp.float32))
+                rows.append(fraction[0, n, 0, row, :] * sign + one)
+                rows.append(fraction[0, n, 1, row, :])
+        out[pl.ds(r * 16, 16), :] = jnp.concatenate(rows, axis=0).astype(BF16)
 
 
 def run_prepare(grid, older, params):
@@ -203,20 +236,31 @@
     )(newest[1], newest[2], taps)
 
 
-def run_step(grid, sides, newest, prepared, weights):
+def run_pack(grid, arrays):
+    return pl.pallas_call(
+        pack_kernel,
+        out_shape=jax.ShapeDtypeStruct((ROWS * 16, W), BF16),
+        in_specs=[SMEM] + [VMEM] * 4,
+        out_specs=VMEM,
+        compiler_params=pltpu.CompilerParams(vmem_limit_bytes=16 * 2**20),
+        name="pack",
+    )(grid[1], *arrays)
+
+
+def run_step(grid, sides, newest, prepared, weights, wide):
     operands = list(grid)
     for trio in sides:
         operands += list(trio)
     operands += (list(newest[:2]) if newest else []) + list(prepared) + list(weights)
     return pl.pallas_call(
-        functools.partial(step_kernel, max(0, len(prepared) - 1), len(sides)),
+        functools.partial(step_kernel, max(0, len(prepared) - 1), len(sides), wide),
         out_shape=jax.ShapeDtypeStruct((ROWS * C, W), BF16),
         in_specs=[SMEM, SMEM] + [VMEM] * (len(operands) - 2),
         out_specs=VMEM,
         scratch_shapes=[
             pltpu.VMEM((C, EARLY * W), BF16),
-            pltpu.VMEM((EXT * C, W), BF16),
-            pltpu.VMEM(((ROWS + 2) * C, W), BF16),
+            pltpu.VMEM((EXT * C * (3 if wide else 1), W), BF16),
+            pltpu.VMEM(((ROWS + 2) * C * (3 if wide else 1), W), BF16),
         ],
         compiler_params=pltpu.CompilerParams(vmem_limit_bytes=16 * 2**20),
         cost_estimate=pl.CostEstimate(flops=10**8, bytes_accessed=2**20, transcendentals=0),
@@ -251,9 +295,11 @@
     return lax.ppermute(for_across, axes, across), lax.ppermute(for_beside, axes, beside)
 
 
-def conv_matrix(kernel, odd):
+def conv_matrix(kernel, odd, wide):
     taps = kernel.reshape(C, 3, 3, C)
     taps = jnp.where(odd, taps[:, ::-1], taps)
+    if wide:
+        return taps.reshape(C, 9 * C)
     return taps.transpose(2, 0, 1, 3).reshape(3 * C, 3 * C)
 
 
@@ -286,16 +332,7 @@
 
     own = oriented(frames[0].transpose(1, 0, 2), 0).reshape(ROWS * C, W)
 
-    raw = jnp.concatenate(
-        [
-            jnp.concatenate([back_shift.astype(jnp.float32), back_fraction], axis=2),
-            jnp.concatenate([ahead_shift.astype(jnp.float32), ahead_fraction], axis=2),
-        ]
-    )
-    first = jnp.where(odd, -1.0 - raw[:, :, 0:1], raw[:, :, 0:1])
-    third = jnp.where(odd, 1.0 - raw[:, :, 2:3], raw[:, :, 2:3])
-    raw = jnp.concatenate([first, raw[:, :, 1:2], third, raw[:, :, 3:4]], axis=2).astype(BF16)
-    own_params = oriented(raw.transpose(3, 0, 1, 2, 4), 0).reshape(ROWS * 16, W)
+    own_params = run_pack(grid, (back_shift, back_fraction, ahead_shift, ahead_fraction))
     mine = jnp.concatenate([own, own_params], axis=0)
     other = lax.ppermute(mine, "tile", [(q, mirror(q)) for q in range(lax.axis_size("tile"))])
     for_even = jnp.where(upper, other, mine)
@@ -330,7 +367,7 @@
             if n:
                 taps, *older = run_prepare(grid, history[1] if n > 1 else None, params[way, t])
                 prepared = [taps, run_middle(history[0], taps)] + older
-            new = run_step(grid, sides, history[0] if n else None, prepared, weights)
+            new = run_step(grid, sides, history[0] if n else None, prepared, weights, bool(extra))
             if n + 1 < FRAMES or not extra:
                 far, near = swap(new, new)
                 done[t] = (far, new, near)
@@ -339,8 +376,8 @@
                 done[t] = (None, new, None)
         return done
 
-    back_weights = (back_mixer, conv_matrix(back_inner, odd), conv_matrix(back_outer, odd))
-    ahead_weights = (ahead_mixer, conv_matrix(ahead_inner, odd), conv_matrix(ahead_outer, odd))
+    back_weights = (back_mixer, conv_matrix(back_inner, odd, False), conv_matrix(back_outer, odd, False))
+    ahead_weights = (ahead_mixer, conv_matrix(ahead_inner, odd, True), conv_matrix(ahead_outer, odd, True))
     back = chain(range(FRAMES - 1, -1, -1), 0, None, back_weights)
     ahead = chain(range(FRAMES), 1, back, ahead_weights)
 

time: 184 us -> 185 us (level)
  the two profiles are of different devices: /device:TPU:8 before, /device:TPU:10 now
where the time goes in v6:
time: 185 us; the launch traced here: 184 us
  starting transfers between devices  110 us (59%)
  waiting for transfers between devices  31 us (17%)
  Pallas kernels  29.7 us (16%)
  local copies, waits for them, and re-layouts  10.4 us (6%)
    ppermute x16, starting transfers between devices, swap(): lax.ppermute(for_beside, axes, beside)  53.9 us
    ppermute x16, starting transfers between devices, swap(): lax.ppermute(for_across, axes, across)  36.5 us
    pallas_call x16, Pallas kernels, run_step(): pl.pallas_call(functools.partial(step_kernel, max(0, len(prepared) - 1),...  18.2 us
    all_to_all x1, waiting for transfers between devices, shards(): lax.all_to_all(jnp.broadcast_to(jnp.stack([for_even, for_odd])[None], (FR...  14.3 us
    ppermute x1, starting transfers between devices, shards(): lax.ppermute(mine, 'tile', [(q, mirror(q)) for q in range(lax.axis_size('...  10.9 us
    pallas_call x14, Pallas kernels, run_prepare(): pl.pallas_call(functools.partial(prepare_kernel, 2 if older else 1), out_...  7.84 us
    all_to_all x1, starting transfers between devices, shards(): lax.all_to_all(jnp.broadcast_to(jnp.stack([for_even, for_odd])[None], (FR...  7.55 us
    unnamed x37, local copies, waits for them, and re-layouts  6.51 us
  transfers between devices with their start and end apart: 35, of which 19 were waited for; matrix products, arithmetic and copies ran while one was open for 2% of the time, Pallas kernels for 6%

profile of v6, /device:TPU:10, one launch (start us, length us, event | category | flops | bytes accessed | tf_op | source)
XLA Modules:
  0.0 184.0 jit_solution(5905334287303034757)
XLA Ops:
  2.3 10.9 %collective-permute-start = (bf16[320,128]{1,0:T(8,128)(2,1)S(1)}, bf16[320,128]{1,0:T(8,128)(2,1)S(1)}, u32[]{:S(2)}, u32[]{:S(2)}) collective-permute-start(bf16[320,128]{1,0:T(8,128)(2,1)S(1)} %pad_maximum_fusion.4), channel_id=1, source_target_pairs={{0,14},{1,15},{2,12},{3,13},{4,10},{5,11},{6,8},{7,9},{8,6},{9,7},... | collective-permute-start | bytes 245768 | tf_op jit(solution)/shard_map/ppermute | solution.py:337
  13.3 4.1 %collective-permute-done = bf16[320,128]{1,0:T(8,128)(2,1)S(1)} collective-permute-done((bf16[320,128]{1,0:T(8,128)(2,1)S(1)}, bf16[320,128]{1,0:T(8,128)(2,1)S(1)}, u32[]{:S(2)}, u32[]{:S(2)}) %collective-permute-start) | collective-permute-done | bytes 81952 | tf_op jit(solution)/shard_map/ppermute | solution.py:337
  18.5 7.5 %all-to-all-start = ((bf16[8,320,128]{2,1,0:T(8,128)(2,1)}), bf16[8,320,128]{2,1,0:T(8,128)(2,1)S(1)}, u32[]{:S(2)}, u32[]{:S(2)}) async-start(bf16[8,320,128]{2,1,0:T(8,128)(2,1)} %bitcast.7), calls=%async_computation | async-start | bytes 1310720 | tf_op jit(solution)/shard_map/all_to_all | solution.py:340
  30.8 14.3 %all-to-all-done = bf16[8,320,128]{2,1,0:T(8,128)(2,1)S(1)} async-done(((bf16[8,320,128]{2,1,0:T(8,128)(2,1)}), bf16[8,320,128]{2,1,0:T(8,128)(2,1)S(1)}, u32[]{:S(2)}, u32[]{:S(2)}) %all-to-all-start) | async-done | bytes 655392 | tf_op jit(solution)/shard_map/all_to_all | solution.py:340
  45.1 1.9 %collective-permute-start.1 = (bf16[8,160,128]{2,1,0:T(8,128)(2,1)S(1)}, bf16[8,160,128]{2,1,0:T(8,128)(2,1)S(1)}, u32[]{:S(2)}, u32[]{:S(2)}) collective-permute-start(bf16[8,160,128]{2,1,0:T(8,128)(2,1)S(1)} %pad_maximum_fusion), channel_id=1, source_target_pairs={{1,2},{2,1},{3,4},{4,3},{5,6},{6,5},{7,70},{70,7},{71,68},{68,71},... | collective-permute-start | bytes 983048 | tf_op jit(solution)/shard_map/ppermute | solution.py:295
  47.1 4.4 %collective-permute-start.2 = (bf16[8,160,128]{2,1,0:T(8,128)(2,1)S(1)}, bf16[8,160,128]{2,1,0:T(8,128)(2,1)S(1)}, u32[]{:S(2)}, u32[]{:S(2)}) collective-permute-start(bf16[8,160,128]{2,1,0:T(8,128)(2,1)S(1)} %pad_maximum_fusion.1), channel_id=1, source_target_pairs={{0,1},{1,0},{2,3},{3,2},{4,5},{5,4},{6,7},{7,6},{70,71},{71,70},{6... | collective-permute-start | bytes 983048 | tf_op jit(solution)/shard_map/ppermute | solution.py:295
  51.7 1.8 collective-permute-done.1
  55.3 1.9 %collective-permute-start.3 = (bf16[256,128]{1,0:T(8,128)(2,1)S(1)}, bf16[256,128]{1,0:T(8,128)(2,1)S(1)}, u32[]{:S(2)}, u32[]{:S(2)}) collective-permute-start(bf16[256,128]{1,0:T(8,128)(2,1)S(1)} %step.16.own.refs_4_.refs_1_), channel_id=1, source_target_pairs={{1,2},{2,1},{3,4},{4,3},{5,6},{6,5},{7,70},{70,7},{71,68},{68,71},... | collective-permute-start | bytes 196616 | tf_op jit(solution)/shard_map/ppermute | solution.py:295
  57.3 5.3 %collective-permute-start.4 = (bf16[256,128]{1,0:T(8,128)(2,1)S(1)}, bf16[256,128]{1,0:T(8,128)(2,1)S(1)}, u32[]{:S(2)}, u32[]{:S(2)}) collective-permute-start(bf16[256,128]{1,0:T(8,128)(2,1)S(1)} %step.16.own.refs_4_.refs_1_), channel_id=1, source_target_pairs={{0,1},{1,0},{2,3},{3,2},{4,5},{5,4},{6,7},{7,6},{70,71},{71,70},{6... | collective-permute-start | bytes 196616 | tf_op jit(solution)/shard_map/ppermute | solution.py:295
  64.3 1.1 step.17.own.refs_4_.refs_1_
  65.4 1.9 %collective-permute-start.5 = (bf16[256,128]{1,0:T(8,128)(2,1)S(1)}, bf16[256,128]{1,0:T(8,128)(2,1)S(1)}, u32[]{:S(2)}, u32[]{:S(2)}) collective-permute-start(bf16[256,128]{1,0:T(8,128)(2,1)S(1)} %step.17.own.refs_4_.refs_1_), channel_id=1, source_target_pairs={{1,2},{2,1},{3,4},{4,3},{5,6},{6,5},{7,70},{70,7},{71,68},{68,71},... | collective-permute-start | bytes 196616 | tf_op jit(solution)/shard_map/ppermute | solution.py:295
  67.4 2.8 %collective-permute-start.6 = (bf16[256,128]{1,0:T(8,128)(2,1)S(1)}, bf16[256,128]{1,0:T(8,128)(2,1)S(1)}, u32[]{:S(2)}, u32[]{:S(2)}) collective-permute-start(bf16[256,128]{1,0:T(8,128)(2,1)S(1)} %step.17.own.refs_4_.refs_1_), channel_id=1, source_target_pairs={{0,1},{1,0},{2,3},{3,2},{4,5},{5,4},{6,7},{7,6},{70,71},{71,70},{6... | collective-permute-start | bytes 196616 | tf_op jit(solution)/shard_map/ppermute | solution.py:295
  71.3 1.1 step.18.own.refs_4_.refs_1_
  72.4 3.1 %collective-permute-start.7 = (bf16[256,128]{1,0:T(8,128)(2,1)S(1)}, bf16[256,128]{1,0:T(8,128)(2,1)S(1)}, u32[]{:S(2)}, u32[]{:S(2)}) collective-permute-start(bf16[256,128]{1,0:T(8,128)(2,1)S(1)} %step.18.own.refs_4_.refs_1_), channel_id=1, source_target_pairs={{1,2},{2,1},{3,4},{4,3},{5,6},{6,5},{7,70},{70,7},{71,68},{68,71},... | collective-permute-start | bytes 196616 | tf_op jit(solution)/shard_map/ppermute | solution.py:295
  75.5 2.8 %collective-permute-start.8 = (bf16[256,128]{1,0:T(8,128)(2,1)S(1)}, bf16[256,128]{1,0:T(8,128)(2,1)S(1)}, u32[]{:S(2)}, u32[]{:S(2)}) collective-permute-start(bf16[256,128]{1,0:T(8,128)(2,1)S(1)} %step.18.own.refs_4_.refs_1_), channel_id=1, source_target_pairs={{0,1},{1,0},{2,3},{3,2},{4,5},{5,4},{6,7},{7,6},{70,71},{71,70},{6... | collective-permute-start | bytes 196616 | tf_op jit(solution)/shard_map/ppermute | solution.py:295
  80.6 1.9 %collective-permute-start.9 = (bf16[256,128]{1,0:T(8,128)(2,1)S(1)}, bf16[256,128]{1,0:T(8,128)(2,1)S(1)}, u32[]{:S(2)}, u32[]{:S(2)}) collective-permute-start(bf16[256,128]{1,0:T(8,128)(2,1)S(1)} %step.19.own.refs_4_.refs_1_), channel_id=1, source_target_pairs={{1,2},{2,1},{3,4},{4,3},{5,6},{6,5},{7,70},{70,7},{71,68},{68,71},... | collective-permute-start | bytes 196616 | tf_op jit(solution)/shard_map/ppermute | solution.py:295
  82.5 3.4 %collective-permute-start.10 = (bf16[256,128]{1,0:T(8,128)(2,1)S(1)}, bf16[256,128]{1,0:T(8,128)(2,1)S(1)}, u32[]{:S(2)}, u32[]{:S(2)}) collective-permute-start(bf16[256,128]{1,0:T(8,128)(2,1)S(1)} %step.19.own.refs_4_.refs_1_), channel_id=1, source_target_pairs={{0,1},{1,0},{2,3},{3,2},{4,5},{5,4},{6,7},{7,6},{70,71},{71,70},{6... | collective-permute-start | bytes 196616 | tf_op jit(solution)/shard_map/ppermute | solution.py:295
  88.2 2.5 %collective-permute-start.11 = (bf16[256,128]{1,0:T(8,128)(2,1)S(1)}, bf16[256,128]{1,0:T(8,128)(2,1)S(1)}, u32[]{:S(2)}, u32[]{:S(2)}) collective-permute-start(bf16[256,128]{1,0:T(8,128)(2,1)S(1)} %step.20.own.refs_4_.refs_1_), channel_id=1, source_target_pairs={{1,2},{2,1},{3,4},{4,3},{5,6},{6,5},{7,70},{70,7},{71,68},{68,71},... | collective-permute-start | bytes 196616 | tf_op jit(solution)/shard_map/ppermute | solution.py:295
  90.7 3.3 %collective-permute-start.12 = (bf16[256,128]{1,0:T(8,128)(2,1)S(1)}, bf16[256,128]{1,0:T(8,128)(2,1)S(1)}, u32[]{:S(2)}, u32[]{:S(2)}) collective-permute-start(bf16[256,128]{1,0:T(8,128)(2,1)S(1)} %step.20.own.refs_4_.refs_1_), channel_id=1, source_target_pairs={{0,1},{1,0},{2,3},{3,2},{4,5},{5,4},{6,7},{7,6},{70,71},{71,70},{6... | collective-permute-start | bytes 196616 | tf_op jit(solution)/shard_map/ppermute | solution.py:295
  96.1 2.2 %collective-permute-start.13 = (bf16[256,128]{1,0:T(8,128)(2,1)S(1)}, bf16[256,128]{1,0:T(8,128)(2,1)S(1)}, u32[]{:S(2)}, u32[]{:S(2)}) collective-permute-start(bf16[256,128]{1,0:T(8,128)(2,1)S(1)} %step.21.own.refs_4_.refs_1_), channel_id=1, source_target_pairs={{1,2},{2,1},{3,4},{4,3},{5,6},{6,5},{7,70},{70,7},{71,68},{68,71},... | collective-permute-start | bytes 196616 | tf_op jit(solution)/shard_map/ppermute | solution.py:295
  98.3 3.2 %collective-permute-start.14 = (bf16[256,128]{1,0:T(8,128)(2,1)S(1)}, bf16[256,128]{1,0:T(8,128)(2,1)S(1)}, u32[]{:S(2)}, u32[]{:S(2)}) collective-permute-start(bf16[256,128]{1,0:T(8,128)(2,1)S(1)} %step.21.own.refs_4_.refs_1_), channel_id=1, source_target_pairs={{0,1},{1,0},{2,3},{3,2},{4,5},{5,4},{6,7},{7,6},{70,71},{71,70},{6... | collective-permute-start | bytes 196616 | tf_op jit(solution)/shard_map/ppermute | solution.py:295
  103.7 2.5 %collective-permute-start.15 = (bf16[256,128]{1,0:T(8,128)(2,1)S(1)}, bf16[256,128]{1,0:T(8,128)(2,1)S(1)}, u32[]{:S(2)}, u32[]{:S(2)}) collective-permute-start(bf16[256,128]{1,0:T(8,128)(2,1)S(1)} %step.22.own.refs_4_), channel_id=1, source_target_pairs={{1,2},{2,1},{3,4},{4,3},{5,6},{6,5},{7,70},{70,7},{71,68},{68,71},... | collective-permute-start | bytes 196616 | tf_op jit(solution)/shard_map/ppermute | solution.py:295
  106.2 3.2 %collective-permute-start.16 = (bf16[256,128]{1,0:T(8,128)(2,1)S(1)}, bf16[256,128]{1,0:T(8,128)(2,1)S(1)}, u32[]{:S(2)}, u32[]{:S(2)}) collective-permute-start(bf16[256,128]{1,0:T(8,128)(2,1)S(1)} %step.22.own.refs_4_), channel_id=1, source_target_pairs={{0,1},{1,0},{2,3},{3,2},{4,5},{5,4},{6,7},{7,6},{70,71},{71,70},{6... | collective-permute-start | bytes 196616 | tf_op jit(solution)/shard_map/ppermute | solution.py:295
  111.7 2.2 %collective-permute-start.17 = (bf16[256,128]{1,0:T(8,128)(2,1)S(1)}, bf16[256,128]{1,0:T(8,128)(2,1)S(1)}, u32[]{:S(2)}, u32[]{:S(2)}) collective-permute-start(bf16[256,128]{1,0:T(8,128)(2,1)S(1)} %step.23.refs_4_), channel_id=1, source_target_pairs={{1,2},{2,1},{3,4},{4,3},{5,6},{6,5},{7,70},{70,7},{71,68},{68,71},... | collective-permute-start | bytes 196616 | tf_op jit(solution)/shard_map/ppermute | solution.py:295
  113.8 3.2 %collective-permute-start.18 = (bf16[256,128]{1,0:T(8,128)(2,1)S(1)}, bf16[256,128]{1,0:T(8,128)(2,1)S(1)}, u32[]{:S(2)}, u32[]{:S(2)}) collective-permute-start(bf16[256,128]{1,0:T(8,128)(2,1)S(1)} %step.23.refs_4_), channel_id=1, source_target_pairs={{0,1},{1,0},{2,3},{3,2},{4,5},{5,4},{6,7},{7,6},{70,71},{71,70},{6... | collective-permute-start | bytes 196616 | tf_op jit(solution)/shard_map/ppermute | solution.py:295
  118.9 2.5 %collective-permute-start.19 = (bf16[256,128]{1,0:T(8,128)(2,1)S(1)}, bf16[256,128]{1,0:T(8,128)(2,1)S(1)}, u32[]{:S(2)}, u32[]{:S(2)}) collective-permute-start(bf16[256,128]{1,0:T(8,128)(2,1)S(1)} %step.24.own.refs_7_.refs_1_), channel_id=1, source_target_pairs={{1,2},{2,1},{3,4},{4,3},{5,6},{6,5},{7,70},{70,7},{71,68},{68,71},... | collective-permute-start | bytes 196616 | tf_op jit(solution)/shard_map/ppermute | solution.py:295
  121.5 3.2 %collective-permute-start.20 = (bf16[256,128]{1,0:T(8,128)(2,1)S(1)}, bf16[256,128]{1,0:T(8,128)(2,1)S(1)}, u32[]{:S(2)}, u32[]{:S(2)}) collective-permute-start(bf16[256,128]{1,0:T(8,128)(2,1)S(1)} %step.24.own.refs_7_.refs_1_), channel_id=1, source_target_pairs={{0,1},{1,0},{2,3},{3,2},{4,5},{5,4},{6,7},{7,6},{70,71},{71,70},{6... | collective-permute-start | bytes 196616 | tf_op jit(solution)/shard_map/ppermute | solution.py:295
  125.8 1.2 step.25.own.refs_7_.refs_1_
  126.9 2.2 %collective-permute-start.21 = (bf16[256,128]{1,0:T(8,128)(2,1)S(1)}, bf16[256,128]{1,0:T(8,128)(2,1)S(1)}, u32[]{:S(2)}, u32[]{:S(2)}) collective-permute-start(bf16[256,128]{1,0:T(8,128)(2,1)S(1)} %step.25.own.refs_7_.refs_1_), channel_id=1, source_target_pairs={{1,2},{2,1},{3,4},{4,3},{5,6},{6,5},{7,70},{70,7},{71,68},{68,71},... | collective-permute-start | bytes 196616 | tf_op jit(solution)/shard_map/ppermute | solution.py:295
  129.1 3.4 %collective-permute-start.22 = (bf16[256,128]{1,0:T(8,128)(2,1)S(1)}, bf16[256,128]{1,0:T(8,128)(2,1)S(1)}, u32[]{:S(2)}, u32[]{:S(2)}) collective-permute-start(bf16[256,128]{1,0:T(8,128)(2,1)S(1)} %step.25.own.refs_7_.refs_1_), channel_id=1, source_target_pairs={{0,1},{1,0},{2,3},{3,2},{4,5},{5,4},{6,7},{7,6},{70,71},{71,70},{6... | collective-permute-start | bytes 196616 | tf_op jit(solution)/shard_map/ppermute | solution.py:295
  133.7 1.2 step.26.own.refs_7_.refs_1_
  134.9 2.2 %collective-permute-start.23 = (bf16[256,128]{1,0:T(8,128)(2,1)S(1)}, bf16[256,128]{1,0:T(8,128)(2,1)S(1)}, u32[]{:S(2)}, u32[]{:S(2)}) collective-permute-start(bf16[256,128]{1,0:T(8,128)(2,1)S(1)} %step.26.own.refs_7_.refs_1_), channel_id=1, source_target_pairs={{1,2},{2,1},{3,4},{4,3},{5,6},{6,5},{7,70},{70,7},{71,68},{68,71},... | collective-permute-start | bytes 196616 | tf_op jit(solution)/shard_map/ppermute | solution.py:295
  137.1 3.2 %collective-permute-start.24 = (bf16[256,128]{1,0:T(8,128)(2,1)S(1)}, bf16[256,128]{1,0:T(8,128)(2,1)S(1)}, u32[]{:S(2)}, u32[]{:S(2)}) collective-permute-start(bf16[256,128]{1,0:T(8,128)(2,1)S(1)} %step.26.own.refs_7_.refs_1_), channel_id=1, source_target_pairs={{0,1},{1,0},{2,3},{3,2},{4,5},{5,4},{6,7},{7,6},{70,71},{71,70},{6... | collective-permute-start | bytes 196616 | tf_op jit(solution)/shard_map/ppermute | solution.py:295
  141.5 1.2 step.27.own.refs_7_.refs_1_
  142.7 2.4 %collective-permute-start.25 = (bf16[256,128]{1,0:T(8,128)(2,1)S(1)}, bf16[256,128]{1,0:T(8,128)(2,1)S(1)}, u32[]{:S(2)}, u32[]{:S(2)}) collective-permute-start(bf16[256,128]{1,0:T(8,128)(2,1)S(1)} %step.27.own.refs_7_.refs_1_), channel_id=1, source_target_pairs={{1,2},{2,1},{3,4},{4,3},{5,6},{6,5},{7,70},{70,7},{71,68},{68,71},... | collective-permute-start | bytes 196616 | tf_op jit(solution)/shard_map/ppermute | solution.py:295
  145.1 3.2 %collective-permute-start.26 = (bf16[256,128]{1,0:T(8,128)(2,1)S(1)}, bf16[256,128]{1,0:T(8,128)(2,1)S(1)}, u32[]{:S(2)}, u32[]{:S(2)}) collective-permute-start(bf16[256,128]{1,0:T(8,128)(2,1)S(1)} %step.27.own.refs_7_.refs_1_), channel_id=1, source_target_pairs={{0,1},{1,0},{2,3},{3,2},{4,5},{5,4},{6,7},{7,6},{70,71},{71,70},{6... | collective-permute-start | bytes 196616 | tf_op jit(solution)/shard_map/ppermute | solution.py:295
  149.5 1.2 step.28.own.refs_7_.refs_1_
  150.7 2.4 %collective-permute-start.27 = (bf16[256,128]{1,0:T(8,128)(2,1)S(1)}, bf16[256,128]{1,0:T(8,128)(2,1)S(1)}, u32[]{:S(2)}, u32[]{:S(2)}) collective-permute-start(bf16[256,128]{1,0:T(8,128)(2,1)S(1)} %step.28.own.refs_7_.refs_1_), channel_id=1, source_target_pairs={{1,2},{2,1},{3,4},{4,3},{5,6},{6,5},{7,70},{70,7},{71,68},{68,71},... | collective-permute-start | bytes 196616 | tf_op jit(solution)/shard_map/ppermute | solution.py:295
  153.1 3.2 %collective-permute-start.28 = (bf16[256,128]{1,0:T(8,128)(2,1)S(1)}, bf16[256,128]{1,0:T(8,128)(2,1)S(1)}, u32[]{:S(2)}, u32[]{:S(2)}) collective-permute-start(bf16[256,128]{1,0:T(8,128)(2,1)S(1)} %step.28.own.refs_7_.refs_1_), channel_id=1, source_target_pairs={{0,1},{1,0},{2,3},{3,2},{4,5},{5,4},{6,7},{7,6},{70,71},{71,70},{6... | collective-permute-start | bytes 196616 | tf_op jit(solution)/shard_map/ppermute | solution.py:295
  157.5 1.2 step.29.own.refs_7_.refs_1_
  158.7 2.4 %collective-permute-start.29 = (bf16[256,128]{1,0:T(8,128)(2,1)S(1)}, bf16[256,128]{1,0:T(8,128)(2,1)S(1)}, u32[]{:S(2)}, u32[]{:S(2)}) collective-permute-start(bf16[256,128]{1,0:T(8,128)(2,1)S(1)} %step.29.own.refs_7_.refs_1_), channel_id=1, source_target_pairs={{1,2},{2,1},{3,4},{4,3},{5,6},{6,5},{7,70},{70,7},{71,68},{68,71},... | collective-permute-start | bytes 196616 | tf_op jit(solution)/shard_map/ppermute | solution.py:295
  161.1 3.2 %collective-permute-start.30 = (bf16[256,128]{1,0:T(8,128)(2,1)S(1)}, bf16[256,128]{1,0:T(8,128)(2,1)S(1)}, u32[]{:S(2)}, u32[]{:S(2)}) collective-permute-start(bf16[256,128]{1,0:T(8,128)(2,1)S(1)} %step.29.own.refs_7_.refs_1_), channel_id=1, source_target_pairs={{0,1},{1,0},{2,3},{3,2},{4,5},{5,4},{6,7},{7,6},{70,71},{71,70},{6... | collective-permute-start | bytes 196616 | tf_op jit(solution)/shard_map/ppermute | solution.py:295
  165.4 1.2 step.30.own.refs_7_
  166.7 2.2 %collective-permute-start.31 = (bf16[256,128]{1,0:T(8,128)(2,1)S(1)}, bf16[256,128]{1,0:T(8,128)(2,1)S(1)}, u32[]{:S(2)}, u32[]{:S(2)}) collective-permute-start(bf16[256,128]{1,0:T(8,128)(2,1)S(1)} %step.30.own.refs_7_), channel_id=1, source_target_pairs={{1,2},{2,1},{3,4},{4,3},{5,6},{6,5},{7,70},{70,7},{71,68},{68,71},... | collective-permute-start | bytes 196616 | tf_op jit(solution)/shard_map/ppermute | solution.py:295
  168.9 3.2 %collective-permute-start.32 = (bf16[256,128]{1,0:T(8,128)(2,1)S(1)}, bf16[256,128]{1,0:T(8,128)(2,1)S(1)}, u32[]{:S(2)}, u32[]{:S(2)}) collective-permute-start(bf16[256,128]{1,0:T(8,128)(2,1)S(1)} %step.30.own.refs_7_), channel_id=1, source_target_pairs={{0,1},{1,0},{2,3},{3,2},{4,5},{5,4},{6,7},{7,6},{70,71},{71,70},{6... | collective-permute-start | bytes 196616 | tf_op jit(solution)/shard_map/ppermute | solution.py:295
  173.8 1.2 step.31
  175.1 1.3 collective-permute-start.33
  176.4 6.3 %collective-permute-done.33 = bf16[2,256,128]{2,1,0:T(8,128)(2,1)S(1)} collective-permute-done((bf16[2,256,128]{2,1,0:T(8,128)(2,1)S(1)}, bf16[2,256,128]{2,1,0:T(8,128)(2,1)S(1)}, u32[]{:S(2)}, u32[]{:S(2)}) %collective-permute-start.33) | collective-permute-done | bytes 131104 | tf_op jit(solution)/shard_map/ppermute | solution.py:400
  (148 shorter events, 34.9 us)
Async XLA Ops:
  1.5 0.7 copy-start.10
  1.5 0.7 copy-start.11
  2.3 15.1 %collective-permute-start = (bf16[320,128]{1,0:T(8,128)(2,1)S(1)}, bf16[320,128]{1,0:T(8,128)(2,1)S(1)}, u32[]{:S(2)}, u32[]{:S(2)}) collective-permute-start(bf16[320,128]{1,0:T(8,128)(2,1)S(1)} %pad_maximum_fusion.4), channel_id=1, source_target_pairs={{0,14},{1,15},{2,12},{3,13},{4,10},{5,11},{6,8},{7,9},{8,6},{9,7},... | collective-permute-start | bytes 245768 | tf_op jit(solution)/shard_map/ppermute | solution.py:337
  18.5 26.6 %all-to-all-start = ((bf16[8,320,128]{2,1,0:T(8,128)(2,1)}), bf16[8,320,128]{2,1,0:T(8,128)(2,1)S(1)}, u32[]{:S(2)}, u32[]{:S(2)}) async-start(bf16[8,320,128]{2,1,0:T(8,128)(2,1)} %bitcast.7), calls=%async_computation | async-start | bytes 1310720 | tf_op jit(solution)/shard_map/all_to_all | solution.py:340
  26.0 0.9 copy-start.12
  26.9 0.9 copy-start.13
  28.5 0.9 copy-start.14
  29.4 0.9 copy-start.15
  45.1 8.4 %collective-permute-start.1 = (bf16[8,160,128]{2,1,0:T(8,128)(2,1)S(1)}, bf16[8,160,128]{2,1,0:T(8,128)(2,1)S(1)}, u32[]{:S(2)}, u32[]{:S(2)}) collective-permute-start(bf16[8,160,128]{2,1,0:T(8,128)(2,1)S(1)} %pad_maximum_fusion), channel_id=1, source_target_pairs={{1,2},{2,1},{3,4},{4,3},{5,6},{6,5},{7,70},{70,7},{71,68},{68,71},... | collective-permute-start | bytes 983048 | tf_op jit(solution)/shard_map/ppermute | solution.py:295
  47.1 6.5 %collective-permute-start.2 = (bf16[8,160,128]{2,1,0:T(8,128)(2,1)S(1)}, bf16[8,160,128]{2,1,0:T(8,128)(2,1)S(1)}, u32[]{:S(2)}, u32[]{:S(2)}) collective-permute-start(bf16[8,160,128]{2,1,0:T(8,128)(2,1)S(1)} %pad_maximum_fusion.1), channel_id=1, source_target_pairs={{0,1},{1,0},{2,3},{3,2},{4,5},{5,4},{6,7},{7,6},{70,71},{71,70},{6... | collective-permute-start | bytes 983048 | tf_op jit(solution)/shard_map/ppermute | solution.py:295
  51.5 2.1 %copy-start.2 = (bf16[256,128]{1,0:T(8,128)(2,1)}, bf16[256,128]{1,0:T(8,128)(2,1)S(1)}, u32[]{:S(2)}) copy-start(bf16[256,128]{1,0:T(8,128)(2,1)S(1)} %get-tuple-element.57.refs_1_) | copy-start | bytes 196612
  53.6 0.8 copy-start.1
  53.6 1.7 copy-start.6
  55.3 9.0 %collective-permute-start.3 = (bf16[256,128]{1,0:T(8,128)(2,1)S(1)}, bf16[256,128]{1,0:T(8,128)(2,1)S(1)}, u32[]{:S(2)}, u32[]{:S(2)}) collective-permute-start(bf16[256,128]{1,0:T(8,128)(2,1)S(1)} %step.16.own.refs_4_.refs_1_), channel_id=1, source_target_pairs={{1,2},{2,1},{3,4},{4,3},{5,6},{6,5},{7,70},{70,7},{71,68},{68,71},... | collective-permute-start | bytes 196616 | tf_op jit(solution)/shard_map/ppermute | solution.py:295
  57.3 6.8 %collective-permute-start.4 = (bf16[256,128]{1,0:T(8,128)(2,1)S(1)}, bf16[256,128]{1,0:T(8,128)(2,1)S(1)}, u32[]{:S(2)}, u32[]{:S(2)}) collective-permute-start(bf16[256,128]{1,0:T(8,128)(2,1)S(1)} %step.16.own.refs_4_.refs_1_), channel_id=1, source_target_pairs={{0,1},{1,0},{2,3},{3,2},{4,5},{5,4},{6,7},{7,6},{70,71},{71,70},{6... | collective-permute-start | bytes 196616 | tf_op jit(solution)/shard_map/ppermute | solution.py:295
  65.4 5.9 %collective-permute-start.5 = (bf16[256,128]{1,0:T(8,128)(2,1)S(1)}, bf16[256,128]{1,0:T(8,128)(2,1)S(1)}, u32[]{:S(2)}, u32[]{:S(2)}) collective-permute-start(bf16[256,128]{1,0:T(8,128)(2,1)S(1)} %step.17.own.refs_4_.refs_1_), channel_id=1, source_target_pairs={{1,2},{2,1},{3,4},{4,3},{5,6},{6,5},{7,70},{70,7},{71,68},{68,71},... | collective-permute-start | bytes 196616 | tf_op jit(solution)/shard_map/ppermute | solution.py:295
  67.4 3.7 %collective-permute-start.6 = (bf16[256,128]{1,0:T(8,128)(2,1)S(1)}, bf16[256,128]{1,0:T(8,128)(2,1)S(1)}, u32[]{:S(2)}, u32[]{:S(2)}) collective-permute-start(bf16[256,128]{1,0:T(8,128)(2,1)S(1)} %step.17.own.refs_4_.refs_1_), channel_id=1, source_target_pairs={{0,1},{1,0},{2,3},{3,2},{4,5},{5,4},{6,7},{7,6},{70,71},{71,70},{6... | collective-permute-start | bytes 196616 | tf_op jit(solution)/shard_map/ppermute | solution.py:295
  72.4 7.1 %collective-permute-start.7 = (bf16[256,128]{1,0:T(8,128)(2,1)S(1)}, bf16[256,128]{1,0:T(8,128)(2,1)S(1)}, u32[]{:S(2)}, u32[]{:S(2)}) collective-permute-start(bf16[256,128]{1,0:T(8,128)(2,1)S(1)} %step.18.own.refs_4_.refs_1_), channel_id=1, source_target_pairs={{1,2},{2,1},{3,4},{4,3},{5,6},{6,5},{7,70},{70,7},{71,68},{68,71},... | collective-permute-start | bytes 196616 | tf_op jit(solution)/shard_map/ppermute | solution.py:295
  75.5 3.7 %collective-permute-start.8 = (bf16[256,128]{1,0:T(8,128)(2,1)S(1)}, bf16[256,128]{1,0:T(8,128)(2,1)S(1)}, u32[]{:S(2)}, u32[]{:S(2)}) collective-permute-start(bf16[256,128]{1,0:T(8,128)(2,1)S(1)} %step.18.own.refs_4_.refs_1_), channel_id=1, source_target_pairs={{0,1},{1,0},{2,3},{3,2},{4,5},{5,4},{6,7},{7,6},{70,71},{71,70},{6... | collective-permute-start | bytes 196616 | tf_op jit(solution)/shard_map/ppermute | solution.py:295
  80.6 6.5 %collective-permute-start.9 = (bf16[256,128]{1,0:T(8,128)(2,1)S(1)}, bf16[256,128]{1,0:T(8,128)(2,1)S(1)}, u32[]{:S(2)}, u32[]{:S(2)}) collective-permute-start(bf16[256,128]{1,0:T(8,128)(2,1)S(1)} %step.19.own.refs_4_.refs_1_), channel_id=1, source_target_pairs={{1,2},{2,1},{3,4},{4,3},{5,6},{6,5},{7,70},{70,7},{71,68},{68,71},... | collective-permute-start | bytes 196616 | tf_op jit(solution)/shard_map/ppermute | solution.py:295
  82.5 4.3 %collective-permute-start.10 = (bf16[256,128]{1,0:T(8,128)(2,1)S(1)}, bf16[256,128]{1,0:T(8,128)(2,1)S(1)}, u32[]{:S(2)}, u32[]{:S(2)}) collective-permute-start(bf16[256,128]{1,0:T(8,128)(2,1)S(1)} %step.19.own.refs_4_.refs_1_), channel_id=1, source_target_pairs={{0,1},{1,0},{2,3},{3,2},{4,5},{5,4},{6,7},{7,6},{70,71},{71,70},{6... | collective-permute-start | bytes 196616 | tf_op jit(solution)/shard_map/ppermute | solution.py:295
  88.2 6.8 %collective-permute-start.11 = (bf16[256,128]{1,0:T(8,128)(2,1)S(1)}, bf16[256,128]{1,0:T(8,128)(2,1)S(1)}, u32[]{:S(2)}, u32[]{:S(2)}) collective-permute-start(bf16[256,128]{1,0:T(8,128)(2,1)S(1)} %step.20.own.refs_4_.refs_1_), channel_id=1, source_target_pairs={{1,2},{2,1},{3,4},{4,3},{5,6},{6,5},{7,70},{70,7},{71,68},{68,71},... | collective-permute-start | bytes 196616 | tf_op jit(solution)/shard_map/ppermute | solution.py:295
  90.7 4.1 %collective-permute-start.12 = (bf16[256,128]{1,0:T(8,128)(2,1)S(1)}, bf16[256,128]{1,0:T(8,128)(2,1)S(1)}, u32[]{:S(2)}, u32[]{:S(2)}) collective-permute-start(bf16[256,128]{1,0:T(8,128)(2,1)S(1)} %step.20.own.refs_4_.refs_1_), channel_id=1, source_target_pairs={{0,1},{1,0},{2,3},{3,2},{4,5},{5,4},{6,7},{7,6},{70,71},{71,70},{6... | collective-permute-start | bytes 196616 | tf_op jit(solution)/shard_map/ppermute | solution.py:295
  96.1 6.5 %collective-permute-start.13 = (bf16[256,128]{1,0:T(8,128)(2,1)S(1)}, bf16[256,128]{1,0:T(8,128)(2,1)S(1)}, u32[]{:S(2)}, u32[]{:S(2)}) collective-permute-start(bf16[256,128]{1,0:T(8,128)(2,1)S(1)} %step.21.own.refs_4_.refs_1_), channel_id=1, source_target_pairs={{1,2},{2,1},{3,4},{4,3},{5,6},{6,5},{7,70},{70,7},{71,68},{68,71},... | collective-permute-start | bytes 196616 | tf_op jit(solution)/shard_map/ppermute | solution.py:295
  98.3 4.0 %collective-permute-start.14 = (bf16[256,128]{1,0:T(8,128)(2,1)S(1)}, bf16[256,128]{1,0:T(8,128)(2,1)S(1)}, u32[]{:S(2)}, u32[]{:S(2)}) collective-permute-start(bf16[256,128]{1,0:T(8,128)(2,1)S(1)} %step.21.own.refs_4_.refs_1_), channel_id=1, source_target_pairs={{0,1},{1,0},{2,3},{3,2},{4,5},{5,4},{6,7},{7,6},{70,71},{71,70},{6... | collective-permute-start | bytes 196616 | tf_op jit(solution)/shard_map/ppermute | solution.py:295
  103.7 6.8 %collective-permute-start.15 = (bf16[256,128]{1,0:T(8,128)(2,1)S(1)}, bf16[256,128]{1,0:T(8,128)(2,1)S(1)}, u32[]{:S(2)}, u32[]{:S(2)}) collective-permute-start(bf16[256,128]{1,0:T(8,128)(2,1)S(1)} %step.22.own.refs_4_), channel_id=1, source_target_pairs={{1,2},{2,1},{3,4},{4,3},{5,6},{6,5},{7,70},{70,7},{71,68},{68,71},... | collective-permute-start | bytes 196616 | tf_op jit(solution)/shard_map/ppermute | solution.py:295
  106.2 4.0 %collective-permute-start.16 = (bf16[256,128]{1,0:T(8,128)(2,1)S(1)}, bf16[256,128]{1,0:T(8,128)(2,1)S(1)}, u32[]{:S(2)}, u32[]{:S(2)}) collective-permute-start(bf16[256,128]{1,0:T(8,128)(2,1)S(1)} %step.22.own.refs_4_), channel_id=1, source_target_pairs={{0,1},{1,0},{2,3},{3,2},{4,5},{5,4},{6,7},{7,6},{70,71},{71,70},{6... | collective-permute-start | bytes 196616 | tf_op jit(solution)/shard_map/ppermute | solution.py:295
  111.7 6.2 %copy-start = (bf16[64,256]{1,0:T(8,128)(2,1)S(1)}, bf16[64,256]{1,0:T(8,128)(2,1)}, u32[]{:S(2)}) copy-start(bf16[64,256]{1,0:T(8,128)(2,1)} %refs_11_.11) | copy-start | bytes 98308
  111.7 5.6 %collective-permute-start.17 = (bf16[256,128]{1,0:T(8,128)(2,1)S(1)}, bf16[256,128]{1,0:T(8,128)(2,1)S(1)}, u32[]{:S(2)}, u32[]{:S(2)}) collective-permute-start(bf16[256,128]{1,0:T(8,128)(2,1)S(1)} %step.23.refs_4_), channel_id=1, source_target_pairs={{1,2},{2,1},{3,4},{4,3},{5,6},{6,5},{7,70},{70,7},{71,68},{68,71},... | collective-permute-start | bytes 196616 | tf_op jit(solution)/shard_map/ppermute | solution.py:295
  113.8 4.0 %collective-permute-start.18 = (bf16[256,128]{1,0:T(8,128)(2,1)S(1)}, bf16[256,128]{1,0:T(8,128)(2,1)S(1)}, u32[]{:S(2)}, u32[]{:S(2)}) collective-permute-start(bf16[256,128]{1,0:T(8,128)(2,1)S(1)} %step.23.refs_4_), channel_id=1, source_target_pairs={{0,1},{1,0},{2,3},{3,2},{4,5},{5,4},{6,7},{7,6},{70,71},{71,70},{6... | collective-permute-start | bytes 196616 | tf_op jit(solution)/shard_map/ppermute | solution.py:295
  118.9 6.8 %collective-permute-start.19 = (bf16[256,128]{1,0:T(8,128)(2,1)S(1)}, bf16[256,128]{1,0:T(8,128)(2,1)S(1)}, u32[]{:S(2)}, u32[]{:S(2)}) collective-permute-start(bf16[256,128]{1,0:T(8,128)(2,1)S(1)} %step.24.own.refs_7_.refs_1_), channel_id=1, source_target_pairs={{1,2},{2,1},{3,4},{4,3},{5,6},{6,5},{7,70},{70,7},{71,68},{68,71},... | collective-permute-start | bytes 196616 | tf_op jit(solution)/shard_map/ppermute | solution.py:295
  121.5 4.0 %collective-permute-start.20 = (bf16[256,128]{1,0:T(8,128)(2,1)S(1)}, bf16[256,128]{1,0:T(8,128)(2,1)S(1)}, u32[]{:S(2)}, u32[]{:S(2)}) collective-permute-start(bf16[256,128]{1,0:T(8,128)(2,1)S(1)} %step.24.own.refs_7_.refs_1_), channel_id=1, source_target_pairs={{0,1},{1,0},{2,3},{3,2},{4,5},{5,4},{6,7},{7,6},{70,71},{71,70},{6... | collective-permute-start | bytes 196616 | tf_op jit(solution)/shard_map/ppermute | solution.py:295
  126.9 6.8 %collective-permute-start.21 = (bf16[256,128]{1,0:T(8,128)(2,1)S(1)}, bf16[256,128]{1,0:T(8,128)(2,1)S(1)}, u32[]{:S(2)}, u32[]{:S(2)}) collective-permute-start(bf16[256,128]{1,0:T(8,128)(2,1)S(1)} %step.25.own.refs_7_.refs_1_), channel_id=1, source_target_pairs={{1,2},{2,1},{3,4},{4,3},{5,6},{6,5},{7,70},{70,7},{71,68},{68,71},... | collective-permute-start | bytes 196616 | tf_op jit(solution)/shard_map/ppermute | solution.py:295
  129.1 4.3 %collective-permute-start.22 = (bf16[256,128]{1,0:T(8,128)(2,1)S(1)}, bf16[256,128]{1,0:T(8,128)(2,1)S(1)}, u32[]{:S(2)}, u32[]{:S(2)}) collective-permute-start(bf16[256,128]{1,0:T(8,128)(2,1)S(1)} %step.25.own.refs_7_.refs_1_), channel_id=1, source_target_pairs={{0,1},{1,0},{2,3},{3,2},{4,5},{5,4},{6,7},{7,6},{70,71},{71,70},{6... | collective-permute-start | bytes 196616 | tf_op jit(solution)/shard_map/ppermute | solution.py:295
  134.9 6.5 %collective-permute-start.23 = (bf16[256,128]{1,0:T(8,128)(2,1)S(1)}, bf16[256,128]{1,0:T(8,128)(2,1)S(1)}, u32[]{:S(2)}, u32[]{:S(2)}) collective-permute-start(bf16[256,128]{1,0:T(8,128)(2,1)S(1)} %step.26.own.refs_7_.refs_1_), channel_id=1, source_target_pairs={{1,2},{2,1},{3,4},{4,3},{5,6},{6,5},{7,70},{70,7},{71,68},{68,71},... | collective-permute-start | bytes 196616 | tf_op jit(solution)/shard_map/ppermute | solution.py:295
  137.1 4.0 %collective-permute-start.24 = (bf16[256,128]{1,0:T(8,128)(2,1)S(1)}, bf16[256,128]{1,0:T(8,128)(2,1)S(1)}, u32[]{:S(2)}, u32[]{:S(2)}) collective-permute-start(bf16[256,128]{1,0:T(8,128)(2,1)S(1)} %step.26.own.refs_7_.refs_1_), channel_id=1, source_target_pairs={{0,1},{1,0},{2,3},{3,2},{4,5},{5,4},{6,7},{7,6},{70,71},{71,70},{6... | collective-permute-start | bytes 196616 | tf_op jit(solution)/shard_map/ppermute | solution.py:295
  142.7 6.8 %collective-permute-start.25 = (bf16[256,128]{1,0:T(8,128)(2,1)S(1)}, bf16[256,128]{1,0:T(8,128)(2,1)S(1)}, u32[]{:S(2)}, u32[]{:S(2)}) collective-permute-start(bf16[256,128]{1,0:T(8,128)(2,1)S(1)} %step.27.own.refs_7_.refs_1_), channel_id=1, source_target_pairs={{1,2},{2,1},{3,4},{4,3},{5,6},{6,5},{7,70},{70,7},{71,68},{68,71},... | collective-permute-start | bytes 196616 | tf_op jit(solution)/shard_map/ppermute | solution.py:295
  145.1 4.0 %collective-permute-start.26 = (bf16[256,128]{1,0:T(8,128)(2,1)S(1)}, bf16[256,128]{1,0:T(8,128)(2,1)S(1)}, u32[]{:S(2)}, u32[]{:S(2)}) collective-permute-start(bf16[256,128]{1,0:T(8,128)(2,1)S(1)} %step.27.own.refs_7_.refs_1_), channel_id=1, source_target_pairs={{0,1},{1,0},{2,3},{3,2},{4,5},{5,4},{6,7},{7,6},{70,71},{71,70},{6... | collective-permute-start | bytes 196616 | tf_op jit(solution)/shard_map/ppermute | solution.py:295
  150.7 6.8 %collective-permute-start.27 = (bf16[256,128]{1,0:T(8,128)(2,1)S(1)}, bf16[256,128]{1,0:T(8,128)(2,1)S(1)}, u32[]{:S(2)}, u32[]{:S(2)}) collective-permute-start(bf16[256,128]{1,0:T(8,128)(2,1)S(1)} %step.28.own.refs_7_.refs_1_), channel_id=1, source_target_pairs={{1,2},{2,1},{3,4},{4,3},{5,6},{6,5},{7,70},{70,7},{71,68},{68,71},... | collective-permute-start | bytes 196616 | tf_op jit(solution)/shard_map/ppermute | solution.py:295
  153.1 4.0 %collective-permute-start.28 = (bf16[256,128]{1,0:T(8,128)(2,1)S(1)}, bf16[256,128]{1,0:T(8,128)(2,1)S(1)}, u32[]{:S(2)}, u32[]{:S(2)}) collective-permute-start(bf16[256,128]{1,0:T(8,128)(2,1)S(1)} %step.28.own.refs_7_.refs_1_), channel_id=1, source_target_pairs={{0,1},{1,0},{2,3},{3,2},{4,5},{5,4},{6,7},{7,6},{70,71},{71,70},{6... | collective-permute-start | bytes 196616 | tf_op jit(solution)/shard_map/ppermute | solution.py:295
  158.7 6.8 %collective-permute-start.29 = (bf16[256,128]{1,0:T(8,128)(2,1)S(1)}, bf16[256,128]{1,0:T(8,128)(2,1)S(1)}, u32[]{:S(2)}, u32[]{:S(2)}) collective-permute-start(bf16[256,128]{1,0:T(8,128)(2,1)S(1)} %step.29.own.refs_7_.refs_1_), channel_id=1, source_target_pairs={{1,2},{2,1},{3,4},{4,3},{5,6},{6,5},{7,70},{70,7},{71,68},{68,71},... | collective-permute-start | bytes 196616 | tf_op jit(solution)/shard_map/ppermute | solution.py:295
  161.1 4.0 %collective-permute-start.30 = (bf16[256,128]{1,0:T(8,128)(2,1)S(1)}, bf16[256,128]{1,0:T(8,128)(2,1)S(1)}, u32[]{:S(2)}, u32[]{:S(2)}) collective-permute-start(bf16[256,128]{1,0:T(8,128)(2,1)S(1)} %step.29.own.refs_7_.refs_1_), channel_id=1, source_target_pairs={{0,1},{1,0},{2,3},{3,2},{4,5},{5,4},{6,7},{7,6},{70,71},{71,70},{6... | collective-permute-start | bytes 196616 | tf_op jit(solution)/shard_map/ppermute | solution.py:295
  166.7 6.6 %collective-permute-start.31 = (bf16[256,128]{1,0:T(8,128)(2,1)S(1)}, bf16[256,128]{1,0:T(8,128)(2,1)S(1)}, u32[]{:S(2)}, u32[]{:S(2)}) collective-permute-start(bf16[256,128]{1,0:T(8,128)(2,1)S(1)} %step.30.own.refs_7_), channel_id=1, source_target_pairs={{1,2},{2,1},{3,4},{4,3},{5,6},{6,5},{7,70},{70,7},{71,68},{68,71},... | collective-permute-start | bytes 196616 | tf_op jit(solution)/shard_map/ppermute | solution.py:295
  168.9 4.0 %collective-permute-start.32 = (bf16[256,128]{1,0:T(8,128)(2,1)S(1)}, bf16[256,128]{1,0:T(8,128)(2,1)S(1)}, u32[]{:S(2)}, u32[]{:S(2)}) collective-permute-start(bf16[256,128]{1,0:T(8,128)(2,1)S(1)} %step.30.own.refs_7_), channel_id=1, source_target_pairs={{0,1},{1,0},{2,3},{3,2},{4,5},{5,4},{6,7},{7,6},{70,71},{71,70},{6... | collective-permute-start | bytes 196616 | tf_op jit(solution)/shard_map/ppermute | solution.py:295
  173.0 0.8 copy-start.3
  173.0 0.8 copy-start.5
  173.0 0.8 copy-start.7
  175.1 7.6 %collective-permute-start.33 = (bf16[2,256,128]{2,1,0:T(8,128)(2,1)S(1)}, bf16[2,256,128]{2,1,0:T(8,128)(2,1)S(1)}, u32[]{:S(2)}, u32[]{:S(2)}) collective-permute-start(bf16[2,256,128]{2,1,0:T(8,128)(2,1)S(1)} %pad_maximum_fusion.3), channel_id=1, source_target_pairs={{0,64},{1,65},{2,66},{3,67},{4,68},{5,69},{6,70},{7,71},{16,80},{1... | collective-permute-start | bytes 393224 | tf_op jit(solution)/shard_map/ppermute | solution.py:400
  (3 other events, 2.0 us)

commit v7 on v5

--- a/solution.py
+++ b/solution.py
@@ -15,6 +15,11 @@
 FRAMES = 8
 EXT = ROWS + 2 * R
 EARLY = EXT // 2
+
+
+VMEM = pl.BlockSpec(memory_space=pltpu.VMEM)
+SMEM = pl.BlockSpec(memory_space=pltpu.SMEM)
+BF16 = jnp.bfloat16
 
 
 def leaky(values):
@@ -169,9 +174,20 @@
             out[pl.ds((r + n) * C, C), :] = (base + value).astype(jnp.bfloat16)
 
 
-VMEM = pl.BlockSpec(memory_space=pltpu.VMEM)
-SMEM = pl.BlockSpec(memory_space=pltpu.SMEM)
-BF16 = jnp.bfloat16
+def pack_kernel(sense, back_shift, back_fraction, ahead_shift, ahead_fraction, out):
+    turned = sense[0] < 0
+    sign = jnp.where(turned, -1.0, 1.0)
+    one = jnp.where(turned, 1.0, 0.0)
+    for r in range(ROWS):
+        row = pl.ds(jnp.where(turned, ROWS - 1 - r, r), 1)
+        rows = []
+        for shift, fraction in ((back_shift, back_fraction), (ahead_shift, ahead_fraction)):
+            for n in range(2):
+                rows.append(shift[0, n, 0, row, :].astype(jnp.float32) * sign - one)
+                rows.append(shift[0, n, 1, row, :].astype(jnp.float32))
+                rows.append(fraction[0, n, 0, row, :] * sign + one)
+                rows.append(fraction[0, n, 1, row, :])
+        out[pl.ds(r * 16, 16), :] = jnp.concatenate(rows, axis=0).astype(BF16)
 
 
 def run_prepare(grid, older, params):
@@ -201,6 +217,17 @@
         cost_estimate=pl.CostEstimate(flops=10**6, bytes_accessed=2**10, transcendentals=0),
         name="middle",
     )(newest[1], newest[2], taps)
+
+
+def run_pack(grid, arrays):
+    return pl.pallas_call(
+        pack_kernel,
+        out_shape=jax.ShapeDtypeStruct((ROWS * 16, W), BF16),
+        in_specs=[SMEM] + [VMEM] * 4,
+        out_specs=VMEM,
+        compiler_params=pltpu.CompilerParams(vmem_limit_bytes=16 * 2**20),
+        name="pack",
+    )(grid[1], *arrays)
 
 
 def run_step(grid, sides, newest, prepared, weights):
@@ -286,16 +313,7 @@
 
     own = oriented(frames[0].transpose(1, 0, 2), 0).reshape(ROWS * C, W)
 
-    raw = jnp.concatenate(
-        [
-            jnp.concatenate([back_shift.astype(jnp.float32), back_fraction], axis=2),
-            jnp.concatenate([ahead_shift.astype(jnp.float32), ahead_fraction], axis=2),
-        ]
-    )
-    first = jnp.where(odd, -1.0 - raw[:, :, 0:1], raw[:, :, 0:1])
-    third = jnp.where(odd, 1.0 - raw[:, :, 2:3], raw[:, :, 2:3])
-    raw = jnp.concatenate([first, raw[:, :, 1:2], third, raw[:, :, 3:4]], axis=2).astype(BF16)
-    own_params = oriented(raw.transpose(3, 0, 1, 2, 4), 0).reshape(ROWS * 16, W)
+    own_params = run_pack(grid, (back_shift, back_fraction, ahead_shift, ahead_fraction))
     mine = jnp.concatenate([own, own_params], axis=0)
     other = lax.ppermute(mine, "tile", [(q, mirror(q)) for q in range(lax.axis_size("tile"))])
     for_even = jnp.where(upper, other, mine)

time: 184 us -> 183 us (level)
  the two profiles are of different devices: /device:TPU:8 before, /device:TPU:10 now
where the time goes in v7:
time: 183 us; the launch traced here: 181 us
  starting transfers between devices  110 us (60%)
  waiting for transfers between devices  30.4 us (17%)
  Pallas kernels  27.3 us (15%)
  local copies, waits for them, and re-layouts  10.8 us (6%)
    ppermute x16, starting transfers between devices, swap(): lax.ppermute(for_beside, axes, beside)  54.2 us
    ppermute x16, starting transfers between devices, swap(): lax.ppermute(for_across, axes, across)  36.3 us
    pallas_call x16, Pallas kernels, run_step(): pl.pallas_call(functools.partial(step_kernel, max(0, len(prepared) - 1),...  15.9 us
    all_to_all x1, waiting for transfers between devices, shards(): lax.all_to_all(jnp.broadcast_to(jnp.stack([for_even, for_odd])[None], (FR...  13.9 us
    ppermute x1, starting transfers between devices, shards(): lax.ppermute(mine, 'tile', [(q, mirror(q)) for q in range(lax.axis_size('...  10.9 us
    pallas_call x14, Pallas kernels, run_prepare(): pl.pallas_call(functools.partial(prepare_kernel, 2 if older else 1), out_...  7.8 us
    all_to_all x1, starting transfers between devices, shards(): lax.all_to_all(jnp.broadcast_to(jnp.stack([for_even, for_odd])[None], (FR...  7.55 us
    unnamed x37, local copies, waits for them, and re-layouts  6.5 us
  transfers between devices with their start and end apart: 35, of which 18 were waited for; matrix products, arithmetic and copies ran while one was open for 2% of the time, Pallas kernels for 6%

profile of v7, /device:TPU:10, one launch (start us, length us, event | category | flops | bytes accessed | tf_op | source)
XLA Modules:
  0.0 181.4 jit_solution(3974242952636539411)
XLA Ops:
  2.3 10.9 %collective-permute-start = (bf16[320,128]{1,0:T(8,128)(2,1)S(1)}, bf16[320,128]{1,0:T(8,128)(2,1)S(1)}, u32[]{:S(2)}, u32[]{:S(2)}) collective-permute-start(bf16[320,128]{1,0:T(8,128)(2,1)S(1)} %pad_maximum_fusion.4), channel_id=1, source_target_pairs={{0,14},{1,15},{2,12},{3,13},{4,10},{5,11},{6,8},{7,9},{8,6},{9,7},... | collective-permute-start | bytes 245768 | tf_op jit(solution)/shard_map/ppermute | solution.py:318
  13.3 4.1 %collective-permute-done = bf16[320,128]{1,0:T(8,128)(2,1)S(1)} collective-permute-done((bf16[320,128]{1,0:T(8,128)(2,1)S(1)}, bf16[320,128]{1,0:T(8,128)(2,1)S(1)}, u32[]{:S(2)}, u32[]{:S(2)}) %collective-permute-start) | collective-permute-done | bytes 81952 | tf_op jit(solution)/shard_map/ppermute | solution.py:318
  18.5 7.5 %all-to-all-start = ((bf16[8,320,128]{2,1,0:T(8,128)(2,1)}), bf16[8,320,128]{2,1,0:T(8,128)(2,1)S(1)}, u32[]{:S(2)}, u32[]{:S(2)}) async-start(bf16[8,320,128]{2,1,0:T(8,128)(2,1)} %bitcast.7), calls=%async_computation | async-start | bytes 1310720 | tf_op jit(solution)/shard_map/all_to_all | solution.py:321
  31.2 13.9 %all-to-all-done = bf16[8,320,128]{2,1,0:T(8,128)(2,1)S(1)} async-done(((bf16[8,320,128]{2,1,0:T(8,128)(2,1)}), bf16[8,320,128]{2,1,0:T(8,128)(2,1)S(1)}, u32[]{:S(2)}, u32[]{:S(2)}) %all-to-all-start) | async-done | bytes 655392 | tf_op jit(solution)/shard_map/all_to_all | solution.py:321
  45.1 1.9 %collective-permute-start.1 = (bf16[8,160,128]{2,1,0:T(8,128)(2,1)S(1)}, bf16[8,160,128]{2,1,0:T(8,128)(2,1)S(1)}, u32[]{:S(2)}, u32[]{:S(2)}) collective-permute-start(bf16[8,160,128]{2,1,0:T(8,128)(2,1)S(1)} %pad_maximum_fusion), channel_id=1, source_target_pairs={{1,2},{2,1},{3,4},{4,3},{5,6},{6,5},{7,70},{70,7},{71,68},{68,71},... | collective-permute-start | bytes 983048 | tf_op jit(solution)/shard_map/ppermute | solution.py:278
  47.1 4.4 %collective-permute-start.2 = (bf16[8,160,128]{2,1,0:T(8,128)(2,1)S(1)}, bf16[8,160,128]{2,1,0:T(8,128)(2,1)S(1)}, u32[]{:S(2)}, u32[]{:S(2)}) collective-permute-start(bf16[8,160,128]{2,1,0:T(8,128)(2,1)S(1)} %pad_maximum_fusion.1), channel_id=1, source_target_pairs={{0,1},{1,0},{2,3},{3,2},{4,5},{5,4},{6,7},{7,6},{70,71},{71,70},{6... | collective-permute-start | bytes 983048 | tf_op jit(solution)/shard_map/ppermute | solution.py:278
  51.7 1.8 %collective-permute-done.1 = bf16[8,160,128]{2,1,0:T(8,128)(2,1)S(1)} collective-permute-done((bf16[8,160,128]{2,1,0:T(8,128)(2,1)S(1)}, bf16[8,160,128]{2,1,0:T(8,128)(2,1)S(1)}, u32[]{:S(2)}, u32[]{:S(2)}) %collective-permute-start.1) | collective-permute-done | bytes 327712 | tf_op jit(solution)/shard_map/ppermute | solution.py:278
  55.1 1.9 %collective-permute-start.3 = (bf16[256,128]{1,0:T(8,128)(2,1)S(1)}, bf16[256,128]{1,0:T(8,128)(2,1)S(1)}, u32[]{:S(2)}, u32[]{:S(2)}) collective-permute-start(bf16[256,128]{1,0:T(8,128)(2,1)S(1)} %step.16.own.refs_4_.refs_1_), channel_id=1, source_target_pairs={{1,2},{2,1},{3,4},{4,3},{5,6},{6,5},{7,70},{70,7},{71,68},{68,71},... | collective-permute-start | bytes 196616 | tf_op jit(solution)/shard_map/ppermute | solution.py:278
  57.0 5.3 %collective-permute-start.4 = (bf16[256,128]{1,0:T(8,128)(2,1)S(1)}, bf16[256,128]{1,0:T(8,128)(2,1)S(1)}, u32[]{:S(2)}, u32[]{:S(2)}) collective-permute-start(bf16[256,128]{1,0:T(8,128)(2,1)S(1)} %step.16.own.refs_4_.refs_1_), channel_id=1, source_target_pairs={{0,1},{1,0},{2,3},{3,2},{4,5},{5,4},{6,7},{7,6},{70,71},{71,70},{6... | collective-permute-start | bytes 196616 | tf_op jit(solution)/shard_map/ppermute | solution.py:278
  65.1 1.9 %collective-permute-start.5 = (bf16[256,128]{1,0:T(8,128)(2,1)S(1)}, bf16[256,128]{1,0:T(8,128)(2,1)S(1)}, u32[]{:S(2)}, u32[]{:S(2)}) collective-permute-start(bf16[256,128]{1,0:T(8,128)(2,1)S(1)} %step.17.own.refs_4_.refs_1_), channel_id=1, source_target_pairs={{1,2},{2,1},{3,4},{4,3},{5,6},{6,5},{7,70},{70,7},{71,68},{68,71},... | collective-permute-start | bytes 196616 | tf_op jit(solution)/shard_map/ppermute | solution.py:278
  67.0 2.8 %collective-permute-start.6 = (bf16[256,128]{1,0:T(8,128)(2,1)S(1)}, bf16[256,128]{1,0:T(8,128)(2,1)S(1)}, u32[]{:S(2)}, u32[]{:S(2)}) collective-permute-start(bf16[256,128]{1,0:T(8,128)(2,1)S(1)} %step.17.own.refs_4_.refs_1_), channel_id=1, source_target_pairs={{0,1},{1,0},{2,3},{3,2},{4,5},{5,4},{6,7},{7,6},{70,71},{71,70},{6... | collective-permute-start | bytes 196616 | tf_op jit(solution)/shard_map/ppermute | solution.py:278
  71.0 1.0 step.18.own.refs_4_.refs_1_
  72.0 3.1 %collective-permute-start.7 = (bf16[256,128]{1,0:T(8,128)(2,1)S(1)}, bf16[256,128]{1,0:T(8,128)(2,1)S(1)}, u32[]{:S(2)}, u32[]{:S(2)}) collective-permute-start(bf16[256,128]{1,0:T(8,128)(2,1)S(1)} %step.18.own.refs_4_.refs_1_), channel_id=1, source_target_pairs={{1,2},{2,1},{3,4},{4,3},{5,6},{6,5},{7,70},{70,7},{71,68},{68,71},... | collective-permute-start | bytes 196616 | tf_op jit(solution)/shard_map/ppermute | solution.py:278
  75.1 2.8 %collective-permute-start.8 = (bf16[256,128]{1,0:T(8,128)(2,1)S(1)}, bf16[256,128]{1,0:T(8,128)(2,1)S(1)}, u32[]{:S(2)}, u32[]{:S(2)}) collective-permute-start(bf16[256,128]{1,0:T(8,128)(2,1)S(1)} %step.18.own.refs_4_.refs_1_), channel_id=1, source_target_pairs={{0,1},{1,0},{2,3},{3,2},{4,5},{5,4},{6,7},{7,6},{70,71},{71,70},{6... | collective-permute-start | bytes 196616 | tf_op jit(solution)/shard_map/ppermute | solution.py:278
  79.1 1.0 step.19.own.refs_4_.refs_1_
  80.1 1.9 %collective-permute-start.9 = (bf16[256,128]{1,0:T(8,128)(2,1)S(1)}, bf16[256,128]{1,0:T(8,128)(2,1)S(1)}, u32[]{:S(2)}, u32[]{:S(2)}) collective-permute-start(bf16[256,128]{1,0:T(8,128)(2,1)S(1)} %step.19.own.refs_4_.refs_1_), channel_id=1, source_target_pairs={{1,2},{2,1},{3,4},{4,3},{5,6},{6,5},{7,70},{70,7},{71,68},{68,71},... | collective-permute-start | bytes 196616 | tf_op jit(solution)/shard_map/ppermute | solution.py:278
  82.1 3.4 %collective-permute-start.10 = (bf16[256,128]{1,0:T(8,128)(2,1)S(1)}, bf16[256,128]{1,0:T(8,128)(2,1)S(1)}, u32[]{:S(2)}, u32[]{:S(2)}) collective-permute-start(bf16[256,128]{1,0:T(8,128)(2,1)S(1)} %step.19.own.refs_4_.refs_1_), channel_id=1, source_target_pairs={{0,1},{1,0},{2,3},{3,2},{4,5},{5,4},{6,7},{7,6},{70,71},{71,70},{6... | collective-permute-start | bytes 196616 | tf_op jit(solution)/shard_map/ppermute | solution.py:278
  86.6 1.0 step.20.own.refs_4_.refs_1_
  87.7 2.5 %collective-permute-start.11 = (bf16[256,128]{1,0:T(8,128)(2,1)S(1)}, bf16[256,128]{1,0:T(8,128)(2,1)S(1)}, u32[]{:S(2)}, u32[]{:S(2)}) collective-permute-start(bf16[256,128]{1,0:T(8,128)(2,1)S(1)} %step.20.own.refs_4_.refs_1_), channel_id=1, source_target_pairs={{1,2},{2,1},{3,4},{4,3},{5,6},{6,5},{7,70},{70,7},{71,68},{68,71},... | collective-permute-start | bytes 196616 | tf_op jit(solution)/shard_map/ppermute | solution.py:278
  90.2 3.3 %collective-permute-start.12 = (bf16[256,128]{1,0:T(8,128)(2,1)S(1)}, bf16[256,128]{1,0:T(8,128)(2,1)S(1)}, u32[]{:S(2)}, u32[]{:S(2)}) collective-permute-start(bf16[256,128]{1,0:T(8,128)(2,1)S(1)} %step.20.own.refs_4_.refs_1_), channel_id=1, source_target_pairs={{0,1},{1,0},{2,3},{3,2},{4,5},{5,4},{6,7},{7,6},{70,71},{71,70},{6... | collective-permute-start | bytes 196616 | tf_op jit(solution)/shard_map/ppermute | solution.py:278
  94.5 1.0 step.21.own.refs_4_.refs_1_
  95.5 2.2 %collective-permute-start.13 = (bf16[256,128]{1,0:T(8,128)(2,1)S(1)}, bf16[256,128]{1,0:T(8,128)(2,1)S(1)}, u32[]{:S(2)}, u32[]{:S(2)}) collective-permute-start(bf16[256,128]{1,0:T(8,128)(2,1)S(1)} %step.21.own.refs_4_.refs_1_), channel_id=1, source_target_pairs={{1,2},{2,1},{3,4},{4,3},{5,6},{6,5},{7,70},{70,7},{71,68},{68,71},... | collective-permute-start | bytes 196616 | tf_op jit(solution)/shard_map/ppermute | solution.py:278
  97.7 3.2 %collective-permute-start.14 = (bf16[256,128]{1,0:T(8,128)(2,1)S(1)}, bf16[256,128]{1,0:T(8,128)(2,1)S(1)}, u32[]{:S(2)}, u32[]{:S(2)}) collective-permute-start(bf16[256,128]{1,0:T(8,128)(2,1)S(1)} %step.21.own.refs_4_.refs_1_), channel_id=1, source_target_pairs={{0,1},{1,0},{2,3},{3,2},{4,5},{5,4},{6,7},{7,6},{70,71},{71,70},{6... | collective-permute-start | bytes 196616 | tf_op jit(solution)/shard_map/ppermute | solution.py:278
  102.0 1.0 step.22.own.refs_4_
  103.0 2.5 %collective-permute-start.15 = (bf16[256,128]{1,0:T(8,128)(2,1)S(1)}, bf16[256,128]{1,0:T(8,128)(2,1)S(1)}, u32[]{:S(2)}, u32[]{:S(2)}) collective-permute-start(bf16[256,128]{1,0:T(8,128)(2,1)S(1)} %step.22.own.refs_4_), channel_id=1, source_target_pairs={{1,2},{2,1},{3,4},{4,3},{5,6},{6,5},{7,70},{70,7},{71,68},{68,71},... | collective-permute-start | bytes 196616 | tf_op jit(solution)/shard_map/ppermute | solution.py:278
  105.6 3.2 %collective-permute-start.16 = (bf16[256,128]{1,0:T(8,128)(2,1)S(1)}, bf16[256,128]{1,0:T(8,128)(2,1)S(1)}, u32[]{:S(2)}, u32[]{:S(2)}) collective-permute-start(bf16[256,128]{1,0:T(8,128)(2,1)S(1)} %step.22.own.refs_4_), channel_id=1, source_target_pairs={{0,1},{1,0},{2,3},{3,2},{4,5},{5,4},{6,7},{7,6},{70,71},{71,70},{6... | collective-permute-start | bytes 196616 | tf_op jit(solution)/shard_map/ppermute | solution.py:278
  109.9 1.0 step.23.refs_4_
  110.9 2.2 %collective-permute-start.17 = (bf16[256,128]{1,0:T(8,128)(2,1)S(1)}, bf16[256,128]{1,0:T(8,128)(2,1)S(1)}, u32[]{:S(2)}, u32[]{:S(2)}) collective-permute-start(bf16[256,128]{1,0:T(8,128)(2,1)S(1)} %step.23.refs_4_), channel_id=1, source_target_pairs={{1,2},{2,1},{3,4},{4,3},{5,6},{6,5},{7,70},{70,7},{71,68},{68,71},... | collective-permute-start | bytes 196616 | tf_op jit(solution)/shard_map/ppermute | solution.py:278
  113.1 3.2 %collective-permute-start.18 = (bf16[256,128]{1,0:T(8,128)(2,1)S(1)}, bf16[256,128]{1,0:T(8,128)(2,1)S(1)}, u32[]{:S(2)}, u32[]{:S(2)}) collective-permute-start(bf16[256,128]{1,0:T(8,128)(2,1)S(1)} %step.23.refs_4_), channel_id=1, source_target_pairs={{0,1},{1,0},{2,3},{3,2},{4,5},{5,4},{6,7},{7,6},{70,71},{71,70},{6... | collective-permute-start | bytes 196616 | tf_op jit(solution)/shard_map/ppermute | solution.py:278
  117.9 2.5 %collective-permute-start.19 = (bf16[256,128]{1,0:T(8,128)(2,1)S(1)}, bf16[256,128]{1,0:T(8,128)(2,1)S(1)}, u32[]{:S(2)}, u32[]{:S(2)}) collective-permute-start(bf16[256,128]{1,0:T(8,128)(2,1)S(1)} %step.24.own.refs_7_.refs_1_), channel_id=1, source_target_pairs={{1,2},{2,1},{3,4},{4,3},{5,6},{6,5},{7,70},{70,7},{71,68},{68,71},... | collective-permute-start | bytes 196616 | tf_op jit(solution)/shard_map/ppermute | solution.py:278
  120.4 3.2 %collective-permute-start.20 = (bf16[256,128]{1,0:T(8,128)(2,1)S(1)}, bf16[256,128]{1,0:T(8,128)(2,1)S(1)}, u32[]{:S(2)}, u32[]{:S(2)}) collective-permute-start(bf16[256,128]{1,0:T(8,128)(2,1)S(1)} %step.24.own.refs_7_.refs_1_), channel_id=1, source_target_pairs={{0,1},{1,0},{2,3},{3,2},{4,5},{5,4},{6,7},{7,6},{70,71},{71,70},{6... | collective-permute-start | bytes 196616 | tf_op jit(solution)/shard_map/ppermute | solution.py:278
  124.7 1.0 step.25.own.refs_7_.refs_1_
  125.8 2.2 %collective-permute-start.21 = (bf16[256,128]{1,0:T(8,128)(2,1)S(1)}, bf16[256,128]{1,0:T(8,128)(2,1)S(1)}, u32[]{:S(2)}, u32[]{:S(2)}) collective-permute-start(bf16[256,128]{1,0:T(8,128)(2,1)S(1)} %step.25.own.refs_7_.refs_1_), channel_id=1, source_target_pairs={{1,2},{2,1},{3,4},{4,3},{5,6},{6,5},{7,70},{70,7},{71,68},{68,71},... | collective-permute-start | bytes 196616 | tf_op jit(solution)/shard_map/ppermute | solution.py:278
  127.9 3.4 %collective-permute-start.22 = (bf16[256,128]{1,0:T(8,128)(2,1)S(1)}, bf16[256,128]{1,0:T(8,128)(2,1)S(1)}, u32[]{:S(2)}, u32[]{:S(2)}) collective-permute-start(bf16[256,128]{1,0:T(8,128)(2,1)S(1)} %step.25.own.refs_7_.refs_1_), channel_id=1, source_target_pairs={{0,1},{1,0},{2,3},{3,2},{4,5},{5,4},{6,7},{7,6},{70,71},{71,70},{6... | collective-permute-start | bytes 196616 | tf_op jit(solution)/shard_map/ppermute | solution.py:278
  133.6 2.2 %collective-permute-start.23 = (bf16[256,128]{1,0:T(8,128)(2,1)S(1)}, bf16[256,128]{1,0:T(8,128)(2,1)S(1)}, u32[]{:S(2)}, u32[]{:S(2)}) collective-permute-start(bf16[256,128]{1,0:T(8,128)(2,1)S(1)} %step.26.own.refs_7_.refs_1_), channel_id=1, source_target_pairs={{1,2},{2,1},{3,4},{4,3},{5,6},{6,5},{7,70},{70,7},{71,68},{68,71},... | collective-permute-start | bytes 196616 | tf_op jit(solution)/shard_map/ppermute | solution.py:278
  135.8 3.2 %collective-permute-start.24 = (bf16[256,128]{1,0:T(8,128)(2,1)S(1)}, bf16[256,128]{1,0:T(8,128)(2,1)S(1)}, u32[]{:S(2)}, u32[]{:S(2)}) collective-permute-start(bf16[256,128]{1,0:T(8,128)(2,1)S(1)} %step.26.own.refs_7_.refs_1_), channel_id=1, source_target_pairs={{0,1},{1,0},{2,3},{3,2},{4,5},{5,4},{6,7},{7,6},{70,71},{71,70},{6... | collective-permute-start | bytes 196616 | tf_op jit(solution)/shard_map/ppermute | solution.py:278
  140.1 1.0 step.27.own.refs_7_.refs_1_
  141.2 2.4 %collective-permute-start.25 = (bf16[256,128]{1,0:T(8,128)(2,1)S(1)}, bf16[256,128]{1,0:T(8,128)(2,1)S(1)}, u32[]{:S(2)}, u32[]{:S(2)}) collective-permute-start(bf16[256,128]{1,0:T(8,128)(2,1)S(1)} %step.27.own.refs_7_.refs_1_), channel_id=1, source_target_pairs={{1,2},{2,1},{3,4},{4,3},{5,6},{6,5},{7,70},{70,7},{71,68},{68,71},... | collective-permute-start | bytes 196616 | tf_op jit(solution)/shard_map/ppermute | solution.py:278
  143.6 3.2 %collective-permute-start.26 = (bf16[256,128]{1,0:T(8,128)(2,1)S(1)}, bf16[256,128]{1,0:T(8,128)(2,1)S(1)}, u32[]{:S(2)}, u32[]{:S(2)}) collective-permute-start(bf16[256,128]{1,0:T(8,128)(2,1)S(1)} %step.27.own.refs_7_.refs_1_), channel_id=1, source_target_pairs={{0,1},{1,0},{2,3},{3,2},{4,5},{5,4},{6,7},{7,6},{70,71},{71,70},{6... | collective-permute-start | bytes 196616 | tf_op jit(solution)/shard_map/ppermute | solution.py:278
  147.9 1.0 step.28.own.refs_7_.refs_1_
  148.9 2.2 %collective-permute-start.27 = (bf16[256,128]{1,0:T(8,128)(2,1)S(1)}, bf16[256,128]{1,0:T(8,128)(2,1)S(1)}, u32[]{:S(2)}, u32[]{:S(2)}) collective-permute-start(bf16[256,128]{1,0:T(8,128)(2,1)S(1)} %step.28.own.refs_7_.refs_1_), channel_id=1, source_target_pairs={{1,2},{2,1},{3,4},{4,3},{5,6},{6,5},{7,70},{70,7},{71,68},{68,71},... | collective-permute-start | bytes 196616 | tf_op jit(solution)/shard_map/ppermute | solution.py:278
  151.2 3.4 %collective-permute-start.28 = (bf16[256,128]{1,0:T(8,128)(2,1)S(1)}, bf16[256,128]{1,0:T(8,128)(2,1)S(1)}, u32[]{:S(2)}, u32[]{:S(2)}) collective-permute-start(bf16[256,128]{1,0:T(8,128)(2,1)S(1)} %step.28.own.refs_7_.refs_1_), channel_id=1, source_target_pairs={{0,1},{1,0},{2,3},{3,2},{4,5},{5,4},{6,7},{7,6},{70,71},{71,70},{6... | collective-permute-start | bytes 196616 | tf_op jit(solution)/shard_map/ppermute | solution.py:278
  156.5 2.4 %collective-permute-start.29 = (bf16[256,128]{1,0:T(8,128)(2,1)S(1)}, bf16[256,128]{1,0:T(8,128)(2,1)S(1)}, u32[]{:S(2)}, u32[]{:S(2)}) collective-permute-start(bf16[256,128]{1,0:T(8,128)(2,1)S(1)} %step.29.own.refs_7_.refs_1_), channel_id=1, source_target_pairs={{1,2},{2,1},{3,4},{4,3},{5,6},{6,5},{7,70},{70,7},{71,68},{68,71},... | collective-permute-start | bytes 196616 | tf_op jit(solution)/shard_map/ppermute | solution.py:278
  159.0 3.2 %collective-permute-start.30 = (bf16[256,128]{1,0:T(8,128)(2,1)S(1)}, bf16[256,128]{1,0:T(8,128)(2,1)S(1)}, u32[]{:S(2)}, u32[]{:S(2)}) collective-permute-start(bf16[256,128]{1,0:T(8,128)(2,1)S(1)} %step.29.own.refs_7_.refs_1_), channel_id=1, source_target_pairs={{0,1},{1,0},{2,3},{3,2},{4,5},{5,4},{6,7},{7,6},{70,71},{71,70},{6... | collective-permute-start | bytes 196616 | tf_op jit(solution)/shard_map/ppermute | solution.py:278
  164.3 2.2 %collective-permute-start.31 = (bf16[256,128]{1,0:T(8,128)(2,1)S(1)}, bf16[256,128]{1,0:T(8,128)(2,1)S(1)}, u32[]{:S(2)}, u32[]{:S(2)}) collective-permute-start(bf16[256,128]{1,0:T(8,128)(2,1)S(1)} %step.30.own.refs_7_), channel_id=1, source_target_pairs={{1,2},{2,1},{3,4},{4,3},{5,6},{6,5},{7,70},{70,7},{71,68},{68,71},... | collective-permute-start | bytes 196616 | tf_op jit(solution)/shard_map/ppermute | solution.py:278
  166.5 3.2 %collective-permute-start.32 = (bf16[256,128]{1,0:T(8,128)(2,1)S(1)}, bf16[256,128]{1,0:T(8,128)(2,1)S(1)}, u32[]{:S(2)}, u32[]{:S(2)}) collective-permute-start(bf16[256,128]{1,0:T(8,128)(2,1)S(1)} %step.30.own.refs_7_), channel_id=1, source_target_pairs={{0,1},{1,0},{2,3},{3,2},{4,5},{5,4},{6,7},{7,6},{70,71},{71,70},{6... | collective-permute-start | bytes 196616 | tf_op jit(solution)/shard_map/ppermute | solution.py:278
  172.5 1.3 collective-permute-start.33
  173.9 6.3 %collective-permute-done.33 = bf16[2,256,128]{2,1,0:T(8,128)(2,1)S(1)} collective-permute-done((bf16[2,256,128]{2,1,0:T(8,128)(2,1)S(1)}, bf16[2,256,128]{2,1,0:T(8,128)(2,1)S(1)}, u32[]{:S(2)}, u32[]{:S(2)}) %collective-permute-start.33) | collective-permute-done | bytes 131104 | tf_op jit(solution)/shard_map/ppermute | solution.py:381
  (150 shorter events, 34.1 us)
Async XLA Ops:
  1.5 0.7 copy-start.10
  1.5 0.7 copy-start.11
  2.3 15.1 %collective-permute-start = (bf16[320,128]{1,0:T(8,128)(2,1)S(1)}, bf16[320,128]{1,0:T(8,128)(2,1)S(1)}, u32[]{:S(2)}, u32[]{:S(2)}) collective-permute-start(bf16[320,128]{1,0:T(8,128)(2,1)S(1)} %pad_maximum_fusion.4), channel_id=1, source_target_pairs={{0,14},{1,15},{2,12},{3,13},{4,10},{5,11},{6,8},{7,9},{8,6},{9,7},... | collective-permute-start | bytes 245768 | tf_op jit(solution)/shard_map/ppermute | solution.py:318
  18.5 26.6 %all-to-all-start = ((bf16[8,320,128]{2,1,0:T(8,128)(2,1)}), bf16[8,320,128]{2,1,0:T(8,128)(2,1)S(1)}, u32[]{:S(2)}, u32[]{:S(2)}) async-start(bf16[8,320,128]{2,1,0:T(8,128)(2,1)} %bitcast.7), calls=%async_computation | async-start | bytes 1310720 | tf_op jit(solution)/shard_map/all_to_all | solution.py:321
  26.0 0.9 copy-start.12
  26.9 0.9 copy-start.13
  28.5 0.9 copy-start.14
  29.4 0.9 copy-start.15
  45.1 8.4 %collective-permute-start.1 = (bf16[8,160,128]{2,1,0:T(8,128)(2,1)S(1)}, bf16[8,160,128]{2,1,0:T(8,128)(2,1)S(1)}, u32[]{:S(2)}, u32[]{:S(2)}) collective-permute-start(bf16[8,160,128]{2,1,0:T(8,128)(2,1)S(1)} %pad_maximum_fusion), channel_id=1, source_target_pairs={{1,2},{2,1},{3,4},{4,3},{5,6},{6,5},{7,70},{70,7},{71,68},{68,71},... | collective-permute-start | bytes 983048 | tf_op jit(solution)/shard_map/ppermute | solution.py:278
  47.1 6.5 %collective-permute-start.2 = (bf16[8,160,128]{2,1,0:T(8,128)(2,1)S(1)}, bf16[8,160,128]{2,1,0:T(8,128)(2,1)S(1)}, u32[]{:S(2)}, u32[]{:S(2)}) collective-permute-start(bf16[8,160,128]{2,1,0:T(8,128)(2,1)S(1)} %pad_maximum_fusion.1), channel_id=1, source_target_pairs={{0,1},{1,0},{2,3},{3,2},{4,5},{5,4},{6,7},{7,6},{70,71},{71,70},{6... | collective-permute-start | bytes 983048 | tf_op jit(solution)/shard_map/ppermute | solution.py:278
  51.5 2.1 %copy-start.2 = (bf16[256,128]{1,0:T(8,128)(2,1)}, bf16[256,128]{1,0:T(8,128)(2,1)S(1)}, u32[]{:S(2)}) copy-start(bf16[256,128]{1,0:T(8,128)(2,1)S(1)} %get-tuple-element.57.refs_1_) | copy-start | bytes 196612
  53.6 0.8 copy-start.1
  53.6 1.5 copy-start.6
  55.1 9.0 %collective-permute-start.3 = (bf16[256,128]{1,0:T(8,128)(2,1)S(1)}, bf16[256,128]{1,0:T(8,128)(2,1)S(1)}, u32[]{:S(2)}, u32[]{:S(2)}) collective-permute-start(bf16[256,128]{1,0:T(8,128)(2,1)S(1)} %step.16.own.refs_4_.refs_1_), channel_id=1, source_target_pairs={{1,2},{2,1},{3,4},{4,3},{5,6},{6,5},{7,70},{70,7},{71,68},{68,71},... | collective-permute-start | bytes 196616 | tf_op jit(solution)/shard_map/ppermute | solution.py:278
  57.0 6.8 %collective-permute-start.4 = (bf16[256,128]{1,0:T(8,128)(2,1)S(1)}, bf16[256,128]{1,0:T(8,128)(2,1)S(1)}, u32[]{:S(2)}, u32[]{:S(2)}) collective-permute-start(bf16[256,128]{1,0:T(8,128)(2,1)S(1)} %step.16.own.refs_4_.refs_1_), channel_id=1, source_target_pairs={{0,1},{1,0},{2,3},{3,2},{4,5},{5,4},{6,7},{7,6},{70,71},{71,70},{6... | collective-permute-start | bytes 196616 | tf_op jit(solution)/shard_map/ppermute | solution.py:278
  65.1 5.9 %collective-permute-start.5 = (bf16[256,128]{1,0:T(8,128)(2,1)S(1)}, bf16[256,128]{1,0:T(8,128)(2,1)S(1)}, u32[]{:S(2)}, u32[]{:S(2)}) collective-permute-start(bf16[256,128]{1,0:T(8,128)(2,1)S(1)} %step.17.own.refs_4_.refs_1_), channel_id=1, source_target_pairs={{1,2},{2,1},{3,4},{4,3},{5,6},{6,5},{7,70},{70,7},{71,68},{68,71},... | collective-permute-start | bytes 196616 | tf_op jit(solution)/shard_map/ppermute | solution.py:278
  67.0 3.7 %collective-permute-start.6 = (bf16[256,128]{1,0:T(8,128)(2,1)S(1)}, bf16[256,128]{1,0:T(8,128)(2,1)S(1)}, u32[]{:S(2)}, u32[]{:S(2)}) collective-permute-start(bf16[256,128]{1,0:T(8,128)(2,1)S(1)} %step.17.own.refs_4_.refs_1_), channel_id=1, source_target_pairs={{0,1},{1,0},{2,3},{3,2},{4,5},{5,4},{6,7},{7,6},{70,71},{71,70},{6... | collective-permute-start | bytes 196616 | tf_op jit(solution)/shard_map/ppermute | solution.py:278
  72.0 7.1 %collective-permute-start.7 = (bf16[256,128]{1,0:T(8,128)(2,1)S(1)}, bf16[256,128]{1,0:T(8,128)(2,1)S(1)}, u32[]{:S(2)}, u32[]{:S(2)}) collective-permute-start(bf16[256,128]{1,0:T(8,128)(2,1)S(1)} %step.18.own.refs_4_.refs_1_), channel_id=1, source_target_pairs={{1,2},{2,1},{3,4},{4,3},{5,6},{6,5},{7,70},{70,7},{71,68},{68,71},... | collective-permute-start | bytes 196616 | tf_op jit(solution)/shard_map/ppermute | solution.py:278
  75.1 3.7 %collective-permute-start.8 = (bf16[256,128]{1,0:T(8,128)(2,1)S(1)}, bf16[256,128]{1,0:T(8,128)(2,1)S(1)}, u32[]{:S(2)}, u32[]{:S(2)}) collective-permute-start(bf16[256,128]{1,0:T(8,128)(2,1)S(1)} %step.18.own.refs_4_.refs_1_), channel_id=1, source_target_pairs={{0,1},{1,0},{2,3},{3,2},{4,5},{5,4},{6,7},{7,6},{70,71},{71,70},{6... | collective-permute-start | bytes 196616 | tf_op jit(solution)/shard_map/ppermute | solution.py:278
  80.1 6.5 %collective-permute-start.9 = (bf16[256,128]{1,0:T(8,128)(2,1)S(1)}, bf16[256,128]{1,0:T(8,128)(2,1)S(1)}, u32[]{:S(2)}, u32[]{:S(2)}) collective-permute-start(bf16[256,128]{1,0:T(8,128)(2,1)S(1)} %step.19.own.refs_4_.refs_1_), channel_id=1, source_target_pairs={{1,2},{2,1},{3,4},{4,3},{5,6},{6,5},{7,70},{70,7},{71,68},{68,71},... | collective-permute-start | bytes 196616 | tf_op jit(solution)/shard_map/ppermute | solution.py:278
  82.1 4.3 %collective-permute-start.10 = (bf16[256,128]{1,0:T(8,128)(2,1)S(1)}, bf16[256,128]{1,0:T(8,128)(2,1)S(1)}, u32[]{:S(2)}, u32[]{:S(2)}) collective-permute-start(bf16[256,128]{1,0:T(8,128)(2,1)S(1)} %step.19.own.refs_4_.refs_1_), channel_id=1, source_target_pairs={{0,1},{1,0},{2,3},{3,2},{4,5},{5,4},{6,7},{7,6},{70,71},{71,70},{6... | collective-permute-start | bytes 196616 | tf_op jit(solution)/shard_map/ppermute | solution.py:278
  87.7 6.8 %collective-permute-start.11 = (bf16[256,128]{1,0:T(8,128)(2,1)S(1)}, bf16[256,128]{1,0:T(8,128)(2,1)S(1)}, u32[]{:S(2)}, u32[]{:S(2)}) collective-permute-start(bf16[256,128]{1,0:T(8,128)(2,1)S(1)} %step.20.own.refs_4_.refs_1_), channel_id=1, source_target_pairs={{1,2},{2,1},{3,4},{4,3},{5,6},{6,5},{7,70},{70,7},{71,68},{68,71},... | collective-permute-start | bytes 196616 | tf_op jit(solution)/shard_map/ppermute | solution.py:278
  90.2 4.0 %collective-permute-start.12 = (bf16[256,128]{1,0:T(8,128)(2,1)S(1)}, bf16[256,128]{1,0:T(8,128)(2,1)S(1)}, u32[]{:S(2)}, u32[]{:S(2)}) collective-permute-start(bf16[256,128]{1,0:T(8,128)(2,1)S(1)} %step.20.own.refs_4_.refs_1_), channel_id=1, source_target_pairs={{0,1},{1,0},{2,3},{3,2},{4,5},{5,4},{6,7},{7,6},{70,71},{71,70},{6... | collective-permute-start | bytes 196616 | tf_op jit(solution)/shard_map/ppermute | solution.py:278
  95.5 6.5 %collective-permute-start.13 = (bf16[256,128]{1,0:T(8,128)(2,1)S(1)}, bf16[256,128]{1,0:T(8,128)(2,1)S(1)}, u32[]{:S(2)}, u32[]{:S(2)}) collective-permute-start(bf16[256,128]{1,0:T(8,128)(2,1)S(1)} %step.21.own.refs_4_.refs_1_), channel_id=1, source_target_pairs={{1,2},{2,1},{3,4},{4,3},{5,6},{6,5},{7,70},{70,7},{71,68},{68,71},... | collective-permute-start | bytes 196616 | tf_op jit(solution)/shard_map/ppermute | solution.py:278
  97.7 4.0 %collective-permute-start.14 = (bf16[256,128]{1,0:T(8,128)(2,1)S(1)}, bf16[256,128]{1,0:T(8,128)(2,1)S(1)}, u32[]{:S(2)}, u32[]{:S(2)}) collective-permute-start(bf16[256,128]{1,0:T(8,128)(2,1)S(1)} %step.21.own.refs_4_.refs_1_), channel_id=1, source_target_pairs={{0,1},{1,0},{2,3},{3,2},{4,5},{5,4},{6,7},{7,6},{70,71},{71,70},{6... | collective-permute-start | bytes 196616 | tf_op jit(solution)/shard_map/ppermute | solution.py:278
  103.0 6.8 %collective-permute-start.15 = (bf16[256,128]{1,0:T(8,128)(2,1)S(1)}, bf16[256,128]{1,0:T(8,128)(2,1)S(1)}, u32[]{:S(2)}, u32[]{:S(2)}) collective-permute-start(bf16[256,128]{1,0:T(8,128)(2,1)S(1)} %step.22.own.refs_4_), channel_id=1, source_target_pairs={{1,2},{2,1},{3,4},{4,3},{5,6},{6,5},{7,70},{70,7},{71,68},{68,71},... | collective-permute-start | bytes 196616 | tf_op jit(solution)/shard_map/ppermute | solution.py:278
  105.6 4.0 %collective-permute-start.16 = (bf16[256,128]{1,0:T(8,128)(2,1)S(1)}, bf16[256,128]{1,0:T(8,128)(2,1)S(1)}, u32[]{:S(2)}, u32[]{:S(2)}) collective-permute-start(bf16[256,128]{1,0:T(8,128)(2,1)S(1)} %step.22.own.refs_4_), channel_id=1, source_target_pairs={{0,1},{1,0},{2,3},{3,2},{4,5},{5,4},{6,7},{7,6},{70,71},{71,70},{6... | collective-permute-start | bytes 196616 | tf_op jit(solution)/shard_map/ppermute | solution.py:278
  110.9 6.2 %copy-start = (bf16[64,256]{1,0:T(8,128)(2,1)S(1)}, bf16[64,256]{1,0:T(8,128)(2,1)}, u32[]{:S(2)}) copy-start(bf16[64,256]{1,0:T(8,128)(2,1)} %refs_11_.11) | copy-start | bytes 98308
  110.9 5.6 %collective-permute-start.17 = (bf16[256,128]{1,0:T(8,128)(2,1)S(1)}, bf16[256,128]{1,0:T(8,128)(2,1)S(1)}, u32[]{:S(2)}, u32[]{:S(2)}) collective-permute-start(bf16[256,128]{1,0:T(8,128)(2,1)S(1)} %step.23.refs_4_), channel_id=1, source_target_pairs={{1,2},{2,1},{3,4},{4,3},{5,6},{6,5},{7,70},{70,7},{71,68},{68,71},... | collective-permute-start | bytes 196616 | tf_op jit(solution)/shard_map/ppermute | solution.py:278
  113.1 4.0 %collective-permute-start.18 = (bf16[256,128]{1,0:T(8,128)(2,1)S(1)}, bf16[256,128]{1,0:T(8,128)(2,1)S(1)}, u32[]{:S(2)}, u32[]{:S(2)}) collective-permute-start(bf16[256,128]{1,0:T(8,128)(2,1)S(1)} %step.23.refs_4_), channel_id=1, source_target_pairs={{0,1},{1,0},{2,3},{3,2},{4,5},{5,4},{6,7},{7,6},{70,71},{71,70},{6... | collective-permute-start | bytes 196616 | tf_op jit(solution)/shard_map/ppermute | solution.py:278
  117.9 6.8 %collective-permute-start.19 = (bf16[256,128]{1,0:T(8,128)(2,1)S(1)}, bf16[256,128]{1,0:T(8,128)(2,1)S(1)}, u32[]{:S(2)}, u32[]{:S(2)}) collective-permute-start(bf16[256,128]{1,0:T(8,128)(2,1)S(1)} %step.24.own.refs_7_.refs_1_), channel_id=1, source_target_pairs={{1,2},{2,1},{3,4},{4,3},{5,6},{6,5},{7,70},{70,7},{71,68},{68,71},... | collective-permute-start | bytes 196616 | tf_op jit(solution)/shard_map/ppermute | solution.py:278
  120.4 4.1 %collective-permute-start.20 = (bf16[256,128]{1,0:T(8,128)(2,1)S(1)}, bf16[256,128]{1,0:T(8,128)(2,1)S(1)}, u32[]{:S(2)}, u32[]{:S(2)}) collective-permute-start(bf16[256,128]{1,0:T(8,128)(2,1)S(1)} %step.24.own.refs_7_.refs_1_), channel_id=1, source_target_pairs={{0,1},{1,0},{2,3},{3,2},{4,5},{5,4},{6,7},{7,6},{70,71},{71,70},{6... | collective-permute-start | bytes 196616 | tf_op jit(solution)/shard_map/ppermute | solution.py:278
  125.8 6.7 %collective-permute-start.21 = (bf16[256,128]{1,0:T(8,128)(2,1)S(1)}, bf16[256,128]{1,0:T(8,128)(2,1)S(1)}, u32[]{:S(2)}, u32[]{:S(2)}) collective-permute-start(bf16[256,128]{1,0:T(8,128)(2,1)S(1)} %step.25.own.refs_7_.refs_1_), channel_id=1, source_target_pairs={{1,2},{2,1},{3,4},{4,3},{5,6},{6,5},{7,70},{70,7},{71,68},{68,71},... | collective-permute-start | bytes 196616 | tf_op jit(solution)/shard_map/ppermute | solution.py:278
  127.9 4.3 %collective-permute-start.22 = (bf16[256,128]{1,0:T(8,128)(2,1)S(1)}, bf16[256,128]{1,0:T(8,128)(2,1)S(1)}, u32[]{:S(2)}, u32[]{:S(2)}) collective-permute-start(bf16[256,128]{1,0:T(8,128)(2,1)S(1)} %step.25.own.refs_7_.refs_1_), channel_id=1, source_target_pairs={{0,1},{1,0},{2,3},{3,2},{4,5},{5,4},{6,7},{7,6},{70,71},{71,70},{6... | collective-permute-start | bytes 196616 | tf_op jit(solution)/shard_map/ppermute | solution.py:278
  133.6 6.6 %collective-permute-start.23 = (bf16[256,128]{1,0:T(8,128)(2,1)S(1)}, bf16[256,128]{1,0:T(8,128)(2,1)S(1)}, u32[]{:S(2)}, u32[]{:S(2)}) collective-permute-start(bf16[256,128]{1,0:T(8,128)(2,1)S(1)} %step.26.own.refs_7_.refs_1_), channel_id=1, source_target_pairs={{1,2},{2,1},{3,4},{4,3},{5,6},{6,5},{7,70},{70,7},{71,68},{68,71},... | collective-permute-start | bytes 196616 | tf_op jit(solution)/shard_map/ppermute | solution.py:278
  135.8 4.0 %collective-permute-start.24 = (bf16[256,128]{1,0:T(8,128)(2,1)S(1)}, bf16[256,128]{1,0:T(8,128)(2,1)S(1)}, u32[]{:S(2)}, u32[]{:S(2)}) collective-permute-start(bf16[256,128]{1,0:T(8,128)(2,1)S(1)} %step.26.own.refs_7_.refs_1_), channel_id=1, source_target_pairs={{0,1},{1,0},{2,3},{3,2},{4,5},{5,4},{6,7},{7,6},{70,71},{71,70},{6... | collective-permute-start | bytes 196616 | tf_op jit(solution)/shard_map/ppermute | solution.py:278
  141.2 6.8 %collective-permute-start.25 = (bf16[256,128]{1,0:T(8,128)(2,1)S(1)}, bf16[256,128]{1,0:T(8,128)(2,1)S(1)}, u32[]{:S(2)}, u32[]{:S(2)}) collective-permute-start(bf16[256,128]{1,0:T(8,128)(2,1)S(1)} %step.27.own.refs_7_.refs_1_), channel_id=1, source_target_pairs={{1,2},{2,1},{3,4},{4,3},{5,6},{6,5},{7,70},{70,7},{71,68},{68,71},... | collective-permute-start | bytes 196616 | tf_op jit(solution)/shard_map/ppermute | solution.py:278
  143.6 4.0 %collective-permute-start.26 = (bf16[256,128]{1,0:T(8,128)(2,1)S(1)}, bf16[256,128]{1,0:T(8,128)(2,1)S(1)}, u32[]{:S(2)}, u32[]{:S(2)}) collective-permute-start(bf16[256,128]{1,0:T(8,128)(2,1)S(1)} %step.27.own.refs_7_.refs_1_), channel_id=1, source_target_pairs={{0,1},{1,0},{2,3},{3,2},{4,5},{5,4},{6,7},{7,6},{70,71},{71,70},{6... | collective-permute-start | bytes 196616 | tf_op jit(solution)/shard_map/ppermute | solution.py:278
  148.9 6.5 %collective-permute-start.27 = (bf16[256,128]{1,0:T(8,128)(2,1)S(1)}, bf16[256,128]{1,0:T(8,128)(2,1)S(1)}, u32[]{:S(2)}, u32[]{:S(2)}) collective-permute-start(bf16[256,128]{1,0:T(8,128)(2,1)S(1)} %step.28.own.refs_7_.refs_1_), channel_id=1, source_target_pairs={{1,2},{2,1},{3,4},{4,3},{5,6},{6,5},{7,70},{70,7},{71,68},{68,71},... | collective-permute-start | bytes 196616 | tf_op jit(solution)/shard_map/ppermute | solution.py:278
  151.2 4.1 %collective-permute-start.28 = (bf16[256,128]{1,0:T(8,128)(2,1)S(1)}, bf16[256,128]{1,0:T(8,128)(2,1)S(1)}, u32[]{:S(2)}, u32[]{:S(2)}) collective-permute-start(bf16[256,128]{1,0:T(8,128)(2,1)S(1)} %step.28.own.refs_7_.refs_1_), channel_id=1, source_target_pairs={{0,1},{1,0},{2,3},{3,2},{4,5},{5,4},{6,7},{7,6},{70,71},{71,70},{6... | collective-permute-start | bytes 196616 | tf_op jit(solution)/shard_map/ppermute | solution.py:278
  156.5 6.7 %collective-permute-start.29 = (bf16[256,128]{1,0:T(8,128)(2,1)S(1)}, bf16[256,128]{1,0:T(8,128)(2,1)S(1)}, u32[]{:S(2)}, u32[]{:S(2)}) collective-permute-start(bf16[256,128]{1,0:T(8,128)(2,1)S(1)} %step.29.own.refs_7_.refs_1_), channel_id=1, source_target_pairs={{1,2},{2,1},{3,4},{4,3},{5,6},{6,5},{7,70},{70,7},{71,68},{68,71},... | collective-permute-start | bytes 196616 | tf_op jit(solution)/shard_map/ppermute | solution.py:278
  159.0 4.0 %collective-permute-start.30 = (bf16[256,128]{1,0:T(8,128)(2,1)S(1)}, bf16[256,128]{1,0:T(8,128)(2,1)S(1)}, u32[]{:S(2)}, u32[]{:S(2)}) collective-permute-start(bf16[256,128]{1,0:T(8,128)(2,1)S(1)} %step.29.own.refs_7_.refs_1_), channel_id=1, source_target_pairs={{0,1},{1,0},{2,3},{3,2},{4,5},{5,4},{6,7},{7,6},{70,71},{71,70},{6... | collective-permute-start | bytes 196616 | tf_op jit(solution)/shard_map/ppermute | solution.py:278
  164.3 6.6 %collective-permute-start.31 = (bf16[256,128]{1,0:T(8,128)(2,1)S(1)}, bf16[256,128]{1,0:T(8,128)(2,1)S(1)}, u32[]{:S(2)}, u32[]{:S(2)}) collective-permute-start(bf16[256,128]{1,0:T(8,128)(2,1)S(1)} %step.30.own.refs_7_), channel_id=1, source_target_pairs={{1,2},{2,1},{3,4},{4,3},{5,6},{6,5},{7,70},{70,7},{71,68},{68,71},... | collective-permute-start | bytes 196616 | tf_op jit(solution)/shard_map/ppermute | solution.py:278
  166.5 4.0 %collective-permute-start.32 = (bf16[256,128]{1,0:T(8,128)(2,1)S(1)}, bf16[256,128]{1,0:T(8,128)(2,1)S(1)}, u32[]{:S(2)}, u32[]{:S(2)}) collective-permute-start(bf16[256,128]{1,0:T(8,128)(2,1)S(1)} %step.30.own.refs_7_), channel_id=1, source_target_pairs={{0,1},{1,0},{2,3},{3,2},{4,5},{5,4},{6,7},{7,6},{70,71},{71,70},{6... | collective-permute-start | bytes 196616 | tf_op jit(solution)/shard_map/ppermute | solution.py:278
  170.6 0.8 copy-start.3
  170.6 0.8 copy-start.5
  170.6 0.8 copy-start.7
  172.5 7.6 %collective-permute-start.33 = (bf16[2,256,128]{2,1,0:T(8,128)(2,1)S(1)}, bf16[2,256,128]{2,1,0:T(8,128)(2,1)S(1)}, u32[]{:S(2)}, u32[]{:S(2)}) collective-permute-start(bf16[2,256,128]{2,1,0:T(8,128)(2,1)S(1)} %pad_maximum_fusion.3), channel_id=1, source_target_pairs={{0,64},{1,65},{2,66},{3,67},{4,68},{5,69},{6,70},{7,71},{16,80},{1... | collective-permute-start | bytes 393224 | tf_op jit(solution)/shard_map/ppermute | solution.py:381
  (3 other events, 2.0 us)

commit v8 on v7

--- a/solution.py
+++ b/solution.py
@@ -95,24 +95,8 @@
         sample_row(older, r, weight, store)
 
 
-def middle_kernel(own, beside, taps, stack):
-    for r in range(EARLY, EXT):
-
-        def store(ch, value):
-            stack[pl.ds(ch, 16), pl.ds((r - EARLY) * W, W)] = value
-
-        sample_row((None, own, beside), r, lambda n: taps[r, n], store)
-
-
-def step_kernel(priors, parts, first, sense, *refs):
-    refs = list(refs)
-    grid = (first[0], sense[0])
-    sides = [[refs.pop(0) for _ in range(3)] for _ in range(parts)]
-    newest = [refs.pop(0) for _ in range(2)] + [None] if priors else None
-    taps = refs.pop(0) if priors else None
-    middle = refs.pop(0) if priors else None
-    older = refs.pop(0) if priors == 2 else None
-    mixer, inner, outer, out, stack, joined, hidden = refs
+def block_parts(grid, sides, mixer, inner, joined, hidden, sampled):
+    cols = lax.broadcasted_iota(jnp.int32, (C, W), 1)
 
     def keep(row):
         at = grid[0] + grid[1] * row
@@ -122,31 +106,18 @@
         ref, at = far_row(trio, r - R)
         return ref[pl.ds(at, C), :]
 
-    depth = (parts + priors) * C
-    for r in (0, 2, 4, 6):
-        for n in range(2 if priors and r < EARLY else 0):
-
-            def store(ch, value):
-                stack[pl.ds(ch, 16), pl.ds((r + n) * W, W)] = value
-
-            sample_row(newest, r + n, lambda k: taps[r + n, k], store)
+    def join(r):
         pieces = [
             jnp.concatenate([side_row(trio, r), side_row(trio, r + 1)], axis=1) for trio in sides
-        ]
-        if priors:
-            near = stack[:, pl.ds(r * W, 2 * W)] if r < EARLY else middle[:, pl.ds((r - EARLY) * W, 2 * W)]
-            pieces.append(near)
-        if priors == 2:
-            pieces.append(older[:, pl.ds(r * W, 2 * W)])
+        ] + sampled(r)
         data = jnp.concatenate(pieces, axis=0)
-        both = leaky(jnp.dot(mixer[:, pl.ds(0, depth)], data, preferred_element_type=jnp.float32))
+        weights = mixer[:, pl.ds(0, data.shape[0])]
+        both = leaky(jnp.dot(weights, data, preferred_element_type=jnp.float32))
         for n in range(2):
             value = both[:, n * W : (n + 1) * W]
             if not R <= r + n < R + ROWS:
                 value = value * keep(r + n - R)
-            joined[pl.ds((r + n) * C, C), :] = value.astype(jnp.bfloat16)
-
-    cols = lax.broadcasted_iota(jnp.int32, (C, W), 1)
+            joined[pl.ds((r + n) * C, C), :] = value.astype(BF16)
 
     def conv_pair(source, kernel, r):
         data = jnp.concatenate(
@@ -161,17 +132,74 @@
             outs.append(left + part[C : 2 * C] + right)
         return outs
 
-    for r in (0, 2, 4):
+    def inside(r):
         for n, value in enumerate(conv_pair(joined, inner, r)):
             value = leaky(value)
             if r + n in (0, ROWS + 1):
                 value = value * keep(r + n - 1)
-            hidden[pl.ds((r + n) * C, C), :] = value.astype(jnp.bfloat16)
-
+            hidden[pl.ds((r + n) * C, C), :] = value.astype(BF16)
+
+    return join, inside, conv_pair
+
+
+def middle_kernel(priors, parts, first, sense, *refs):
+    refs = list(refs)
+    grid = (first[0], sense[0])
+    sides = [[None] + [refs.pop(0) for _ in range(2)] for _ in range(parts)]
+    own, beside, taps = (refs.pop(0) for _ in range(3))
+    older = refs.pop(0) if priors == 2 else None
+    mixer, inner, joined_out, hidden_out, stack, joined, hidden = refs
+    for r in range(EARLY, EXT):
+
+        def store(ch, value):
+            stack[pl.ds(ch, 16), pl.ds((r - EARLY) * W, W)] = value
+
+        sample_row((None, own, beside), r, lambda n: taps[r, n], store)
+
+    def sampled(r):
+        near = [stack[:, pl.ds((r - EARLY) * W, 2 * W)]]
+        return near + ([older[:, pl.ds(r * W, 2 * W)]] if older is not None else [])
+
+    join, inside, _ = block_parts(grid, sides, mixer, inner, joined, hidden, sampled)
+    join(4)
+    join(6)
+    inside(4)
+    joined_out[...] = joined[pl.ds(EARLY * C, (EXT - EARLY) * C), :]
+    hidden_out[...] = hidden[pl.ds(ROWS * C, 2 * C), :]
+
+
+def step_kernel(priors, parts, first, sense, *refs):
+    refs = list(refs)
+    grid = (first[0], sense[0])
+    sides = [[refs.pop(0) for _ in range(3)] for _ in range(parts)]
+    newest = [refs.pop(0) for _ in range(2)] + [None] if priors else None
+    taps = refs.pop(0) if priors else None
+    ready = [refs.pop(0) for _ in range(2)] if priors else None
+    older = refs.pop(0) if priors == 2 else None
+    mixer, inner, outer, out, stack, joined, hidden = refs
+
+    def sampled(r):
+        near = [stack[:, pl.ds(r * W, 2 * W)]] if priors else []
+        return near + ([older[:, pl.ds(r * W, 2 * W)]] if older is not None else [])
+
+    join, inside, conv_pair = block_parts(grid, sides, mixer, inner, joined, hidden, sampled)
+    if priors:
+        joined[pl.ds(EARLY * C, (EXT - EARLY) * C), :] = ready[0][...]
+        hidden[pl.ds(ROWS * C, 2 * C), :] = ready[1][...]
+    for r in (0, 2) if priors else (0, 2, 4, 6):
+        for n in range(2 if priors else 0):
+
+            def store(ch, value):
+                stack[pl.ds(ch, 16), pl.ds((r + n) * W, W)] = value
+
+            sample_row(newest, r + n, lambda k: taps[r + n, k], store)
+        join(r)
+    for r in (0, 2) if priors else (0, 2, 4):
+        inside(r)
     for r in (0, 2):
         for n, value in enumerate(conv_pair(hidden, outer, r)):
             base = joined[pl.ds((r + n + R) * C, C), :].astype(jnp.float32)
-            out[pl.ds((r + n) * C, C), :] = (base + value).astype(jnp.bfloat16)
+            out[pl.ds((r + n) * C, C), :] = (base + value).astype(BF16)
 
 
 def pack_kernel(sense, back_shift, back_fraction, ahead_shift, ahead_fraction, out):
@@ -207,16 +235,28 @@
     )(*operands)
 
 
-def run_middle(newest, taps):
+def run_middle(grid, sides, newest, taps, older, weights):
+    operands = list(grid)
+    for trio in sides:
+        operands += list(trio[1:])
+    operands += list(newest[1:]) + [taps] + older + list(weights[:2])
     return pl.pallas_call(
-        middle_kernel,
-        out_shape=jax.ShapeDtypeStruct((C, (EXT - EARLY) * W), BF16),
-        in_specs=[VMEM] * 3,
-        out_specs=VMEM,
+        functools.partial(middle_kernel, 1 + len(older), len(sides)),
+        out_shape=[
+            jax.ShapeDtypeStruct(((EXT - EARLY) * C, W), BF16),
+            jax.ShapeDtypeStruct((2 * C, W), BF16),
+        ],
+        in_specs=[SMEM, SMEM] + [VMEM] * (len(operands) - 2),
+        out_specs=[VMEM] * 2,
+        scratch_shapes=[
+            pltpu.VMEM((C, (EXT - EARLY) * W), BF16),
+            pltpu.VMEM((EXT * C, W), BF16),
+            pltpu.VMEM(((ROWS + 2) * C, W), BF16),
+        ],
         compiler_params=pltpu.CompilerParams(vmem_limit_bytes=16 * 2**20),
         cost_estimate=pl.CostEstimate(flops=10**6, bytes_accessed=2**10, transcendentals=0),
         name="middle",
-    )(newest[1], newest[2], taps)
+    )(*operands)
 
 
 def run_pack(grid, arrays):
@@ -236,7 +276,7 @@
         operands += list(trio)
     operands += (list(newest[:2]) if newest else []) + list(prepared) + list(weights)
     return pl.pallas_call(
-        functools.partial(step_kernel, max(0, len(prepared) - 1), len(sides)),
+        functools.partial(step_kernel, max(0, len(prepared) - 2), len(sides)),
         out_shape=jax.ShapeDtypeStruct((ROWS * C, W), BF16),
         in_specs=[SMEM, SMEM] + [VMEM] * (len(operands) - 2),
         out_specs=VMEM,
@@ -347,7 +387,7 @@
             prepared = []
             if n:
                 taps, *older = run_prepare(grid, history[1] if n > 1 else None, params[way, t])
-                prepared = [taps, run_middle(history[0], taps)] + older
+                prepared = [taps, *run_middle(grid, sides, history[0], taps, older, weights)] + older
             new = run_step(grid, sides, history[0] if n else None, prepared, weights)
             if n + 1 < FRAMES or not extra:
                 far, near = swap(new, new)

time: 183 us -> 188 us (1.027)
  the two profiles are of different devices: /device:TPU:10 before, /device:TPU:8 now
where the time goes in v8:
time: 188 us; the launch traced here: 187 us
  starting transfers between devices  110 us (59%)
  Pallas kernels  33.4 us (18%)
  waiting for transfers between devices  30.4 us (16%)
  local copies, waits for them, and re-layouts  10.3 us (5%)
    ppermute x16, starting transfers between devices, swap(): lax.ppermute(for_beside, axes, beside)  53.1 us
    ppermute x16, starting transfers between devices, swap(): lax.ppermute(for_across, axes, across)  37.4 us
    pallas_call x16, Pallas kernels, run_step(): pl.pallas_call(functools.partial(step_kernel, max(0, len(prepared) - 2),...  16 us
    all_to_all x1, waiting for transfers between devices, shards(): lax.all_to_all(jnp.broadcast_to(jnp.stack([for_even, for_odd])[None], (FR...  13.9 us
    ppermute x1, starting transfers between devices, shards(): lax.ppermute(mine, 'tile', [(q, mirror(q)) for q in range(lax.axis_size('...  10.9 us
    pallas_call x14, Pallas kernels, run_middle(): pl.pallas_call(functools.partial(middle_kernel, 1 + len(older), len(sides...  9.55 us
    pallas_call x14, Pallas kernels, run_prepare(): pl.pallas_call(functools.partial(prepare_kernel, 2 if older else 1), out_...  7.79 us
    all_to_all x1, starting transfers between devices, shards(): lax.all_to_all(jnp.broadcast_to(jnp.stack([for_even, for_odd])[None], (FR...  7.55 us
  transfers between devices with their start and end apart: 35, of which 18 were waited for; matrix products, arithmetic and copies ran while one was open for 2% of the time, Pallas kernels for 9%

profile of v8, /device:TPU:8, one launch (start us, length us, event | category | flops | bytes accessed | tf_op | source)
XLA Modules:
  0.0 186.9 jit_solution(3440392499397534252)
XLA Ops:
  2.3 10.9 %collective-permute-start = (bf16[320,128]{1,0:T(8,128)(2,1)S(1)}, bf16[320,128]{1,0:T(8,128)(2,1)S(1)}, u32[]{:S(2)}, u32[]{:S(2)}) collective-permute-start(bf16[320,128]{1,0:T(8,128)(2,1)S(1)} %pad_maximum_fusion.4), channel_id=1, source_target_pairs={{0,14},{1,15},{2,12},{3,13},{4,10},{5,11},{6,8},{7,9},{8,6},{9,7},... | collective-permute-start | bytes 245768 | tf_op jit(solution)/shard_map/ppermute | solution.py:358
  13.3 4.1 %collective-permute-done = bf16[320,128]{1,0:T(8,128)(2,1)S(1)} collective-permute-done((bf16[320,128]{1,0:T(8,128)(2,1)S(1)}, bf16[320,128]{1,0:T(8,128)(2,1)S(1)}, u32[]{:S(2)}, u32[]{:S(2)}) %collective-permute-start) | collective-permute-done | bytes 81952 | tf_op jit(solution)/shard_map/ppermute | solution.py:358
  18.4 7.5 %all-to-all-start = ((bf16[8,320,128]{2,1,0:T(8,128)(2,1)}), bf16[8,320,128]{2,1,0:T(8,128)(2,1)S(1)}, u32[]{:S(2)}, u32[]{:S(2)}) async-start(bf16[8,320,128]{2,1,0:T(8,128)(2,1)} %bitcast.7), calls=%async_computation | async-start | bytes 1310720 | tf_op jit(solution)/shard_map/all_to_all | solution.py:361
  31.2 13.9 %all-to-all-done = bf16[8,320,128]{2,1,0:T(8,128)(2,1)S(1)} async-done(((bf16[8,320,128]{2,1,0:T(8,128)(2,1)}), bf16[8,320,128]{2,1,0:T(8,128)(2,1)S(1)}, u32[]{:S(2)}, u32[]{:S(2)}) %all-to-all-start) | async-done | bytes 655392 | tf_op jit(solution)/shard_map/all_to_all | solution.py:361
  45.1 1.9 %collective-permute-start.1 = (bf16[8,160,128]{2,1,0:T(8,128)(2,1)S(1)}, bf16[8,160,128]{2,1,0:T(8,128)(2,1)S(1)}, u32[]{:S(2)}, u32[]{:S(2)}) collective-permute-start(bf16[8,160,128]{2,1,0:T(8,128)(2,1)S(1)} %pad_maximum_fusion), channel_id=1, source_target_pairs={{1,2},{2,1},{3,4},{4,3},{5,6},{6,5},{7,70},{70,7},{71,68},{68,71},... | collective-permute-start | bytes 983048 | tf_op jit(solution)/shard_map/ppermute | solution.py:318
  47.1 4.4 %collective-permute-start.2 = (bf16[8,160,128]{2,1,0:T(8,128)(2,1)S(1)}, bf16[8,160,128]{2,1,0:T(8,128)(2,1)S(1)}, u32[]{:S(2)}, u32[]{:S(2)}) collective-permute-start(bf16[8,160,128]{2,1,0:T(8,128)(2,1)S(1)} %pad_maximum_fusion.1), channel_id=1, source_target_pairs={{0,1},{1,0},{2,3},{3,2},{4,5},{5,4},{6,7},{7,6},{70,71},{71,70},{6... | collective-permute-start | bytes 983048 | tf_op jit(solution)/shard_map/ppermute | solution.py:318
  51.7 1.8 collective-permute-done.1
  55.1 1.9 %collective-permute-start.3 = (bf16[256,128]{1,0:T(8,128)(2,1)S(1)}, bf16[256,128]{1,0:T(8,128)(2,1)S(1)}, u32[]{:S(2)}, u32[]{:S(2)}) collective-permute-start(bf16[256,128]{1,0:T(8,128)(2,1)S(1)} %step.16.refs_2_.refs_4_.refs_1_), channel_id=1, source_target_pairs={{1,2},{2,1},{3,4},{4,3},{5,6},{6,5},{7,70},{70,7},{71,68},{68,71},... | collective-permute-start | bytes 196616 | tf_op jit(solution)/shard_map/ppermute | solution.py:318
  57.0 5.3 %collective-permute-start.4 = (bf16[256,128]{1,0:T(8,128)(2,1)S(1)}, bf16[256,128]{1,0:T(8,128)(2,1)S(1)}, u32[]{:S(2)}, u32[]{:S(2)}) collective-permute-start(bf16[256,128]{1,0:T(8,128)(2,1)S(1)} %step.16.refs_2_.refs_4_.refs_1_), channel_id=1, source_target_pairs={{0,1},{1,0},{2,3},{3,2},{4,5},{5,4},{6,7},{7,6},{70,71},{71,70},{6... | collective-permute-start | bytes 196616 | tf_op jit(solution)/shard_map/ppermute | solution.py:318
  65.5 1.9 %collective-permute-start.5 = (bf16[256,128]{1,0:T(8,128)(2,1)S(1)}, bf16[256,128]{1,0:T(8,128)(2,1)S(1)}, u32[]{:S(2)}, u32[]{:S(2)}) collective-permute-start(bf16[256,128]{1,0:T(8,128)(2,1)S(1)} %step.17.refs_2_.refs_4_.refs_1_), channel_id=1, source_target_pairs={{1,2},{2,1},{3,4},{4,3},{5,6},{6,5},{7,70},{70,7},{71,68},{68,71},... | collective-permute-start | bytes 196616 | tf_op jit(solution)/shard_map/ppermute | solution.py:318
  67.4 2.4 %collective-permute-start.6 = (bf16[256,128]{1,0:T(8,128)(2,1)S(1)}, bf16[256,128]{1,0:T(8,128)(2,1)S(1)}, u32[]{:S(2)}, u32[]{:S(2)}) collective-permute-start(bf16[256,128]{1,0:T(8,128)(2,1)S(1)} %step.17.refs_2_.refs_4_.refs_1_), channel_id=1, source_target_pairs={{0,1},{1,0},{2,3},{3,2},{4,5},{5,4},{6,7},{7,6},{70,71},{71,70},{6... | collective-permute-start | bytes 196616 | tf_op jit(solution)/shard_map/ppermute | solution.py:318
  71.4 1.0 step.18.refs_2_.refs_4_.refs_1_
  72.5 3.5 %collective-permute-start.7 = (bf16[256,128]{1,0:T(8,128)(2,1)S(1)}, bf16[256,128]{1,0:T(8,128)(2,1)S(1)}, u32[]{:S(2)}, u32[]{:S(2)}) collective-permute-start(bf16[256,128]{1,0:T(8,128)(2,1)S(1)} %step.18.refs_2_.refs_4_.refs_1_), channel_id=1, source_target_pairs={{1,2},{2,1},{3,4},{4,3},{5,6},{6,5},{7,70},{70,7},{71,68},{68,71},... | collective-permute-start | bytes 196616 | tf_op jit(solution)/shard_map/ppermute | solution.py:318
  76.0 2.8 %collective-permute-start.8 = (bf16[256,128]{1,0:T(8,128)(2,1)S(1)}, bf16[256,128]{1,0:T(8,128)(2,1)S(1)}, u32[]{:S(2)}, u32[]{:S(2)}) collective-permute-start(bf16[256,128]{1,0:T(8,128)(2,1)S(1)} %step.18.refs_2_.refs_4_.refs_1_), channel_id=1, source_target_pairs={{0,1},{1,0},{2,3},{3,2},{4,5},{5,4},{6,7},{7,6},{70,71},{71,70},{6... | collective-permute-start | bytes 196616 | tf_op jit(solution)/shard_map/ppermute | solution.py:318
  80.4 1.0 step.19.refs_2_.refs_4_.refs_1_
  81.4 1.9 %collective-permute-start.9 = (bf16[256,128]{1,0:T(8,128)(2,1)S(1)}, bf16[256,128]{1,0:T(8,128)(2,1)S(1)}, u32[]{:S(2)}, u32[]{:S(2)}) collective-permute-start(bf16[256,128]{1,0:T(8,128)(2,1)S(1)} %step.19.refs_2_.refs_4_.refs_1_), channel_id=1, source_target_pairs={{1,2},{2,1},{3,4},{4,3},{5,6},{6,5},{7,70},{70,7},{71,68},{68,71},... | collective-permute-start | bytes 196616 | tf_op jit(solution)/shard_map/ppermute | solution.py:318
  83.4 3.0 %collective-permute-start.10 = (bf16[256,128]{1,0:T(8,128)(2,1)S(1)}, bf16[256,128]{1,0:T(8,128)(2,1)S(1)}, u32[]{:S(2)}, u32[]{:S(2)}) collective-permute-start(bf16[256,128]{1,0:T(8,128)(2,1)S(1)} %step.19.refs_2_.refs_4_.refs_1_), channel_id=1, source_target_pairs={{0,1},{1,0},{2,3},{3,2},{4,5},{5,4},{6,7},{7,6},{70,71},{71,70},{6... | collective-permute-start | bytes 196616 | tf_op jit(solution)/shard_map/ppermute | solution.py:318
  87.9 1.0 step.20.refs_2_.refs_4_.refs_1_
  89.0 2.9 %collective-permute-start.11 = (bf16[256,128]{1,0:T(8,128)(2,1)S(1)}, bf16[256,128]{1,0:T(8,128)(2,1)S(1)}, u32[]{:S(2)}, u32[]{:S(2)}) collective-permute-start(bf16[256,128]{1,0:T(8,128)(2,1)S(1)} %step.20.refs_2_.refs_4_.refs_1_), channel_id=1, source_target_pairs={{1,2},{2,1},{3,4},{4,3},{5,6},{6,5},{7,70},{70,7},{71,68},{68,71},... | collective-permute-start | bytes 196616 | tf_op jit(solution)/shard_map/ppermute | solution.py:318
  91.9 3.3 %collective-permute-start.12 = (bf16[256,128]{1,0:T(8,128)(2,1)S(1)}, bf16[256,128]{1,0:T(8,128)(2,1)S(1)}, u32[]{:S(2)}, u32[]{:S(2)}) collective-permute-start(bf16[256,128]{1,0:T(8,128)(2,1)S(1)} %step.20.refs_2_.refs_4_.refs_1_), channel_id=1, source_target_pairs={{0,1},{1,0},{2,3},{3,2},{4,5},{5,4},{6,7},{7,6},{70,71},{71,70},{6... | collective-permute-start | bytes 196616 | tf_op jit(solution)/shard_map/ppermute | solution.py:318
  96.6 1.0 step.21.refs_2_.refs_4_.refs_1_
  97.7 1.9 %collective-permute-start.13 = (bf16[256,128]{1,0:T(8,128)(2,1)S(1)}, bf16[256,128]{1,0:T(8,128)(2,1)S(1)}, u32[]{:S(2)}, u32[]{:S(2)}) collective-permute-start(bf16[256,128]{1,0:T(8,128)(2,1)S(1)} %step.21.refs_2_.refs_4_.refs_1_), channel_id=1, source_target_pairs={{1,2},{2,1},{3,4},{4,3},{5,6},{6,5},{7,70},{70,7},{71,68},{68,71},... | collective-permute-start | bytes 196616 | tf_op jit(solution)/shard_map/ppermute | solution.py:318
  99.6 3.0 %collective-permute-start.14 = (bf16[256,128]{1,0:T(8,128)(2,1)S(1)}, bf16[256,128]{1,0:T(8,128)(2,1)S(1)}, u32[]{:S(2)}, u32[]{:S(2)}) collective-permute-start(bf16[256,128]{1,0:T(8,128)(2,1)S(1)} %step.21.refs_2_.refs_4_.refs_1_), channel_id=1, source_target_pairs={{0,1},{1,0},{2,3},{3,2},{4,5},{5,4},{6,7},{7,6},{70,71},{71,70},{6... | collective-permute-start | bytes 196616 | tf_op jit(solution)/shard_map/ppermute | solution.py:318
  105.2 2.9 %collective-permute-start.15 = (bf16[256,128]{1,0:T(8,128)(2,1)S(1)}, bf16[256,128]{1,0:T(8,128)(2,1)S(1)}, u32[]{:S(2)}, u32[]{:S(2)}) collective-permute-start(bf16[256,128]{1,0:T(8,128)(2,1)S(1)} %step.22.refs_2_.refs_4_), channel_id=1, source_target_pairs={{1,2},{2,1},{3,4},{4,3},{5,6},{6,5},{7,70},{70,7},{71,68},{68,71},... | collective-permute-start | bytes 196616 | tf_op jit(solution)/shard_map/ppermute | solution.py:318
  108.1 3.2 %collective-permute-start.16 = (bf16[256,128]{1,0:T(8,128)(2,1)S(1)}, bf16[256,128]{1,0:T(8,128)(2,1)S(1)}, u32[]{:S(2)}, u32[]{:S(2)}) collective-permute-start(bf16[256,128]{1,0:T(8,128)(2,1)S(1)} %step.22.refs_2_.refs_4_), channel_id=1, source_target_pairs={{0,1},{1,0},{2,3},{3,2},{4,5},{5,4},{6,7},{7,6},{70,71},{71,70},{6... | collective-permute-start | bytes 196616 | tf_op jit(solution)/shard_map/ppermute | solution.py:318
  113.9 1.9 %collective-permute-start.17 = (bf16[256,128]{1,0:T(8,128)(2,1)S(1)}, bf16[256,128]{1,0:T(8,128)(2,1)S(1)}, u32[]{:S(2)}, u32[]{:S(2)}) collective-permute-start(bf16[256,128]{1,0:T(8,128)(2,1)S(1)} %step.23.refs_4_), channel_id=1, source_target_pairs={{1,2},{2,1},{3,4},{4,3},{5,6},{6,5},{7,70},{70,7},{71,68},{68,71},... | collective-permute-start | bytes 196616 | tf_op jit(solution)/shard_map/ppermute | solution.py:318
  115.9 3.0 %collective-permute-start.18 = (bf16[256,128]{1,0:T(8,128)(2,1)S(1)}, bf16[256,128]{1,0:T(8,128)(2,1)S(1)}, u32[]{:S(2)}, u32[]{:S(2)}) collective-permute-start(bf16[256,128]{1,0:T(8,128)(2,1)S(1)} %step.23.refs_4_), channel_id=1, source_target_pairs={{0,1},{1,0},{2,3},{3,2},{4,5},{5,4},{6,7},{7,6},{70,71},{71,70},{6... | collective-permute-start | bytes 196616 | tf_op jit(solution)/shard_map/ppermute | solution.py:318
  120.5 2.9 %collective-permute-start.19 = (bf16[256,128]{1,0:T(8,128)(2,1)S(1)}, bf16[256,128]{1,0:T(8,128)(2,1)S(1)}, u32[]{:S(2)}, u32[]{:S(2)}) collective-permute-start(bf16[256,128]{1,0:T(8,128)(2,1)S(1)} %step.24.refs_4_.refs_7_.refs_1_), channel_id=1, source_target_pairs={{1,2},{2,1},{3,4},{4,3},{5,6},{6,5},{7,70},{70,7},{71,68},{68,71},... | collective-permute-start | bytes 196616 | tf_op jit(solution)/shard_map/ppermute | solution.py:318
  123.5 3.2 %collective-permute-start.20 = (bf16[256,128]{1,0:T(8,128)(2,1)S(1)}, bf16[256,128]{1,0:T(8,128)(2,1)S(1)}, u32[]{:S(2)}, u32[]{:S(2)}) collective-permute-start(bf16[256,128]{1,0:T(8,128)(2,1)S(1)} %step.24.refs_4_.refs_7_.refs_1_), channel_id=1, source_target_pairs={{0,1},{1,0},{2,3},{3,2},{4,5},{5,4},{6,7},{7,6},{70,71},{71,70},{6... | collective-permute-start | bytes 196616 | tf_op jit(solution)/shard_map/ppermute | solution.py:318
  129.2 1.9 %collective-permute-start.21 = (bf16[256,128]{1,0:T(8,128)(2,1)S(1)}, bf16[256,128]{1,0:T(8,128)(2,1)S(1)}, u32[]{:S(2)}, u32[]{:S(2)}) collective-permute-start(bf16[256,128]{1,0:T(8,128)(2,1)S(1)} %step.25.refs_4_.refs_7_.refs_1_), channel_id=1, source_target_pairs={{1,2},{2,1},{3,4},{4,3},{5,6},{6,5},{7,70},{70,7},{71,68},{68,71},... | collective-permute-start | bytes 196616 | tf_op jit(solution)/shard_map/ppermute | solution.py:318
  131.1 3.7 %collective-permute-start.22 = (bf16[256,128]{1,0:T(8,128)(2,1)S(1)}, bf16[256,128]{1,0:T(8,128)(2,1)S(1)}, u32[]{:S(2)}, u32[]{:S(2)}) collective-permute-start(bf16[256,128]{1,0:T(8,128)(2,1)S(1)} %step.25.refs_4_.refs_7_.refs_1_), channel_id=1, source_target_pairs={{0,1},{1,0},{2,3},{3,2},{4,5},{5,4},{6,7},{7,6},{70,71},{71,70},{6... | collective-permute-start | bytes 196616 | tf_op jit(solution)/shard_map/ppermute | solution.py:318
  136.4 1.0 step.26.refs_4_.refs_7_.refs_1_
  137.4 2.2 %collective-permute-start.23 = (bf16[256,128]{1,0:T(8,128)(2,1)S(1)}, bf16[256,128]{1,0:T(8,128)(2,1)S(1)}, u32[]{:S(2)}, u32[]{:S(2)}) collective-permute-start(bf16[256,128]{1,0:T(8,128)(2,1)S(1)} %step.26.refs_4_.refs_7_.refs_1_), channel_id=1, source_target_pairs={{1,2},{2,1},{3,4},{4,3},{5,6},{6,5},{7,70},{70,7},{71,68},{68,71},... | collective-permute-start | bytes 196616 | tf_op jit(solution)/shard_map/ppermute | solution.py:318
  139.7 3.1 %collective-permute-start.24 = (bf16[256,128]{1,0:T(8,128)(2,1)S(1)}, bf16[256,128]{1,0:T(8,128)(2,1)S(1)}, u32[]{:S(2)}, u32[]{:S(2)}) collective-permute-start(bf16[256,128]{1,0:T(8,128)(2,1)S(1)} %step.26.refs_4_.refs_7_.refs_1_), channel_id=1, source_target_pairs={{0,1},{1,0},{2,3},{3,2},{4,5},{5,4},{6,7},{7,6},{70,71},{71,70},{6... | collective-permute-start | bytes 196616 | tf_op jit(solution)/shard_map/ppermute | solution.py:318
  144.4 1.0 step.27.refs_4_.refs_7_.refs_1_
  145.5 2.4 %collective-permute-start.25 = (bf16[256,128]{1,0:T(8,128)(2,1)S(1)}, bf16[256,128]{1,0:T(8,128)(2,1)S(1)}, u32[]{:S(2)}, u32[]{:S(2)}) collective-permute-start(bf16[256,128]{1,0:T(8,128)(2,1)S(1)} %step.27.refs_4_.refs_7_.refs_1_), channel_id=1, source_target_pairs={{1,2},{2,1},{3,4},{4,3},{5,6},{6,5},{7,70},{70,7},{71,68},{68,71},... | collective-permute-start | bytes 196616 | tf_op jit(solution)/shard_map/ppermute | solution.py:318
  147.9 3.4 %collective-permute-start.26 = (bf16[256,128]{1,0:T(8,128)(2,1)S(1)}, bf16[256,128]{1,0:T(8,128)(2,1)S(1)}, u32[]{:S(2)}, u32[]{:S(2)}) collective-permute-start(bf16[256,128]{1,0:T(8,128)(2,1)S(1)} %step.27.refs_4_.refs_7_.refs_1_), channel_id=1, source_target_pairs={{0,1},{1,0},{2,3},{3,2},{4,5},{5,4},{6,7},{7,6},{70,71},{71,70},{6... | collective-permute-start | bytes 196616 | tf_op jit(solution)/shard_map/ppermute | solution.py:318
  152.6 1.0 step.28.refs_4_.refs_7_.refs_1_
  153.7 2.2 %collective-permute-start.27 = (bf16[256,128]{1,0:T(8,128)(2,1)S(1)}, bf16[256,128]{1,0:T(8,128)(2,1)S(1)}, u32[]{:S(2)}, u32[]{:S(2)}) collective-permute-start(bf16[256,128]{1,0:T(8,128)(2,1)S(1)} %step.28.refs_4_.refs_7_.refs_1_), channel_id=1, source_target_pairs={{1,2},{2,1},{3,4},{4,3},{5,6},{6,5},{7,70},{70,7},{71,68},{68,71},... | collective-permute-start | bytes 196616 | tf_op jit(solution)/shard_map/ppermute | solution.py:318
  155.9 3.1 %collective-permute-start.28 = (bf16[256,128]{1,0:T(8,128)(2,1)S(1)}, bf16[256,128]{1,0:T(8,128)(2,1)S(1)}, u32[]{:S(2)}, u32[]{:S(2)}) collective-permute-start(bf16[256,128]{1,0:T(8,128)(2,1)S(1)} %step.28.refs_4_.refs_7_.refs_1_), channel_id=1, source_target_pairs={{0,1},{1,0},{2,3},{3,2},{4,5},{5,4},{6,7},{7,6},{70,71},{71,70},{6... | collective-permute-start | bytes 196616 | tf_op jit(solution)/shard_map/ppermute | solution.py:318
  160.6 1.0 step.29.refs_4_.refs_7_.refs_1_
  161.7 2.4 %collective-permute-start.29 = (bf16[256,128]{1,0:T(8,128)(2,1)S(1)}, bf16[256,128]{1,0:T(8,128)(2,1)S(1)}, u32[]{:S(2)}, u32[]{:S(2)}) collective-permute-start(bf16[256,128]{1,0:T(8,128)(2,1)S(1)} %step.29.refs_4_.refs_7_.refs_1_), channel_id=1, source_target_pairs={{1,2},{2,1},{3,4},{4,3},{5,6},{6,5},{7,70},{70,7},{71,68},{68,71},... | collective-permute-start | bytes 196616 | tf_op jit(solution)/shard_map/ppermute | solution.py:318
  164.1 3.1 %collective-permute-start.30 = (bf16[256,128]{1,0:T(8,128)(2,1)S(1)}, bf16[256,128]{1,0:T(8,128)(2,1)S(1)}, u32[]{:S(2)}, u32[]{:S(2)}) collective-permute-start(bf16[256,128]{1,0:T(8,128)(2,1)S(1)} %step.29.refs_4_.refs_7_.refs_1_), channel_id=1, source_target_pairs={{0,1},{1,0},{2,3},{3,2},{4,5},{5,4},{6,7},{7,6},{70,71},{71,70},{6... | collective-permute-start | bytes 196616 | tf_op jit(solution)/shard_map/ppermute | solution.py:318
  168.9 1.0 step.30.refs_4_.refs_7_
  169.9 2.2 %collective-permute-start.31 = (bf16[256,128]{1,0:T(8,128)(2,1)S(1)}, bf16[256,128]{1,0:T(8,128)(2,1)S(1)}, u32[]{:S(2)}, u32[]{:S(2)}) collective-permute-start(bf16[256,128]{1,0:T(8,128)(2,1)S(1)} %step.30.refs_4_.refs_7_), channel_id=1, source_target_pairs={{1,2},{2,1},{3,4},{4,3},{5,6},{6,5},{7,70},{70,7},{71,68},{68,71},... | collective-permute-start | bytes 196616 | tf_op jit(solution)/shard_map/ppermute | solution.py:318
  172.1 3.1 %collective-permute-start.32 = (bf16[256,128]{1,0:T(8,128)(2,1)S(1)}, bf16[256,128]{1,0:T(8,128)(2,1)S(1)}, u32[]{:S(2)}, u32[]{:S(2)}) collective-permute-start(bf16[256,128]{1,0:T(8,128)(2,1)S(1)} %step.30.refs_4_.refs_7_), channel_id=1, source_target_pairs={{0,1},{1,0},{2,3},{3,2},{4,5},{5,4},{6,7},{7,6},{70,71},{71,70},{6... | collective-permute-start | bytes 196616 | tf_op jit(solution)/shard_map/ppermute | solution.py:318
  178.0 1.3 collective-permute-start.33
  179.4 6.3 %collective-permute-done.33 = bf16[2,256,128]{2,1,0:T(8,128)(2,1)S(1)} collective-permute-done((bf16[2,256,128]{2,1,0:T(8,128)(2,1)S(1)}, bf16[2,256,128]{2,1,0:T(8,128)(2,1)S(1)}, u32[]{:S(2)}, u32[]{:S(2)}) %collective-permute-start.33) | collective-permute-done | bytes 131104 | tf_op jit(solution)/shard_map/ppermute | solution.py:421
  (150 shorter events, 39.6 us)
Async XLA Ops:
  1.5 0.7 copy-start.10
  1.5 0.7 copy-start.11
  2.3 15.1 %collective-permute-start = (bf16[320,128]{1,0:T(8,128)(2,1)S(1)}, bf16[320,128]{1,0:T(8,128)(2,1)S(1)}, u32[]{:S(2)}, u32[]{:S(2)}) collective-permute-start(bf16[320,128]{1,0:T(8,128)(2,1)S(1)} %pad_maximum_fusion.4), channel_id=1, source_target_pairs={{0,14},{1,15},{2,12},{3,13},{4,10},{5,11},{6,8},{7,9},{8,6},{9,7},... | collective-permute-start | bytes 245768 | tf_op jit(solution)/shard_map/ppermute | solution.py:358
  18.4 26.6 %all-to-all-start = ((bf16[8,320,128]{2,1,0:T(8,128)(2,1)}), bf16[8,320,128]{2,1,0:T(8,128)(2,1)S(1)}, u32[]{:S(2)}, u32[]{:S(2)}) async-start(bf16[8,320,128]{2,1,0:T(8,128)(2,1)} %bitcast.7), calls=%async_computation | async-start | bytes 1310720 | tf_op jit(solution)/shard_map/all_to_all | solution.py:361
  26.0 0.9 copy-start.12
  26.9 0.9 copy-start.13
  28.5 0.9 copy-start.14
  29.4 0.9 copy-start.15
  45.1 8.4 %collective-permute-start.1 = (bf16[8,160,128]{2,1,0:T(8,128)(2,1)S(1)}, bf16[8,160,128]{2,1,0:T(8,128)(2,1)S(1)}, u32[]{:S(2)}, u32[]{:S(2)}) collective-permute-start(bf16[8,160,128]{2,1,0:T(8,128)(2,1)S(1)} %pad_maximum_fusion), channel_id=1, source_target_pairs={{1,2},{2,1},{3,4},{4,3},{5,6},{6,5},{7,70},{70,7},{71,68},{68,71},... | collective-permute-start | bytes 983048 | tf_op jit(solution)/shard_map/ppermute | solution.py:318
  47.1 6.5 %collective-permute-start.2 = (bf16[8,160,128]{2,1,0:T(8,128)(2,1)S(1)}, bf16[8,160,128]{2,1,0:T(8,128)(2,1)S(1)}, u32[]{:S(2)}, u32[]{:S(2)}) collective-permute-start(bf16[8,160,128]{2,1,0:T(8,128)(2,1)S(1)} %pad_maximum_fusion.1), channel_id=1, source_target_pairs={{0,1},{1,0},{2,3},{3,2},{4,5},{5,4},{6,7},{7,6},{70,71},{71,70},{6... | collective-permute-start | bytes 983048 | tf_op jit(solution)/shard_map/ppermute | solution.py:318
  51.5 2.1 %copy-start.2 = (bf16[256,128]{1,0:T(8,128)(2,1)}, bf16[256,128]{1,0:T(8,128)(2,1)S(1)}, u32[]{:S(2)}) copy-start(bf16[256,128]{1,0:T(8,128)(2,1)S(1)} %get-tuple-element.113.refs_1_.refs_0_) | copy-start | bytes 196612
  53.6 0.8 copy-start.1
  53.6 1.5 copy-start.4
  55.1 9.4 %collective-permute-start.3 = (bf16[256,128]{1,0:T(8,128)(2,1)S(1)}, bf16[256,128]{1,0:T(8,128)(2,1)S(1)}, u32[]{:S(2)}, u32[]{:S(2)}) collective-permute-start(bf16[256,128]{1,0:T(8,128)(2,1)S(1)} %step.16.refs_2_.refs_4_.refs_1_), channel_id=1, source_target_pairs={{1,2},{2,1},{3,4},{4,3},{5,6},{6,5},{7,70},{70,7},{71,68},{68,71},... | collective-permute-start | bytes 196616 | tf_op jit(solution)/shard_map/ppermute | solution.py:318
  57.0 6.8 %collective-permute-start.4 = (bf16[256,128]{1,0:T(8,128)(2,1)S(1)}, bf16[256,128]{1,0:T(8,128)(2,1)S(1)}, u32[]{:S(2)}, u32[]{:S(2)}) collective-permute-start(bf16[256,128]{1,0:T(8,128)(2,1)S(1)} %step.16.refs_2_.refs_4_.refs_1_), channel_id=1, source_target_pairs={{0,1},{1,0},{2,3},{3,2},{4,5},{5,4},{6,7},{7,6},{70,71},{71,70},{6... | collective-permute-start | bytes 196616 | tf_op jit(solution)/shard_map/ppermute | solution.py:318
  65.5 5.9 %collective-permute-start.5 = (bf16[256,128]{1,0:T(8,128)(2,1)S(1)}, bf16[256,128]{1,0:T(8,128)(2,1)S(1)}, u32[]{:S(2)}, u32[]{:S(2)}) collective-permute-start(bf16[256,128]{1,0:T(8,128)(2,1)S(1)} %step.17.refs_2_.refs_4_.refs_1_), channel_id=1, source_target_pairs={{1,2},{2,1},{3,4},{4,3},{5,6},{6,5},{7,70},{70,7},{71,68},{68,71},... | collective-permute-start | bytes 196616 | tf_op jit(solution)/shard_map/ppermute | solution.py:318
  67.4 3.3 %collective-permute-start.6 = (bf16[256,128]{1,0:T(8,128)(2,1)S(1)}, bf16[256,128]{1,0:T(8,128)(2,1)S(1)}, u32[]{:S(2)}, u32[]{:S(2)}) collective-permute-start(bf16[256,128]{1,0:T(8,128)(2,1)S(1)} %step.17.refs_2_.refs_4_.refs_1_), channel_id=1, source_target_pairs={{0,1},{1,0},{2,3},{3,2},{4,5},{5,4},{6,7},{7,6},{70,71},{71,70},{6... | collective-permute-start | bytes 196616 | tf_op jit(solution)/shard_map/ppermute | solution.py:318
  72.5 7.9 %collective-permute-start.7 = (bf16[256,128]{1,0:T(8,128)(2,1)S(1)}, bf16[256,128]{1,0:T(8,128)(2,1)S(1)}, u32[]{:S(2)}, u32[]{:S(2)}) collective-permute-start(bf16[256,128]{1,0:T(8,128)(2,1)S(1)} %step.18.refs_2_.refs_4_.refs_1_), channel_id=1, source_target_pairs={{1,2},{2,1},{3,4},{4,3},{5,6},{6,5},{7,70},{70,7},{71,68},{68,71},... | collective-permute-start | bytes 196616 | tf_op jit(solution)/shard_map/ppermute | solution.py:318
  76.0 3.7 %collective-permute-start.8 = (bf16[256,128]{1,0:T(8,128)(2,1)S(1)}, bf16[256,128]{1,0:T(8,128)(2,1)S(1)}, u32[]{:S(2)}, u32[]{:S(2)}) collective-permute-start(bf16[256,128]{1,0:T(8,128)(2,1)S(1)} %step.18.refs_2_.refs_4_.refs_1_), channel_id=1, source_target_pairs={{0,1},{1,0},{2,3},{3,2},{4,5},{5,4},{6,7},{7,6},{70,71},{71,70},{6... | collective-permute-start | bytes 196616 | tf_op jit(solution)/shard_map/ppermute | solution.py:318
  81.4 6.5 %collective-permute-start.9 = (bf16[256,128]{1,0:T(8,128)(2,1)S(1)}, bf16[256,128]{1,0:T(8,128)(2,1)S(1)}, u32[]{:S(2)}, u32[]{:S(2)}) collective-permute-start(bf16[256,128]{1,0:T(8,128)(2,1)S(1)} %step.19.refs_2_.refs_4_.refs_1_), channel_id=1, source_target_pairs={{1,2},{2,1},{3,4},{4,3},{5,6},{6,5},{7,70},{70,7},{71,68},{68,71},... | collective-permute-start | bytes 196616 | tf_op jit(solution)/shard_map/ppermute | solution.py:318
  83.4 3.8 %collective-permute-start.10 = (bf16[256,128]{1,0:T(8,128)(2,1)S(1)}, bf16[256,128]{1,0:T(8,128)(2,1)S(1)}, u32[]{:S(2)}, u32[]{:S(2)}) collective-permute-start(bf16[256,128]{1,0:T(8,128)(2,1)S(1)} %step.19.refs_2_.refs_4_.refs_1_), channel_id=1, source_target_pairs={{0,1},{1,0},{2,3},{3,2},{4,5},{5,4},{6,7},{7,6},{70,71},{71,70},{6... | collective-permute-start | bytes 196616 | tf_op jit(solution)/shard_map/ppermute | solution.py:318
  89.0 7.7 %collective-permute-start.11 = (bf16[256,128]{1,0:T(8,128)(2,1)S(1)}, bf16[256,128]{1,0:T(8,128)(2,1)S(1)}, u32[]{:S(2)}, u32[]{:S(2)}) collective-permute-start(bf16[256,128]{1,0:T(8,128)(2,1)S(1)} %step.20.refs_2_.refs_4_.refs_1_), channel_id=1, source_target_pairs={{1,2},{2,1},{3,4},{4,3},{5,6},{6,5},{7,70},{70,7},{71,68},{68,71},... | collective-permute-start | bytes 196616 | tf_op jit(solution)/shard_map/ppermute | solution.py:318
  91.9 4.0 %collective-permute-start.12 = (bf16[256,128]{1,0:T(8,128)(2,1)S(1)}, bf16[256,128]{1,0:T(8,128)(2,1)S(1)}, u32[]{:S(2)}, u32[]{:S(2)}) collective-permute-start(bf16[256,128]{1,0:T(8,128)(2,1)S(1)} %step.20.refs_2_.refs_4_.refs_1_), channel_id=1, source_target_pairs={{0,1},{1,0},{2,3},{3,2},{4,5},{5,4},{6,7},{7,6},{70,71},{71,70},{6... | collective-permute-start | bytes 196616 | tf_op jit(solution)/shard_map/ppermute | solution.py:318
  97.7 6.5 %collective-permute-start.13 = (bf16[256,128]{1,0:T(8,128)(2,1)S(1)}, bf16[256,128]{1,0:T(8,128)(2,1)S(1)}, u32[]{:S(2)}, u32[]{:S(2)}) collective-permute-start(bf16[256,128]{1,0:T(8,128)(2,1)S(1)} %step.21.refs_2_.refs_4_.refs_1_), channel_id=1, source_target_pairs={{1,2},{2,1},{3,4},{4,3},{5,6},{6,5},{7,70},{70,7},{71,68},{68,71},... | collective-permute-start | bytes 196616 | tf_op jit(solution)/shard_map/ppermute | solution.py:318
  99.6 3.9 %collective-permute-start.14 = (bf16[256,128]{1,0:T(8,128)(2,1)S(1)}, bf16[256,128]{1,0:T(8,128)(2,1)S(1)}, u32[]{:S(2)}, u32[]{:S(2)}) collective-permute-start(bf16[256,128]{1,0:T(8,128)(2,1)S(1)} %step.21.refs_2_.refs_4_.refs_1_), channel_id=1, source_target_pairs={{0,1},{1,0},{2,3},{3,2},{4,5},{5,4},{6,7},{7,6},{70,71},{71,70},{6... | collective-permute-start | bytes 196616 | tf_op jit(solution)/shard_map/ppermute | solution.py:318
  105.2 7.7 %collective-permute-start.15 = (bf16[256,128]{1,0:T(8,128)(2,1)S(1)}, bf16[256,128]{1,0:T(8,128)(2,1)S(1)}, u32[]{:S(2)}, u32[]{:S(2)}) collective-permute-start(bf16[256,128]{1,0:T(8,128)(2,1)S(1)} %step.22.refs_2_.refs_4_), channel_id=1, source_target_pairs={{1,2},{2,1},{3,4},{4,3},{5,6},{6,5},{7,70},{70,7},{71,68},{68,71},... | collective-permute-start | bytes 196616 | tf_op jit(solution)/shard_map/ppermute | solution.py:318
  108.1 4.0 %collective-permute-start.16 = (bf16[256,128]{1,0:T(8,128)(2,1)S(1)}, bf16[256,128]{1,0:T(8,128)(2,1)S(1)}, u32[]{:S(2)}, u32[]{:S(2)}) collective-permute-start(bf16[256,128]{1,0:T(8,128)(2,1)S(1)} %step.22.refs_2_.refs_4_), channel_id=1, source_target_pairs={{0,1},{1,0},{2,3},{3,2},{4,5},{5,4},{6,7},{7,6},{70,71},{71,70},{6... | collective-permute-start | bytes 196616 | tf_op jit(solution)/shard_map/ppermute | solution.py:318
  113.9 5.8 %copy-start = (bf16[64,256]{1,0:T(8,128)(2,1)S(1)}, bf16[64,256]{1,0:T(8,128)(2,1)}, u32[]{:S(2)}) copy-start(bf16[64,256]{1,0:T(8,128)(2,1)} %refs_12_.11) | copy-start | bytes 98308
  113.9 5.6 %collective-permute-start.17 = (bf16[256,128]{1,0:T(8,128)(2,1)S(1)}, bf16[256,128]{1,0:T(8,128)(2,1)S(1)}, u32[]{:S(2)}, u32[]{:S(2)}) collective-permute-start(bf16[256,128]{1,0:T(8,128)(2,1)S(1)} %step.23.refs_4_), channel_id=1, source_target_pairs={{1,2},{2,1},{3,4},{4,3},{5,6},{6,5},{7,70},{70,7},{71,68},{68,71},... | collective-permute-start | bytes 196616 | tf_op jit(solution)/shard_map/ppermute | solution.py:318
  115.9 3.9 %collective-permute-start.18 = (bf16[256,128]{1,0:T(8,128)(2,1)S(1)}, bf16[256,128]{1,0:T(8,128)(2,1)S(1)}, u32[]{:S(2)}, u32[]{:S(2)}) collective-permute-start(bf16[256,128]{1,0:T(8,128)(2,1)S(1)} %step.23.refs_4_), channel_id=1, source_target_pairs={{0,1},{1,0},{2,3},{3,2},{4,5},{5,4},{6,7},{7,6},{70,71},{71,70},{6... | collective-permute-start | bytes 196616 | tf_op jit(solution)/shard_map/ppermute | solution.py:318
  120.5 7.7 %collective-permute-start.19 = (bf16[256,128]{1,0:T(8,128)(2,1)S(1)}, bf16[256,128]{1,0:T(8,128)(2,1)S(1)}, u32[]{:S(2)}, u32[]{:S(2)}) collective-permute-start(bf16[256,128]{1,0:T(8,128)(2,1)S(1)} %step.24.refs_4_.refs_7_.refs_1_), channel_id=1, source_target_pairs={{1,2},{2,1},{3,4},{4,3},{5,6},{6,5},{7,70},{70,7},{71,68},{68,71},... | collective-permute-start | bytes 196616 | tf_op jit(solution)/shard_map/ppermute | solution.py:318
  123.5 4.0 %collective-permute-start.20 = (bf16[256,128]{1,0:T(8,128)(2,1)S(1)}, bf16[256,128]{1,0:T(8,128)(2,1)S(1)}, u32[]{:S(2)}, u32[]{:S(2)}) collective-permute-start(bf16[256,128]{1,0:T(8,128)(2,1)S(1)} %step.24.refs_4_.refs_7_.refs_1_), channel_id=1, source_target_pairs={{0,1},{1,0},{2,3},{3,2},{4,5},{5,4},{6,7},{7,6},{70,71},{71,70},{6... | collective-permute-start | bytes 196616 | tf_op jit(solution)/shard_map/ppermute | solution.py:318
  129.2 7.2 %collective-permute-start.21 = (bf16[256,128]{1,0:T(8,128)(2,1)S(1)}, bf16[256,128]{1,0:T(8,128)(2,1)S(1)}, u32[]{:S(2)}, u32[]{:S(2)}) collective-permute-start(bf16[256,128]{1,0:T(8,128)(2,1)S(1)} %step.25.refs_4_.refs_7_.refs_1_), channel_id=1, source_target_pairs={{1,2},{2,1},{3,4},{4,3},{5,6},{6,5},{7,70},{70,7},{71,68},{68,71},... | collective-permute-start | bytes 196616 | tf_op jit(solution)/shard_map/ppermute | solution.py:318
  131.1 4.6 %collective-permute-start.22 = (bf16[256,128]{1,0:T(8,128)(2,1)S(1)}, bf16[256,128]{1,0:T(8,128)(2,1)S(1)}, u32[]{:S(2)}, u32[]{:S(2)}) collective-permute-start(bf16[256,128]{1,0:T(8,128)(2,1)S(1)} %step.25.refs_4_.refs_7_.refs_1_), channel_id=1, source_target_pairs={{0,1},{1,0},{2,3},{3,2},{4,5},{5,4},{6,7},{7,6},{70,71},{71,70},{6... | collective-permute-start | bytes 196616 | tf_op jit(solution)/shard_map/ppermute | solution.py:318
  137.4 7.0 %collective-permute-start.23 = (bf16[256,128]{1,0:T(8,128)(2,1)S(1)}, bf16[256,128]{1,0:T(8,128)(2,1)S(1)}, u32[]{:S(2)}, u32[]{:S(2)}) collective-permute-start(bf16[256,128]{1,0:T(8,128)(2,1)S(1)} %step.26.refs_4_.refs_7_.refs_1_), channel_id=1, source_target_pairs={{1,2},{2,1},{3,4},{4,3},{5,6},{6,5},{7,70},{70,7},{71,68},{68,71},... | collective-permute-start | bytes 196616 | tf_op jit(solution)/shard_map/ppermute | solution.py:318
  139.7 4.0 %collective-permute-start.24 = (bf16[256,128]{1,0:T(8,128)(2,1)S(1)}, bf16[256,128]{1,0:T(8,128)(2,1)S(1)}, u32[]{:S(2)}, u32[]{:S(2)}) collective-permute-start(bf16[256,128]{1,0:T(8,128)(2,1)S(1)} %step.26.refs_4_.refs_7_.refs_1_), channel_id=1, source_target_pairs={{0,1},{1,0},{2,3},{3,2},{4,5},{5,4},{6,7},{7,6},{70,71},{71,70},{6... | collective-permute-start | bytes 196616 | tf_op jit(solution)/shard_map/ppermute | solution.py:318
  145.5 7.2 %collective-permute-start.25 = (bf16[256,128]{1,0:T(8,128)(2,1)S(1)}, bf16[256,128]{1,0:T(8,128)(2,1)S(1)}, u32[]{:S(2)}, u32[]{:S(2)}) collective-permute-start(bf16[256,128]{1,0:T(8,128)(2,1)S(1)} %step.27.refs_4_.refs_7_.refs_1_), channel_id=1, source_target_pairs={{1,2},{2,1},{3,4},{4,3},{5,6},{6,5},{7,70},{70,7},{71,68},{68,71},... | collective-permute-start | bytes 196616 | tf_op jit(solution)/shard_map/ppermute | solution.py:318
  147.9 4.0 %collective-permute-start.26 = (bf16[256,128]{1,0:T(8,128)(2,1)S(1)}, bf16[256,128]{1,0:T(8,128)(2,1)S(1)}, u32[]{:S(2)}, u32[]{:S(2)}) collective-permute-start(bf16[256,128]{1,0:T(8,128)(2,1)S(1)} %step.27.refs_4_.refs_7_.refs_1_), channel_id=1, source_target_pairs={{0,1},{1,0},{2,3},{3,2},{4,5},{5,4},{6,7},{7,6},{70,71},{71,70},{6... | collective-permute-start | bytes 196616 | tf_op jit(solution)/shard_map/ppermute | solution.py:318
  153.7 7.0 %collective-permute-start.27 = (bf16[256,128]{1,0:T(8,128)(2,1)S(1)}, bf16[256,128]{1,0:T(8,128)(2,1)S(1)}, u32[]{:S(2)}, u32[]{:S(2)}) collective-permute-start(bf16[256,128]{1,0:T(8,128)(2,1)S(1)} %step.28.refs_4_.refs_7_.refs_1_), channel_id=1, source_target_pairs={{1,2},{2,1},{3,4},{4,3},{5,6},{6,5},{7,70},{70,7},{71,68},{68,71},... | collective-permute-start | bytes 196616 | tf_op jit(solution)/shard_map/ppermute | solution.py:318
  155.9 4.0 %collective-permute-start.28 = (bf16[256,128]{1,0:T(8,128)(2,1)S(1)}, bf16[256,128]{1,0:T(8,128)(2,1)S(1)}, u32[]{:S(2)}, u32[]{:S(2)}) collective-permute-start(bf16[256,128]{1,0:T(8,128)(2,1)S(1)} %step.28.refs_4_.refs_7_.refs_1_), channel_id=1, source_target_pairs={{0,1},{1,0},{2,3},{3,2},{4,5},{5,4},{6,7},{7,6},{70,71},{71,70},{6... | collective-permute-start | bytes 196616 | tf_op jit(solution)/shard_map/ppermute | solution.py:318
  161.7 7.2 %collective-permute-start.29 = (bf16[256,128]{1,0:T(8,128)(2,1)S(1)}, bf16[256,128]{1,0:T(8,128)(2,1)S(1)}, u32[]{:S(2)}, u32[]{:S(2)}) collective-permute-start(bf16[256,128]{1,0:T(8,128)(2,1)S(1)} %step.29.refs_4_.refs_7_.refs_1_), channel_id=1, source_target_pairs={{1,2},{2,1},{3,4},{4,3},{5,6},{6,5},{7,70},{70,7},{71,68},{68,71},... | collective-permute-start | bytes 196616 | tf_op jit(solution)/shard_map/ppermute | solution.py:318
  164.1 4.0 %collective-permute-start.30 = (bf16[256,128]{1,0:T(8,128)(2,1)S(1)}, bf16[256,128]{1,0:T(8,128)(2,1)S(1)}, u32[]{:S(2)}, u32[]{:S(2)}) collective-permute-start(bf16[256,128]{1,0:T(8,128)(2,1)S(1)} %step.29.refs_4_.refs_7_.refs_1_), channel_id=1, source_target_pairs={{0,1},{1,0},{2,3},{3,2},{4,5},{5,4},{6,7},{7,6},{70,71},{71,70},{6... | collective-permute-start | bytes 196616 | tf_op jit(solution)/shard_map/ppermute | solution.py:318
  169.9 7.0 %collective-permute-start.31 = (bf16[256,128]{1,0:T(8,128)(2,1)S(1)}, bf16[256,128]{1,0:T(8,128)(2,1)S(1)}, u32[]{:S(2)}, u32[]{:S(2)}) collective-permute-start(bf16[256,128]{1,0:T(8,128)(2,1)S(1)} %step.30.refs_4_.refs_7_), channel_id=1, source_target_pairs={{1,2},{2,1},{3,4},{4,3},{5,6},{6,5},{7,70},{70,7},{71,68},{68,71},... | collective-permute-start | bytes 196616 | tf_op jit(solution)/shard_map/ppermute | solution.py:318
  172.1 4.0 %collective-permute-start.32 = (bf16[256,128]{1,0:T(8,128)(2,1)S(1)}, bf16[256,128]{1,0:T(8,128)(2,1)S(1)}, u32[]{:S(2)}, u32[]{:S(2)}) collective-permute-start(bf16[256,128]{1,0:T(8,128)(2,1)S(1)} %step.30.refs_4_.refs_7_), channel_id=1, source_target_pairs={{0,1},{1,0},{2,3},{3,2},{4,5},{5,4},{6,7},{7,6},{70,71},{71,70},{6... | collective-permute-start | bytes 196616 | tf_op jit(solution)/shard_map/ppermute | solution.py:318
  175.3 0.9 copy-start.3
  175.3 0.9 copy-start.5
  176.2 0.8 copy-start.7
  178.0 7.7 %collective-permute-start.33 = (bf16[2,256,128]{2,1,0:T(8,128)(2,1)S(1)}, bf16[2,256,128]{2,1,0:T(8,128)(2,1)S(1)}, u32[]{:S(2)}, u32[]{:S(2)}) collective-permute-start(bf16[2,256,128]{2,1,0:T(8,128)(2,1)S(1)} %pad_maximum_fusion.3), channel_id=1, source_target_pairs={{0,64},{1,65},{2,66},{3,67},{4,68},{5,69},{6,70},{7,71},{16,80},{1... | collective-permute-start | bytes 393224 | tf_op jit(solution)/shard_map/ppermute | solution.py:421
  (3 other events, 2.0 us)
